TPU v7x, 32 devices: a whole 2x2x4 slice. The times are simulated.
32 devices in a mesh: seq: 16 (over z, y, x), head: 2 (over core).
Axes of the slice: x: 2, y: 2, z: 4, core: 2. Of those that a mesh axis runs over, the one named last changes fastest.
Arguments:
- queries: bfloat16 [4096, 1024], P('seq', 'head'), may hold values from -6 to 6
- key_rows: bfloat16 [4096, 1024], P('seq', 'head'), may hold values from -6 to 6
- values: bfloat16 [4096, 1024], P('seq', 'head'), may hold values from -12 to 12
- cotangent: bfloat16 [4096, 1024], P('seq', 'head'), may hold values from -12 to 12
- carried_state: float32 [8, 128, 128], P('head'), may hold values from -192 to 192
- norm_gain: float32 [1024], P('head'), may hold values from 0.25 to 1.75
Outputs:
- attended: bfloat16 [4096, 1024], P('seq', 'head')
- gradient_queries: bfloat16 [4096, 1024], P('seq', 'head')
- gradient_keys: bfloat16 [4096, 1024], P('seq', 'head')
- grad_value: bfloat16 [4096, 1024], P('seq', 'head')
- grad_state: float32 [8, 128, 128], P('head')
- grad_gain: float32 [1024], P('head')
All inputs are finite; a program needn't handle non-finite values.
Results may differ from a plain program's by a relative error of at most 0.0065.
Values may be sent and summed in bfloat16 or wider, within the bound.
No kernel may reach another device: no remote copies, remote signals or barrier semaphores. Data moves between devices by JAX's collectives and lax.ppermute only.
A program may use at most 64 MiB of HBM per device.

v0:
```python
import jax
import jax.numpy as jnp
from jax import lax
from jax.sharding import PartitionSpec as P

EPS = 1e-05


def prefix(x, axis, combine, identity, reverse):
    count, mine = (lax.axis_size(axis), lax.axis_index(axis))
    everything = lax.all_gather(x, axis)
    start = jnp.broadcast_to(jnp.asarray(identity, x.dtype), x.shape)

    def lap(k, before):
        at = count - 1 - k if reverse else k
        reached = at > mine if reverse else at < mine
        new = combine(before, everything[at])
        return jnp.where(reached, new, before)

    return lax.fori_loop(0, count, lap, start)


def add_states(earlier, later):
    return earlier + later


def chain_rounded(states, offset, reverse):
    summed = prefix(states, "seq", add_states, jnp.zeros_like(states), reverse)
    return (offset + summed).astype(jnp.bfloat16)


def on_device(queries, key_rows, values, cotangent, carried_state, norm_gain):
    length, width = queries.shape
    heads = carried_state.shape[0]
    head_dim = carried_state.shape[1]
    total_width = width * lax.axis_size("head")
    head_queries = queries.reshape(length, heads, head_dim)
    head_keys = key_rows.reshape(length, heads, head_dim)
    head_values = values.reshape(length, heads, head_dim)
    causal_mask = jnp.arange(length)[:, None] >= jnp.arange(length)[None, :]
    gain_heads = norm_gain.reshape(heads, head_dim)
    local_state = jnp.einsum(
        "lhd,lhe->hde", head_keys, head_values, preferred_element_type=jnp.float32
    )
    preceding_part = chain_rounded(local_state, carried_state, False)
    score_matrix = jnp.einsum(
        "ftz,ytz->tfy", head_queries, head_keys, preferred_element_type=jnp.float32
    )
    score_matrix = jnp.where(causal_mask, score_matrix, jnp.float32(0.0)).astype(jnp.bfloat16)
    unnormed = jnp.einsum(
        "hlm,mhe->lhe", score_matrix, head_values, preferred_element_type=jnp.float32
    )
    unnormed = unnormed + jnp.einsum(
        "lhd,hde->lhe", head_queries, preceding_part, preferred_element_type=jnp.float32
    )
    cot_wide = cotangent.reshape(length, heads, head_dim).astype(jnp.float32)
    scaled = cot_wide * gain_heads
    square_part = jnp.sum(unnormed * unnormed, axis=(1, 2))
    dot_part = jnp.sum(scaled * unnormed, axis=(1, 2))
    square_sum, dot_sum = lax.psum((square_part, dot_part), "head")
    norm_scale = jnp.sqrt(square_sum / total_width + EPS)[:, None, None]
    normed = unnormed / norm_scale
    attended = (gain_heads * normed).astype(jnp.bfloat16).reshape(length, width)
    grad_unnormed = (
        (scaled - normed * (dot_sum[:, None, None] / (total_width * norm_scale))) / norm_scale
    ).astype(jnp.bfloat16)
    gain_part = jnp.sum(cot_wide * normed, axis=0).reshape(width)
    grad_local = jnp.einsum(
        "lhd,lhe->hde", head_queries, grad_unnormed, preferred_element_type=jnp.float32
    )
    following_part = chain_rounded(grad_local, jnp.zeros_like(grad_local), True)
    grad_state, grad_gain = lax.psum((grad_local, gain_part), "seq")
    blended_output = jnp.einsum(
        "lhe,mhe->hlm", grad_unnormed, head_values, preferred_element_type=jnp.float32
    )
    blended_output = jnp.where(causal_mask, blended_output, jnp.float32(0.0)).astype(jnp.bfloat16)
    gradient_queries = jnp.einsum(
        "krx,xkn->rkn", blended_output, head_keys, preferred_element_type=jnp.float32
    )
    gradient_queries = gradient_queries + jnp.einsum(
        "xif,iuf->xiu", grad_unnormed, preceding_part, preferred_element_type=jnp.float32
    )
    gradient_keys = jnp.einsum(
        "nox,ony->xny", blended_output, head_queries, preferred_element_type=jnp.float32
    )
    gradient_keys = gradient_keys + jnp.einsum(
        "yon,otn->yot", head_values, following_part, preferred_element_type=jnp.float32
    )
    grad_value = jnp.einsum(
        "nou,onk->unk", score_matrix, grad_unnormed, preferred_element_type=jnp.float32
    )
    grad_value = grad_value + jnp.einsum(
        "klj,ljr->klr", head_keys, following_part, preferred_element_type=jnp.float32
    )
    return (
        attended,
        gradient_queries.astype(jnp.bfloat16).reshape(length, width),
        gradient_keys.astype(jnp.bfloat16).reshape(length, width),
        grad_value.astype(jnp.bfloat16).reshape(length, width),
        grad_state,
        grad_gain,
    )


def solution(mesh):
    in_specs = (
        P("seq", "head"),
        P("seq", "head"),
        P("seq", "head"),
        P("seq", "head"),
        P("head", None, None),
        P("head"),
    )
    out_specs = (
        P("seq", "head"),
        P("seq", "head"),
        P("seq", "head"),
        P("seq", "head"),
        P("head", None, None),
        P("head"),
    )
    return jax.shard_map(
        on_device, mesh=mesh, in_specs=in_specs, out_specs=out_specs, check_vma=False
    )
```

profile of v0, /device:TPU:0, one launch (start us, length us, event | category | flops | bytes accessed | tf_op | source)
XLA Modules:
  0.0 330.7 jit_solution(10756838758852131324)
XLA Ops:
  7.2 1.1 copy.105
  8.4 1.9 fusion.11
  10.3 1.1 copy.42
  11.5 1.3 fusion
  12.8 1.3 convolution_bitcast_fusion.5
  14.0 76.2 %all-gather.5.cloned.1.call-done = f32[64,128,128]{2,1,0:T(8,128)} async-done(((f32[4,128,128]{2,1,0:T(8,128)}), f32[64,128,128]{2,1,0:T(8,128)}) %all-gather.5.cloned.1.call-update) | async-done | bytes 4194320 | tf_op jit(solution)/shard_map/all_gather | solution.py:11
  90.2 17.0 %while.30 = (s32[]{:T(128)}, f32[4,128,128]{2,1,0:T(8,128)S(1)}, s32[]{:T(128)}, f32[16,4,128,128]{3,2,1,0:T(8,128)}, s32[]{:T(128)}, /*index=5*/s32[]{:T(128)}) while((s32[]{:T(128)}, f32[4,128,128]{2,1,0:T(8,128)S(1)}, s32[]{:T(128)}, f32[16,4,128,128]{3,2,1,0:T(8,128)}, s32[]{:T(128)}, /*index=5*/s32[]{:T(128)}) %tuple.90), condition=%wide.region_1.2_spmd.clone, body=%wide.region_0.1_spmd.clone.sunk | while | flops 196612 | bytes 786533 | solution.py:20
  90.2 1.0 add_select_fusion.4
  91.2 1.0 add_select_fusion.4
  92.3 1.0 add_select_fusion.4
  93.4 1.0 add_select_fusion.4
  94.4 1.0 add_select_fusion.4
  95.5 1.0 add_select_fusion.4
  96.6 1.0 add_select_fusion.4
  97.6 1.0 add_select_fusion.4
  98.7 1.0 add_select_fusion.4
  99.7 1.0 add_select_fusion.4
  100.8 1.0 add_select_fusion.4
  101.9 1.0 add_select_fusion.4
  102.9 1.0 add_select_fusion.4
  104.0 1.0 add_select_fusion.4
  105.1 1.0 add_select_fusion.4
  106.1 1.0 add_select_fusion.4
  107.6 2.5 psum.28
  110.3 2.5 psum.29
  116.3 1.2 fusion.1
  118.9 40.0 %psum.31 = f32[512]{0:T(512)} all-reduce(f32[512]{0:T(512)S(1)} %bitcast.127), channel_id=1, replica_groups=mesh['seq'=16,'head'=2] {'seq'}, use_global_device_ids=true, to_apply=%region_10.11 | all-reduce | flops 512 | bytes 4096 | tf_op jit(solution)/shard_map/psum | solution.py:72
  159.4 66.7 %all-reduce.2.cloned.1.call-done = f32[4,128,128]{1,2,0:T(8,128)} async-done(((f32[4,128,128]{1,2,0:T(8,128)}), f32[4,128,128]{1,2,0:T(8,128)}) %all-reduce.2.cloned.1.call-update) | async-done | bytes 262160 | tf_op jit(solution)/shard_map/psum | solution.py:72
  226.0 1.8 copy.57
  227.8 77.1 %all-gather.7.cloned.1.call-done = f32[64,128,128]{2,1,0:T(8,128)} async-done(((f32[4,128,128]{2,1,0:T(8,128)}), f32[64,128,128]{2,1,0:T(8,128)}) %all-gather.7.cloned.1.call-update) | async-done | bytes 4194320 | tf_op jit(solution)/shard_map/all_gather | solution.py:11
  304.9 17.1 %while.31 = (s32[]{:T(128)}, f32[4,128,128]{2,1,0:T(8,128)S(1)}, s32[]{:T(128)}, f32[16,4,128,128]{3,2,1,0:T(8,128)}, s32[]{:T(128)}, /*index=5*/s32[]{:T(128)}, s32[]{:T(128)}, s32[]{:T(128)}) while((s32[]{:T(128)}, f32[4,128,128]{2,1,0:T(8,128)S(1)}, s32[]{:T(128)}, f32[16,4,128,128]{3,2,1,0:T(8,128)}, s32[]{:T(128)}, ...), condition=%wide.region_7.8_spmd.clone, body=%wide.region_6.7_spmd.clone.sunk | while | flops 196616 | bytes 786595 | solution.py:20
  304.9 1.0 add_select_fusion.5
  306.0 1.0 add_select_fusion.5
  307.0 1.0 add_select_fusion.5
  308.1 1.0 add_select_fusion.5
  309.2 1.0 add_select_fusion.5
  310.3 1.0 add_select_fusion.5
  311.3 1.0 add_select_fusion.5
  312.4 1.0 add_select_fusion.5
  313.5 1.0 add_select_fusion.5
  314.5 1.0 add_select_fusion.5
  315.6 1.0 add_select_fusion.5
  316.7 1.0 add_select_fusion.5
  317.7 1.0 add_select_fusion.5
  318.8 1.0 add_select_fusion.5
  319.9 1.0 add_select_fusion.5
  321.0 1.0 add_select_fusion.5
  323.4 0.8 copy.55
  (40 shorter events, 7.4 us)
Async XLA Ops:
  7.2 4.3 %copy-start = (bf16[256,512]{1,0:T(8,128)(2,1)S(1)}, bf16[256,512]{1,0:T(8,128)(2,1)}, u32[]{:S(2)}) copy-start(bf16[256,512]{1,0:T(8,128)(2,1)} %param.10) | copy-start | bytes 786436
  7.2 83.0 %all-gather.5.cloned.1.call-start = ((), (), s32[]{:S(2)}) async-start(), calls=%async_computation.1 | async-start | bytes 4456448 | tf_op jit(solution)/shard_map/all_gather | solution.py:11
  8.3 98.9 %copy-start.4 = (f32[4,128,128]{2,1,0:T(8,128)S(1)}, f32[4,128,128]{2,1,0:T(8,128)}, u32[]{:S(2)}) copy-start(f32[4,128,128]{2,1,0:T(8,128)} %param.14) | copy-start | bytes 786436
  11.5 95.7 %copy-start.5 = (pred[256,256]{1,0:T(8,128)(4,1)}, pred[256,256]{1,0:T(8,128)(4,1)S(1)}, u32[]{:S(2)}) copy-start(pred[256,256]{1,0:T(8,128)(4,1)S(1)} %iota_compare_fusion) | copy-start | bytes 196612
  11.5 98.6 %copy-start.6 = (f32[512]{0:T(512)S(1)}, f32[512]{0:T(512)}, u32[]{:S(2)}) copy-start(f32[512]{0:T(512)} %param.15) | copy-start | bytes 6148
  107.2 9.2 %copy-start.1 = (bf16[256,512]{1,0:T(8,128)(2,1)S(1)}, bf16[256,512]{1,0:T(8,128)(2,1)}, u32[]{:S(2)}) copy-start(bf16[256,512]{1,0:T(8,128)(2,1)} %param.12) | copy-start | bytes 786436
  113.2 0.9 copy-start.2
  114.0 112.0 %all-reduce.2.cloned.1.call-start = ((), (), s32[]{:S(2)}) async-start(), calls=%async_computation | async-start | bytes 524288 | tf_op jit(solution)/shard_map/psum | solution.py:72
  114.8 190.2 %all-gather.7.cloned.1.call-start = ((), (), s32[]{:S(2)}) async-start(), calls=%async_computation.2 | async-start | bytes 4456448 | tf_op jit(solution)/shard_map/all_gather | solution.py:11
  118.1 203.9 %copy-start.3 = (bf16[256,512]{1,0:T(8,128)(2,1)S(1)}, bf16[256,512]{1,0:T(8,128)(2,1)}, u32[]{:S(2)}) copy-start(bf16[256,512]{1,0:T(8,128)(2,1)} %param.11) | copy-start | bytes 786436
Sparse Core Ops, SparseCore 0:
  11.4 78.7 all-gather.4
  120.6 105.3 all-reduce.1
  229.8 75.0 all-gather.6
where the time goes:
time: 332 us; the launch traced here: 331 us
  waiting for transfers between devices  221 us (67%)
  blocking collectives  44.9 us (14%)
  other arithmetic  33.8 us (10%)
  between operations  14 us (4%)
  local copies, waits for them, and re-layouts  8.25 us (2%)
  matrix products  7.66 us (2%)
    all_gather x2, waiting for transfers between devices, prefix(): everything = lax.all_gather(x, axis)  153 us
    psum x1, waiting for transfers between devices, on_device(): grad_state, grad_gain = lax.psum((grad_local, gain_part), 'seq')  66.7 us
    psum x1, blocking collectives, on_device(): grad_state, grad_gain = lax.psum((grad_local, gain_part), 'seq')  40 us
    select_n x32, other arithmetic, lap(): return jnp.where(reached, new, before)  33.3 us
  transfers between devices with their start and end apart: 3, of which 3 were waited for; matrix products, arithmetic and copies ran while one was open for 3% of the time, Pallas kernels for 0%

commit v1 on v0

v1 whole, which is shorter than its diff:
```python
import functools

import jax
import jax.numpy as jnp
from jax import lax
from jax.experimental import pallas as pl
from jax.experimental.pallas import tpu as pltpu
from jax.sharding import PartitionSpec as P

EPS = 1e-05
F32 = jnp.float32
BF16 = jnp.bfloat16


def dot(a, b, ca, cb):
    return lax.dot_general(a, b, (((ca,), (cb,)), ((), ())), preferred_element_type=F32)


def call(kernel, outs, flops, nbytes):
    return pl.pallas_call(
        kernel,
        out_shape=outs,
        cost_estimate=pl.CostEstimate(flops=flops, bytes_accessed=nbytes, transcendentals=0),
    )


def cols(h, dim):
    return slice(h * dim, (h + 1) * dim)


def state_kernel(heads, dim, k_ref, v_ref, out_ref):
    for h in range(heads):
        c = cols(h, dim)
        out_ref[c, :] = dot(k_ref[:, c], v_ref[:, c], 0, 0).astype(BF16)


def causal(length):
    rows = lax.broadcasted_iota(jnp.int32, (length, length), 0)
    return rows >= lax.broadcasted_iota(jnp.int32, (length, length), 1)


def scores_kernel(heads, dim, q_ref, k_ref, v_ref, local_ref):
    mask = causal(q_ref.shape[0])
    for h in range(heads):
        c = cols(h, dim)
        scores = jnp.where(mask, dot(q_ref[:, c], k_ref[:, c], 1, 1), 0.0).astype(BF16)
        local_ref[:, c] = dot(scores, v_ref[:, c], 1, 0)


def gathered(parts, rows, reverse):
    mine = lax.axis_index("seq")
    total = None
    for bit, part in enumerate(parts):
        reached = ((mine >> bit) & 1) == (0 if reverse else 1)
        term = jnp.where(reached, part[rows, :].astype(F32), 0.0)
        total = term if total is None else total + term
    return total


def unnormed_kernel(heads, dim, rounds, *refs):
    parts = refs[:rounds]
    q_ref, local_ref, cot_ref, carried_ref, gain_ref = refs[rounds : rounds + 5]
    un_ref, prefix_ref, sums_ref = refs[rounds + 5 :]
    square = None
    for h in range(heads):
        c = cols(h, dim)
        prefix = carried_ref[h]
        if parts:
            prefix = prefix + gathered(parts, c, False)
        prefix = prefix.astype(BF16)
        prefix_ref[c, :] = prefix
        un = local_ref[:, c] + dot(q_ref[:, c], prefix, 1, 0)
        un_ref[:, c] = un
        scaled = cot_ref[:, c].astype(F32) * gain_ref[:, c]
        square = un * un if square is None else square + un * un
        product = scaled * un if h == 0 else product + scaled * un
    square = jnp.sum(square, axis=1, keepdims=True)
    product = jnp.sum(product, axis=1, keepdims=True)
    lane = lax.broadcasted_iota(jnp.int32, sums_ref.shape, 1)
    sums_ref[...] = jnp.where(lane < sums_ref.shape[1] // 2, square, product)


def norm_kernel(heads, dim, width, sums_ref, other_ref, un_ref, cot_ref, gain_ref, q_ref, att_ref, gun_ref, msg_ref):
    sums = sums_ref[...] + other_ref[...]
    half = sums.shape[1] // 2
    inverse = 1.0 / jnp.sqrt(sums[:, 0:1] / width + EPS)
    factor = (sums[:, half : half + 1] * inverse) / width * inverse * inverse
    for h in range(heads):
        c = cols(h, dim)
        un = un_ref[:, c]
        cot = cot_ref[:, c].astype(F32)
        gain = gain_ref[:, c]
        normed = un * inverse
        att_ref[:, c] = (gain * normed).astype(BF16)
        gun = (cot * gain * inverse - un * factor).astype(BF16)
        gun_ref[:, c] = gun
        msg_ref[c, :] = dot(q_ref[:, c], gun, 0, 0).astype(BF16)
        row = heads * dim + h
        msg_ref[row : row + 1, :] = jnp.sum(cot * normed, axis=0, keepdims=True).astype(BF16)
    rest = heads * dim + heads
    msg_ref[rest:, :] = jnp.zeros((msg_ref.shape[0] - rest, dim), BF16)


def local_grad_kernel(heads, dim, q_ref, k_ref, v_ref, gun_ref, prefix_ref, gq_ref, gk_ref, gv_ref):
    mask = causal(q_ref.shape[0])
    for h in range(heads):
        c = cols(h, dim)
        q, k, v, gun = q_ref[:, c], k_ref[:, c], v_ref[:, c], gun_ref[:, c]
        mixed = jnp.where(mask, dot(gun, v, 1, 1), 0.0).astype(BF16)
        scores = jnp.where(mask, dot(q, k, 1, 1), 0.0).astype(BF16)
        gq_ref[:, c] = (dot(mixed, k, 1, 0) + dot(gun, prefix_ref[c, :], 1, 1)).astype(BF16)
        gk_ref[:, c] = dot(mixed, q, 0, 0)
        gv_ref[:, c] = dot(scores, gun, 0, 0)


def final_kernel(heads, dim, rounds, *refs):
    parts = refs[:rounds]
    total_ref, k_ref, v_ref, gk_ref, gv_ref = refs[rounds : rounds + 5]
    gk_out, gv_out, state_out, gain_out = refs[rounds + 5 :]
    for h in range(heads):
        c = cols(h, dim)
        total = total_ref[c, :].astype(F32)
        gk, gv = gk_ref[:, c], gv_ref[:, c]
        row = slice(heads * dim + h, heads * dim + h + 1)
        gain = total_ref[row, :].astype(F32)
        if parts:
            suffix = gathered(parts, c, True).astype(BF16)
            gk = gk + dot(v_ref[:, c], suffix, 1, 1)
            gv = gv + dot(k_ref[:, c], suffix, 1, 0)
            total = total + parts[-1][c, :].astype(F32)
            gain = gain + parts[-1][row, :].astype(F32)
        gk_out[:, c] = gk.astype(BF16)
        gv_out[:, c] = gv.astype(BF16)
        state_out[h] = total
        gain_out[:, c] = gain


def exchange(message, count):
    received = []
    distance = 1
    while distance < count:
        if received:
            message = message + received[-1]
        pairs = [(i, i ^ distance) for i in range(count)]
        received.append(lax.ppermute(message, "seq", pairs))
        distance *= 2
    return message, received


def on_device(queries, key_rows, values, cotangent, carried_state, norm_gain):
    length, width = queries.shape
    heads, dim = carried_state.shape[:2]
    count = lax.axis_size("seq")
    head_count = lax.axis_size("head")
    assert count & (count - 1) == 0
    assert width == heads * dim
    total_width = width * head_count
    gain = norm_gain.reshape(1, width)
    shape = jax.ShapeDtypeStruct
    tokens_bf = shape((length, width), BF16)
    tokens_f32 = shape((length, width), F32)
    block = 2 * length * dim * dim * heads
    square = 2 * length * length * dim * heads
    size = length * width * 2
    state_size = heads * dim * dim * 2

    state = call(
        functools.partial(state_kernel, heads, dim),
        shape((heads * dim, dim), BF16), block, 2 * size + state_size,
    )(key_rows, values)
    _, received = exchange(state, count)
    local = call(
        functools.partial(scores_kernel, heads, dim), tokens_f32, 2 * square, 5 * size,
    )(queries, key_rows, values)
    rounds = len(received)
    unnormed, prefix, sums = call(
        functools.partial(unnormed_kernel, heads, dim, rounds),
        (tokens_f32, shape((heads * dim, dim), BF16), shape((length, 128), F32)),
        block, 6 * size + (rounds + 3) * state_size,
    )(*received, queries, local, cotangent, carried_state, gain)
    other = jnp.zeros_like(sums)
    partner = sums
    for step in range(1, head_count):
        partner = lax.ppermute(partner, "head", [(i, (i + 1) % head_count) for i in range(head_count)])
        other = other + partner if step > 1 else partner
    rows = heads * dim + -(-heads // 16) * 16
    attended, grad_unnormed, message = call(
        functools.partial(norm_kernel, heads, dim, total_width),
        (tokens_bf, tokens_bf, shape((rows, dim), BF16)), block, 6 * size + state_size,
    )(sums, other, unnormed, cotangent, gain, queries)
    message, received = exchange(message, count)
    grad_q, local_k, local_v = call(
        functools.partial(local_grad_kernel, heads, dim),
        (tokens_bf, tokens_f32, tokens_f32), 5 * square + block, 9 * size + state_size,
    )(queries, key_rows, values, grad_unnormed, prefix)
    grad_k, grad_v, grad_state, grad_gain = call(
        functools.partial(final_kernel, heads, dim, rounds),
        (tokens_bf, tokens_bf, shape((heads, dim, dim), F32), shape((1, width), F32)),
        2 * block, 8 * size + (rounds + 2) * state_size,
    )(*received, message, key_rows, values, local_k, local_v)
    return attended, grad_q, grad_k, grad_v, grad_state, grad_gain.reshape(width)


def solution(mesh):
    tokens = P("seq", "head")
    specs = (P("head", None, None), P("head"))
    return jax.shard_map(
        on_device,
        mesh=mesh,
        in_specs=(tokens,) * 4 + specs,
        out_specs=(tokens,) * 4 + specs,
        check_vma=False,
    )
```

time: 332 us -> 66.3 us (0.20)
  waiting for transfers between devices: 221 us -> 26.4 us
  blocking collectives: 44.9 us -> 0 us
  other arithmetic: 33.8 us -> 2.14 us
  starting transfers between devices: 0.08 us -> 16.3 us
  Pallas kernels: 0 us -> 16.1 us
  between operations: 14 us -> 0.69 us
  matrix products: 7.66 us -> 0 us
  local copies, waits for them, and re-layouts: 8.25 us -> 4.41 us
    all_gather x2 -> x0, waiting for transfers between devices: 153 us -> none  [prefix(): everything = lax.all_gather(x, axis)]
    psum x1 -> x0, waiting for transfers between devices: 66.7 us -> none  [on_device(): grad_state, grad_gain = lax.psum((grad_local, gain_part), 'seq')]
    psum x3 -> x0, blocking collectives: 44.9 us -> none  [the longest x1 40 us: on_device(): grad_state, grad_gain = lax.psum((grad_local, gain_part), 'seq')]
    select_n x32 -> x0, other arithmetic: 33.3 us -> none  [lap(): return jnp.where(reached, new, before)]
    ppermute x0 -> x9, waiting for transfers between devices: none -> 26.4 us  [the longest x8 24.8 us: exchange(): received.append(lax.ppermute(message, 'seq', pairs))]
    ppermute x0 -> x9, starting transfers between devices: none -> 16.3 us  [the longest x8 16.3 us: exchange(): received.append(lax.ppermute(message, 'seq', pairs))]
    pallas_call x0 -> x6, Pallas kernels: none -> 16.1 us  [the longest x1 3.62 us: on_device(): call(functools.partial(local_grad_kernel, heads, dim), (tokens_bf, tokens...]
    dot_general x12 -> x0, matrix products: 7.66 us -> none  [the longest x1 1.91 us: on_device(): jnp.einsum('lhd,lhe->hde', head_keys, head_values, preferred_element_type...]
  transfers between devices with their start and end apart: 3 -> 9, of which waited for: 3 -> 9; matrix products, arithmetic and copies ran while one was open for 3% -> 0% of each run, Pallas kernels for 0% -> 9%
where the time goes in v1:
time: 66.3 us; the launch traced here: 66 us
  waiting for transfers between devices  26.4 us (40%)
  starting transfers between devices  16.3 us (25%)
  Pallas kernels  16.1 us (24%)
  local copies, waits for them, and re-layouts  4.41 us (7%)
  other arithmetic  2.14 us (3%)
  between operations  0.69 us (1%)
    ppermute x8, waiting for transfers between devices, exchange(): received.append(lax.ppermute(message, 'seq', pairs))  24.8 us
    ppermute x8, starting transfers between devices, exchange(): received.append(lax.ppermute(message, 'seq', pairs))  16.3 us
    unnamed x20, local copies, waits for them, and re-layouts  4.41 us
    pallas_call x1, Pallas kernels, on_device(): call(functools.partial(local_grad_kernel, heads, dim), (tokens_bf, tokens...  3.62 us
    pallas_call x1, Pallas kernels, on_device(): call(functools.partial(final_kernel, heads, dim, rounds), (tokens_bf, tok...  2.8 us
    pallas_call x1, Pallas kernels, on_device(): call(functools.partial(unnormed_kernel, heads, dim, rounds), (tokens_f32,...  2.63 us
    pallas_call x1, Pallas kernels, on_device(): call(functools.partial(scores_kernel, heads, dim), tokens_f32, 2 * square...  2.57 us
    pallas_call x1, Pallas kernels, on_device(): call(functools.partial(norm_kernel, heads, dim, total_width), (tokens_bf,...  2.52 us
  transfers between devices with their start and end apart: 9, of which 9 were waited for; matrix products, arithmetic and copies ran while one was open for 0% of the time, Pallas kernels for 9%

profile of v1, /device:TPU:0, one launch (start us, length us, event | category | flops | bytes accessed | tf_op | source)
XLA Modules:
  0.0 66.0 jit_solution(3225932678431196314)
XLA Ops:
  0.6 2.0 %shard_map.109 = bf16[512,128]{1,0:T(8,128)(2,1)} custom-call(bf16[256,512]{1,0:T(8,128)(2,1)} %refs_5_.1, bf16[256,512]{1,0:T(8,128)(2,1)} %refs_6_.3), custom_call_target="tpu_custom_call" | custom-call | flops 33554432 | bytes 655360 | tf_op jit(solution)/shard_map/pallas_call | solution.py:167
  2.6 2.9 %collective-permute-start = (bf16[512,128]{1,0:T(8,128)(2,1)}, bf16[512,128]{1,0:T(8,128)(2,1)S(1)}, u32[]{:S(2)}, u32[]{:S(2)}) collective-permute-start(bf16[512,128]{1,0:T(8,128)(2,1)} %shard_map.109), channel_id=1, source_target_pairs={{0,2},{2,0},{4,6},{6,4},{8,10},{10,8},{12,14},{14,12},{16,18},{18,... | collective-permute-start | bytes 393224 | tf_op jit(solution)/shard_map/ppermute | solution.py:145
  5.5 3.7 %collective-permute-done.refs_0_ = bf16[512,128]{1,0:T(8,128)(2,1)S(1)} collective-permute-done((bf16[512,128]{1,0:T(8,128)(2,1)}, bf16[512,128]{1,0:T(8,128)(2,1)S(1)}, u32[]{:S(2)}, u32[]{:S(2)}) %collective-permute-start) | collective-permute-done | bytes 131104 | tf_op jit(solution)/shard_map/ppermute | solution.py:145
  9.2 0.0 copy-start.4
  9.2 1.0 %add.18 = bf16[512,128]{1,0:T(8,128)(2,1)S(1)} add(bf16[512,128]{1,0:T(8,128)(2,1)} %shard_map.109, bf16[512,128]{1,0:T(8,128)(2,1)S(1)} %collective-permute-done.refs_0_) | non-fusion elementwise | flops 65536 | bytes 393216 | tf_op jit(solution)/shard_map/add | solution.py:143
  10.2 0.0 copy-done.4
  10.2 1.8 %collective-permute-start.1 = (bf16[512,128]{1,0:T(8,128)(2,1)S(1)}, bf16[512,128]{1,0:T(8,128)(2,1)S(1)}, u32[]{:S(2)}, u32[]{:S(2)}) collective-permute-start(bf16[512,128]{1,0:T(8,128)(2,1)S(1)} %add.18), channel_id=1, source_target_pairs={{0,4},{2,6},{4,0},{6,2},{8,12},{10,14},{12,8},{14,10},{16,20},{18,... | collective-permute-start | bytes 393224 | tf_op jit(solution)/shard_map/ppermute | solution.py:145
  12.1 3.2 %collective-permute-done.1.refs_1_ = bf16[512,128]{1,0:T(8,128)(2,1)S(1)} collective-permute-done((bf16[512,128]{1,0:T(8,128)(2,1)S(1)}, bf16[512,128]{1,0:T(8,128)(2,1)S(1)}, u32[]{:S(2)}, u32[]{:S(2)}) %collective-permute-start.1) | collective-permute-done | bytes 131104 | tf_op jit(solution)/shard_map/ppermute | solution.py:145
  15.3 0.0 copy-start.5
  15.3 0.6 copy-done.5
  15.9 1.8 %collective-permute-start.2 = (bf16[512,128]{1,0:T(8,128)(2,1)S(1)}, bf16[512,128]{1,0:T(8,128)(2,1)S(1)}, u32[]{:S(2)}, u32[]{:S(2)}) collective-permute-start(bf16[512,128]{1,0:T(8,128)(2,1)S(1)} %add.19), channel_id=1, source_target_pairs={{0,8},{2,10},{4,12},{6,14},{8,0},{10,2},{12,4},{14,6},{16,24},{18,... | collective-permute-start | bytes 393224 | tf_op jit(solution)/shard_map/ppermute | solution.py:145
  17.8 3.1 %collective-permute-done.2.refs_2_ = bf16[512,128]{1,0:T(8,128)(2,1)S(1)} collective-permute-done((bf16[512,128]{1,0:T(8,128)(2,1)S(1)}, bf16[512,128]{1,0:T(8,128)(2,1)S(1)}, u32[]{:S(2)}, u32[]{:S(2)}) %collective-permute-start.2) | collective-permute-done | bytes 131104 | tf_op jit(solution)/shard_map/ppermute | solution.py:145
  20.9 0.0 copy-start.6
  20.9 0.6 copy-done.6
  21.6 3.0 %collective-permute-start.3 = (bf16[512,128]{1,0:T(8,128)(2,1)S(1)}, bf16[512,128]{1,0:T(8,128)(2,1)S(1)}, u32[]{:S(2)}, u32[]{:S(2)}) collective-permute-start(bf16[512,128]{1,0:T(8,128)(2,1)S(1)} %add.20), channel_id=1, source_target_pairs={{0,16},{2,18},{4,20},{6,22},{8,24},{10,26},{12,28},{14,30},{16,0},... | collective-permute-start | bytes 393224 | tf_op jit(solution)/shard_map/ppermute | solution.py:145
  24.6 2.6 %shard_map.110.refs_5_ = f32[256,512]{1,0:T(8,128)} custom-call(bf16[256,512]{1,0:T(8,128)(2,1)} %q_ref.5, bf16[256,512]{1,0:T(8,128)(2,1)} %refs_5_.1, bf16[256,512]{1,0:T(8,128)(2,1)} %refs_6_.3), custom_call_target="tpu_custom_call" | custom-call | flops 134217728 | bytes 1310720 | tf_op jit(solution)/shard_map/pallas_call | solution.py:172
  27.1 1.8 %collective-permute-done.3.refs_3_ = bf16[512,128]{1,0:T(8,128)(2,1)S(1)} collective-permute-done((bf16[512,128]{1,0:T(8,128)(2,1)S(1)}, bf16[512,128]{1,0:T(8,128)(2,1)S(1)}, u32[]{:S(2)}, u32[]{:S(2)}) %collective-permute-start.3) | collective-permute-done | bytes 131104 | tf_op jit(solution)/shard_map/ppermute | solution.py:145
  28.9 0.0 copy-start.8
  28.9 0.7 copy-done.8
  29.6 2.6 %shard_map.111 = (f32[256,512]{1,0:T(8,128)}, bf16[512,128]{1,0:T(8,128)(2,1)}, f32[256,128]{1,0:T(8,128)}) custom-call(bf16[512,128]{1,0:T(8,128)(2,1)} %copy-done.4, bf16[512,128]{1,0:T(8,128)(2,1)} %copy-done.5, bf16[512,128]{1,0:T(8,128)(2,1)} %copy-done.6, bf16[512,128]{1,0:T(8,128)(2,1)} %copy-done.8, bf16[256,512]{1,0:T(8,128)(2,1)} %q_ref.5, ...), custom_call_target="tpu_custom_call" | custom-call | flops 33554432 | bytes 2490368 | tf_op jit(solution)/shard_map/pallas_call | solution.py:176
  32.2 0.0 collective-permute-start.4
  32.2 1.6 %collective-permute-done.4.other_ref = f32[256,128]{1,0:T(8,128)S(1)} collective-permute-done((f32[256,128]{1,0:T(8,128)}, f32[256,128]{1,0:T(8,128)S(1)}, u32[]{:S(2)}, u32[]{:S(2)}) %collective-permute-start.4) | collective-permute-done | bytes 131104 | tf_op jit(solution)/shard_map/ppermute | solution.py:184
  33.8 0.0 copy-start.9
  33.8 0.7 copy-done.9
  34.4 2.5 %shard_map.112 = (bf16[256,512]{1,0:T(8,128)(2,1)}, bf16[256,512]{1,0:T(8,128)(2,1)}, bf16[528,128]{1,0:T(8,128)(2,1)}) custom-call(f32[256,128]{1,0:T(8,128)} %get-tuple-element.19.sums_ref, f32[256,128]{1,0:T(8,128)} %copy-done.9, f32[256,512]{1,0:T(8,128)} %get-tuple-element.20.un_ref, bf16[256,512]{1,0:T(8,128)(2,1)} %cot_ref.1, f32[1,512]{1,0:T(1,128)} %bitcast.3, ...), custom_call_target="tpu_custom_call" | custom-call | flops 33554432 | bytes 1703936 | tf_op jit(solution)/shard_map/pallas_call | solution.py:187
  36.9 1.7 %collective-permute-start.5 = (bf16[528,128]{1,0:T(8,128)(2,1)}, bf16[528,128]{1,0:T(8,128)(2,1)S(1)}, u32[]{:S(2)}, u32[]{:S(2)}) collective-permute-start(bf16[528,128]{1,0:T(8,128)(2,1)} %get-tuple-element.25), channel_id=1, source_target_pairs={{0,2},{2,0},{4,6},{6,4},{8,10},{10,8},{12,14},{14,12},{16,18},{18,... | collective-permute-start | bytes 405512 | tf_op jit(solution)/shard_map/ppermute | solution.py:145
  38.6 4.2 %collective-permute-done.5.refs_0_ = bf16[528,128]{1,0:T(8,128)(2,1)S(1)} collective-permute-done((bf16[528,128]{1,0:T(8,128)(2,1)}, bf16[528,128]{1,0:T(8,128)(2,1)S(1)}, u32[]{:S(2)}, u32[]{:S(2)}) %collective-permute-start.5) | collective-permute-done | bytes 135200 | tf_op jit(solution)/shard_map/ppermute | solution.py:145
  42.8 0.0 copy-start
  42.8 1.0 %add.21 = bf16[528,128]{1,0:T(8,128)(2,1)S(1)} add(bf16[528,128]{1,0:T(8,128)(2,1)} %get-tuple-element.25, bf16[528,128]{1,0:T(8,128)(2,1)S(1)} %collective-permute-done.5.refs_0_) | non-fusion elementwise | flops 67584 | bytes 405504 | tf_op jit(solution)/shard_map/add | solution.py:143
  43.8 0.0 copy-done
  43.8 1.7 %collective-permute-start.6 = (bf16[528,128]{1,0:T(8,128)(2,1)S(1)}, bf16[528,128]{1,0:T(8,128)(2,1)S(1)}, u32[]{:S(2)}, u32[]{:S(2)}) collective-permute-start(bf16[528,128]{1,0:T(8,128)(2,1)S(1)} %add.21), channel_id=1, source_target_pairs={{0,4},{2,6},{4,0},{6,2},{8,12},{10,14},{12,8},{14,10},{16,20},{18,... | collective-permute-start | bytes 405512 | tf_op jit(solution)/shard_map/ppermute | solution.py:145
  45.5 3.3 %collective-permute-done.6.refs_1_ = bf16[528,128]{1,0:T(8,128)(2,1)S(1)} collective-permute-done((bf16[528,128]{1,0:T(8,128)(2,1)S(1)}, bf16[528,128]{1,0:T(8,128)(2,1)S(1)}, u32[]{:S(2)}, u32[]{:S(2)}) %collective-permute-start.6) | collective-permute-done | bytes 135200 | tf_op jit(solution)/shard_map/ppermute | solution.py:145
  48.9 0.0 copy-start.1
  48.9 0.6 copy-done.1
  49.5 0.9 %collective-permute-start.7 = (bf16[528,128]{1,0:T(8,128)(2,1)S(1)}, bf16[528,128]{1,0:T(8,128)(2,1)S(1)}, u32[]{:S(2)}, u32[]{:S(2)}) collective-permute-start(bf16[528,128]{1,0:T(8,128)(2,1)S(1)} %add.22), channel_id=1, source_target_pairs={{0,8},{2,10},{4,12},{6,14},{8,0},{10,2},{12,4},{14,6},{16,24},{18,... | collective-permute-start | bytes 405512 | tf_op jit(solution)/shard_map/ppermute | solution.py:145
  50.5 4.1 %collective-permute-done.7.refs_2_ = bf16[528,128]{1,0:T(8,128)(2,1)S(1)} collective-permute-done((bf16[528,128]{1,0:T(8,128)(2,1)S(1)}, bf16[528,128]{1,0:T(8,128)(2,1)S(1)}, u32[]{:S(2)}, u32[]{:S(2)}) %collective-permute-start.7) | collective-permute-done | bytes 135200 | tf_op jit(solution)/shard_map/ppermute | solution.py:145
  54.5 0.0 copy-start.2
  54.6 0.6 copy-done.2
  55.2 0.0 copy-start.3
  55.2 2.3 %collective-permute-start.8 = (bf16[528,128]{1,0:T(8,128)(2,1)S(1)}, bf16[528,128]{1,0:T(8,128)(2,1)S(1)}, u32[]{:S(2)}, u32[]{:S(2)}) collective-permute-start(bf16[528,128]{1,0:T(8,128)(2,1)S(1)} %add.23.refs_4_), channel_id=1, source_target_pairs={{0,16},{2,18},{4,20},{6,22},{8,24},{10,26},{12,28},{14,30},{16,0},... | collective-permute-start | bytes 405512 | tf_op jit(solution)/shard_map/ppermute | solution.py:145
  57.5 3.6 %shard_map.113 = (bf16[256,512]{1,0:T(8,128)(2,1)}, f32[256,512]{1,0:T(8,128)}, f32[256,512]{1,0:T(8,128)}) custom-call(bf16[256,512]{1,0:T(8,128)(2,1)} %q_ref.5, bf16[256,512]{1,0:T(8,128)(2,1)} %refs_5_.1, bf16[256,512]{1,0:T(8,128)(2,1)} %refs_6_.3, bf16[256,512]{1,0:T(8,128)(2,1)} %get-tuple-element.22.gun_ref, ...), custom_call_target="tpu_custom_call" | custom-call | flops 369098752 | bytes 2490368 | tf_op jit(solution)/shard_map/pallas_call | solution.py:192
  61.1 0.0 copy-done.3
  61.1 1.4 %collective-permute-done.8.refs_3_ = bf16[528,128]{1,0:T(8,128)(2,1)S(1)} collective-permute-done((bf16[528,128]{1,0:T(8,128)(2,1)S(1)}, bf16[528,128]{1,0:T(8,128)(2,1)S(1)}, u32[]{:S(2)}, u32[]{:S(2)}) %collective-permute-start.8) | collective-permute-done | bytes 135200 | tf_op jit(solution)/shard_map/ppermute | solution.py:145
  62.6 0.0 copy-start.7
  62.6 0.6 copy-done.7
  63.2 2.8 %shard_map.114 = (bf16[256,512]{1,0:T(8,128)(2,1)}, bf16[256,512]{1,0:T(8,128)(2,1)}, f32[4,128,128]{2,1,0:T(8,128)}, f32[1,512]{1,0:T(1,128)}) custom-call(bf16[528,128]{1,0:T(8,128)(2,1)} %copy-done, bf16[528,128]{1,0:T(8,128)(2,1)} %copy-done.1, bf16[528,128]{1,0:T(8,128)(2,1)} %copy-done.2, bf16[528,128]{1,0:T(8,128)(2,1)} %copy-done.7, ...), custom_call_target="tpu_custom_call" | custom-call | flops 67108864 | bytes 2883584 | tf_op jit(solution)/shard_map/pallas_call | solution.py:196
  (4 shorter events, 0.2 us)
Async XLA Ops:
  2.6 6.6 %collective-permute-start = (bf16[512,128]{1,0:T(8,128)(2,1)}, bf16[512,128]{1,0:T(8,128)(2,1)S(1)}, u32[]{:S(2)}, u32[]{:S(2)}) collective-permute-start(bf16[512,128]{1,0:T(8,128)(2,1)} %shard_map.109), channel_id=1, source_target_pairs={{0,2},{2,0},{4,6},{6,4},{8,10},{10,8},{12,14},{14,12},{16,18},{18,... | collective-permute-start | bytes 393224 | tf_op jit(solution)/shard_map/ppermute | solution.py:145
  9.2 1.0 %copy-start.4 = (bf16[512,128]{1,0:T(8,128)(2,1)}, bf16[512,128]{1,0:T(8,128)(2,1)S(1)}, u32[]{:S(2)}) copy-start(bf16[512,128]{1,0:T(8,128)(2,1)S(1)} %collective-permute-done.refs_0_) | copy-start | bytes 393220
  10.2 5.0 %collective-permute-start.1 = (bf16[512,128]{1,0:T(8,128)(2,1)S(1)}, bf16[512,128]{1,0:T(8,128)(2,1)S(1)}, u32[]{:S(2)}, u32[]{:S(2)}) collective-permute-start(bf16[512,128]{1,0:T(8,128)(2,1)S(1)} %add.18), channel_id=1, source_target_pairs={{0,4},{2,6},{4,0},{6,2},{8,12},{10,14},{12,8},{14,10},{16,20},{18,... | collective-permute-start | bytes 393224 | tf_op jit(solution)/shard_map/ppermute | solution.py:145
  15.3 0.7 copy-start.5
  15.9 5.0 %collective-permute-start.2 = (bf16[512,128]{1,0:T(8,128)(2,1)S(1)}, bf16[512,128]{1,0:T(8,128)(2,1)S(1)}, u32[]{:S(2)}, u32[]{:S(2)}) collective-permute-start(bf16[512,128]{1,0:T(8,128)(2,1)S(1)} %add.19), channel_id=1, source_target_pairs={{0,8},{2,10},{4,12},{6,14},{8,0},{10,2},{12,4},{14,6},{16,24},{18,... | collective-permute-start | bytes 393224 | tf_op jit(solution)/shard_map/ppermute | solution.py:145
  20.9 0.7 copy-start.6
  21.6 7.4 %collective-permute-start.3 = (bf16[512,128]{1,0:T(8,128)(2,1)S(1)}, bf16[512,128]{1,0:T(8,128)(2,1)S(1)}, u32[]{:S(2)}, u32[]{:S(2)}) collective-permute-start(bf16[512,128]{1,0:T(8,128)(2,1)S(1)} %add.20), channel_id=1, source_target_pairs={{0,16},{2,18},{4,20},{6,22},{8,24},{10,26},{12,28},{14,30},{16,0},... | collective-permute-start | bytes 393224 | tf_op jit(solution)/shard_map/ppermute | solution.py:145
  28.9 0.7 copy-start.8
  32.2 1.6 %collective-permute-start.4 = (f32[256,128]{1,0:T(8,128)}, f32[256,128]{1,0:T(8,128)S(1)}, u32[]{:S(2)}, u32[]{:S(2)}) collective-permute-start(f32[256,128]{1,0:T(8,128)} %get-tuple-element.19.sums_ref), channel_id=1, source_target_pairs={{0,1},{1,0},{2,3},{3,2},{4,5},{5,4},{6,7},{7,6},{8,9},{9,8},{10,11... | collective-permute-start | bytes 393224 | tf_op jit(solution)/shard_map/ppermute | solution.py:184
  33.8 0.7 copy-start.9
  36.9 5.8 %collective-permute-start.5 = (bf16[528,128]{1,0:T(8,128)(2,1)}, bf16[528,128]{1,0:T(8,128)(2,1)S(1)}, u32[]{:S(2)}, u32[]{:S(2)}) collective-permute-start(bf16[528,128]{1,0:T(8,128)(2,1)} %get-tuple-element.25), channel_id=1, source_target_pairs={{0,2},{2,0},{4,6},{6,4},{8,10},{10,8},{12,14},{14,12},{16,18},{18,... | collective-permute-start | bytes 405512 | tf_op jit(solution)/shard_map/ppermute | solution.py:145
  42.8 1.0 %copy-start = (bf16[528,128]{1,0:T(8,128)(2,1)}, bf16[528,128]{1,0:T(8,128)(2,1)S(1)}, u32[]{:S(2)}) copy-start(bf16[528,128]{1,0:T(8,128)(2,1)S(1)} %collective-permute-done.5.refs_0_) | copy-start | bytes 405508
  43.8 5.1 %collective-permute-start.6 = (bf16[528,128]{1,0:T(8,128)(2,1)S(1)}, bf16[528,128]{1,0:T(8,128)(2,1)S(1)}, u32[]{:S(2)}, u32[]{:S(2)}) collective-permute-start(bf16[528,128]{1,0:T(8,128)(2,1)S(1)} %add.21), channel_id=1, source_target_pairs={{0,4},{2,6},{4,0},{6,2},{8,12},{10,14},{12,8},{14,10},{16,20},{18,... | collective-permute-start | bytes 405512 | tf_op jit(solution)/shard_map/ppermute | solution.py:145
  48.9 0.7 copy-start.1
  49.5 5.0 %collective-permute-start.7 = (bf16[528,128]{1,0:T(8,128)(2,1)S(1)}, bf16[528,128]{1,0:T(8,128)(2,1)S(1)}, u32[]{:S(2)}, u32[]{:S(2)}) collective-permute-start(bf16[528,128]{1,0:T(8,128)(2,1)S(1)} %add.22), channel_id=1, source_target_pairs={{0,8},{2,10},{4,12},{6,14},{8,0},{10,2},{12,4},{14,6},{16,24},{18,... | collective-permute-start | bytes 405512 | tf_op jit(solution)/shard_map/ppermute | solution.py:145
  54.5 0.7 copy-start.2
  55.2 5.9 %copy-start.3 = (bf16[528,128]{1,0:T(8,128)(2,1)}, bf16[528,128]{1,0:T(8,128)(2,1)S(1)}, u32[]{:S(2)}) copy-start(bf16[528,128]{1,0:T(8,128)(2,1)S(1)} %add.23.refs_4_) | copy-start | bytes 405508
  55.2 7.4 %collective-permute-start.8 = (bf16[528,128]{1,0:T(8,128)(2,1)S(1)}, bf16[528,128]{1,0:T(8,128)(2,1)S(1)}, u32[]{:S(2)}, u32[]{:S(2)}) collective-permute-start(bf16[528,128]{1,0:T(8,128)(2,1)S(1)} %add.23.refs_4_), channel_id=1, source_target_pairs={{0,16},{2,18},{4,20},{6,22},{8,24},{10,26},{12,28},{14,30},{16,0},... | collective-permute-start | bytes 405512 | tf_op jit(solution)/shard_map/ppermute | solution.py:145
  62.6 0.6 copy-start.7

commit v2 on v1

--- a/solution.py
+++ b/solution.py
@@ -10,6 +10,7 @@
 EPS = 1e-05
 F32 = jnp.float32
 BF16 = jnp.bfloat16
+VMEM = 16 * 2**20
 
 
 def dot(a, b, ca, cb):
@@ -20,6 +21,7 @@
     return pl.pallas_call(
         kernel,
         out_shape=outs,
+        compiler_params=pltpu.CompilerParams(vmem_limit_bytes=VMEM),
         cost_estimate=pl.CostEstimate(flops=flops, bytes_accessed=nbytes, transcendentals=0),
     )
 

time: 66.3 us -> 55.2 us (0.83)
  Pallas kernels: 16.1 us -> 5.59 us
  waiting for transfers between devices: 26.4 us -> 30.8 us
  local copies, waits for them, and re-layouts: 4.41 us -> 1.93 us
  other arithmetic: 2.14 us -> 0.23 us
    ppermute x8, waiting for transfers between devices: 24.8 us -> 29.5 us  [exchange(): received.append(lax.ppermute(message, 'seq', pairs))]
    unnamed x20 -> x16, local copies, waits for them, and re-layouts: 4.41 us -> 1.93 us
    pallas_call x1, Pallas kernels: 2.63 us -> 0.42 us  [on_device(): call(functools.partial(unnormed_kernel, heads, dim, rounds), (tokens_f32,...]
    pallas_call x1, Pallas kernels: 2.57 us -> 0.65 us  [on_device(): call(functools.partial(scores_kernel, heads, dim), tokens_f32, 2 * square...]
    add x6, other arithmetic: 2.14 us -> 0.23 us  [exchange(): message = message + received[-1]]
    pallas_call x1, Pallas kernels: 1.96 us -> 0.26 us  [on_device(): call(functools.partial(state_kernel, heads, dim), shape((heads * dim, dim...]
    pallas_call x1, Pallas kernels: 3.62 us -> 1.98 us  [on_device(): call(functools.partial(local_grad_kernel, heads, dim), (tokens_bf, tokens...]
    pallas_call x1, Pallas kernels: 2.8 us -> 1.19 us  [on_device(): call(functools.partial(final_kernel, heads, dim, rounds), (tokens_bf, tok...]
  transfers between devices with their start and end apart: 9 -> 9, of which waited for: 9 -> 9; matrix products, arithmetic and copies ran while one was open for 0% -> 0% of each run, Pallas kernels for 9% -> 5%
where the time goes in v2:
time: 55.2 us; the launch traced here: 55 us
  waiting for transfers between devices  30.8 us (56%)
  starting transfers between devices  15.7 us (28%)
  Pallas kernels  5.59 us (10%)
  local copies, waits for them, and re-layouts  1.93 us (3%)
  between operations  0.74 us (1%)
    ppermute x8, waiting for transfers between devices, exchange(): received.append(lax.ppermute(message, 'seq', pairs))  29.5 us
    ppermute x8, starting transfers between devices, exchange(): received.append(lax.ppermute(message, 'seq', pairs))  15.7 us
    pallas_call x1, Pallas kernels, on_device(): call(functools.partial(local_grad_kernel, heads, dim), (tokens_bf, tokens...  1.98 us
    unnamed x16, local copies, waits for them, and re-layouts  1.93 us
    ppermute x1, waiting for transfers between devices, on_device(): lax.ppermute(partner, 'head', [(i, (i + 1) % head_count) for i in range(h...  1.33 us
    pallas_call x1, Pallas kernels, on_device(): call(functools.partial(final_kernel, heads, dim, rounds), (tokens_bf, tok...  1.19 us
  transfers between devices with their start and end apart: 9, of which 9 were waited for; matrix products, arithmetic and copies ran while one was open for 0% of the time, Pallas kernels for 5%

profile of v2, /device:TPU:0, one launch (start us, length us, event | category | flops | bytes accessed | tf_op | source)
XLA Modules:
  0.0 55.0 jit_solution(12426583502371353957)
XLA Ops:
  0.6 0.0 copy-start
  0.6 0.9 %copy-done = bf16[256,512]{1,0:T(8,128)(2,1)S(1)} copy-done((bf16[256,512]{1,0:T(8,128)(2,1)S(1)}, bf16[256,512]{1,0:T(8,128)(2,1)}, u32[]{:S(2)}) %copy-start) | copy-done | bytes 262168
  1.6 0.0 copy-start.2
  1.6 0.9 %copy-done.2 = bf16[256,512]{1,0:T(8,128)(2,1)S(1)} copy-done((bf16[256,512]{1,0:T(8,128)(2,1)S(1)}, bf16[256,512]{1,0:T(8,128)(2,1)}, u32[]{:S(2)}) %copy-start.2) | copy-done | bytes 262168
  2.5 0.3 shard_map.109
  2.8 3.0 %collective-permute-start = (bf16[512,128]{1,0:T(8,128)(2,1)S(1)}, bf16[512,128]{1,0:T(8,128)(2,1)S(1)}, u32[]{:S(2)}, u32[]{:S(2)}) collective-permute-start(bf16[512,128]{1,0:T(8,128)(2,1)S(1)} %shard_map.109), channel_id=1, source_target_pairs={{0,2},{2,0},{4,6},{6,4},{8,10},{10,8},{12,14},{14,12},{16,18},{18,... | collective-permute-start | bytes 393224 | tf_op jit(solution)/shard_map/ppermute | solution.py:147
  5.8 3.5 %collective-permute-done.refs_0_ = bf16[512,128]{1,0:T(8,128)(2,1)S(1)} collective-permute-done((bf16[512,128]{1,0:T(8,128)(2,1)S(1)}, bf16[512,128]{1,0:T(8,128)(2,1)S(1)}, u32[]{:S(2)}, u32[]{:S(2)}) %collective-permute-start) | collective-permute-done | bytes 131104 | tf_op jit(solution)/shard_map/ppermute | solution.py:147
  9.3 1.8 %collective-permute-start.1 = (bf16[512,128]{1,0:T(8,128)(2,1)S(1)}, bf16[512,128]{1,0:T(8,128)(2,1)S(1)}, u32[]{:S(2)}, u32[]{:S(2)}) collective-permute-start(bf16[512,128]{1,0:T(8,128)(2,1)S(1)} %add.18), channel_id=1, source_target_pairs={{0,4},{2,6},{4,0},{6,2},{8,12},{10,14},{12,8},{14,10},{16,20},{18,... | collective-permute-start | bytes 393224 | tf_op jit(solution)/shard_map/ppermute | solution.py:147
  11.2 3.2 %collective-permute-done.1.refs_1_ = bf16[512,128]{1,0:T(8,128)(2,1)S(1)} collective-permute-done((bf16[512,128]{1,0:T(8,128)(2,1)S(1)}, bf16[512,128]{1,0:T(8,128)(2,1)S(1)}, u32[]{:S(2)}, u32[]{:S(2)}) %collective-permute-start.1) | collective-permute-done | bytes 131104 | tf_op jit(solution)/shard_map/ppermute | solution.py:147
  14.4 0.0 copy-start.4
  14.4 1.9 %collective-permute-start.2 = (bf16[512,128]{1,0:T(8,128)(2,1)S(1)}, bf16[512,128]{1,0:T(8,128)(2,1)S(1)}, u32[]{:S(2)}, u32[]{:S(2)}) collective-permute-start(bf16[512,128]{1,0:T(8,128)(2,1)S(1)} %add.19), channel_id=1, source_target_pairs={{0,8},{2,10},{4,12},{6,14},{8,0},{10,2},{12,4},{14,6},{16,24},{18,... | collective-permute-start | bytes 393224 | tf_op jit(solution)/shard_map/ppermute | solution.py:147
  16.3 3.1 %collective-permute-done.2.refs_2_ = bf16[512,128]{1,0:T(8,128)(2,1)S(1)} collective-permute-done((bf16[512,128]{1,0:T(8,128)(2,1)S(1)}, bf16[512,128]{1,0:T(8,128)(2,1)S(1)}, u32[]{:S(2)}, u32[]{:S(2)}) %collective-permute-start.2) | collective-permute-done | bytes 131104 | tf_op jit(solution)/shard_map/ppermute | solution.py:147
  19.5 0.0 copy-start.5
  19.5 0.0 copy-start.6
  19.5 3.7 %collective-permute-start.3 = (bf16[512,128]{1,0:T(8,128)(2,1)S(1)}, bf16[512,128]{1,0:T(8,128)(2,1)S(1)}, u32[]{:S(2)}, u32[]{:S(2)}) collective-permute-start(bf16[512,128]{1,0:T(8,128)(2,1)S(1)} %add.20), channel_id=1, source_target_pairs={{0,16},{2,18},{4,20},{6,22},{8,24},{10,26},{12,28},{14,30},{16,0},... | collective-permute-start | bytes 393224 | tf_op jit(solution)/shard_map/ppermute | solution.py:147
  23.2 0.0 copy-done.4
  23.2 0.0 copy-start.7
  23.2 0.7 %shard_map.110.refs_5_ = f32[256,512]{1,0:T(8,128)S(1)} custom-call(bf16[256,512]{1,0:T(8,128)(2,1)S(1)} %copy-done.4, bf16[256,512]{1,0:T(8,128)(2,1)S(1)} %copy-done, bf16[256,512]{1,0:T(8,128)(2,1)S(1)} %copy-done.2), custom_call_target="tpu_custom_call" | custom-call | flops 134217728 | bytes 1310720 | tf_op jit(solution)/shard_map/pallas_call | solution.py:174
  23.9 3.7 %collective-permute-done.3.refs_3_ = bf16[512,128]{1,0:T(8,128)(2,1)S(1)} collective-permute-done((bf16[512,128]{1,0:T(8,128)(2,1)S(1)}, bf16[512,128]{1,0:T(8,128)(2,1)S(1)}, u32[]{:S(2)}, u32[]{:S(2)}) %collective-permute-start.3) | collective-permute-done | bytes 131104 | tf_op jit(solution)/shard_map/ppermute | solution.py:147
  27.6 0.0 copy-done.5
  27.6 0.0 copy-done.6
  27.6 0.0 copy-done.7
  27.6 0.4 shard_map.111
  28.0 0.1 collective-permute-start.4
  28.1 1.3 %collective-permute-done.4.other_ref = f32[256,128]{1,0:T(8,128)S(1)} collective-permute-done((f32[256,128]{1,0:T(8,128)S(1)}, f32[256,128]{1,0:T(8,128)S(1)}, u32[]{:S(2)}, u32[]{:S(2)}) %collective-permute-start.4) | collective-permute-done | bytes 131104 | tf_op jit(solution)/shard_map/ppermute | solution.py:186
  29.4 1.1 %shard_map.112 = (bf16[256,512]{1,0:T(8,128)(2,1)}, bf16[256,512]{1,0:T(8,128)(2,1)S(1)}, bf16[528,128]{1,0:T(8,128)(2,1)S(1)}) custom-call(f32[256,128]{1,0:T(8,128)S(1)} %get-tuple-element.19.sums_ref, f32[256,128]{1,0:T(8,128)S(1)} %collective-permute-done.4.other_ref, f32[256,512]{1,0:T(8,128)S(1)} %get-tuple-element.20.un_ref, ...), custom_call_target="tpu_custom_call" | custom-call | flops 33554432 | bytes 1703936 | tf_op jit(solution)/shard_map/pallas_call | solution.py:189
  30.5 1.5 %collective-permute-start.5 = (bf16[528,128]{1,0:T(8,128)(2,1)S(1)}, bf16[528,128]{1,0:T(8,128)(2,1)S(1)}, u32[]{:S(2)}, u32[]{:S(2)}) collective-permute-start(bf16[528,128]{1,0:T(8,128)(2,1)S(1)} %get-tuple-element.25), channel_id=1, source_target_pairs={{0,2},{2,0},{4,6},{6,4},{8,10},{10,8},{12,14},{14,12},{16,18},{18,... | collective-permute-start | bytes 405512 | tf_op jit(solution)/shard_map/ppermute | solution.py:147
  32.0 4.1 %collective-permute-done.5.refs_0_ = bf16[528,128]{1,0:T(8,128)(2,1)S(1)} collective-permute-done((bf16[528,128]{1,0:T(8,128)(2,1)S(1)}, bf16[528,128]{1,0:T(8,128)(2,1)S(1)}, u32[]{:S(2)}, u32[]{:S(2)}) %collective-permute-start.5) | collective-permute-done | bytes 135200 | tf_op jit(solution)/shard_map/ppermute | solution.py:147
  36.2 1.6 %collective-permute-start.6 = (bf16[528,128]{1,0:T(8,128)(2,1)S(1)}, bf16[528,128]{1,0:T(8,128)(2,1)S(1)}, u32[]{:S(2)}, u32[]{:S(2)}) collective-permute-start(bf16[528,128]{1,0:T(8,128)(2,1)S(1)} %add.21), channel_id=1, source_target_pairs={{0,4},{2,6},{4,0},{6,2},{8,12},{10,14},{12,8},{14,10},{16,20},{18,... | collective-permute-start | bytes 405512 | tf_op jit(solution)/shard_map/ppermute | solution.py:147
  37.8 3.5 %collective-permute-done.6.refs_1_ = bf16[528,128]{1,0:T(8,128)(2,1)S(1)} collective-permute-done((bf16[528,128]{1,0:T(8,128)(2,1)S(1)}, bf16[528,128]{1,0:T(8,128)(2,1)S(1)}, u32[]{:S(2)}, u32[]{:S(2)}) %collective-permute-start.6) | collective-permute-done | bytes 135200 | tf_op jit(solution)/shard_map/ppermute | solution.py:147
  41.2 0.0 copy-start.3
  41.3 0.0 copy-start.1
  41.3 0.4 collective-permute-start.7
  41.7 4.7 %collective-permute-done.7.refs_2_ = bf16[528,128]{1,0:T(8,128)(2,1)S(1)} collective-permute-done((bf16[528,128]{1,0:T(8,128)(2,1)S(1)}, bf16[528,128]{1,0:T(8,128)(2,1)S(1)}, u32[]{:S(2)}, u32[]{:S(2)}) %collective-permute-start.7) | collective-permute-done | bytes 135200 | tf_op jit(solution)/shard_map/ppermute | solution.py:147
  46.4 1.8 %collective-permute-start.8 = (bf16[528,128]{1,0:T(8,128)(2,1)S(1)}, bf16[528,128]{1,0:T(8,128)(2,1)S(1)}, u32[]{:S(2)}, u32[]{:S(2)}) collective-permute-start(bf16[528,128]{1,0:T(8,128)(2,1)S(1)} %add.23.refs_4_), channel_id=1, source_target_pairs={{0,16},{2,18},{4,20},{6,22},{8,24},{10,26},{12,28},{14,30},{16,0},... | collective-permute-start | bytes 405512 | tf_op jit(solution)/shard_map/ppermute | solution.py:147
  48.2 0.0 copy-done.3
  48.2 0.0 copy-done.1
  48.2 2.0 %shard_map.113 = (bf16[256,512]{1,0:T(8,128)(2,1)}, f32[256,512]{1,0:T(8,128)S(1)}, f32[256,512]{1,0:T(8,128)S(1)}) custom-call(bf16[256,512]{1,0:T(8,128)(2,1)S(1)} %copy-done.4, bf16[256,512]{1,0:T(8,128)(2,1)S(1)} %copy-done.1, bf16[256,512]{1,0:T(8,128)(2,1)S(1)} %copy-done.3, bf16[256,512]{1,0:T(8,128)(2,1)S(1)} %get-tuple-element.22.gun_ref, ...), custom_call_target="tpu_custom_call" | custom-call | flops 369098752 | bytes 2490368 | tf_op jit(solution)/shard_map/pallas_call | solution.py:194
  50.2 3.7 %collective-permute-done.8.refs_3_ = bf16[528,128]{1,0:T(8,128)(2,1)S(1)} collective-permute-done((bf16[528,128]{1,0:T(8,128)(2,1)S(1)}, bf16[528,128]{1,0:T(8,128)(2,1)S(1)}, u32[]{:S(2)}, u32[]{:S(2)}) %collective-permute-start.8) | collective-permute-done | bytes 135200 | tf_op jit(solution)/shard_map/ppermute | solution.py:147
  53.8 1.2 %shard_map.114 = (bf16[256,512]{1,0:T(8,128)(2,1)}, bf16[256,512]{1,0:T(8,128)(2,1)}, f32[4,128,128]{2,1,0:T(8,128)}, f32[1,512]{1,0:T(1,128)}) custom-call(bf16[528,128]{1,0:T(8,128)(2,1)S(1)} %collective-permute-done.5.refs_0_, bf16[528,128]{1,0:T(8,128)(2,1)S(1)} %collective-permute-done.6.refs_1_, bf16[528,128]{1,0:T(8,128)(2,1)S(1)} %collective-permute-done.7.refs_2_, ...), custom_call_target="tpu_custom_call" | custom-call | flops 67108864 | bytes 2883584 | tf_op jit(solution)/shard_map/pallas_call | solution.py:198
  (6 shorter events, 0.2 us)
Async XLA Ops:
  0.6 1.0 %copy-start = (bf16[256,512]{1,0:T(8,128)(2,1)S(1)}, bf16[256,512]{1,0:T(8,128)(2,1)}, u32[]{:S(2)}) copy-start(bf16[256,512]{1,0:T(8,128)(2,1)} %refs_5_.1) | copy-start | bytes 786436
  1.6 0.9 %copy-start.2 = (bf16[256,512]{1,0:T(8,128)(2,1)S(1)}, bf16[256,512]{1,0:T(8,128)(2,1)}, u32[]{:S(2)}) copy-start(bf16[256,512]{1,0:T(8,128)(2,1)} %refs_6_.3) | copy-start | bytes 786436
  2.8 6.5 %collective-permute-start = (bf16[512,128]{1,0:T(8,128)(2,1)S(1)}, bf16[512,128]{1,0:T(8,128)(2,1)S(1)}, u32[]{:S(2)}, u32[]{:S(2)}) collective-permute-start(bf16[512,128]{1,0:T(8,128)(2,1)S(1)} %shard_map.109), channel_id=1, source_target_pairs={{0,2},{2,0},{4,6},{6,4},{8,10},{10,8},{12,14},{14,12},{16,18},{18,... | collective-permute-start | bytes 393224 | tf_op jit(solution)/shard_map/ppermute | solution.py:147
  9.3 5.0 %collective-permute-start.1 = (bf16[512,128]{1,0:T(8,128)(2,1)S(1)}, bf16[512,128]{1,0:T(8,128)(2,1)S(1)}, u32[]{:S(2)}, u32[]{:S(2)}) collective-permute-start(bf16[512,128]{1,0:T(8,128)(2,1)S(1)} %add.18), channel_id=1, source_target_pairs={{0,4},{2,6},{4,0},{6,2},{8,12},{10,14},{12,8},{14,10},{16,20},{18,... | collective-permute-start | bytes 393224 | tf_op jit(solution)/shard_map/ppermute | solution.py:147
  14.4 8.8 %copy-start.4 = (bf16[256,512]{1,0:T(8,128)(2,1)S(1)}, bf16[256,512]{1,0:T(8,128)(2,1)}, u32[]{:S(2)}) copy-start(bf16[256,512]{1,0:T(8,128)(2,1)} %q_ref.5) | copy-start | bytes 786436
  14.4 5.0 %collective-permute-start.2 = (bf16[512,128]{1,0:T(8,128)(2,1)S(1)}, bf16[512,128]{1,0:T(8,128)(2,1)S(1)}, u32[]{:S(2)}, u32[]{:S(2)}) collective-permute-start(bf16[512,128]{1,0:T(8,128)(2,1)S(1)} %add.19), channel_id=1, source_target_pairs={{0,8},{2,10},{4,12},{6,14},{8,0},{10,2},{12,4},{14,6},{16,24},{18,... | collective-permute-start | bytes 393224 | tf_op jit(solution)/shard_map/ppermute | solution.py:147
  19.5 8.1 %copy-start.5 = (bf16[256,512]{1,0:T(8,128)(2,1)S(1)}, bf16[256,512]{1,0:T(8,128)(2,1)}, u32[]{:S(2)}) copy-start(bf16[256,512]{1,0:T(8,128)(2,1)} %cot_ref.1) | copy-start | bytes 786436
  19.5 8.0 %copy-start.6 = (f32[4,128,128]{2,1,0:T(8,128)S(1)}, f32[4,128,128]{2,1,0:T(8,128)}, u32[]{:S(2)}) copy-start(f32[4,128,128]{2,1,0:T(8,128)} %refs_7_.1) | copy-start | bytes 786436
  19.5 8.0 %collective-permute-start.3 = (bf16[512,128]{1,0:T(8,128)(2,1)S(1)}, bf16[512,128]{1,0:T(8,128)(2,1)S(1)}, u32[]{:S(2)}, u32[]{:S(2)}) collective-permute-start(bf16[512,128]{1,0:T(8,128)(2,1)S(1)} %add.20), channel_id=1, source_target_pairs={{0,16},{2,18},{4,20},{6,22},{8,24},{10,26},{12,28},{14,30},{16,0},... | collective-permute-start | bytes 393224 | tf_op jit(solution)/shard_map/ppermute | solution.py:147
  23.2 4.4 %copy-start.7 = (f32[512]{0:T(512)S(1)}, f32[512]{0:T(512)}, u32[]{:S(2)}) copy-start(f32[512]{0:T(512)} %param.11) | copy-start | bytes 6148
  28.0 1.4 %collective-permute-start.4 = (f32[256,128]{1,0:T(8,128)S(1)}, f32[256,128]{1,0:T(8,128)S(1)}, u32[]{:S(2)}, u32[]{:S(2)}) collective-permute-start(f32[256,128]{1,0:T(8,128)S(1)} %get-tuple-element.19.sums_ref), channel_id=1, source_target_pairs={{0,1},{1,0},{2,3},{3,2},{4,5},{5,4},{6,7},{7,6},{8,9},{9,8},{10,11... | collective-permute-start | bytes 393224 | tf_op jit(solution)/shard_map/ppermute | solution.py:186
  30.5 5.6 %collective-permute-start.5 = (bf16[528,128]{1,0:T(8,128)(2,1)S(1)}, bf16[528,128]{1,0:T(8,128)(2,1)S(1)}, u32[]{:S(2)}, u32[]{:S(2)}) collective-permute-start(bf16[528,128]{1,0:T(8,128)(2,1)S(1)} %get-tuple-element.25), channel_id=1, source_target_pairs={{0,2},{2,0},{4,6},{6,4},{8,10},{10,8},{12,14},{14,12},{16,18},{18,... | collective-permute-start | bytes 405512 | tf_op jit(solution)/shard_map/ppermute | solution.py:147
  36.2 5.1 %collective-permute-start.6 = (bf16[528,128]{1,0:T(8,128)(2,1)S(1)}, bf16[528,128]{1,0:T(8,128)(2,1)S(1)}, u32[]{:S(2)}, u32[]{:S(2)}) collective-permute-start(bf16[528,128]{1,0:T(8,128)(2,1)S(1)} %add.21), channel_id=1, source_target_pairs={{0,4},{2,6},{4,0},{6,2},{8,12},{10,14},{12,8},{14,10},{16,20},{18,... | collective-permute-start | bytes 405512 | tf_op jit(solution)/shard_map/ppermute | solution.py:147
  41.2 7.0 %copy-start.3 = (bf16[256,512]{1,0:T(8,128)(2,1)S(1)}, bf16[256,512]{1,0:T(8,128)(2,1)}, u32[]{:S(2)}) copy-start(bf16[256,512]{1,0:T(8,128)(2,1)} %refs_6_.3) | copy-start | bytes 786436
  41.3 6.9 %copy-start.1 = (bf16[256,512]{1,0:T(8,128)(2,1)S(1)}, bf16[256,512]{1,0:T(8,128)(2,1)}, u32[]{:S(2)}) copy-start(bf16[256,512]{1,0:T(8,128)(2,1)} %refs_5_.1) | copy-start | bytes 786436
  41.3 5.1 %collective-permute-start.7 = (bf16[528,128]{1,0:T(8,128)(2,1)S(1)}, bf16[528,128]{1,0:T(8,128)(2,1)S(1)}, u32[]{:S(2)}, u32[]{:S(2)}) collective-permute-start(bf16[528,128]{1,0:T(8,128)(2,1)S(1)} %add.22), channel_id=1, source_target_pairs={{0,8},{2,10},{4,12},{6,14},{8,0},{10,2},{12,4},{14,6},{16,24},{18,... | collective-permute-start | bytes 405512 | tf_op jit(solution)/shard_map/ppermute | solution.py:147
  46.4 7.4 %collective-permute-start.8 = (bf16[528,128]{1,0:T(8,128)(2,1)S(1)}, bf16[528,128]{1,0:T(8,128)(2,1)S(1)}, u32[]{:S(2)}, u32[]{:S(2)}) collective-permute-start(bf16[528,128]{1,0:T(8,128)(2,1)S(1)} %add.23.refs_4_), channel_id=1, source_target_pairs={{0,16},{2,18},{4,20},{6,22},{8,24},{10,26},{12,28},{14,30},{16,0},... | collective-permute-start | bytes 405512 | tf_op jit(solution)/shard_map/ppermute | solution.py:147

commit v3 on v2

v3 whole, which is shorter than its diff:
```python
import functools

import jax
import jax.numpy as jnp
from jax import lax
from jax.experimental import pallas as pl
from jax.experimental.pallas import tpu as pltpu
from jax.sharding import PartitionSpec as P

EPS = 1e-05
F32 = jnp.float32
BF16 = jnp.bfloat16
VMEM = 16 * 2**20
PLANE = 4
EXTRA = 16
WHOLE = pl.BlockSpec(memory_space=pltpu.VMEM)
shape = jax.ShapeDtypeStruct


def dot(a, b, ca, cb):
    return lax.dot_general(a, b, (((ca,), (cb,)), ((), ())), preferred_element_type=F32)


def call(kernel, outs, flops, nbytes, **options):
    return pl.pallas_call(
        kernel,
        out_shape=outs,
        compiler_params=pltpu.CompilerParams(vmem_limit_bytes=VMEM),
        cost_estimate=pl.CostEstimate(flops=flops, bytes_accessed=nbytes, transcendentals=0),
        **options,
    )


def cols(h, dim):
    return slice(h * dim, (h + 1) * dim)


def causal(length):
    rows = lax.broadcasted_iota(jnp.int32, (length, length), 0)
    return rows >= lax.broadcasted_iota(jnp.int32, (length, length), 1)


def state_kernel(halves, dim, k_hbm, v_hbm, *refs):
    wide, narrow = refs[: len(halves)], refs[len(halves) : 2 * len(halves)]
    k_ref, v_ref, k_sem, v_sem = refs[2 * len(halves) :]
    k_copy = pltpu.make_async_copy(k_hbm, k_ref, k_sem)
    v_copy = pltpu.make_async_copy(v_hbm, v_ref, v_sem)
    k_copy.start()
    v_copy.start()
    k_copy.wait()
    v_copy.wait()
    for heads, wide_ref, narrow_ref in zip(halves, wide, narrow):
        for i, h in enumerate(heads):
            state = dot(k_ref[:, cols(h, dim)], v_ref[:, cols(h, dim)], 0, 0)
            wide_ref[cols(i, dim), :] = state
            narrow_ref[cols(i, dim), :] = state.astype(BF16)


def scores_kernel(heads, dim, q_ref, k_ref, v_ref, local_ref):
    mask = causal(q_ref.shape[0])
    for h in range(heads):
        c = cols(h, dim)
        scores = jnp.where(mask, dot(q_ref[:, c], k_ref[:, c], 1, 1), 0.0).astype(BF16)
        local_ref[:, c] = dot(scores, v_ref[:, c], 1, 0)


def gathered(partners, parts, rows, reverse):
    mine = lax.axis_index("seq")
    total = None
    for partner, part in zip(partners, parts):
        top = 1 << (partner.bit_length() - 1)
        reached = (mine & top) == (0 if reverse else top)
        term = jnp.where(reached, part[rows, :].astype(F32), 0.0)
        total = term if total is None else total + term
    return total


def unnormed_kernel(heads, dim, partners, first, *refs):
    parts = refs[: len(partners)]
    refs = refs[len(partners) :]
    if not first:
        before, refs = refs[0], refs[1:]
    q_ref, local_ref, cot_ref, carried_ref, gain_ref, un_ref, prefix_ref, sums_ref = refs
    square = product = 0.0
    for i, h in enumerate(heads):
        c, r = cols(h, dim), cols(i, dim)
        prefix = carried_ref[h]
        if parts:
            prefix = prefix + gathered(partners, parts, r, False)
        prefix = prefix.astype(BF16)
        prefix_ref[r, :] = prefix
        un = local_ref[:, c] + dot(q_ref[:, c], prefix, 1, 0)
        un_ref[:, r] = un
        square = square + un * un
        product = product + cot_ref[:, c].astype(F32) * gain_ref[:, c] * un
    square = jnp.sum(square, axis=1, keepdims=True)
    product = jnp.sum(product, axis=1, keepdims=True)
    lane = lax.broadcasted_iota(jnp.int32, sums_ref.shape, 1)
    sums = jnp.where(lane < sums_ref.shape[1] // 2, square, product)
    sums_ref[...] = sums if first else sums + before[...]


def scales(sums_ref, other_ref, width):
    sums = sums_ref[...] + other_ref[...]
    half = sums.shape[1] // 2
    inverse = 1.0 / jnp.sqrt(sums[:, 0:1] / width + EPS)
    return inverse, (sums[:, half : half + 1] * inverse) / width * inverse * inverse


def norm_kernel(heads, dim, width, sums_ref, other_ref, un_ref, cot_ref, gain_ref, q_ref, gun_ref, msg_ref):
    inverse, factor = scales(sums_ref, other_ref, width)
    for i, h in enumerate(heads):
        c, r = cols(h, dim), cols(i, dim)
        un = un_ref[:, r]
        cot = cot_ref[:, c].astype(F32)
        gun = (cot * gain_ref[:, c] * inverse - un * factor).astype(BF16)
        gun_ref[:, r] = gun
        msg_ref[r, :] = dot(q_ref[:, c], gun, 0, 0).astype(BF16)
        row = len(heads) * dim + i
        msg_ref[row : row + 1, :] = jnp.sum(cot * (un * inverse), axis=0, keepdims=True).astype(BF16)
    rest = len(heads) * (dim + 1)
    msg_ref[rest:, :] = jnp.zeros((msg_ref.shape[0] - rest, dim), BF16)


def attended_kernel(halves, dim, width, *refs):
    n = len(halves)
    uns, guns, prefixes = refs[:n], refs[n : 2 * n], refs[2 * n : 3 * n]
    sums_ref, other_ref, gain_ref, k_ref, v_ref, att_ref, gq_ref = refs[3 * n :]
    inverse, _ = scales(sums_ref, other_ref, width)
    mask = causal(k_ref.shape[0])
    for heads, un_ref, gun_ref, prefix_ref in zip(halves, uns, guns, prefixes):
        for i, h in enumerate(heads):
            c, r = cols(h, dim), cols(i, dim)
            att_ref[:, c] = (gain_ref[:, c] * (un_ref[:, r] * inverse)).astype(BF16)
            gun = gun_ref[:, r]
            mixed = jnp.where(mask, dot(gun, v_ref[:, c], 1, 1), 0.0).astype(BF16)
            gq = dot(mixed, k_ref[:, c], 1, 0) + dot(gun, prefix_ref[r, :], 1, 1)
            gq_ref[:, c] = gq.astype(BF16)


def local_kernel(halves, dim, *refs):
    n = len(halves)
    guns = refs[:n]
    q_ref, k_ref, v_ref, gk_ref, gv_ref = refs[n:]
    mask = causal(q_ref.shape[0])
    for heads, gun_ref in zip(halves, guns):
        for i, h in enumerate(heads):
            c = cols(h, dim)
            q, k, gun = q_ref[:, c], k_ref[:, c], gun_ref[:, cols(i, dim)]
            mixed = jnp.where(mask, dot(gun, v_ref[:, c], 1, 1), 0.0).astype(BF16)
            scores = jnp.where(mask, dot(q, k, 1, 1), 0.0).astype(BF16)
            gk_ref[:, c] = dot(mixed, q, 0, 0)
            gv_ref[:, c] = dot(scores, gun, 0, 0)


def final_kernel(heads, dim, partners, first, *refs):
    parts = refs[: len(partners)]
    refs = refs[len(partners) :]
    message_ref, k_ref, v_ref, gk_ref, gv_ref = refs[:5]
    gk_out, gv_out, state_out, gain_out = refs[5 if first else 9 :]
    for i, h in enumerate(heads):
        c, r = cols(h, dim), cols(i, dim)
        total = message_ref[r, :].astype(F32)
        gk, gv = gk_ref[:, c], gv_ref[:, c]
        row = slice(len(heads) * dim + i, len(heads) * dim + i + 1)
        gain = message_ref[row, :].astype(F32)
        if parts:
            suffix = gathered(partners, parts, r, True).astype(BF16)
            gk = gk + dot(v_ref[:, c], suffix, 1, 1)
            gv = gv + dot(k_ref[:, c], suffix, 1, 0)
            total = total + parts[-1][r, :].astype(F32)
            gain = gain + parts[-1][row, :].astype(F32)
        gk_out[:, r] = gk.astype(BF16)
        gv_out[:, r] = gv.astype(BF16)
        state_out[i] = total
        gain_out[:, r] = gain


def swap(message, count, partner):
    return lax.ppermute(message, "seq", [(i, i ^ partner) for i in range(count)])


def scan(messages, owns, count):
    partners, received = [], [[] for _ in messages]
    distance = 1
    if count >= PLANE:
        partners = list(range(1, PLANE))
        for parts, message in zip(received, messages):
            parts.extend(swap(message, count, partner) for partner in partners)
        distance = PLANE
    while distance < count:
        for n, parts in enumerate(received):
            if parts:
                own = messages[n].astype(F32) if owns is None else owns[n]
                got = [part.astype(F32) for part in parts]
                if distance == PLANE:
                    own = (own + got[0]) + (got[1] + got[2])
                else:
                    own = own + got[-1]
                messages[n] = own.astype(BF16)
                if owns is not None:
                    owns[n] = own
        for n, parts in enumerate(received):
            parts.append(swap(messages[n], count, distance))
        partners.append(distance)
        distance *= 2
    return partners, messages, received


def on_device(queries, key_rows, values, cotangent, carried_state, norm_gain):
    length, width = queries.shape
    heads, dim = carried_state.shape[:2]
    count = lax.axis_size("seq")
    head_count = lax.axis_size("head")
    assert count & (count - 1) == 0 and count >= 2 * PLANE
    assert width == heads * dim and heads % 2 == 0
    total_width = width * head_count
    per = heads // 2
    assert per <= EXTRA
    halves = [list(range(per)), list(range(per, heads))]
    gain = norm_gain.reshape(1, width)
    half_f32 = shape((length, per * dim), F32)
    half_bf = shape((length, per * dim), BF16)
    state_f32 = shape((per * dim, dim), F32)
    state_bf = shape((per * dim, dim), BF16)
    tokens_bf = shape((length, width), BF16)
    tokens_f32 = shape((length, width), F32)
    block = 2 * length * dim * dim * heads
    square = 2 * length * length * dim * heads
    size = length * width * 2
    state_size = heads * dim * dim * 2

    hbm = pl.BlockSpec(memory_space=pltpu.HBM)
    states = call(
        functools.partial(state_kernel, halves, dim),
        [state_f32] * 2 + [state_bf] * 2, block, 2 * size + state_size,
        in_specs=[hbm, hbm],
        scratch_shapes=[pltpu.VMEM((length, width), BF16)] * 2 + [pltpu.SemaphoreType.DMA] * 2,
    )(key_rows, values)
    partners, _, received = scan(list(states[2:]), list(states[:2]), count)
    local = call(
        functools.partial(scores_kernel, heads, dim), tokens_f32, 2 * square, 5 * size,
    )(queries, key_rows, values)
    unnormed, prefixes, sums = [], [], ()
    for n, members in enumerate(halves):
        un, prefix, both = call(
            functools.partial(unnormed_kernel, members, dim, partners, n == 0),
            (half_f32, state_bf, shape((length, 128), F32)), block // 2, 3 * size + 4 * state_size,
        )(*received[n], *sums, queries, local, cotangent, carried_state, gain)
        unnormed.append(un)
        prefixes.append(prefix)
        sums = (both,)
    sums = sums[0]
    other = partner = sums
    for step in range(1, head_count):
        partner = lax.ppermute(partner, "head", [(i, (i + 1) % head_count) for i in range(head_count)])
        other = other + partner if step > 1 else partner

    guns, messages = [], []
    for n, members in enumerate(halves):
        gun, message = call(
            functools.partial(norm_kernel, members, dim, total_width),
            (half_bf, shape((per * dim + EXTRA, dim), BF16)), block // 2, 3 * size,
        )(sums, other, unnormed[n], cotangent, gain, queries)
        guns.append(gun)
        messages.append(message)
    partners, messages, received = scan(messages, None, count)
    attended, grad_q = call(
        functools.partial(attended_kernel, halves, dim, total_width),
        (tokens_bf, tokens_bf), 2 * square + block, 8 * size,
    )(*unnormed, *guns, *prefixes, sums, other, gain, key_rows, values)
    local_k, local_v = call(
        functools.partial(local_kernel, halves, dim), (tokens_f32, tokens_f32), 4 * square, 8 * size,
    )(*guns, queries, key_rows, values)

    outs = ()
    for n, members in enumerate(halves):
        operands = (*received[n], messages[n], key_rows, values, local_k, local_v)
        column = functools.partial(lambda at, i: (0, at), n)
        outs = call(
            functools.partial(final_kernel, members, dim, partners, n == 0),
            (tokens_bf, tokens_bf, shape((heads, dim, dim), F32), shape((1, width), F32)),
            block, 5 * size + 4 * state_size,
            grid=(1,),
            in_specs=[WHOLE] * len(operands) + [hbm] * len(outs),
            out_specs=[
                pl.BlockSpec((length, per * dim), column),
                pl.BlockSpec((length, per * dim), column),
                pl.BlockSpec((per, dim, dim), functools.partial(lambda at, i: (at, 0, 0), n)),
                pl.BlockSpec((1, per * dim), column),
            ],
            input_output_aliases={len(operands) + i: i for i in range(len(outs))},
        )(*operands, *outs)
    grad_k, grad_v, grad_state, grad_gain = outs
    return attended, grad_q, grad_k, grad_v, grad_state, grad_gain.reshape(width)


def solution(mesh):
    tokens = P("seq", "head")
    specs = (P("head", None, None), P("head"))
    return jax.shard_map(
        on_device,
        mesh=mesh,
        in_specs=(tokens,) * 4 + specs,
        out_specs=(tokens,) * 4 + specs,
        check_vma=False,
    )
```

time: 55.2 us -> 49.9 us (0.904)
  waiting for transfers between devices: 30.8 us -> 6.88 us
  starting transfers between devices: 15.7 us -> 32.6 us
  Pallas kernels: 5.59 us -> 7.25 us
    ppermute x8 -> x20, waiting for transfers between devices: 29.5 us -> 5.54 us  [swap(): lax.ppermute(message, 'seq', [(i, i ^ partner) for i in range(count)])]
    ppermute x8 -> x20, starting transfers between devices: 15.7 us -> 32.5 us  [swap(): lax.ppermute(message, 'seq', [(i, i ^ partner) for i in range(count)])]
    pallas_call x5 -> x9, Pallas kernels: 4.93 us -> 6.6 us  [the longest x2 2 us: on_device(): call(functools.partial(final_kernel, members, dim, partners, n == 0), (to...]
  transfers between devices with their start and end apart: 9 -> 21, of which waited for: 9 -> 11; matrix products, arithmetic and copies ran while one was open for 0% -> 1% of each run, Pallas kernels for 5% -> 10%
where the time goes in v3:
time: 49.9 us; the launch traced here: 49.7 us
  starting transfers between devices  32.6 us (65%)
  Pallas kernels  7.25 us (15%)
  waiting for transfers between devices  6.88 us (14%)
  local copies, waits for them, and re-layouts  1.93 us (4%)
  between operations  0.79 us (2%)
    ppermute x20, starting transfers between devices, swap(): lax.ppermute(message, 'seq', [(i, i ^ partner) for i in range(count)])  32.5 us
    ppermute x20, waiting for transfers between devices, swap(): lax.ppermute(message, 'seq', [(i, i ^ partner) for i in range(count)])  5.54 us
    pallas_call x2, Pallas kernels, on_device(): call(functools.partial(final_kernel, members, dim, partners, n == 0), (to...  2 us
    unnamed x16, local copies, waits for them, and re-layouts  1.93 us
    pallas_call x1, Pallas kernels, on_device(): call(functools.partial(local_kernel, halves, dim), (tokens_f32, tokens_f3...  1.45 us
    pallas_call x1, Pallas kernels, on_device(): call(functools.partial(attended_kernel, halves, dim, total_width), (token...  1.35 us
    ppermute x1, waiting for transfers between devices, on_device(): lax.ppermute(partner, 'head', [(i, (i + 1) % head_count) for i in range(h...  1.33 us
  transfers between devices with their start and end apart: 21, of which 11 were waited for; matrix products, arithmetic and copies ran while one was open for 1% of the time, Pallas kernels for 10%

profile of v3, /device:TPU:0, one launch (start us, length us, event | category | flops | bytes accessed | tf_op | source)
XLA Modules:
  0.0 49.7 jit_solution(1529118933133274684)
XLA Ops:
  0.6 0.0 copy-start
  0.6 0.9 %copy-done = bf16[256,512]{1,0:T(8,128)(2,1)S(1)} copy-done((bf16[256,512]{1,0:T(8,128)(2,1)S(1)}, bf16[256,512]{1,0:T(8,128)(2,1)}, u32[]{:S(2)}) %copy-start) | copy-done | bytes 262168
  1.6 0.9 %copy-done.2 = bf16[256,512]{1,0:T(8,128)(2,1)S(1)} copy-done((bf16[256,512]{1,0:T(8,128)(2,1)S(1)}, bf16[256,512]{1,0:T(8,128)(2,1)}, u32[]{:S(2)}) %copy-start.2) | copy-done | bytes 262168
  2.5 0.3 shard_map.109
  2.9 4.0 %collective-permute-start.2 = (bf16[256,128]{1,0:T(8,128)(2,1)S(1)}, bf16[256,128]{1,0:T(8,128)(2,1)S(1)}, u32[]{:S(2)}, u32[]{:S(2)}) collective-permute-start(bf16[256,128]{1,0:T(8,128)(2,1)S(1)} %get-tuple-element.32), channel_id=1, source_target_pairs={{0,6},{2,4},{4,2},{6,0},{8,14},{10,12},{12,10},{14,8},{16,22},{18,... | collective-permute-start | bytes 196616 | tf_op jit(solution)/shard_map/ppermute | solution.py:180
  6.8 0.5 %collective-permute-start.1 = (bf16[256,128]{1,0:T(8,128)(2,1)S(1)}, bf16[256,128]{1,0:T(8,128)(2,1)S(1)}, u32[]{:S(2)}, u32[]{:S(2)}) collective-permute-start(bf16[256,128]{1,0:T(8,128)(2,1)S(1)} %get-tuple-element.32), channel_id=1, source_target_pairs={{0,4},{2,6},{4,0},{6,2},{8,12},{10,14},{12,8},{14,10},{16,20},{18,... | collective-permute-start | bytes 196616 | tf_op jit(solution)/shard_map/ppermute | solution.py:180
  7.3 0.1 collective-permute-start
  7.5 2.8 %collective-permute-start.7 = (bf16[256,128]{1,0:T(8,128)(2,1)S(1)}, bf16[256,128]{1,0:T(8,128)(2,1)S(1)}, u32[]{:S(2)}, u32[]{:S(2)}) collective-permute-start(bf16[256,128]{1,0:T(8,128)(2,1)S(1)} %get-tuple-element.35), channel_id=1, source_target_pairs={{0,6},{2,4},{4,2},{6,0},{8,14},{10,12},{12,10},{14,8},{16,22},{18,... | collective-permute-start | bytes 196616 | tf_op jit(solution)/shard_map/ppermute | solution.py:180
  10.3 0.5 %collective-permute-start.6 = (bf16[256,128]{1,0:T(8,128)(2,1)S(1)}, bf16[256,128]{1,0:T(8,128)(2,1)S(1)}, u32[]{:S(2)}, u32[]{:S(2)}) collective-permute-start(bf16[256,128]{1,0:T(8,128)(2,1)S(1)} %get-tuple-element.35), channel_id=1, source_target_pairs={{0,4},{2,6},{4,0},{6,2},{8,12},{10,14},{12,8},{14,10},{16,20},{18,... | collective-permute-start | bytes 196616 | tf_op jit(solution)/shard_map/ppermute | solution.py:180
  10.8 0.6 %collective-permute-start.5 = (bf16[256,128]{1,0:T(8,128)(2,1)S(1)}, bf16[256,128]{1,0:T(8,128)(2,1)S(1)}, u32[]{:S(2)}, u32[]{:S(2)}) collective-permute-start(bf16[256,128]{1,0:T(8,128)(2,1)S(1)} %get-tuple-element.35), channel_id=1, source_target_pairs={{0,2},{2,0},{4,6},{6,4},{8,10},{10,8},{12,14},{14,12},{16,18},{18,... | collective-permute-start | bytes 196616 | tf_op jit(solution)/shard_map/ppermute | solution.py:180
  11.5 0.4 collective-permute-done.1.refs_1_
  11.9 1.6 %collective-permute-start.3 = (bf16[256,128]{1,0:T(8,128)(2,1)S(1)}, bf16[256,128]{1,0:T(8,128)(2,1)S(1)}, u32[]{:S(2)}, u32[]{:S(2)}) collective-permute-start(bf16[256,128]{1,0:T(8,128)(2,1)S(1)} %fusion), channel_id=1, source_target_pairs={{0,8},{2,10},{4,12},{6,14},{8,0},{10,2},{12,4},{14,6},{16,24},{18,... | collective-permute-start | bytes 196616 | tf_op jit(solution)/shard_map/ppermute | solution.py:180
  13.6 0.1 collective-permute-done.7.refs_2_
  13.7 0.9 %collective-permute-done.6.refs_1_ = bf16[256,128]{1,0:T(8,128)(2,1)S(1)} collective-permute-done((bf16[256,128]{1,0:T(8,128)(2,1)S(1)}, bf16[256,128]{1,0:T(8,128)(2,1)S(1)}, u32[]{:S(2)}, u32[]{:S(2)}) %collective-permute-start.6) | collective-permute-done | bytes 65568 | tf_op jit(solution)/shard_map/ppermute | solution.py:180
  14.6 0.5 %collective-permute-done.5.refs_0_ = bf16[256,128]{1,0:T(8,128)(2,1)S(1)} collective-permute-done((bf16[256,128]{1,0:T(8,128)(2,1)S(1)}, bf16[256,128]{1,0:T(8,128)(2,1)S(1)}, u32[]{:S(2)}, u32[]{:S(2)}) %collective-permute-start.5) | collective-permute-done | bytes 65568 | tf_op jit(solution)/shard_map/ppermute | solution.py:180
  15.1 1.6 %collective-permute-start.8 = (bf16[256,128]{1,0:T(8,128)(2,1)S(1)}, bf16[256,128]{1,0:T(8,128)(2,1)S(1)}, u32[]{:S(2)}, u32[]{:S(2)}) collective-permute-start(bf16[256,128]{1,0:T(8,128)(2,1)S(1)} %fusion.1), channel_id=1, source_target_pairs={{0,8},{2,10},{4,12},{6,14},{8,0},{10,2},{12,4},{14,6},{16,24},{18,... | collective-permute-start | bytes 196616 | tf_op jit(solution)/shard_map/ppermute | solution.py:180
  16.8 0.2 collective-permute-done.3.refs_3_
  17.0 0.0 copy-start.4
  17.0 2.7 %collective-permute-start.4 = (bf16[256,128]{1,0:T(8,128)(2,1)S(1)}, bf16[256,128]{1,0:T(8,128)(2,1)S(1)}, u32[]{:S(2)}, u32[]{:S(2)}) collective-permute-start(bf16[256,128]{1,0:T(8,128)(2,1)S(1)} %add_convert_fusion.5), channel_id=1, source_target_pairs={{0,16},{2,18},{4,20},{6,22},{8,24},{10,26},{12,28},{14,30},{16,0},... | collective-permute-start | bytes 196616 | tf_op jit(solution)/shard_map/ppermute | solution.py:180
  19.7 2.5 %collective-permute-start.9 = (bf16[256,128]{1,0:T(8,128)(2,1)S(1)}, bf16[256,128]{1,0:T(8,128)(2,1)S(1)}, u32[]{:S(2)}, u32[]{:S(2)}) collective-permute-start(bf16[256,128]{1,0:T(8,128)(2,1)S(1)} %add_convert_fusion.4), channel_id=1, source_target_pairs={{0,16},{2,18},{4,20},{6,22},{8,24},{10,26},{12,28},{14,30},{16,0},... | collective-permute-start | bytes 196616 | tf_op jit(solution)/shard_map/ppermute | solution.py:180
  22.2 0.7 %shard_map.110.refs_6_.refs_7_ = f32[256,512]{1,0:T(8,128)S(1)} custom-call(bf16[256,512]{1,0:T(8,128)(2,1)S(1)} %copy-done.4, bf16[256,512]{1,0:T(8,128)(2,1)S(1)} %copy-done, bf16[256,512]{1,0:T(8,128)(2,1)S(1)} %copy-done.2), custom_call_target="tpu_custom_call" | custom-call | flops 134217728 | bytes 1310720 | tf_op jit(solution)/shard_map/pallas_call | solution.py:241
  22.9 0.8 %collective-permute-done.4.refs_4_ = bf16[256,128]{1,0:T(8,128)(2,1)S(1)} collective-permute-done((bf16[256,128]{1,0:T(8,128)(2,1)S(1)}, bf16[256,128]{1,0:T(8,128)(2,1)S(1)}, u32[]{:S(2)}, u32[]{:S(2)}) %collective-permute-start.4) | collective-permute-done | bytes 65568 | tf_op jit(solution)/shard_map/ppermute | solution.py:180
  23.7 0.3 shard_map.111
  24.0 1.0 %collective-permute-done.9.refs_4_ = bf16[256,128]{1,0:T(8,128)(2,1)S(1)} collective-permute-done((bf16[256,128]{1,0:T(8,128)(2,1)S(1)}, bf16[256,128]{1,0:T(8,128)(2,1)S(1)}, u32[]{:S(2)}, u32[]{:S(2)}) %collective-permute-start.9) | collective-permute-done | bytes 65568 | tf_op jit(solution)/shard_map/ppermute | solution.py:180
  25.0 0.3 shard_map.112
  25.3 0.1 collective-permute-start.10
  25.4 1.3 %collective-permute-done.10.other_ref.refs_7_ = f32[256,128]{1,0:T(8,128)S(1)} collective-permute-done((f32[256,128]{1,0:T(8,128)S(1)}, f32[256,128]{1,0:T(8,128)S(1)}, u32[]{:S(2)}, u32[]{:S(2)}) %collective-permute-start.10) | collective-permute-done | bytes 131104 | tf_op jit(solution)/shard_map/ppermute | solution.py:256
  26.7 0.4 shard_map.113
  27.1 1.6 %collective-permute-start.18 = (bf16[272,128]{1,0:T(8,128)(2,1)S(1)}, bf16[272,128]{1,0:T(8,128)(2,1)S(1)}, u32[]{:S(2)}, u32[]{:S(2)}) collective-permute-start(bf16[272,128]{1,0:T(8,128)(2,1)S(1)} %get-tuple-element.49), channel_id=1, source_target_pairs={{0,6},{2,4},{4,2},{6,0},{8,14},{10,12},{12,10},{14,8},{16,22},{18,... | collective-permute-start | bytes 208904 | tf_op jit(solution)/shard_map/ppermute | solution.py:180
  28.7 0.4 collective-permute-start.17
  29.2 1.5 %collective-permute-start.16 = (bf16[272,128]{1,0:T(8,128)(2,1)S(1)}, bf16[272,128]{1,0:T(8,128)(2,1)S(1)}, u32[]{:S(2)}, u32[]{:S(2)}) collective-permute-start(bf16[272,128]{1,0:T(8,128)(2,1)S(1)} %get-tuple-element.49), channel_id=1, source_target_pairs={{0,2},{2,0},{4,6},{6,4},{8,10},{10,8},{12,14},{14,12},{16,18},{18,... | collective-permute-start | bytes 208904 | tf_op jit(solution)/shard_map/ppermute | solution.py:180
  30.7 0.4 shard_map.114
  31.1 1.6 %collective-permute-start.13 = (bf16[272,128]{1,0:T(8,128)(2,1)S(1)}, bf16[272,128]{1,0:T(8,128)(2,1)S(1)}, u32[]{:S(2)}, u32[]{:S(2)}) collective-permute-start(bf16[272,128]{1,0:T(8,128)(2,1)S(1)} %get-tuple-element.46), channel_id=1, source_target_pairs={{0,6},{2,4},{4,2},{6,0},{8,14},{10,12},{12,10},{14,8},{16,22},{18,... | collective-permute-start | bytes 208904 | tf_op jit(solution)/shard_map/ppermute | solution.py:180
  32.7 0.4 collective-permute-start.12
  33.1 1.5 %collective-permute-start.11 = (bf16[272,128]{1,0:T(8,128)(2,1)S(1)}, bf16[272,128]{1,0:T(8,128)(2,1)S(1)}, u32[]{:S(2)}, u32[]{:S(2)}) collective-permute-start(bf16[272,128]{1,0:T(8,128)(2,1)S(1)} %get-tuple-element.46), channel_id=1, source_target_pairs={{0,2},{2,0},{4,6},{6,4},{8,10},{10,8},{12,14},{14,12},{16,18},{18,... | collective-permute-start | bytes 208904 | tf_op jit(solution)/shard_map/ppermute | solution.py:180
  34.7 1.6 %collective-permute-start.19 = (bf16[272,128]{1,0:T(8,128)(2,1)S(1)}, bf16[272,128]{1,0:T(8,128)(2,1)S(1)}, u32[]{:S(2)}, u32[]{:S(2)}) collective-permute-start(bf16[272,128]{1,0:T(8,128)(2,1)S(1)} %add_convert_fusion.1), channel_id=1, source_target_pairs={{0,8},{2,10},{4,12},{6,14},{8,0},{10,2},{12,4},{14,6},{16,24},{18,... | collective-permute-start | bytes 208904 | tf_op jit(solution)/shard_map/ppermute | solution.py:180
  36.3 0.7 %collective-permute-done.13.refs_2_ = bf16[272,128]{1,0:T(8,128)(2,1)S(1)} collective-permute-done((bf16[272,128]{1,0:T(8,128)(2,1)S(1)}, bf16[272,128]{1,0:T(8,128)(2,1)S(1)}, u32[]{:S(2)}, u32[]{:S(2)}) %collective-permute-start.13) | collective-permute-done | bytes 69664 | tf_op jit(solution)/shard_map/ppermute | solution.py:180
  37.0 0.4 collective-permute-done.12.refs_1_
  37.4 0.0 collective-permute-done.11.refs_0_
  37.5 1.6 %collective-permute-start.14 = (bf16[272,128]{1,0:T(8,128)(2,1)S(1)}, bf16[272,128]{1,0:T(8,128)(2,1)S(1)}, u32[]{:S(2)}, u32[]{:S(2)}) collective-permute-start(bf16[272,128]{1,0:T(8,128)(2,1)S(1)} %add_convert_fusion.3), channel_id=1, source_target_pairs={{0,8},{2,10},{4,12},{6,14},{8,0},{10,2},{12,4},{14,6},{16,24},{18,... | collective-permute-start | bytes 208904 | tf_op jit(solution)/shard_map/ppermute | solution.py:180
  39.1 0.5 %collective-permute-done.19.refs_3_ = bf16[272,128]{1,0:T(8,128)(2,1)S(1)} collective-permute-done((bf16[272,128]{1,0:T(8,128)(2,1)S(1)}, bf16[272,128]{1,0:T(8,128)(2,1)S(1)}, u32[]{:S(2)}, u32[]{:S(2)}) %collective-permute-start.19) | collective-permute-done | bytes 69664 | tf_op jit(solution)/shard_map/ppermute | solution.py:180
  39.7 2.9 %collective-permute-start.20 = (bf16[272,128]{1,0:T(8,128)(2,1)S(1)}, bf16[272,128]{1,0:T(8,128)(2,1)S(1)}, u32[]{:S(2)}, u32[]{:S(2)}) collective-permute-start(bf16[272,128]{1,0:T(8,128)(2,1)S(1)} %add_convert_fusion.refs_5_), channel_id=1, source_target_pairs={{0,16},{2,18},{4,20},{6,22},{8,24},{10,26},{12,28},{14,30},{16,0},... | collective-permute-start | bytes 208904 | tf_op jit(solution)/shard_map/ppermute | solution.py:180
  42.6 0.0 collective-permute-done.14.refs_3_
  42.6 2.2 %collective-permute-start.15 = (bf16[272,128]{1,0:T(8,128)(2,1)S(1)}, bf16[272,128]{1,0:T(8,128)(2,1)S(1)}, u32[]{:S(2)}, u32[]{:S(2)}) collective-permute-start(bf16[272,128]{1,0:T(8,128)(2,1)S(1)} %add_convert_fusion.2.refs_5_), channel_id=1, source_target_pairs={{0,16},{2,18},{4,20},{6,22},{8,24},{10,26},{12,28},{14,30},{16,0},... | collective-permute-start | bytes 208904 | tf_op jit(solution)/shard_map/ppermute | solution.py:180
  44.9 1.3 %shard_map.115 = (bf16[256,512]{1,0:T(8,128)(2,1)}, bf16[256,512]{1,0:T(8,128)(2,1)}) custom-call(f32[256,256]{1,0:T(8,128)S(1)} %get-tuple-element.34.un_ref.refs_0_, f32[256,256]{1,0:T(8,128)S(1)} %get-tuple-element.38.un_ref.refs_1_, bf16[256,256]{1,0:T(8,128)(2,1)S(1)} %get-tuple-element.40.refs_2_.refs_0_, ...), custom_call_target="tpu_custom_call" | custom-call | flops 167772160 | bytes 2097152 | tf_op jit(solution)/shard_map/pallas_call | solution.py:268
  46.2 1.5 %shard_map.116 = (f32[256,512]{1,0:T(8,128)S(1)}, f32[256,512]{1,0:T(8,128)S(1)}) custom-call(bf16[256,256]{1,0:T(8,128)(2,1)S(1)} %get-tuple-element.40.refs_2_.refs_0_, bf16[256,256]{1,0:T(8,128)(2,1)S(1)} %get-tuple-element.41.refs_3_.refs_1_, bf16[256,512]{1,0:T(8,128)(2,1)S(1)} %copy-done.4, bf16[256,512]{1,0:T(8,128)(2,1)S(1)} %copy-done.1, ...), custom_call_target="tpu_custom_call" | custom-call | flops 268435456 | bytes 2097152 | tf_op jit(solution)/shard_map/pallas_call | solution.py:272
  47.7 1.0 %shard_map.117 = (bf16[256,512]{1,0:T(8,128)(2,1)}, bf16[256,512]{1,0:T(8,128)(2,1)}, f32[4,128,128]{2,1,0:T(8,128)}, f32[1,512]{1,0:T(1,128)}) custom-call(bf16[272,128]{1,0:T(8,128)(2,1)S(1)} %collective-permute-done.16.refs_0_, bf16[272,128]{1,0:T(8,128)(2,1)S(1)} %collective-permute-done.17.refs_1_, ...), custom_call_target="tpu_custom_call" | custom-call | flops 33554432 | bytes 1835008 | tf_op jit(solution)/shard_map/pallas_call | solution.py:280
  48.7 1.0 %shard_map.118 = (bf16[256,512]{1,0:T(8,128)(2,1)}, bf16[256,512]{1,0:T(8,128)(2,1)}, f32[4,128,128]{2,1,0:T(8,128)}, f32[1,512]{1,0:T(1,128)}) custom-call(bf16[272,128]{1,0:T(8,128)(2,1)S(1)} %collective-permute-done.11.refs_0_, ...), custom_call_target="tpu_custom_call", output_to_operand_aliasing={{0}: (10, {}), {1}: (11, {}), {2}: (12, {}), {3}: (13, {})} | custom-call | flops 33554432 | bytes 1835008 | tf_op jit(solution)/shard_map/pallas_call | solution.py:280
  (28 shorter events, 0.3 us)
Async XLA Ops:
  0.6 1.0 %copy-start = (bf16[256,512]{1,0:T(8,128)(2,1)S(1)}, bf16[256,512]{1,0:T(8,128)(2,1)}, u32[]{:S(2)}) copy-start(bf16[256,512]{1,0:T(8,128)(2,1)} %refs_6_.5) | copy-start | bytes 786436
  1.6 0.9 %copy-start.2 = (bf16[256,512]{1,0:T(8,128)(2,1)S(1)}, bf16[256,512]{1,0:T(8,128)(2,1)}, u32[]{:S(2)}) copy-start(bf16[256,512]{1,0:T(8,128)(2,1)} %refs_7_.5) | copy-start | bytes 786436
  2.9 8.0 %collective-permute-start.2 = (bf16[256,128]{1,0:T(8,128)(2,1)S(1)}, bf16[256,128]{1,0:T(8,128)(2,1)S(1)}, u32[]{:S(2)}, u32[]{:S(2)}) collective-permute-start(bf16[256,128]{1,0:T(8,128)(2,1)S(1)} %get-tuple-element.32), channel_id=1, source_target_pairs={{0,6},{2,4},{4,2},{6,0},{8,14},{10,12},{12,10},{14,8},{16,22},{18,... | collective-permute-start | bytes 196616 | tf_op jit(solution)/shard_map/ppermute | solution.py:180
  6.8 5.1 %collective-permute-start.1 = (bf16[256,128]{1,0:T(8,128)(2,1)S(1)}, bf16[256,128]{1,0:T(8,128)(2,1)S(1)}, u32[]{:S(2)}, u32[]{:S(2)}) collective-permute-start(bf16[256,128]{1,0:T(8,128)(2,1)S(1)} %get-tuple-element.32), channel_id=1, source_target_pairs={{0,4},{2,6},{4,0},{6,2},{8,12},{10,14},{12,8},{14,10},{16,20},{18,... | collective-permute-start | bytes 196616 | tf_op jit(solution)/shard_map/ppermute | solution.py:180
  7.3 4.6 %collective-permute-start = (bf16[256,128]{1,0:T(8,128)(2,1)S(1)}, bf16[256,128]{1,0:T(8,128)(2,1)S(1)}, u32[]{:S(2)}, u32[]{:S(2)}) collective-permute-start(bf16[256,128]{1,0:T(8,128)(2,1)S(1)} %get-tuple-element.32), channel_id=1, source_target_pairs={{0,2},{2,0},{4,6},{6,4},{8,10},{10,8},{12,14},{14,12},{16,18},{18,... | collective-permute-start | bytes 196616 | tf_op jit(solution)/shard_map/ppermute | solution.py:180
  7.5 6.2 %collective-permute-start.7 = (bf16[256,128]{1,0:T(8,128)(2,1)S(1)}, bf16[256,128]{1,0:T(8,128)(2,1)S(1)}, u32[]{:S(2)}, u32[]{:S(2)}) collective-permute-start(bf16[256,128]{1,0:T(8,128)(2,1)S(1)} %get-tuple-element.35), channel_id=1, source_target_pairs={{0,6},{2,4},{4,2},{6,0},{8,14},{10,12},{12,10},{14,8},{16,22},{18,... | collective-permute-start | bytes 196616 | tf_op jit(solution)/shard_map/ppermute | solution.py:180
  10.3 4.3 %collective-permute-start.6 = (bf16[256,128]{1,0:T(8,128)(2,1)S(1)}, bf16[256,128]{1,0:T(8,128)(2,1)S(1)}, u32[]{:S(2)}, u32[]{:S(2)}) collective-permute-start(bf16[256,128]{1,0:T(8,128)(2,1)S(1)} %get-tuple-element.35), channel_id=1, source_target_pairs={{0,4},{2,6},{4,0},{6,2},{8,12},{10,14},{12,8},{14,10},{16,20},{18,... | collective-permute-start | bytes 196616 | tf_op jit(solution)/shard_map/ppermute | solution.py:180
  10.8 4.3 %collective-permute-start.5 = (bf16[256,128]{1,0:T(8,128)(2,1)S(1)}, bf16[256,128]{1,0:T(8,128)(2,1)S(1)}, u32[]{:S(2)}, u32[]{:S(2)}) collective-permute-start(bf16[256,128]{1,0:T(8,128)(2,1)S(1)} %get-tuple-element.35), channel_id=1, source_target_pairs={{0,2},{2,0},{4,6},{6,4},{8,10},{10,8},{12,14},{14,12},{16,18},{18,... | collective-permute-start | bytes 196616 | tf_op jit(solution)/shard_map/ppermute | solution.py:180
  11.9 5.0 %collective-permute-start.3 = (bf16[256,128]{1,0:T(8,128)(2,1)S(1)}, bf16[256,128]{1,0:T(8,128)(2,1)S(1)}, u32[]{:S(2)}, u32[]{:S(2)}) collective-permute-start(bf16[256,128]{1,0:T(8,128)(2,1)S(1)} %fusion), channel_id=1, source_target_pairs={{0,8},{2,10},{4,12},{6,14},{8,0},{10,2},{12,4},{14,6},{16,24},{18,... | collective-permute-start | bytes 196616 | tf_op jit(solution)/shard_map/ppermute | solution.py:180
  15.1 4.5 %collective-permute-start.8 = (bf16[256,128]{1,0:T(8,128)(2,1)S(1)}, bf16[256,128]{1,0:T(8,128)(2,1)S(1)}, u32[]{:S(2)}, u32[]{:S(2)}) collective-permute-start(bf16[256,128]{1,0:T(8,128)(2,1)S(1)} %fusion.1), channel_id=1, source_target_pairs={{0,8},{2,10},{4,12},{6,14},{8,0},{10,2},{12,4},{14,6},{16,24},{18,... | collective-permute-start | bytes 196616 | tf_op jit(solution)/shard_map/ppermute | solution.py:180
  17.0 5.2 %copy-start.4 = (bf16[256,512]{1,0:T(8,128)(2,1)S(1)}, bf16[256,512]{1,0:T(8,128)(2,1)}, u32[]{:S(2)}) copy-start(bf16[256,512]{1,0:T(8,128)(2,1)} %refs_2_.1) | copy-start | bytes 786436
  17.0 6.6 %collective-permute-start.4 = (bf16[256,128]{1,0:T(8,128)(2,1)S(1)}, bf16[256,128]{1,0:T(8,128)(2,1)S(1)}, u32[]{:S(2)}, u32[]{:S(2)}) collective-permute-start(bf16[256,128]{1,0:T(8,128)(2,1)S(1)} %add_convert_fusion.5), channel_id=1, source_target_pairs={{0,16},{2,18},{4,20},{6,22},{8,24},{10,26},{12,28},{14,30},{16,0},... | collective-permute-start | bytes 196616 | tf_op jit(solution)/shard_map/ppermute | solution.py:180
  19.7 3.9 %copy-start.5 = (bf16[256,512]{1,0:T(8,128)(2,1)S(1)}, bf16[256,512]{1,0:T(8,128)(2,1)}, u32[]{:S(2)}) copy-start(bf16[256,512]{1,0:T(8,128)(2,1)} %cot_ref.3) | copy-start | bytes 786436
  19.7 3.9 %copy-start.6 = (f32[4,128,128]{2,1,0:T(8,128)S(1)}, f32[4,128,128]{2,1,0:T(8,128)}, u32[]{:S(2)}) copy-start(f32[4,128,128]{2,1,0:T(8,128)} %refs_9_.2) | copy-start | bytes 786436
  19.7 5.2 %collective-permute-start.9 = (bf16[256,128]{1,0:T(8,128)(2,1)S(1)}, bf16[256,128]{1,0:T(8,128)(2,1)S(1)}, u32[]{:S(2)}, u32[]{:S(2)}) collective-permute-start(bf16[256,128]{1,0:T(8,128)(2,1)S(1)} %add_convert_fusion.4), channel_id=1, source_target_pairs={{0,16},{2,18},{4,20},{6,22},{8,24},{10,26},{12,28},{14,30},{16,0},... | collective-permute-start | bytes 196616 | tf_op jit(solution)/shard_map/ppermute | solution.py:180
  22.2 1.5 %copy-start.7 = (f32[512]{0:T(512)S(1)}, f32[512]{0:T(512)}, u32[]{:S(2)}) copy-start(f32[512]{0:T(512)} %param.11) | copy-start | bytes 6148
  25.3 1.4 %collective-permute-start.10 = (f32[256,128]{1,0:T(8,128)S(1)}, f32[256,128]{1,0:T(8,128)S(1)}, u32[]{:S(2)}, u32[]{:S(2)}) collective-permute-start(f32[256,128]{1,0:T(8,128)S(1)} %get-tuple-element.39.sums_ref.refs_6_), channel_id=1, source_target_pairs={{0,1},{1,0},{2,3},{3,2},{4,5},{5,4},{6,7},{7,6},{8,9},{9,8},{10,11... | collective-permute-start | bytes 393224 | tf_op jit(solution)/shard_map/ppermute | solution.py:256
  27.1 6.0 %collective-permute-start.18 = (bf16[272,128]{1,0:T(8,128)(2,1)S(1)}, bf16[272,128]{1,0:T(8,128)(2,1)S(1)}, u32[]{:S(2)}, u32[]{:S(2)}) collective-permute-start(bf16[272,128]{1,0:T(8,128)(2,1)S(1)} %get-tuple-element.49), channel_id=1, source_target_pairs={{0,6},{2,4},{4,2},{6,0},{8,14},{10,12},{12,10},{14,8},{16,22},{18,... | collective-permute-start | bytes 208904 | tf_op jit(solution)/shard_map/ppermute | solution.py:180
  28.7 5.9 %collective-permute-start.17 = (bf16[272,128]{1,0:T(8,128)(2,1)S(1)}, bf16[272,128]{1,0:T(8,128)(2,1)S(1)}, u32[]{:S(2)}, u32[]{:S(2)}) collective-permute-start(bf16[272,128]{1,0:T(8,128)(2,1)S(1)} %get-tuple-element.49), channel_id=1, source_target_pairs={{0,4},{2,6},{4,0},{6,2},{8,12},{10,14},{12,8},{14,10},{16,20},{18,... | collective-permute-start | bytes 208904 | tf_op jit(solution)/shard_map/ppermute | solution.py:180
  29.2 5.5 %collective-permute-start.16 = (bf16[272,128]{1,0:T(8,128)(2,1)S(1)}, bf16[272,128]{1,0:T(8,128)(2,1)S(1)}, u32[]{:S(2)}, u32[]{:S(2)}) collective-permute-start(bf16[272,128]{1,0:T(8,128)(2,1)S(1)} %get-tuple-element.49), channel_id=1, source_target_pairs={{0,2},{2,0},{4,6},{6,4},{8,10},{10,8},{12,14},{14,12},{16,18},{18,... | collective-permute-start | bytes 208904 | tf_op jit(solution)/shard_map/ppermute | solution.py:180
  31.1 5.9 %collective-permute-start.13 = (bf16[272,128]{1,0:T(8,128)(2,1)S(1)}, bf16[272,128]{1,0:T(8,128)(2,1)S(1)}, u32[]{:S(2)}, u32[]{:S(2)}) collective-permute-start(bf16[272,128]{1,0:T(8,128)(2,1)S(1)} %get-tuple-element.46), channel_id=1, source_target_pairs={{0,6},{2,4},{4,2},{6,0},{8,14},{10,12},{12,10},{14,8},{16,22},{18,... | collective-permute-start | bytes 208904 | tf_op jit(solution)/shard_map/ppermute | solution.py:180
  32.7 4.7 %collective-permute-start.12 = (bf16[272,128]{1,0:T(8,128)(2,1)S(1)}, bf16[272,128]{1,0:T(8,128)(2,1)S(1)}, u32[]{:S(2)}, u32[]{:S(2)}) collective-permute-start(bf16[272,128]{1,0:T(8,128)(2,1)S(1)} %get-tuple-element.46), channel_id=1, source_target_pairs={{0,4},{2,6},{4,0},{6,2},{8,12},{10,14},{12,8},{14,10},{16,20},{18,... | collective-permute-start | bytes 208904 | tf_op jit(solution)/shard_map/ppermute | solution.py:180
  33.1 4.3 %collective-permute-start.11 = (bf16[272,128]{1,0:T(8,128)(2,1)S(1)}, bf16[272,128]{1,0:T(8,128)(2,1)S(1)}, u32[]{:S(2)}, u32[]{:S(2)}) collective-permute-start(bf16[272,128]{1,0:T(8,128)(2,1)S(1)} %get-tuple-element.46), channel_id=1, source_target_pairs={{0,2},{2,0},{4,6},{6,4},{8,10},{10,8},{12,14},{14,12},{16,18},{18,... | collective-permute-start | bytes 208904 | tf_op jit(solution)/shard_map/ppermute | solution.py:180
  34.7 5.0 %collective-permute-start.19 = (bf16[272,128]{1,0:T(8,128)(2,1)S(1)}, bf16[272,128]{1,0:T(8,128)(2,1)S(1)}, u32[]{:S(2)}, u32[]{:S(2)}) collective-permute-start(bf16[272,128]{1,0:T(8,128)(2,1)S(1)} %add_convert_fusion.1), channel_id=1, source_target_pairs={{0,8},{2,10},{4,12},{6,14},{8,0},{10,2},{12,4},{14,6},{16,24},{18,... | collective-permute-start | bytes 208904 | tf_op jit(solution)/shard_map/ppermute | solution.py:180
  37.4 7.4 %copy-start.3 = (bf16[256,512]{1,0:T(8,128)(2,1)S(1)}, bf16[256,512]{1,0:T(8,128)(2,1)}, u32[]{:S(2)}) copy-start(bf16[256,512]{1,0:T(8,128)(2,1)} %refs_7_.5) | copy-start | bytes 786436
  37.5 7.4 %copy-start.1 = (bf16[256,512]{1,0:T(8,128)(2,1)S(1)}, bf16[256,512]{1,0:T(8,128)(2,1)}, u32[]{:S(2)}) copy-start(bf16[256,512]{1,0:T(8,128)(2,1)} %refs_6_.5) | copy-start | bytes 786436
  37.5 5.1 %collective-permute-start.14 = (bf16[272,128]{1,0:T(8,128)(2,1)S(1)}, bf16[272,128]{1,0:T(8,128)(2,1)S(1)}, u32[]{:S(2)}, u32[]{:S(2)}) collective-permute-start(bf16[272,128]{1,0:T(8,128)(2,1)S(1)} %add_convert_fusion.3), channel_id=1, source_target_pairs={{0,8},{2,10},{4,12},{6,14},{8,0},{10,2},{12,4},{14,6},{16,24},{18,... | collective-permute-start | bytes 208904 | tf_op jit(solution)/shard_map/ppermute | solution.py:180
  39.7 8.0 %collective-permute-start.20 = (bf16[272,128]{1,0:T(8,128)(2,1)S(1)}, bf16[272,128]{1,0:T(8,128)(2,1)S(1)}, u32[]{:S(2)}, u32[]{:S(2)}) collective-permute-start(bf16[272,128]{1,0:T(8,128)(2,1)S(1)} %add_convert_fusion.refs_5_), channel_id=1, source_target_pairs={{0,16},{2,18},{4,20},{6,22},{8,24},{10,26},{12,28},{14,30},{16,0},... | collective-permute-start | bytes 208904 | tf_op jit(solution)/shard_map/ppermute | solution.py:180
  42.6 6.0 %collective-permute-start.15 = (bf16[272,128]{1,0:T(8,128)(2,1)S(1)}, bf16[272,128]{1,0:T(8,128)(2,1)S(1)}, u32[]{:S(2)}, u32[]{:S(2)}) collective-permute-start(bf16[272,128]{1,0:T(8,128)(2,1)S(1)} %add_convert_fusion.2.refs_5_), channel_id=1, source_target_pairs={{0,16},{2,18},{4,20},{6,22},{8,24},{10,26},{12,28},{14,30},{16,0},... | collective-permute-start | bytes 208904 | tf_op jit(solution)/shard_map/ppermute | solution.py:180

commit v4 on v3

--- a/solution.py
+++ b/solution.py
@@ -40,28 +40,23 @@
     return rows >= lax.broadcasted_iota(jnp.int32, (length, length), 1)
 
 
-def state_kernel(halves, dim, k_hbm, v_hbm, *refs):
-    wide, narrow = refs[: len(halves)], refs[len(halves) : 2 * len(halves)]
-    k_ref, v_ref, k_sem, v_sem = refs[2 * len(halves) :]
-    k_copy = pltpu.make_async_copy(k_hbm, k_ref, k_sem)
-    v_copy = pltpu.make_async_copy(v_hbm, v_ref, v_sem)
-    k_copy.start()
-    v_copy.start()
-    k_copy.wait()
-    v_copy.wait()
-    for heads, wide_ref, narrow_ref in zip(halves, wide, narrow):
+def state_kernel(halves, dim, kv_ref, *refs):
+    length = kv_ref.shape[0] // 2
+    for heads, wide_ref, narrow_ref in zip(halves, refs, refs[len(halves) :]):
         for i, h in enumerate(heads):
-            state = dot(k_ref[:, cols(h, dim)], v_ref[:, cols(h, dim)], 0, 0)
-            wide_ref[cols(i, dim), :] = state
-            narrow_ref[cols(i, dim), :] = state.astype(BF16)
-
-
-def scores_kernel(heads, dim, q_ref, k_ref, v_ref, local_ref):
-    mask = causal(q_ref.shape[0])
+            c, r = cols(h, dim), cols(i, dim)
+            state = dot(kv_ref[:length, c], kv_ref[length:, c], 0, 0)
+            wide_ref[r, :] = state
+            narrow_ref[r, :] = state.astype(BF16)
+
+
+def scores_kernel(heads, dim, q_ref, kv_ref, local_ref):
+    length = q_ref.shape[0]
+    mask = causal(length)
     for h in range(heads):
         c = cols(h, dim)
-        scores = jnp.where(mask, dot(q_ref[:, c], k_ref[:, c], 1, 1), 0.0).astype(BF16)
-        local_ref[:, c] = dot(scores, v_ref[:, c], 1, 0)
+        scores = jnp.where(mask, dot(q_ref[:, c], kv_ref[:length, c], 1, 1), 0.0).astype(BF16)
+        local_ref[:, c] = dot(scores, kv_ref[length:, c], 1, 0)
 
 
 def gathered(partners, parts, rows, reverse):
@@ -125,29 +120,31 @@
 def attended_kernel(halves, dim, width, *refs):
     n = len(halves)
     uns, guns, prefixes = refs[:n], refs[n : 2 * n], refs[2 * n : 3 * n]
-    sums_ref, other_ref, gain_ref, k_ref, v_ref, att_ref, gq_ref = refs[3 * n :]
+    sums_ref, other_ref, gain_ref, kv_ref, att_ref, gq_ref = refs[3 * n :]
     inverse, _ = scales(sums_ref, other_ref, width)
-    mask = causal(k_ref.shape[0])
+    length = kv_ref.shape[0] // 2
+    mask = causal(length)
     for heads, un_ref, gun_ref, prefix_ref in zip(halves, uns, guns, prefixes):
         for i, h in enumerate(heads):
             c, r = cols(h, dim), cols(i, dim)
             att_ref[:, c] = (gain_ref[:, c] * (un_ref[:, r] * inverse)).astype(BF16)
             gun = gun_ref[:, r]
-            mixed = jnp.where(mask, dot(gun, v_ref[:, c], 1, 1), 0.0).astype(BF16)
-            gq = dot(mixed, k_ref[:, c], 1, 0) + dot(gun, prefix_ref[r, :], 1, 1)
+            mixed = jnp.where(mask, dot(gun, kv_ref[length:, c], 1, 1), 0.0).astype(BF16)
+            gq = dot(mixed, kv_ref[:length, c], 1, 0) + dot(gun, prefix_ref[r, :], 1, 1)
             gq_ref[:, c] = gq.astype(BF16)
 
 
 def local_kernel(halves, dim, *refs):
     n = len(halves)
     guns = refs[:n]
-    q_ref, k_ref, v_ref, gk_ref, gv_ref = refs[n:]
-    mask = causal(q_ref.shape[0])
+    q_ref, kv_ref, gk_ref, gv_ref = refs[n:]
+    length = q_ref.shape[0]
+    mask = causal(length)
     for heads, gun_ref in zip(halves, guns):
         for i, h in enumerate(heads):
             c = cols(h, dim)
-            q, k, gun = q_ref[:, c], k_ref[:, c], gun_ref[:, cols(i, dim)]
-            mixed = jnp.where(mask, dot(gun, v_ref[:, c], 1, 1), 0.0).astype(BF16)
+            q, k, gun = q_ref[:, c], kv_ref[:length, c], gun_ref[:, cols(i, dim)]
+            mixed = jnp.where(mask, dot(gun, kv_ref[length:, c], 1, 1), 0.0).astype(BF16)
             scores = jnp.where(mask, dot(q, k, 1, 1), 0.0).astype(BF16)
             gk_ref[:, c] = dot(mixed, q, 0, 0)
             gv_ref[:, c] = dot(scores, gun, 0, 0)
@@ -156,8 +153,9 @@
 def final_kernel(heads, dim, partners, first, *refs):
     parts = refs[: len(partners)]
     refs = refs[len(partners) :]
-    message_ref, k_ref, v_ref, gk_ref, gv_ref = refs[:5]
-    gk_out, gv_out, state_out, gain_out = refs[5 if first else 9 :]
+    message_ref, kv_ref, gk_ref, gv_ref = refs[:4]
+    gk_out, gv_out, state_out, gain_out = refs[4 if first else 8 :]
+    length = kv_ref.shape[0] // 2
     for i, h in enumerate(heads):
         c, r = cols(h, dim), cols(i, dim)
         total = message_ref[r, :].astype(F32)
@@ -166,8 +164,8 @@
         gain = message_ref[row, :].astype(F32)
         if parts:
             suffix = gathered(partners, parts, r, True).astype(BF16)
-            gk = gk + dot(v_ref[:, c], suffix, 1, 1)
-            gv = gv + dot(k_ref[:, c], suffix, 1, 0)
+            gk = gk + dot(kv_ref[length:, c], suffix, 1, 1)
+            gv = gv + dot(kv_ref[:length, c], suffix, 1, 0)
             total = total + parts[-1][r, :].astype(F32)
             gain = gain + parts[-1][row, :].astype(F32)
         gk_out[:, r] = gk.astype(BF16)
@@ -180,31 +178,31 @@
     return lax.ppermute(message, "seq", [(i, i ^ partner) for i in range(count)])
 
 
-def scan(messages, owns, count):
-    partners, received = [], [[] for _ in messages]
-    distance = 1
-    if count >= PLANE:
-        partners = list(range(1, PLANE))
-        for parts, message in zip(received, messages):
-            parts.extend(swap(message, count, partner) for partner in partners)
-        distance = PLANE
+def scan(messages, owns, count, beside):
+    beside = dict(beside)
+    received = [[swap(m, count, partner) for partner in range(1, PLANE)] for m in messages]
+    partners = list(range(1, PLANE))
+    distance = PLANE
     while distance < count:
         for n, parts in enumerate(received):
-            if parts:
-                own = messages[n].astype(F32) if owns is None else owns[n]
-                got = [part.astype(F32) for part in parts]
-                if distance == PLANE:
-                    own = (own + got[0]) + (got[1] + got[2])
-                else:
-                    own = own + got[-1]
-                messages[n] = own.astype(BF16)
-                if owns is not None:
-                    owns[n] = own
+            got = parts if distance == PLANE else parts[-1:]
+            if (n, distance) in beside:
+                earlier = received[0]
+                earlier[0], operands = lax.optimization_barrier((earlier[0], beside[n, distance][1:]))
+                work = beside[n, distance][0](*operands)
+                got, beside[n, distance] = lax.optimization_barrier((got, work))
+                parts[-len(got) :] = got
+            own = messages[n].astype(F32) if owns is None else owns[n]
+            got = [part.astype(F32) for part in got]
+            own = (own + got[0]) + (got[1] + got[2]) if distance == PLANE else own + got[0]
+            messages[n] = own.astype(BF16)
+            if owns is not None:
+                owns[n] = own
         for n, parts in enumerate(received):
             parts.append(swap(messages[n], count, distance))
         partners.append(distance)
         distance *= 2
-    return partners, messages, received
+    return partners, messages, received, beside
 
 
 def on_device(queries, key_rows, values, cotangent, carried_state, norm_gain):
@@ -212,7 +210,7 @@
     heads, dim = carried_state.shape[:2]
     count = lax.axis_size("seq")
     head_count = lax.axis_size("head")
-    assert count & (count - 1) == 0 and count >= 2 * PLANE
+    assert count & (count - 1) == 0 and count > 2 * PLANE
     assert width == heads * dim and heads % 2 == 0
     total_width = width * head_count
     per = heads // 2
@@ -230,17 +228,17 @@
     size = length * width * 2
     state_size = heads * dim * dim * 2
 
-    hbm = pl.BlockSpec(memory_space=pltpu.HBM)
+    kv = jnp.concatenate([key_rows, values], axis=0)
     states = call(
         functools.partial(state_kernel, halves, dim),
         [state_f32] * 2 + [state_bf] * 2, block, 2 * size + state_size,
-        in_specs=[hbm, hbm],
-        scratch_shapes=[pltpu.VMEM((length, width), BF16)] * 2 + [pltpu.SemaphoreType.DMA] * 2,
-    )(key_rows, values)
-    partners, _, received = scan(list(states[2:]), list(states[:2]), count)
-    local = call(
+    )(kv)
+    local = (call(
         functools.partial(scores_kernel, heads, dim), tokens_f32, 2 * square, 5 * size,
-    )(queries, key_rows, values)
+    ), queries, kv)
+    spot = (1, PLANE)
+    partners, _, received, done = scan(list(states[2:]), list(states[:2]), count, {spot: local})
+    local = done[spot]
     unnormed, prefixes, sums = [], [], ()
     for n, members in enumerate(halves):
         un, prefix, both = call(
@@ -264,25 +262,26 @@
         )(sums, other, unnormed[n], cotangent, gain, queries)
         guns.append(gun)
         messages.append(message)
-    partners, messages, received = scan(messages, None, count)
-    attended, grad_q = call(
+    outer = (call(
         functools.partial(attended_kernel, halves, dim, total_width),
         (tokens_bf, tokens_bf), 2 * square + block, 8 * size,
-    )(*unnormed, *guns, *prefixes, sums, other, gain, key_rows, values)
+    ), *unnormed, *guns, *prefixes, sums, other, gain, kv)
     local_k, local_v = call(
         functools.partial(local_kernel, halves, dim), (tokens_f32, tokens_f32), 4 * square, 8 * size,
-    )(*guns, queries, key_rows, values)
+    )(*guns, queries, kv)
+    partners, messages, received, done = scan(messages, None, count, {spot: outer})
+    attended, grad_q = done[spot]
 
     outs = ()
     for n, members in enumerate(halves):
-        operands = (*received[n], messages[n], key_rows, values, local_k, local_v)
+        operands = (*received[n], messages[n], kv, local_k, local_v)
         column = functools.partial(lambda at, i: (0, at), n)
         outs = call(
             functools.partial(final_kernel, members, dim, partners, n == 0),
             (tokens_bf, tokens_bf, shape((heads, dim, dim), F32), shape((1, width), F32)),
             block, 5 * size + 4 * state_size,
             grid=(1,),
-            in_specs=[WHOLE] * len(operands) + [hbm] * len(outs),
+            in_specs=[WHOLE] * len(operands) + [pl.BlockSpec(memory_space=pl.ANY)] * len(outs),
             out_specs=[
                 pl.BlockSpec((length, per * dim), column),
                 pl.BlockSpec((length, per * dim), column),

time: 49.9 us -> 48.4 us (0.970)
  waiting for transfers between devices: 6.88 us -> 5.97 us
  local copies, waits for them, and re-layouts: 1.93 us -> 1.06 us
    ppermute x20, waiting for transfers between devices: 5.54 us -> 4.64 us  [swap(): lax.ppermute(message, 'seq', [(i, i ^ partner) for i in range(count)])]
    unnamed x16 -> x11, local copies, waits for them, and re-layouts: 1.93 us -> 1.04 us
  transfers between devices with their start and end apart: 21 -> 21, of which waited for: 11 -> 10; matrix products, arithmetic and copies ran while one was open for 1% -> 1% of each run, Pallas kernels for 10% -> 11%
where the time goes in v4:
time: 48.4 us; the launch traced here: 48.3 us
  starting transfers between devices  32.9 us (68%)
  Pallas kernels  7.2 us (15%)
  waiting for transfers between devices  5.97 us (12%)
  local copies, waits for them, and re-layouts  1.06 us (2%)
  between operations  0.8 us (2%)
    ppermute x20, starting transfers between devices, swap(): lax.ppermute(message, 'seq', [(i, i ^ partner) for i in range(count)])  32.9 us
    ppermute x20, waiting for transfers between devices, swap(): lax.ppermute(message, 'seq', [(i, i ^ partner) for i in range(count)])  4.64 us
    pallas_call x2, Pallas kernels, on_device(): call(functools.partial(final_kernel, members, dim, partners, n == 0), (to...  2 us
    pallas_call x2, Pallas kernels, scan(): work = beside[n, distance][0](*operands)  2 us
    pallas_call x1, Pallas kernels, on_device(): call(functools.partial(local_kernel, halves, dim), (tokens_f32, tokens_f3...  1.45 us
    ppermute x1, waiting for transfers between devices, on_device(): lax.ppermute(partner, 'head', [(i, (i + 1) % head_count) for i in range(h...  1.33 us
    unnamed x11, local copies, waits for them, and re-layouts  1.04 us
  transfers between devices with their start and end apart: 21, of which 10 were waited for; matrix products, arithmetic and copies ran while one was open for 1% of the time, Pallas kernels for 11%

profile of v4, /device:TPU:0, one launch (start us, length us, event | category | flops | bytes accessed | tf_op | source)
XLA Modules:
  0.0 48.3 jit_solution(4657663607688658906)
XLA Ops:
  0.6 1.0 %constant_dynamic-update-slice_fusion.1 = bf16[512,512]{1,0:T(8,128)(2,1)S(1)} fusion(bf16[256,512]{1,0:T(8,128)(2,1)} %param.7), kind=kLoop, calls=%fused_computation.11 | loop fusion | bytes 524288
  1.7 0.0 copy-done.4
  1.7 0.3 shard_map.109
  2.0 0.0 copy-start
  2.0 4.0 %collective-permute-start.7 = (bf16[256,128]{1,0:T(8,128)(2,1)S(1)}, bf16[256,128]{1,0:T(8,128)(2,1)S(1)}, u32[]{:S(2)}, u32[]{:S(2)}) collective-permute-start(bf16[256,128]{1,0:T(8,128)(2,1)S(1)} %get-tuple-element.56), channel_id=1, source_target_pairs={{0,6},{2,4},{4,2},{6,0},{8,14},{10,12},{12,10},{14,8},{16,22},{18,... | collective-permute-start | bytes 196616 | tf_op jit(solution)/shard_map/ppermute | solution.py:178
  5.9 0.5 %collective-permute-start.6 = (bf16[256,128]{1,0:T(8,128)(2,1)S(1)}, bf16[256,128]{1,0:T(8,128)(2,1)S(1)}, u32[]{:S(2)}, u32[]{:S(2)}) collective-permute-start(bf16[256,128]{1,0:T(8,128)(2,1)S(1)} %get-tuple-element.56), channel_id=1, source_target_pairs={{0,4},{2,6},{4,0},{6,2},{8,12},{10,14},{12,8},{14,10},{16,20},{18,... | collective-permute-start | bytes 196616 | tf_op jit(solution)/shard_map/ppermute | solution.py:178
  6.4 0.1 collective-permute-start.3
  6.6 2.8 %collective-permute-start.2 = (bf16[256,128]{1,0:T(8,128)(2,1)S(1)}, bf16[256,128]{1,0:T(8,128)(2,1)S(1)}, u32[]{:S(2)}, u32[]{:S(2)}) collective-permute-start(bf16[256,128]{1,0:T(8,128)(2,1)S(1)} %get-tuple-element.55), channel_id=1, source_target_pairs={{0,6},{2,4},{4,2},{6,0},{8,14},{10,12},{12,10},{14,8},{16,22},{18,... | collective-permute-start | bytes 196616 | tf_op jit(solution)/shard_map/ppermute | solution.py:178
  9.4 0.5 %collective-permute-start.1 = (bf16[256,128]{1,0:T(8,128)(2,1)S(1)}, bf16[256,128]{1,0:T(8,128)(2,1)S(1)}, u32[]{:S(2)}, u32[]{:S(2)}) collective-permute-start(bf16[256,128]{1,0:T(8,128)(2,1)S(1)} %get-tuple-element.55), channel_id=1, source_target_pairs={{0,4},{2,6},{4,0},{6,2},{8,12},{10,14},{12,8},{14,10},{16,20},{18,... | collective-permute-start | bytes 196616 | tf_op jit(solution)/shard_map/ppermute | solution.py:178
  9.9 0.0 collective-permute-done.7.refs_2_
  9.9 0.6 %collective-permute-start = (bf16[256,128]{1,0:T(8,128)(2,1)S(1)}, bf16[256,128]{1,0:T(8,128)(2,1)S(1)}, u32[]{:S(2)}, u32[]{:S(2)}) collective-permute-start(bf16[256,128]{1,0:T(8,128)(2,1)S(1)} %get-tuple-element.55), channel_id=1, source_target_pairs={{0,2},{2,0},{4,6},{6,4},{8,10},{10,8},{12,14},{14,12},{16,18},{18,... | collective-permute-start | bytes 196616 | tf_op jit(solution)/shard_map/ppermute | solution.py:178
  10.6 0.4 collective-permute-done.6.refs_1_
  11.0 0.0 collective-permute-done.3.refs_0_
  11.1 1.6 %collective-permute-start.8 = (bf16[256,128]{1,0:T(8,128)(2,1)S(1)}, bf16[256,128]{1,0:T(8,128)(2,1)S(1)}, u32[]{:S(2)}, u32[]{:S(2)}) collective-permute-start(bf16[256,128]{1,0:T(8,128)(2,1)S(1)} %fusion.1), channel_id=1, source_target_pairs={{0,8},{2,10},{4,12},{6,14},{8,0},{10,2},{12,4},{14,6},{16,24},{18,... | collective-permute-start | bytes 196616 | tf_op jit(solution)/shard_map/ppermute | solution.py:178
  12.7 0.7 %shard_map.110.refs_6_.refs_7_ = f32[256,512]{1,0:T(8,128)S(1)} custom-call(bf16[256,512]{1,0:T(8,128)(2,1)S(1)} %copy-done, bf16[512,512]{1,0:T(8,128)(2,1)S(1)} %constant_dynamic-update-slice_fusion.kv_ref.refs_9_.refs_3_.refs_6_), custom_call_target="tpu_custom_call" | custom-call | flops 134217728 | bytes 1310720 | tf_op jit(solution)/shard_map/pallas_call | solution.py:192
  13.4 0.3 collective-permute-done.1.refs_1_
  13.7 0.5 %collective-permute-done.refs_0_ = bf16[256,128]{1,0:T(8,128)(2,1)S(1)} collective-permute-done((bf16[256,128]{1,0:T(8,128)(2,1)S(1)}, bf16[256,128]{1,0:T(8,128)(2,1)S(1)}, u32[]{:S(2)}, u32[]{:S(2)}) %collective-permute-start) | collective-permute-done | bytes 65568 | tf_op jit(solution)/shard_map/ppermute | solution.py:178
  14.2 1.6 %collective-permute-start.4 = (bf16[256,128]{1,0:T(8,128)(2,1)S(1)}, bf16[256,128]{1,0:T(8,128)(2,1)S(1)}, u32[]{:S(2)}, u32[]{:S(2)}) collective-permute-start(bf16[256,128]{1,0:T(8,128)(2,1)S(1)} %fusion), channel_id=1, source_target_pairs={{0,8},{2,10},{4,12},{6,14},{8,0},{10,2},{12,4},{14,6},{16,24},{18,... | collective-permute-start | bytes 196616 | tf_op jit(solution)/shard_map/ppermute | solution.py:178
  15.9 0.2 collective-permute-done.8.refs_3_
  16.1 0.0 copy-start.1
  16.1 2.7 %collective-permute-start.9 = (bf16[256,128]{1,0:T(8,128)(2,1)S(1)}, bf16[256,128]{1,0:T(8,128)(2,1)S(1)}, u32[]{:S(2)}, u32[]{:S(2)}) collective-permute-start(bf16[256,128]{1,0:T(8,128)(2,1)S(1)} %add_convert_fusion.4), channel_id=1, source_target_pairs={{0,16},{2,18},{4,20},{6,22},{8,24},{10,26},{12,28},{14,30},{16,0},... | collective-permute-start | bytes 196616 | tf_op jit(solution)/shard_map/ppermute | solution.py:178
  18.8 2.5 %collective-permute-start.5 = (bf16[256,128]{1,0:T(8,128)(2,1)S(1)}, bf16[256,128]{1,0:T(8,128)(2,1)S(1)}, u32[]{:S(2)}, u32[]{:S(2)}) collective-permute-start(bf16[256,128]{1,0:T(8,128)(2,1)S(1)} %add_convert_fusion.5), channel_id=1, source_target_pairs={{0,16},{2,18},{4,20},{6,22},{8,24},{10,26},{12,28},{14,30},{16,0},... | collective-permute-start | bytes 196616 | tf_op jit(solution)/shard_map/ppermute | solution.py:178
  21.3 1.5 %collective-permute-done.9.refs_4_ = bf16[256,128]{1,0:T(8,128)(2,1)S(1)} collective-permute-done((bf16[256,128]{1,0:T(8,128)(2,1)S(1)}, bf16[256,128]{1,0:T(8,128)(2,1)S(1)}, u32[]{:S(2)}, u32[]{:S(2)}) %collective-permute-start.9) | collective-permute-done | bytes 65568 | tf_op jit(solution)/shard_map/ppermute | solution.py:178
  22.8 0.3 shard_map.111
  23.1 0.9 %collective-permute-done.5.refs_4_ = bf16[256,128]{1,0:T(8,128)(2,1)S(1)} collective-permute-done((bf16[256,128]{1,0:T(8,128)(2,1)S(1)}, bf16[256,128]{1,0:T(8,128)(2,1)S(1)}, u32[]{:S(2)}, u32[]{:S(2)}) %collective-permute-start.5) | collective-permute-done | bytes 65568 | tf_op jit(solution)/shard_map/ppermute | solution.py:178
  24.0 0.3 shard_map.112
  24.4 0.1 collective-permute-start.10
  24.5 1.3 %collective-permute-done.10.other_ref.refs_7_ = f32[256,128]{1,0:T(8,128)S(1)} collective-permute-done((f32[256,128]{1,0:T(8,128)S(1)}, f32[256,128]{1,0:T(8,128)S(1)}, u32[]{:S(2)}, u32[]{:S(2)}) %collective-permute-start.10) | collective-permute-done | bytes 131104 | tf_op jit(solution)/shard_map/ppermute | solution.py:254
  25.8 0.4 shard_map.114
  26.2 1.6 %collective-permute-start.18 = (bf16[272,128]{1,0:T(8,128)(2,1)S(1)}, bf16[272,128]{1,0:T(8,128)(2,1)S(1)}, u32[]{:S(2)}, u32[]{:S(2)}) collective-permute-start(bf16[272,128]{1,0:T(8,128)(2,1)S(1)} %get-tuple-element.71), channel_id=1, source_target_pairs={{0,6},{2,4},{4,2},{6,0},{8,14},{10,12},{12,10},{14,8},{16,22},{18,... | collective-permute-start | bytes 208904 | tf_op jit(solution)/shard_map/ppermute | solution.py:178
  27.9 0.6 %collective-permute-start.17 = (bf16[272,128]{1,0:T(8,128)(2,1)S(1)}, bf16[272,128]{1,0:T(8,128)(2,1)S(1)}, u32[]{:S(2)}, u32[]{:S(2)}) collective-permute-start(bf16[272,128]{1,0:T(8,128)(2,1)S(1)} %get-tuple-element.71), channel_id=1, source_target_pairs={{0,4},{2,6},{4,0},{6,2},{8,12},{10,14},{12,8},{14,10},{16,20},{18,... | collective-permute-start | bytes 208904 | tf_op jit(solution)/shard_map/ppermute | solution.py:178
  28.5 1.3 %collective-permute-start.14 = (bf16[272,128]{1,0:T(8,128)(2,1)S(1)}, bf16[272,128]{1,0:T(8,128)(2,1)S(1)}, u32[]{:S(2)}, u32[]{:S(2)}) collective-permute-start(bf16[272,128]{1,0:T(8,128)(2,1)S(1)} %get-tuple-element.71), channel_id=1, source_target_pairs={{0,2},{2,0},{4,6},{6,4},{8,10},{10,8},{12,14},{14,12},{16,18},{18,... | collective-permute-start | bytes 208904 | tf_op jit(solution)/shard_map/ppermute | solution.py:178
  29.8 0.4 shard_map.113
  30.2 1.6 %collective-permute-start.13 = (bf16[272,128]{1,0:T(8,128)(2,1)S(1)}, bf16[272,128]{1,0:T(8,128)(2,1)S(1)}, u32[]{:S(2)}, u32[]{:S(2)}) collective-permute-start(bf16[272,128]{1,0:T(8,128)(2,1)S(1)} %get-tuple-element.69), channel_id=1, source_target_pairs={{0,6},{2,4},{4,2},{6,0},{8,14},{10,12},{12,10},{14,8},{16,22},{18,... | collective-permute-start | bytes 208904 | tf_op jit(solution)/shard_map/ppermute | solution.py:178
  31.8 0.6 %collective-permute-start.12 = (bf16[272,128]{1,0:T(8,128)(2,1)S(1)}, bf16[272,128]{1,0:T(8,128)(2,1)S(1)}, u32[]{:S(2)}, u32[]{:S(2)}) collective-permute-start(bf16[272,128]{1,0:T(8,128)(2,1)S(1)} %get-tuple-element.69), channel_id=1, source_target_pairs={{0,4},{2,6},{4,0},{6,2},{8,12},{10,14},{12,8},{14,10},{16,20},{18,... | collective-permute-start | bytes 208904 | tf_op jit(solution)/shard_map/ppermute | solution.py:178
  32.4 1.3 %collective-permute-start.11 = (bf16[272,128]{1,0:T(8,128)(2,1)S(1)}, bf16[272,128]{1,0:T(8,128)(2,1)S(1)}, u32[]{:S(2)}, u32[]{:S(2)}) collective-permute-start(bf16[272,128]{1,0:T(8,128)(2,1)S(1)} %get-tuple-element.69), channel_id=1, source_target_pairs={{0,2},{2,0},{4,6},{6,4},{8,10},{10,8},{12,14},{14,12},{16,18},{18,... | collective-permute-start | bytes 208904 | tf_op jit(solution)/shard_map/ppermute | solution.py:178
  33.7 0.0 collective-permute-done.17.refs_1_
  33.8 1.6 %collective-permute-start.19 = (bf16[272,128]{1,0:T(8,128)(2,1)S(1)}, bf16[272,128]{1,0:T(8,128)(2,1)S(1)}, u32[]{:S(2)}, u32[]{:S(2)}) collective-permute-start(bf16[272,128]{1,0:T(8,128)(2,1)S(1)} %add_convert_fusion.1), channel_id=1, source_target_pairs={{0,8},{2,10},{4,12},{6,14},{8,0},{10,2},{12,4},{14,6},{16,24},{18,... | collective-permute-start | bytes 208904 | tf_op jit(solution)/shard_map/ppermute | solution.py:178
  35.4 1.3 %shard_map.115 = (bf16[256,512]{1,0:T(8,128)(2,1)}, bf16[256,512]{1,0:T(8,128)(2,1)}) custom-call(f32[256,256]{1,0:T(8,128)S(1)} %get-tuple-element.76.un_ref.refs_0_, f32[256,256]{1,0:T(8,128)S(1)} %get-tuple-element.77.un_ref.refs_1_, bf16[256,256]{1,0:T(8,128)(2,1)S(1)} %get-tuple-element.78.refs_2_.refs_0_, ...), custom_call_target="tpu_custom_call" | custom-call | flops 167772160 | bytes 2097152 | tf_op jit(solution)/shard_map/pallas_call | solution.py:192
  36.8 1.4 %collective-permute-start.15 = (bf16[272,128]{1,0:T(8,128)(2,1)S(1)}, bf16[272,128]{1,0:T(8,128)(2,1)S(1)}, u32[]{:S(2)}, u32[]{:S(2)}) collective-permute-start(bf16[272,128]{1,0:T(8,128)(2,1)S(1)} %add_convert_fusion.3), channel_id=1, source_target_pairs={{0,8},{2,10},{4,12},{6,14},{8,0},{10,2},{12,4},{14,6},{16,24},{18,... | collective-permute-start | bytes 208904 | tf_op jit(solution)/shard_map/ppermute | solution.py:178
  38.3 3.4 %collective-permute-start.20 = (bf16[272,128]{1,0:T(8,128)(2,1)S(1)}, bf16[272,128]{1,0:T(8,128)(2,1)S(1)}, u32[]{:S(2)}, u32[]{:S(2)}) collective-permute-start(bf16[272,128]{1,0:T(8,128)(2,1)S(1)} %add_convert_fusion.refs_5_), channel_id=1, source_target_pairs={{0,16},{2,18},{4,20},{6,22},{8,24},{10,26},{12,28},{14,30},{16,0},... | collective-permute-start | bytes 208904 | tf_op jit(solution)/shard_map/ppermute | solution.py:178
  41.7 0.3 collective-permute-done.15.refs_3_
  42.0 2.3 %collective-permute-start.16 = (bf16[272,128]{1,0:T(8,128)(2,1)S(1)}, bf16[272,128]{1,0:T(8,128)(2,1)S(1)}, u32[]{:S(2)}, u32[]{:S(2)}) collective-permute-start(bf16[272,128]{1,0:T(8,128)(2,1)S(1)} %add_convert_fusion.2.refs_5_), channel_id=1, source_target_pairs={{0,16},{2,18},{4,20},{6,22},{8,24},{10,26},{12,28},{14,30},{16,0},... | collective-permute-start | bytes 208904 | tf_op jit(solution)/shard_map/ppermute | solution.py:178
  44.3 1.5 %shard_map.116 = (f32[256,512]{1,0:T(8,128)S(1)}, f32[256,512]{1,0:T(8,128)S(1)}) custom-call(bf16[256,256]{1,0:T(8,128)(2,1)S(1)} %get-tuple-element.78.refs_2_.refs_0_, bf16[256,256]{1,0:T(8,128)(2,1)S(1)} %get-tuple-element.79.refs_3_.refs_1_, bf16[256,512]{1,0:T(8,128)(2,1)S(1)} %copy-done, ...), custom_call_target="tpu_custom_call" | custom-call | flops 268435456 | bytes 2097152 | tf_op jit(solution)/shard_map/pallas_call | solution.py:269
  45.8 0.2 collective-permute-done.20.refs_4_
  45.9 1.0 %shard_map.117 = (bf16[256,512]{1,0:T(8,128)(2,1)}, bf16[256,512]{1,0:T(8,128)(2,1)}, f32[4,128,128]{2,1,0:T(8,128)}, f32[1,512]{1,0:T(1,128)}) custom-call(bf16[272,128]{1,0:T(8,128)(2,1)S(1)} %collective-permute-done.14.refs_0_, bf16[272,128]{1,0:T(8,128)(2,1)S(1)} %collective-permute-done.17.refs_1_, ...), custom_call_target="tpu_custom_call" | custom-call | flops 33554432 | bytes 1835008 | tf_op jit(solution)/shard_map/pallas_call | solution.py:279
  47.0 0.3 collective-permute-done.16.refs_4_
  47.3 1.0 %shard_map.118 = (bf16[256,512]{1,0:T(8,128)(2,1)}, bf16[256,512]{1,0:T(8,128)(2,1)}, f32[4,128,128]{2,1,0:T(8,128)}, f32[1,512]{1,0:T(1,128)}) custom-call(bf16[272,128]{1,0:T(8,128)(2,1)S(1)} %collective-permute-done.11.refs_0_, ...), custom_call_target="tpu_custom_call", output_to_operand_aliasing={{0}: (9, {}), {1}: (10, {}), {2}: (11, {}), {3}: (12, {})} | custom-call | flops 33554432 | bytes 1835008 | tf_op jit(solution)/shard_map/pallas_call | solution.py:279
  (24 shorter events, 0.4 us)
Async XLA Ops:
  0.6 1.0 %copy-start.4 = (bf16[256,512]{1,0:T(8,128)(2,1)S(1)}, bf16[256,512]{1,0:T(8,128)(2,1)}, u32[]{:S(2)}) copy-start(bf16[256,512]{1,0:T(8,128)(2,1)} %param.8) | copy-start | bytes 786436
  2.0 10.7 %copy-start = (bf16[256,512]{1,0:T(8,128)(2,1)S(1)}, bf16[256,512]{1,0:T(8,128)(2,1)}, u32[]{:S(2)}) copy-start(bf16[256,512]{1,0:T(8,128)(2,1)} %refs_2_.1) | copy-start | bytes 786436
  2.0 8.0 %collective-permute-start.7 = (bf16[256,128]{1,0:T(8,128)(2,1)S(1)}, bf16[256,128]{1,0:T(8,128)(2,1)S(1)}, u32[]{:S(2)}, u32[]{:S(2)}) collective-permute-start(bf16[256,128]{1,0:T(8,128)(2,1)S(1)} %get-tuple-element.56), channel_id=1, source_target_pairs={{0,6},{2,4},{4,2},{6,0},{8,14},{10,12},{12,10},{14,8},{16,22},{18,... | collective-permute-start | bytes 196616 | tf_op jit(solution)/shard_map/ppermute | solution.py:178
  5.9 5.1 %collective-permute-start.6 = (bf16[256,128]{1,0:T(8,128)(2,1)S(1)}, bf16[256,128]{1,0:T(8,128)(2,1)S(1)}, u32[]{:S(2)}, u32[]{:S(2)}) collective-permute-start(bf16[256,128]{1,0:T(8,128)(2,1)S(1)} %get-tuple-element.56), channel_id=1, source_target_pairs={{0,4},{2,6},{4,0},{6,2},{8,12},{10,14},{12,8},{14,10},{16,20},{18,... | collective-permute-start | bytes 196616 | tf_op jit(solution)/shard_map/ppermute | solution.py:178
  6.4 4.6 %collective-permute-start.3 = (bf16[256,128]{1,0:T(8,128)(2,1)S(1)}, bf16[256,128]{1,0:T(8,128)(2,1)S(1)}, u32[]{:S(2)}, u32[]{:S(2)}) collective-permute-start(bf16[256,128]{1,0:T(8,128)(2,1)S(1)} %get-tuple-element.56), channel_id=1, source_target_pairs={{0,2},{2,0},{4,6},{6,4},{8,10},{10,8},{12,14},{14,12},{16,18},{18,... | collective-permute-start | bytes 196616 | tf_op jit(solution)/shard_map/ppermute | solution.py:178
  6.6 6.8 %collective-permute-start.2 = (bf16[256,128]{1,0:T(8,128)(2,1)S(1)}, bf16[256,128]{1,0:T(8,128)(2,1)S(1)}, u32[]{:S(2)}, u32[]{:S(2)}) collective-permute-start(bf16[256,128]{1,0:T(8,128)(2,1)S(1)} %get-tuple-element.55), channel_id=1, source_target_pairs={{0,6},{2,4},{4,2},{6,0},{8,14},{10,12},{12,10},{14,8},{16,22},{18,... | collective-permute-start | bytes 196616 | tf_op jit(solution)/shard_map/ppermute | solution.py:178
  9.4 4.3 %collective-permute-start.1 = (bf16[256,128]{1,0:T(8,128)(2,1)S(1)}, bf16[256,128]{1,0:T(8,128)(2,1)S(1)}, u32[]{:S(2)}, u32[]{:S(2)}) collective-permute-start(bf16[256,128]{1,0:T(8,128)(2,1)S(1)} %get-tuple-element.55), channel_id=1, source_target_pairs={{0,4},{2,6},{4,0},{6,2},{8,12},{10,14},{12,8},{14,10},{16,20},{18,... | collective-permute-start | bytes 196616 | tf_op jit(solution)/shard_map/ppermute | solution.py:178
  9.9 4.3 %collective-permute-start = (bf16[256,128]{1,0:T(8,128)(2,1)S(1)}, bf16[256,128]{1,0:T(8,128)(2,1)S(1)}, u32[]{:S(2)}, u32[]{:S(2)}) collective-permute-start(bf16[256,128]{1,0:T(8,128)(2,1)S(1)} %get-tuple-element.55), channel_id=1, source_target_pairs={{0,2},{2,0},{4,6},{6,4},{8,10},{10,8},{12,14},{14,12},{16,18},{18,... | collective-permute-start | bytes 196616 | tf_op jit(solution)/shard_map/ppermute | solution.py:178
  11.1 5.0 %collective-permute-start.8 = (bf16[256,128]{1,0:T(8,128)(2,1)S(1)}, bf16[256,128]{1,0:T(8,128)(2,1)S(1)}, u32[]{:S(2)}, u32[]{:S(2)}) collective-permute-start(bf16[256,128]{1,0:T(8,128)(2,1)S(1)} %fusion.1), channel_id=1, source_target_pairs={{0,8},{2,10},{4,12},{6,14},{8,0},{10,2},{12,4},{14,6},{16,24},{18,... | collective-permute-start | bytes 196616 | tf_op jit(solution)/shard_map/ppermute | solution.py:178
  14.2 4.5 %collective-permute-start.4 = (bf16[256,128]{1,0:T(8,128)(2,1)S(1)}, bf16[256,128]{1,0:T(8,128)(2,1)S(1)}, u32[]{:S(2)}, u32[]{:S(2)}) collective-permute-start(bf16[256,128]{1,0:T(8,128)(2,1)S(1)} %fusion), channel_id=1, source_target_pairs={{0,8},{2,10},{4,12},{6,14},{8,0},{10,2},{12,4},{14,6},{16,24},{18,... | collective-permute-start | bytes 196616 | tf_op jit(solution)/shard_map/ppermute | solution.py:178
  16.0 6.7 %copy-start.2 = (f32[4,128,128]{2,1,0:T(8,128)S(1)}, f32[4,128,128]{2,1,0:T(8,128)}, u32[]{:S(2)}) copy-start(f32[4,128,128]{2,1,0:T(8,128)} %refs_9_.1) | copy-start | bytes 786436
  16.1 6.7 %copy-start.1 = (bf16[256,512]{1,0:T(8,128)(2,1)S(1)}, bf16[256,512]{1,0:T(8,128)(2,1)}, u32[]{:S(2)}) copy-start(bf16[256,512]{1,0:T(8,128)(2,1)} %cot_ref.3) | copy-start | bytes 786436
  16.1 6.6 %collective-permute-start.9 = (bf16[256,128]{1,0:T(8,128)(2,1)S(1)}, bf16[256,128]{1,0:T(8,128)(2,1)S(1)}, u32[]{:S(2)}, u32[]{:S(2)}) collective-permute-start(bf16[256,128]{1,0:T(8,128)(2,1)S(1)} %add_convert_fusion.4), channel_id=1, source_target_pairs={{0,16},{2,18},{4,20},{6,22},{8,24},{10,26},{12,28},{14,30},{16,0},... | collective-permute-start | bytes 196616 | tf_op jit(solution)/shard_map/ppermute | solution.py:178
  18.8 4.0 %copy-start.3 = (f32[512]{0:T(512)S(1)}, f32[512]{0:T(512)}, u32[]{:S(2)}) copy-start(f32[512]{0:T(512)} %param.11) | copy-start | bytes 6148
  18.8 5.2 %collective-permute-start.5 = (bf16[256,128]{1,0:T(8,128)(2,1)S(1)}, bf16[256,128]{1,0:T(8,128)(2,1)S(1)}, u32[]{:S(2)}, u32[]{:S(2)}) collective-permute-start(bf16[256,128]{1,0:T(8,128)(2,1)S(1)} %add_convert_fusion.5), channel_id=1, source_target_pairs={{0,16},{2,18},{4,20},{6,22},{8,24},{10,26},{12,28},{14,30},{16,0},... | collective-permute-start | bytes 196616 | tf_op jit(solution)/shard_map/ppermute | solution.py:178
  24.4 1.4 %collective-permute-start.10 = (f32[256,128]{1,0:T(8,128)S(1)}, f32[256,128]{1,0:T(8,128)S(1)}, u32[]{:S(2)}, u32[]{:S(2)}) collective-permute-start(f32[256,128]{1,0:T(8,128)S(1)} %get-tuple-element.82.sums_ref.refs_6_), channel_id=1, source_target_pairs={{0,1},{1,0},{2,3},{3,2},{4,5},{5,4},{6,7},{7,6},{8,9},{9,8},{10,11... | collective-permute-start | bytes 393224 | tf_op jit(solution)/shard_map/ppermute | solution.py:254
  26.2 6.2 %collective-permute-start.18 = (bf16[272,128]{1,0:T(8,128)(2,1)S(1)}, bf16[272,128]{1,0:T(8,128)(2,1)S(1)}, u32[]{:S(2)}, u32[]{:S(2)}) collective-permute-start(bf16[272,128]{1,0:T(8,128)(2,1)S(1)} %get-tuple-element.71), channel_id=1, source_target_pairs={{0,6},{2,4},{4,2},{6,0},{8,14},{10,12},{12,10},{14,8},{16,22},{18,... | collective-permute-start | bytes 208904 | tf_op jit(solution)/shard_map/ppermute | solution.py:178
  27.9 5.9 %collective-permute-start.17 = (bf16[272,128]{1,0:T(8,128)(2,1)S(1)}, bf16[272,128]{1,0:T(8,128)(2,1)S(1)}, u32[]{:S(2)}, u32[]{:S(2)}) collective-permute-start(bf16[272,128]{1,0:T(8,128)(2,1)S(1)} %get-tuple-element.71), channel_id=1, source_target_pairs={{0,4},{2,6},{4,0},{6,2},{8,12},{10,14},{12,8},{14,10},{16,20},{18,... | collective-permute-start | bytes 208904 | tf_op jit(solution)/shard_map/ppermute | solution.py:178
  28.5 5.3 %collective-permute-start.14 = (bf16[272,128]{1,0:T(8,128)(2,1)S(1)}, bf16[272,128]{1,0:T(8,128)(2,1)S(1)}, u32[]{:S(2)}, u32[]{:S(2)}) collective-permute-start(bf16[272,128]{1,0:T(8,128)(2,1)S(1)} %get-tuple-element.71), channel_id=1, source_target_pairs={{0,2},{2,0},{4,6},{6,4},{8,10},{10,8},{12,14},{14,12},{16,18},{18,... | collective-permute-start | bytes 208904 | tf_op jit(solution)/shard_map/ppermute | solution.py:178
  30.2 6.6 %collective-permute-start.13 = (bf16[272,128]{1,0:T(8,128)(2,1)S(1)}, bf16[272,128]{1,0:T(8,128)(2,1)S(1)}, u32[]{:S(2)}, u32[]{:S(2)}) collective-permute-start(bf16[272,128]{1,0:T(8,128)(2,1)S(1)} %get-tuple-element.69), channel_id=1, source_target_pairs={{0,6},{2,4},{4,2},{6,0},{8,14},{10,12},{12,10},{14,8},{16,22},{18,... | collective-permute-start | bytes 208904 | tf_op jit(solution)/shard_map/ppermute | solution.py:178
  31.8 5.0 %collective-permute-start.12 = (bf16[272,128]{1,0:T(8,128)(2,1)S(1)}, bf16[272,128]{1,0:T(8,128)(2,1)S(1)}, u32[]{:S(2)}, u32[]{:S(2)}) collective-permute-start(bf16[272,128]{1,0:T(8,128)(2,1)S(1)} %get-tuple-element.69), channel_id=1, source_target_pairs={{0,4},{2,6},{4,0},{6,2},{8,12},{10,14},{12,8},{14,10},{16,20},{18,... | collective-permute-start | bytes 208904 | tf_op jit(solution)/shard_map/ppermute | solution.py:178
  32.4 4.4 %collective-permute-start.11 = (bf16[272,128]{1,0:T(8,128)(2,1)S(1)}, bf16[272,128]{1,0:T(8,128)(2,1)S(1)}, u32[]{:S(2)}, u32[]{:S(2)}) collective-permute-start(bf16[272,128]{1,0:T(8,128)(2,1)S(1)} %get-tuple-element.69), channel_id=1, source_target_pairs={{0,2},{2,0},{4,6},{6,4},{8,10},{10,8},{12,14},{14,12},{16,18},{18,... | collective-permute-start | bytes 208904 | tf_op jit(solution)/shard_map/ppermute | solution.py:178
  33.8 4.5 %collective-permute-start.19 = (bf16[272,128]{1,0:T(8,128)(2,1)S(1)}, bf16[272,128]{1,0:T(8,128)(2,1)S(1)}, u32[]{:S(2)}, u32[]{:S(2)}) collective-permute-start(bf16[272,128]{1,0:T(8,128)(2,1)S(1)} %add_convert_fusion.1), channel_id=1, source_target_pairs={{0,8},{2,10},{4,12},{6,14},{8,0},{10,2},{12,4},{14,6},{16,24},{18,... | collective-permute-start | bytes 208904 | tf_op jit(solution)/shard_map/ppermute | solution.py:178
  36.8 5.1 %collective-permute-start.15 = (bf16[272,128]{1,0:T(8,128)(2,1)S(1)}, bf16[272,128]{1,0:T(8,128)(2,1)S(1)}, u32[]{:S(2)}, u32[]{:S(2)}) collective-permute-start(bf16[272,128]{1,0:T(8,128)(2,1)S(1)} %add_convert_fusion.3), channel_id=1, source_target_pairs={{0,8},{2,10},{4,12},{6,14},{8,0},{10,2},{12,4},{14,6},{16,24},{18,... | collective-permute-start | bytes 208904 | tf_op jit(solution)/shard_map/ppermute | solution.py:178
  38.3 7.7 %collective-permute-start.20 = (bf16[272,128]{1,0:T(8,128)(2,1)S(1)}, bf16[272,128]{1,0:T(8,128)(2,1)S(1)}, u32[]{:S(2)}, u32[]{:S(2)}) collective-permute-start(bf16[272,128]{1,0:T(8,128)(2,1)S(1)} %add_convert_fusion.refs_5_), channel_id=1, source_target_pairs={{0,16},{2,18},{4,20},{6,22},{8,24},{10,26},{12,28},{14,30},{16,0},... | collective-permute-start | bytes 208904 | tf_op jit(solution)/shard_map/ppermute | solution.py:178
  42.0 5.3 %collective-permute-start.16 = (bf16[272,128]{1,0:T(8,128)(2,1)S(1)}, bf16[272,128]{1,0:T(8,128)(2,1)S(1)}, u32[]{:S(2)}, u32[]{:S(2)}) collective-permute-start(bf16[272,128]{1,0:T(8,128)(2,1)S(1)} %add_convert_fusion.2.refs_5_), channel_id=1, source_target_pairs={{0,16},{2,18},{4,20},{6,22},{8,24},{10,26},{12,28},{14,30},{16,0},... | collective-permute-start | bytes 208904 | tf_op jit(solution)/shard_map/ppermute | solution.py:178

commit v5 on v4

--- a/solution.py
+++ b/solution.py
@@ -13,6 +13,7 @@
 VMEM = 16 * 2**20
 PLANE = 4
 EXTRA = 16
+ROWS = 8
 WHOLE = pl.BlockSpec(memory_space=pltpu.VMEM)
 shape = jax.ShapeDtypeStruct
 
@@ -35,9 +36,9 @@
     return slice(h * dim, (h + 1) * dim)
 
 
-def causal(length):
-    rows = lax.broadcasted_iota(jnp.int32, (length, length), 0)
-    return rows >= lax.broadcasted_iota(jnp.int32, (length, length), 1)
+def causal(length, turned=False):
+    rows = lax.broadcasted_iota(jnp.int32, (length, length), 1 if turned else 0)
+    return rows >= lax.broadcasted_iota(jnp.int32, (length, length), 0 if turned else 1)
 
 
 def state_kernel(halves, dim, kv_ref, *refs):
@@ -50,12 +51,14 @@
             narrow_ref[r, :] = state.astype(BF16)
 
 
-def scores_kernel(heads, dim, q_ref, kv_ref, local_ref):
+def scores_kernel(heads, dim, q_ref, kv_ref, local_ref, turned_ref):
     length = q_ref.shape[0]
     mask = causal(length)
     for h in range(heads):
         c = cols(h, dim)
-        scores = jnp.where(mask, dot(q_ref[:, c], kv_ref[:length, c], 1, 1), 0.0).astype(BF16)
+        q = q_ref[:, c]
+        turned_ref[c, :] = q.T
+        scores = jnp.where(mask, dot(q, kv_ref[:length, c], 1, 1), 0.0).astype(BF16)
         local_ref[:, c] = dot(scores, kv_ref[length:, c], 1, 0)
 
 
@@ -88,29 +91,30 @@
         un_ref[:, r] = un
         square = square + un * un
         product = product + cot_ref[:, c].astype(F32) * gain_ref[:, c] * un
-    square = jnp.sum(square, axis=1, keepdims=True)
-    product = jnp.sum(product, axis=1, keepdims=True)
-    lane = lax.broadcasted_iota(jnp.int32, sums_ref.shape, 1)
-    sums = jnp.where(lane < sums_ref.shape[1] // 2, square, product)
+    square = jnp.sum(square.T, axis=0, keepdims=True)
+    product = jnp.sum(product.T, axis=0, keepdims=True)
+    row = lax.broadcasted_iota(jnp.int32, sums_ref.shape, 0)
+    sums = jnp.where(row < ROWS // 2, square, product)
     sums_ref[...] = sums if first else sums + before[...]
 
 
-def scales(sums_ref, other_ref, width):
+def scales(sums_ref, other_ref, width, dim):
     sums = sums_ref[...] + other_ref[...]
-    half = sums.shape[1] // 2
-    inverse = 1.0 / jnp.sqrt(sums[:, 0:1] / width + EPS)
-    return inverse, (sums[:, half : half + 1] * inverse) / width * inverse * inverse
+    inverse = lax.rsqrt(sums[0:1, :] / width + EPS)
+    factor = (sums[ROWS // 2 : ROWS // 2 + 1, :] * inverse) / width * inverse * inverse
+    length = sums.shape[1]
+    return [jnp.broadcast_to(row, (dim, length)).T for row in (inverse, factor)]
 
 
 def norm_kernel(heads, dim, width, sums_ref, other_ref, un_ref, cot_ref, gain_ref, q_ref, gun_ref, msg_ref):
-    inverse, factor = scales(sums_ref, other_ref, width)
+    inverse, factor = scales(sums_ref, other_ref, width, dim)
     for i, h in enumerate(heads):
         c, r = cols(h, dim), cols(i, dim)
         un = un_ref[:, r]
         cot = cot_ref[:, c].astype(F32)
         gun = (cot * gain_ref[:, c] * inverse - un * factor).astype(BF16)
         gun_ref[:, r] = gun
-        msg_ref[r, :] = dot(q_ref[:, c], gun, 0, 0).astype(BF16)
+        msg_ref[r, :] = dot(q_ref[c, :], gun, 1, 0).astype(BF16)
         row = len(heads) * dim + i
         msg_ref[row : row + 1, :] = jnp.sum(cot * (un * inverse), axis=0, keepdims=True).astype(BF16)
     rest = len(heads) * (dim + 1)
@@ -121,7 +125,7 @@
     n = len(halves)
     uns, guns, prefixes = refs[:n], refs[n : 2 * n], refs[2 * n : 3 * n]
     sums_ref, other_ref, gain_ref, kv_ref, att_ref, gq_ref = refs[3 * n :]
-    inverse, _ = scales(sums_ref, other_ref, width)
+    inverse, _ = scales(sums_ref, other_ref, width, dim)
     length = kv_ref.shape[0] // 2
     mask = causal(length)
     for heads, un_ref, gun_ref, prefix_ref in zip(halves, uns, guns, prefixes):
@@ -139,15 +143,15 @@
     guns = refs[:n]
     q_ref, kv_ref, gk_ref, gv_ref = refs[n:]
     length = q_ref.shape[0]
-    mask = causal(length)
+    mask = causal(length, True)
     for heads, gun_ref in zip(halves, guns):
         for i, h in enumerate(heads):
             c = cols(h, dim)
             q, k, gun = q_ref[:, c], kv_ref[:length, c], gun_ref[:, cols(i, dim)]
-            mixed = jnp.where(mask, dot(gun, kv_ref[length:, c], 1, 1), 0.0).astype(BF16)
-            scores = jnp.where(mask, dot(q, k, 1, 1), 0.0).astype(BF16)
-            gk_ref[:, c] = dot(mixed, q, 0, 0)
-            gv_ref[:, c] = dot(scores, gun, 0, 0)
+            mixed = jnp.where(mask, dot(kv_ref[length:, c], gun, 1, 1), 0.0).astype(BF16)
+            scores = jnp.where(mask, dot(k, q, 1, 1), 0.0).astype(BF16)
+            gk_ref[:, c] = dot(mixed, q, 1, 0)
+            gv_ref[:, c] = dot(scores, gun, 1, 0)
 
 
 def final_kernel(heads, dim, partners, first, *refs):
@@ -234,16 +238,17 @@
         [state_f32] * 2 + [state_bf] * 2, block, 2 * size + state_size,
     )(kv)
     local = (call(
-        functools.partial(scores_kernel, heads, dim), tokens_f32, 2 * square, 5 * size,
+        functools.partial(scores_kernel, heads, dim),
+        (tokens_f32, shape((width, length), BF16)), 2 * square, 5 * size,
     ), queries, kv)
     spot = (1, PLANE)
-    partners, _, received, done = scan(list(states[2:]), list(states[:2]), count, {spot: local})
-    local = done[spot]
+    partners, _, received, done = scan(list(states[2:]), list(states[:2]), count, {})
+    local, turned = local[0](*local[1:])
     unnormed, prefixes, sums = [], [], ()
     for n, members in enumerate(halves):
         un, prefix, both = call(
             functools.partial(unnormed_kernel, members, dim, partners, n == 0),
-            (half_f32, state_bf, shape((length, 128), F32)), block // 2, 3 * size + 4 * state_size,
+            (half_f32, state_bf, shape((ROWS, length), F32)), block // 2, 3 * size + 4 * state_size,
         )(*received[n], *sums, queries, local, cotangent, carried_state, gain)
         unnormed.append(un)
         prefixes.append(prefix)
@@ -259,18 +264,18 @@
         gun, message = call(
             functools.partial(norm_kernel, members, dim, total_width),
             (half_bf, shape((per * dim + EXTRA, dim), BF16)), block // 2, 3 * size,
-        )(sums, other, unnormed[n], cotangent, gain, queries)
+        )(sums, other, unnormed[n], cotangent, gain, turned)
         guns.append(gun)
         messages.append(message)
-    outer = (call(
+    inner = (call(
+        functools.partial(local_kernel, halves, dim), (tokens_f32, tokens_f32), 4 * square, 8 * size,
+    ), *guns, queries, kv)
+    attended, grad_q = call(
         functools.partial(attended_kernel, halves, dim, total_width),
         (tokens_bf, tokens_bf), 2 * square + block, 8 * size,
-    ), *unnormed, *guns, *prefixes, sums, other, gain, kv)
-    local_k, local_v = call(
-        functools.partial(local_kernel, halves, dim), (tokens_f32, tokens_f32), 4 * square, 8 * size,
-    )(*guns, queries, kv)
-    partners, messages, received, done = scan(messages, None, count, {spot: outer})
-    attended, grad_q = done[spot]
+    )(*unnormed, *guns, *prefixes, sums, other, gain, kv)
+    partners, messages, received, done = scan(messages, None, count, {spot: inner})
+    local_k, local_v = done[spot]
 
     outs = ()
     for n, members in enumerate(halves):

time: 48.4 us -> 47.9 us (0.990)
  Pallas kernels: 7.2 us -> 6.67 us
    pallas_call x2 -> x1, Pallas kernels: 2 us -> 1 us  [scan(): work = beside[n, distance][0](*operands)]
    pallas_call x1 -> x2, Pallas kernels: 1.45 us -> 2.04 us  [the longest x1 1.39 us: on_device(): call(functools.partial(attended_kernel, halves, dim, total_width), (token...]
  transfers between devices with their start and end apart: 21 -> 21, of which waited for: 10 -> 11; matrix products, arithmetic and copies ran while one was open for 1% -> 1% of each run, Pallas kernels for 11% -> 10%
where the time goes in v5:
time: 47.9 us; the launch traced here: 47.7 us
  starting transfers between devices  33.1 us (69%)
  Pallas kernels  6.67 us (14%)
  waiting for transfers between devices  5.74 us (12%)
  local copies, waits for them, and re-layouts  1.06 us (2%)
  between operations  0.8 us (2%)
    ppermute x20, starting transfers between devices, swap(): lax.ppermute(message, 'seq', [(i, i ^ partner) for i in range(count)])  33.1 us
    ppermute x20, waiting for transfers between devices, swap(): lax.ppermute(message, 'seq', [(i, i ^ partner) for i in range(count)])  4.59 us
    pallas_call x2, Pallas kernels, on_device(): call(functools.partial(final_kernel, members, dim, partners, n == 0), (to...  1.99 us
    pallas_call x1, Pallas kernels, on_device(): call(functools.partial(attended_kernel, halves, dim, total_width), (token...  1.39 us
    ppermute x1, waiting for transfers between devices, on_device(): lax.ppermute(partner, 'head', [(i, (i + 1) % head_count) for i in range(h...  1.16 us
    unnamed x11, local copies, waits for them, and re-layouts  1.04 us
    pallas_call x1, Pallas kernels, scan(): work = beside[n, distance][0](*operands)  1 us
  transfers between devices with their start and end apart: 21, of which 11 were waited for; matrix products, arithmetic and copies ran while one was open for 1% of the time, Pallas kernels for 10%

profile of v5, /device:TPU:0, one launch (start us, length us, event | category | flops | bytes accessed | tf_op | source)
XLA Modules:
  0.0 47.7 jit_solution(12813364553645033929)
XLA Ops:
  0.6 1.0 %constant_dynamic-update-slice_fusion.1 = bf16[512,512]{1,0:T(8,128)(2,1)S(1)} fusion(bf16[256,512]{1,0:T(8,128)(2,1)} %param.7), kind=kLoop, calls=%fused_computation.11 | loop fusion | bytes 524288
  1.7 0.0 copy-done.4
  1.7 0.3 shard_map.109
  2.0 4.0 %collective-permute-start.2 = (bf16[256,128]{1,0:T(8,128)(2,1)S(1)}, bf16[256,128]{1,0:T(8,128)(2,1)S(1)}, u32[]{:S(2)}, u32[]{:S(2)}) collective-permute-start(bf16[256,128]{1,0:T(8,128)(2,1)S(1)} %get-tuple-element.44), channel_id=1, source_target_pairs={{0,6},{2,4},{4,2},{6,0},{8,14},{10,12},{12,10},{14,8},{16,22},{18,... | collective-permute-start | bytes 196616 | tf_op jit(solution)/shard_map/ppermute | solution.py:182
  5.9 0.5 %collective-permute-start.1 = (bf16[256,128]{1,0:T(8,128)(2,1)S(1)}, bf16[256,128]{1,0:T(8,128)(2,1)S(1)}, u32[]{:S(2)}, u32[]{:S(2)}) collective-permute-start(bf16[256,128]{1,0:T(8,128)(2,1)S(1)} %get-tuple-element.44), channel_id=1, source_target_pairs={{0,4},{2,6},{4,0},{6,2},{8,12},{10,14},{12,8},{14,10},{16,20},{18,... | collective-permute-start | bytes 196616 | tf_op jit(solution)/shard_map/ppermute | solution.py:182
  6.4 0.1 collective-permute-start
  6.6 2.8 %collective-permute-start.7 = (bf16[256,128]{1,0:T(8,128)(2,1)S(1)}, bf16[256,128]{1,0:T(8,128)(2,1)S(1)}, u32[]{:S(2)}, u32[]{:S(2)}) collective-permute-start(bf16[256,128]{1,0:T(8,128)(2,1)S(1)} %get-tuple-element.48), channel_id=1, source_target_pairs={{0,6},{2,4},{4,2},{6,0},{8,14},{10,12},{12,10},{14,8},{16,22},{18,... | collective-permute-start | bytes 196616 | tf_op jit(solution)/shard_map/ppermute | solution.py:182
  9.4 0.5 %collective-permute-start.6 = (bf16[256,128]{1,0:T(8,128)(2,1)S(1)}, bf16[256,128]{1,0:T(8,128)(2,1)S(1)}, u32[]{:S(2)}, u32[]{:S(2)}) collective-permute-start(bf16[256,128]{1,0:T(8,128)(2,1)S(1)} %get-tuple-element.48), channel_id=1, source_target_pairs={{0,4},{2,6},{4,0},{6,2},{8,12},{10,14},{12,8},{14,10},{16,20},{18,... | collective-permute-start | bytes 196616 | tf_op jit(solution)/shard_map/ppermute | solution.py:182
  9.9 0.6 %collective-permute-start.5 = (bf16[256,128]{1,0:T(8,128)(2,1)S(1)}, bf16[256,128]{1,0:T(8,128)(2,1)S(1)}, u32[]{:S(2)}, u32[]{:S(2)}) collective-permute-start(bf16[256,128]{1,0:T(8,128)(2,1)S(1)} %get-tuple-element.48), channel_id=1, source_target_pairs={{0,2},{2,0},{4,6},{6,4},{8,10},{10,8},{12,14},{14,12},{16,18},{18,... | collective-permute-start | bytes 196616 | tf_op jit(solution)/shard_map/ppermute | solution.py:182
  10.6 0.4 collective-permute-done.1.refs_1_
  11.0 1.6 %collective-permute-start.3 = (bf16[256,128]{1,0:T(8,128)(2,1)S(1)}, bf16[256,128]{1,0:T(8,128)(2,1)S(1)}, u32[]{:S(2)}, u32[]{:S(2)}) collective-permute-start(bf16[256,128]{1,0:T(8,128)(2,1)S(1)} %fusion), channel_id=1, source_target_pairs={{0,8},{2,10},{4,12},{6,14},{8,0},{10,2},{12,4},{14,6},{16,24},{18,... | collective-permute-start | bytes 196616 | tf_op jit(solution)/shard_map/ppermute | solution.py:182
  12.7 0.1 collective-permute-done.7.refs_2_
  12.8 0.9 %collective-permute-done.6.refs_1_ = bf16[256,128]{1,0:T(8,128)(2,1)S(1)} collective-permute-done((bf16[256,128]{1,0:T(8,128)(2,1)S(1)}, bf16[256,128]{1,0:T(8,128)(2,1)S(1)}, u32[]{:S(2)}, u32[]{:S(2)}) %collective-permute-start.6) | collective-permute-done | bytes 65568 | tf_op jit(solution)/shard_map/ppermute | solution.py:182
  13.7 0.5 %collective-permute-done.5.refs_0_ = bf16[256,128]{1,0:T(8,128)(2,1)S(1)} collective-permute-done((bf16[256,128]{1,0:T(8,128)(2,1)S(1)}, bf16[256,128]{1,0:T(8,128)(2,1)S(1)}, u32[]{:S(2)}, u32[]{:S(2)}) %collective-permute-start.5) | collective-permute-done | bytes 65568 | tf_op jit(solution)/shard_map/ppermute | solution.py:182
  14.2 1.6 %collective-permute-start.8 = (bf16[256,128]{1,0:T(8,128)(2,1)S(1)}, bf16[256,128]{1,0:T(8,128)(2,1)S(1)}, u32[]{:S(2)}, u32[]{:S(2)}) collective-permute-start(bf16[256,128]{1,0:T(8,128)(2,1)S(1)} %fusion.1), channel_id=1, source_target_pairs={{0,8},{2,10},{4,12},{6,14},{8,0},{10,2},{12,4},{14,6},{16,24},{18,... | collective-permute-start | bytes 196616 | tf_op jit(solution)/shard_map/ppermute | solution.py:182
  15.9 0.2 collective-permute-done.3.refs_3_
  16.1 2.6 %collective-permute-start.4 = (bf16[256,128]{1,0:T(8,128)(2,1)S(1)}, bf16[256,128]{1,0:T(8,128)(2,1)S(1)}, u32[]{:S(2)}, u32[]{:S(2)}) collective-permute-start(bf16[256,128]{1,0:T(8,128)(2,1)S(1)} %add_convert_fusion.5), channel_id=1, source_target_pairs={{0,16},{2,18},{4,20},{6,22},{8,24},{10,26},{12,28},{14,30},{16,0},... | collective-permute-start | bytes 196616 | tf_op jit(solution)/shard_map/ppermute | solution.py:182
  18.7 0.1 add_convert_fusion.4
  18.8 0.0 copy-start
  18.8 2.5 %collective-permute-start.9 = (bf16[256,128]{1,0:T(8,128)(2,1)S(1)}, bf16[256,128]{1,0:T(8,128)(2,1)S(1)}, u32[]{:S(2)}, u32[]{:S(2)}) collective-permute-start(bf16[256,128]{1,0:T(8,128)(2,1)S(1)} %add_convert_fusion.4), channel_id=1, source_target_pairs={{0,16},{2,18},{4,20},{6,22},{8,24},{10,26},{12,28},{14,30},{16,0},... | collective-permute-start | bytes 196616 | tf_op jit(solution)/shard_map/ppermute | solution.py:182
  21.3 0.7 %shard_map.110 = (f32[256,512]{1,0:T(8,128)S(1)}, bf16[512,256]{1,0:T(8,128)(2,1)S(1)}) custom-call(bf16[256,512]{1,0:T(8,128)(2,1)S(1)} %copy-done.1, bf16[512,512]{1,0:T(8,128)(2,1)S(1)} %constant_dynamic-update-slice_fusion.kv_ref.refs_9_.refs_3_.refs_6_), custom_call_target="tpu_custom_call" | custom-call | flops 134217728 | bytes 1310720 | tf_op jit(solution)/shard_map/pallas_call | solution.py:246
  22.0 0.8 %collective-permute-done.4.refs_4_ = bf16[256,128]{1,0:T(8,128)(2,1)S(1)} collective-permute-done((bf16[256,128]{1,0:T(8,128)(2,1)S(1)}, bf16[256,128]{1,0:T(8,128)(2,1)S(1)}, u32[]{:S(2)}, u32[]{:S(2)}) %collective-permute-start.4) | collective-permute-done | bytes 65568 | tf_op jit(solution)/shard_map/ppermute | solution.py:182
  22.7 0.4 shard_map.111
  23.1 0.9 %collective-permute-done.9.refs_4_ = bf16[256,128]{1,0:T(8,128)(2,1)S(1)} collective-permute-done((bf16[256,128]{1,0:T(8,128)(2,1)S(1)}, bf16[256,128]{1,0:T(8,128)(2,1)S(1)}, u32[]{:S(2)}, u32[]{:S(2)}) %collective-permute-start.9) | collective-permute-done | bytes 65568 | tf_op jit(solution)/shard_map/ppermute | solution.py:182
  24.0 0.4 shard_map.112
  24.4 0.1 collective-permute-start.10
  24.5 1.2 %collective-permute-done.10.other_ref.refs_7_ = f32[8,256]{1,0:T(8,128)S(1)} collective-permute-done((f32[8,256]{1,0:T(8,128)S(1)}, f32[8,256]{1,0:T(8,128)S(1)}, u32[]{:S(2)}, u32[]{:S(2)}) %collective-permute-start.10) | collective-permute-done | bytes 8224 | tf_op jit(solution)/shard_map/ppermute | solution.py:259
  25.7 0.3 shard_map.113
  26.0 1.7 %collective-permute-start.18 = (bf16[272,128]{1,0:T(8,128)(2,1)S(1)}, bf16[272,128]{1,0:T(8,128)(2,1)S(1)}, u32[]{:S(2)}, u32[]{:S(2)}) collective-permute-start(bf16[272,128]{1,0:T(8,128)(2,1)S(1)} %get-tuple-element.61), channel_id=1, source_target_pairs={{0,6},{2,4},{4,2},{6,0},{8,14},{10,12},{12,10},{14,8},{16,22},{18,... | collective-permute-start | bytes 208904 | tf_op jit(solution)/shard_map/ppermute | solution.py:182
  27.6 0.4 collective-permute-start.17
  28.0 1.5 %collective-permute-start.14 = (bf16[272,128]{1,0:T(8,128)(2,1)S(1)}, bf16[272,128]{1,0:T(8,128)(2,1)S(1)}, u32[]{:S(2)}, u32[]{:S(2)}) collective-permute-start(bf16[272,128]{1,0:T(8,128)(2,1)S(1)} %get-tuple-element.61), channel_id=1, source_target_pairs={{0,2},{2,0},{4,6},{6,4},{8,10},{10,8},{12,14},{14,12},{16,18},{18,... | collective-permute-start | bytes 208904 | tf_op jit(solution)/shard_map/ppermute | solution.py:182
  29.5 0.3 shard_map.114
  29.9 1.7 %collective-permute-start.13 = (bf16[272,128]{1,0:T(8,128)(2,1)S(1)}, bf16[272,128]{1,0:T(8,128)(2,1)S(1)}, u32[]{:S(2)}, u32[]{:S(2)}) collective-permute-start(bf16[272,128]{1,0:T(8,128)(2,1)S(1)} %get-tuple-element.60), channel_id=1, source_target_pairs={{0,6},{2,4},{4,2},{6,0},{8,14},{10,12},{12,10},{14,8},{16,22},{18,... | collective-permute-start | bytes 208904 | tf_op jit(solution)/shard_map/ppermute | solution.py:182
  31.5 0.4 collective-permute-start.12
  31.9 1.5 %collective-permute-start.11 = (bf16[272,128]{1,0:T(8,128)(2,1)S(1)}, bf16[272,128]{1,0:T(8,128)(2,1)S(1)}, u32[]{:S(2)}, u32[]{:S(2)}) collective-permute-start(bf16[272,128]{1,0:T(8,128)(2,1)S(1)} %get-tuple-element.60), channel_id=1, source_target_pairs={{0,2},{2,0},{4,6},{6,4},{8,10},{10,8},{12,14},{14,12},{16,18},{18,... | collective-permute-start | bytes 208904 | tf_op jit(solution)/shard_map/ppermute | solution.py:182
  33.5 1.6 %collective-permute-start.19 = (bf16[272,128]{1,0:T(8,128)(2,1)S(1)}, bf16[272,128]{1,0:T(8,128)(2,1)S(1)}, u32[]{:S(2)}, u32[]{:S(2)}) collective-permute-start(bf16[272,128]{1,0:T(8,128)(2,1)S(1)} %add_convert_fusion.1), channel_id=1, source_target_pairs={{0,8},{2,10},{4,12},{6,14},{8,0},{10,2},{12,4},{14,6},{16,24},{18,... | collective-permute-start | bytes 208904 | tf_op jit(solution)/shard_map/ppermute | solution.py:182
  35.1 1.0 %shard_map.116 = (f32[256,512]{1,0:T(8,128)S(1)}, f32[256,512]{1,0:T(8,128)S(1)}) custom-call(bf16[256,256]{1,0:T(8,128)(2,1)S(1)} %get-tuple-element.62.refs_2_.refs_0_, bf16[256,256]{1,0:T(8,128)(2,1)S(1)} %get-tuple-element.63.refs_3_.refs_1_, bf16[256,512]{1,0:T(8,128)(2,1)S(1)} %copy-done.1, ...), custom_call_target="tpu_custom_call" | custom-call | flops 268435456 | bytes 2097152 | tf_op jit(solution)/shard_map/pallas_call | solution.py:196
  36.1 0.1 collective-permute-done.12.refs_1_
  36.2 0.0 collective-permute-done.11.refs_0_
  36.3 1.6 %collective-permute-start.15 = (bf16[272,128]{1,0:T(8,128)(2,1)S(1)}, bf16[272,128]{1,0:T(8,128)(2,1)S(1)}, u32[]{:S(2)}, u32[]{:S(2)}) collective-permute-start(bf16[272,128]{1,0:T(8,128)(2,1)S(1)} %add_convert_fusion.3), channel_id=1, source_target_pairs={{0,8},{2,10},{4,12},{6,14},{8,0},{10,2},{12,4},{14,6},{16,24},{18,... | collective-permute-start | bytes 208904 | tf_op jit(solution)/shard_map/ppermute | solution.py:182
  38.0 3.4 %collective-permute-start.20 = (bf16[272,128]{1,0:T(8,128)(2,1)S(1)}, bf16[272,128]{1,0:T(8,128)(2,1)S(1)}, u32[]{:S(2)}, u32[]{:S(2)}) collective-permute-start(bf16[272,128]{1,0:T(8,128)(2,1)S(1)} %add_convert_fusion.refs_5_), channel_id=1, source_target_pairs={{0,16},{2,18},{4,20},{6,22},{8,24},{10,26},{12,28},{14,30},{16,0},... | collective-permute-start | bytes 208904 | tf_op jit(solution)/shard_map/ppermute | solution.py:182
  41.4 0.0 collective-permute-done.15.refs_3_
  41.4 2.3 %collective-permute-start.16 = (bf16[272,128]{1,0:T(8,128)(2,1)S(1)}, bf16[272,128]{1,0:T(8,128)(2,1)S(1)}, u32[]{:S(2)}, u32[]{:S(2)}) collective-permute-start(bf16[272,128]{1,0:T(8,128)(2,1)S(1)} %add_convert_fusion.2.refs_5_), channel_id=1, source_target_pairs={{0,16},{2,18},{4,20},{6,22},{8,24},{10,26},{12,28},{14,30},{16,0},... | collective-permute-start | bytes 208904 | tf_op jit(solution)/shard_map/ppermute | solution.py:182
  43.7 1.4 %shard_map.115 = (bf16[256,512]{1,0:T(8,128)(2,1)}, bf16[256,512]{1,0:T(8,128)(2,1)}) custom-call(f32[256,256]{1,0:T(8,128)S(1)} %get-tuple-element.47.un_ref.refs_0_, f32[256,256]{1,0:T(8,128)S(1)} %get-tuple-element.51.un_ref.refs_1_, bf16[256,256]{1,0:T(8,128)(2,1)S(1)} %get-tuple-element.62.refs_2_.refs_0_, ...), custom_call_target="tpu_custom_call" | custom-call | flops 167772160 | bytes 2097152 | tf_op jit(solution)/shard_map/pallas_call | solution.py:273
  45.1 0.3 collective-permute-done.20.refs_4_
  45.4 1.0 %shard_map.117 = (bf16[256,512]{1,0:T(8,128)(2,1)}, bf16[256,512]{1,0:T(8,128)(2,1)}, f32[4,128,128]{2,1,0:T(8,128)}, f32[1,512]{1,0:T(1,128)}) custom-call(bf16[272,128]{1,0:T(8,128)(2,1)S(1)} %collective-permute-done.14.refs_0_, bf16[272,128]{1,0:T(8,128)(2,1)S(1)} %collective-permute-done.17.refs_1_, ...), custom_call_target="tpu_custom_call" | custom-call | flops 33554432 | bytes 1835008 | tf_op jit(solution)/shard_map/pallas_call | solution.py:284
  46.4 0.3 collective-permute-done.16.refs_4_
  46.7 1.0 %shard_map.118 = (bf16[256,512]{1,0:T(8,128)(2,1)}, bf16[256,512]{1,0:T(8,128)(2,1)}, f32[4,128,128]{2,1,0:T(8,128)}, f32[1,512]{1,0:T(1,128)}) custom-call(bf16[272,128]{1,0:T(8,128)(2,1)S(1)} %collective-permute-done.11.refs_0_, ...), custom_call_target="tpu_custom_call", output_to_operand_aliasing={{0}: (9, {}), {1}: (10, {}), {2}: (11, {}), {3}: (12, {})} | custom-call | flops 33554432 | bytes 1835008 | tf_op jit(solution)/shard_map/pallas_call | solution.py:284
  (24 shorter events, 0.3 us)
Async XLA Ops:
  0.6 1.0 %copy-start.4 = (bf16[256,512]{1,0:T(8,128)(2,1)S(1)}, bf16[256,512]{1,0:T(8,128)(2,1)}, u32[]{:S(2)}) copy-start(bf16[256,512]{1,0:T(8,128)(2,1)} %param.8) | copy-start | bytes 786436
  2.0 8.0 %collective-permute-start.2 = (bf16[256,128]{1,0:T(8,128)(2,1)S(1)}, bf16[256,128]{1,0:T(8,128)(2,1)S(1)}, u32[]{:S(2)}, u32[]{:S(2)}) collective-permute-start(bf16[256,128]{1,0:T(8,128)(2,1)S(1)} %get-tuple-element.44), channel_id=1, source_target_pairs={{0,6},{2,4},{4,2},{6,0},{8,14},{10,12},{12,10},{14,8},{16,22},{18,... | collective-permute-start | bytes 196616 | tf_op jit(solution)/shard_map/ppermute | solution.py:182
  5.9 5.1 %collective-permute-start.1 = (bf16[256,128]{1,0:T(8,128)(2,1)S(1)}, bf16[256,128]{1,0:T(8,128)(2,1)S(1)}, u32[]{:S(2)}, u32[]{:S(2)}) collective-permute-start(bf16[256,128]{1,0:T(8,128)(2,1)S(1)} %get-tuple-element.44), channel_id=1, source_target_pairs={{0,4},{2,6},{4,0},{6,2},{8,12},{10,14},{12,8},{14,10},{16,20},{18,... | collective-permute-start | bytes 196616 | tf_op jit(solution)/shard_map/ppermute | solution.py:182
  6.4 4.6 %collective-permute-start = (bf16[256,128]{1,0:T(8,128)(2,1)S(1)}, bf16[256,128]{1,0:T(8,128)(2,1)S(1)}, u32[]{:S(2)}, u32[]{:S(2)}) collective-permute-start(bf16[256,128]{1,0:T(8,128)(2,1)S(1)} %get-tuple-element.44), channel_id=1, source_target_pairs={{0,2},{2,0},{4,6},{6,4},{8,10},{10,8},{12,14},{14,12},{16,18},{18,... | collective-permute-start | bytes 196616 | tf_op jit(solution)/shard_map/ppermute | solution.py:182
  6.6 6.2 %collective-permute-start.7 = (bf16[256,128]{1,0:T(8,128)(2,1)S(1)}, bf16[256,128]{1,0:T(8,128)(2,1)S(1)}, u32[]{:S(2)}, u32[]{:S(2)}) collective-permute-start(bf16[256,128]{1,0:T(8,128)(2,1)S(1)} %get-tuple-element.48), channel_id=1, source_target_pairs={{0,6},{2,4},{4,2},{6,0},{8,14},{10,12},{12,10},{14,8},{16,22},{18,... | collective-permute-start | bytes 196616 | tf_op jit(solution)/shard_map/ppermute | solution.py:182
  9.4 4.3 %collective-permute-start.6 = (bf16[256,128]{1,0:T(8,128)(2,1)S(1)}, bf16[256,128]{1,0:T(8,128)(2,1)S(1)}, u32[]{:S(2)}, u32[]{:S(2)}) collective-permute-start(bf16[256,128]{1,0:T(8,128)(2,1)S(1)} %get-tuple-element.48), channel_id=1, source_target_pairs={{0,4},{2,6},{4,0},{6,2},{8,12},{10,14},{12,8},{14,10},{16,20},{18,... | collective-permute-start | bytes 196616 | tf_op jit(solution)/shard_map/ppermute | solution.py:182
  9.9 4.3 %collective-permute-start.5 = (bf16[256,128]{1,0:T(8,128)(2,1)S(1)}, bf16[256,128]{1,0:T(8,128)(2,1)S(1)}, u32[]{:S(2)}, u32[]{:S(2)}) collective-permute-start(bf16[256,128]{1,0:T(8,128)(2,1)S(1)} %get-tuple-element.48), channel_id=1, source_target_pairs={{0,2},{2,0},{4,6},{6,4},{8,10},{10,8},{12,14},{14,12},{16,18},{18,... | collective-permute-start | bytes 196616 | tf_op jit(solution)/shard_map/ppermute | solution.py:182
  11.0 5.0 %collective-permute-start.3 = (bf16[256,128]{1,0:T(8,128)(2,1)S(1)}, bf16[256,128]{1,0:T(8,128)(2,1)S(1)}, u32[]{:S(2)}, u32[]{:S(2)}) collective-permute-start(bf16[256,128]{1,0:T(8,128)(2,1)S(1)} %fusion), channel_id=1, source_target_pairs={{0,8},{2,10},{4,12},{6,14},{8,0},{10,2},{12,4},{14,6},{16,24},{18,... | collective-permute-start | bytes 196616 | tf_op jit(solution)/shard_map/ppermute | solution.py:182
  14.2 4.5 %collective-permute-start.8 = (bf16[256,128]{1,0:T(8,128)(2,1)S(1)}, bf16[256,128]{1,0:T(8,128)(2,1)S(1)}, u32[]{:S(2)}, u32[]{:S(2)}) collective-permute-start(bf16[256,128]{1,0:T(8,128)(2,1)S(1)} %fusion.1), channel_id=1, source_target_pairs={{0,8},{2,10},{4,12},{6,14},{8,0},{10,2},{12,4},{14,6},{16,24},{18,... | collective-permute-start | bytes 196616 | tf_op jit(solution)/shard_map/ppermute | solution.py:182
  16.1 5.2 %copy-start.1 = (bf16[256,512]{1,0:T(8,128)(2,1)S(1)}, bf16[256,512]{1,0:T(8,128)(2,1)}, u32[]{:S(2)}) copy-start(bf16[256,512]{1,0:T(8,128)(2,1)} %refs_2_) | copy-start | bytes 786436
  16.1 6.6 %collective-permute-start.4 = (bf16[256,128]{1,0:T(8,128)(2,1)S(1)}, bf16[256,128]{1,0:T(8,128)(2,1)S(1)}, u32[]{:S(2)}, u32[]{:S(2)}) collective-permute-start(bf16[256,128]{1,0:T(8,128)(2,1)S(1)} %add_convert_fusion.5), channel_id=1, source_target_pairs={{0,16},{2,18},{4,20},{6,22},{8,24},{10,26},{12,28},{14,30},{16,0},... | collective-permute-start | bytes 196616 | tf_op jit(solution)/shard_map/ppermute | solution.py:182
  18.8 3.9 %copy-start = (bf16[256,512]{1,0:T(8,128)(2,1)S(1)}, bf16[256,512]{1,0:T(8,128)(2,1)}, u32[]{:S(2)}) copy-start(bf16[256,512]{1,0:T(8,128)(2,1)} %cot_ref.3) | copy-start | bytes 786436
  18.8 3.9 %copy-start.2 = (f32[4,128,128]{2,1,0:T(8,128)S(1)}, f32[4,128,128]{2,1,0:T(8,128)}, u32[]{:S(2)}) copy-start(f32[4,128,128]{2,1,0:T(8,128)} %refs_9_.1) | copy-start | bytes 786436
  18.8 5.2 %collective-permute-start.9 = (bf16[256,128]{1,0:T(8,128)(2,1)S(1)}, bf16[256,128]{1,0:T(8,128)(2,1)S(1)}, u32[]{:S(2)}, u32[]{:S(2)}) collective-permute-start(bf16[256,128]{1,0:T(8,128)(2,1)S(1)} %add_convert_fusion.4), channel_id=1, source_target_pairs={{0,16},{2,18},{4,20},{6,22},{8,24},{10,26},{12,28},{14,30},{16,0},... | collective-permute-start | bytes 196616 | tf_op jit(solution)/shard_map/ppermute | solution.py:182
  22.0 0.8 %copy-start.3 = (f32[512]{0:T(512)S(1)}, f32[512]{0:T(512)}, u32[]{:S(2)}) copy-start(f32[512]{0:T(512)} %param.11) | copy-start | bytes 6148
  24.4 1.2 %collective-permute-start.10 = (f32[8,256]{1,0:T(8,128)S(1)}, f32[8,256]{1,0:T(8,128)S(1)}, u32[]{:S(2)}, u32[]{:S(2)}) collective-permute-start(f32[8,256]{1,0:T(8,128)S(1)} %get-tuple-element.52.sums_ref.refs_6_), channel_id=1, source_target_pairs={{0,1},{1,0},{2,3},{3,2},{4,5},{5,4},{6,7},{7,6},{8,9},{9,8},{10,11... | collective-permute-start | bytes 24584 | tf_op jit(solution)/shard_map/ppermute | solution.py:259
  26.0 6.0 %collective-permute-start.18 = (bf16[272,128]{1,0:T(8,128)(2,1)S(1)}, bf16[272,128]{1,0:T(8,128)(2,1)S(1)}, u32[]{:S(2)}, u32[]{:S(2)}) collective-permute-start(bf16[272,128]{1,0:T(8,128)(2,1)S(1)} %get-tuple-element.61), channel_id=1, source_target_pairs={{0,6},{2,4},{4,2},{6,0},{8,14},{10,12},{12,10},{14,8},{16,22},{18,... | collective-permute-start | bytes 208904 | tf_op jit(solution)/shard_map/ppermute | solution.py:182
  27.6 5.8 %collective-permute-start.17 = (bf16[272,128]{1,0:T(8,128)(2,1)S(1)}, bf16[272,128]{1,0:T(8,128)(2,1)S(1)}, u32[]{:S(2)}, u32[]{:S(2)}) collective-permute-start(bf16[272,128]{1,0:T(8,128)(2,1)S(1)} %get-tuple-element.61), channel_id=1, source_target_pairs={{0,4},{2,6},{4,0},{6,2},{8,12},{10,14},{12,8},{14,10},{16,20},{18,... | collective-permute-start | bytes 208904 | tf_op jit(solution)/shard_map/ppermute | solution.py:182
  28.0 5.4 %collective-permute-start.14 = (bf16[272,128]{1,0:T(8,128)(2,1)S(1)}, bf16[272,128]{1,0:T(8,128)(2,1)S(1)}, u32[]{:S(2)}, u32[]{:S(2)}) collective-permute-start(bf16[272,128]{1,0:T(8,128)(2,1)S(1)} %get-tuple-element.61), channel_id=1, source_target_pairs={{0,2},{2,0},{4,6},{6,4},{8,10},{10,8},{12,14},{14,12},{16,18},{18,... | collective-permute-start | bytes 208904 | tf_op jit(solution)/shard_map/ppermute | solution.py:182
  29.9 6.3 %collective-permute-start.13 = (bf16[272,128]{1,0:T(8,128)(2,1)S(1)}, bf16[272,128]{1,0:T(8,128)(2,1)S(1)}, u32[]{:S(2)}, u32[]{:S(2)}) collective-permute-start(bf16[272,128]{1,0:T(8,128)(2,1)S(1)} %get-tuple-element.60), channel_id=1, source_target_pairs={{0,6},{2,4},{4,2},{6,0},{8,14},{10,12},{12,10},{14,8},{16,22},{18,... | collective-permute-start | bytes 208904 | tf_op jit(solution)/shard_map/ppermute | solution.py:182
  31.5 4.7 %collective-permute-start.12 = (bf16[272,128]{1,0:T(8,128)(2,1)S(1)}, bf16[272,128]{1,0:T(8,128)(2,1)S(1)}, u32[]{:S(2)}, u32[]{:S(2)}) collective-permute-start(bf16[272,128]{1,0:T(8,128)(2,1)S(1)} %get-tuple-element.60), channel_id=1, source_target_pairs={{0,4},{2,6},{4,0},{6,2},{8,12},{10,14},{12,8},{14,10},{16,20},{18,... | collective-permute-start | bytes 208904 | tf_op jit(solution)/shard_map/ppermute | solution.py:182
  31.9 4.3 %collective-permute-start.11 = (bf16[272,128]{1,0:T(8,128)(2,1)S(1)}, bf16[272,128]{1,0:T(8,128)(2,1)S(1)}, u32[]{:S(2)}, u32[]{:S(2)}) collective-permute-start(bf16[272,128]{1,0:T(8,128)(2,1)S(1)} %get-tuple-element.60), channel_id=1, source_target_pairs={{0,2},{2,0},{4,6},{6,4},{8,10},{10,8},{12,14},{14,12},{16,18},{18,... | collective-permute-start | bytes 208904 | tf_op jit(solution)/shard_map/ppermute | solution.py:182
  33.5 4.5 %collective-permute-start.19 = (bf16[272,128]{1,0:T(8,128)(2,1)S(1)}, bf16[272,128]{1,0:T(8,128)(2,1)S(1)}, u32[]{:S(2)}, u32[]{:S(2)}) collective-permute-start(bf16[272,128]{1,0:T(8,128)(2,1)S(1)} %add_convert_fusion.1), channel_id=1, source_target_pairs={{0,8},{2,10},{4,12},{6,14},{8,0},{10,2},{12,4},{14,6},{16,24},{18,... | collective-permute-start | bytes 208904 | tf_op jit(solution)/shard_map/ppermute | solution.py:182
  36.3 5.1 %collective-permute-start.15 = (bf16[272,128]{1,0:T(8,128)(2,1)S(1)}, bf16[272,128]{1,0:T(8,128)(2,1)S(1)}, u32[]{:S(2)}, u32[]{:S(2)}) collective-permute-start(bf16[272,128]{1,0:T(8,128)(2,1)S(1)} %add_convert_fusion.3), channel_id=1, source_target_pairs={{0,8},{2,10},{4,12},{6,14},{8,0},{10,2},{12,4},{14,6},{16,24},{18,... | collective-permute-start | bytes 208904 | tf_op jit(solution)/shard_map/ppermute | solution.py:182
  38.0 7.5 %collective-permute-start.20 = (bf16[272,128]{1,0:T(8,128)(2,1)S(1)}, bf16[272,128]{1,0:T(8,128)(2,1)S(1)}, u32[]{:S(2)}, u32[]{:S(2)}) collective-permute-start(bf16[272,128]{1,0:T(8,128)(2,1)S(1)} %add_convert_fusion.refs_5_), channel_id=1, source_target_pairs={{0,16},{2,18},{4,20},{6,22},{8,24},{10,26},{12,28},{14,30},{16,0},... | collective-permute-start | bytes 208904 | tf_op jit(solution)/shard_map/ppermute | solution.py:182
  41.4 5.3 %collective-permute-start.16 = (bf16[272,128]{1,0:T(8,128)(2,1)S(1)}, bf16[272,128]{1,0:T(8,128)(2,1)S(1)}, u32[]{:S(2)}, u32[]{:S(2)}) collective-permute-start(bf16[272,128]{1,0:T(8,128)(2,1)S(1)} %add_convert_fusion.2.refs_5_), channel_id=1, source_target_pairs={{0,16},{2,18},{4,20},{6,22},{8,24},{10,26},{12,28},{14,30},{16,0},... | collective-permute-start | bytes 208904 | tf_op jit(solution)/shard_map/ppermute | solution.py:182

commit v6 on v5

--- a/solution.py
+++ b/solution.py
@@ -82,10 +82,7 @@
     square = product = 0.0
     for i, h in enumerate(heads):
         c, r = cols(h, dim), cols(i, dim)
-        prefix = carried_ref[h]
-        if parts:
-            prefix = prefix + gathered(partners, parts, r, False)
-        prefix = prefix.astype(BF16)
+        prefix = (carried_ref[h] + gathered(partners, parts, r, False)).astype(BF16)
         prefix_ref[r, :] = prefix
         un = local_ref[:, c] + dot(q_ref[:, c], prefix, 1, 0)
         un_ref[:, r] = un
@@ -108,6 +105,8 @@
 
 def norm_kernel(heads, dim, width, sums_ref, other_ref, un_ref, cot_ref, gain_ref, q_ref, gun_ref, msg_ref):
     inverse, factor = scales(sums_ref, other_ref, width, dim)
+    row = lax.broadcasted_iota(jnp.int32, (EXTRA, dim), 0)
+    gains = jnp.zeros((EXTRA, dim), F32)
     for i, h in enumerate(heads):
         c, r = cols(h, dim), cols(i, dim)
         un = un_ref[:, r]
@@ -115,10 +114,8 @@
         gun = (cot * gain_ref[:, c] * inverse - un * factor).astype(BF16)
         gun_ref[:, r] = gun
         msg_ref[r, :] = dot(q_ref[c, :], gun, 1, 0).astype(BF16)
-        row = len(heads) * dim + i
-        msg_ref[row : row + 1, :] = jnp.sum(cot * (un * inverse), axis=0, keepdims=True).astype(BF16)
-    rest = len(heads) * (dim + 1)
-    msg_ref[rest:, :] = jnp.zeros((msg_ref.shape[0] - rest, dim), BF16)
+        gains = jnp.where(row == i, jnp.sum(cot * (un * inverse), axis=0, keepdims=True), gains)
+    msg_ref[len(heads) * dim :, :] = gains.astype(BF16)
 
 
 def attended_kernel(halves, dim, width, *refs):
@@ -160,22 +157,17 @@
     message_ref, kv_ref, gk_ref, gv_ref = refs[:4]
     gk_out, gv_out, state_out, gain_out = refs[4 if first else 8 :]
     length = kv_ref.shape[0] // 2
+    tail = slice(len(heads) * dim, len(heads) * dim + EXTRA)
+    gains = message_ref[tail, :].astype(F32) + parts[-1][tail, :].astype(F32)
     for i, h in enumerate(heads):
         c, r = cols(h, dim), cols(i, dim)
-        total = message_ref[r, :].astype(F32)
-        gk, gv = gk_ref[:, c], gv_ref[:, c]
-        row = slice(len(heads) * dim + i, len(heads) * dim + i + 1)
-        gain = message_ref[row, :].astype(F32)
-        if parts:
-            suffix = gathered(partners, parts, r, True).astype(BF16)
-            gk = gk + dot(kv_ref[length:, c], suffix, 1, 1)
-            gv = gv + dot(kv_ref[:length, c], suffix, 1, 0)
-            total = total + parts[-1][r, :].astype(F32)
-            gain = gain + parts[-1][row, :].astype(F32)
+        suffix = gathered(partners, parts, r, True).astype(BF16)
+        gk = gk_ref[:, c] + dot(kv_ref[length:, c], suffix, 1, 1)
+        gv = gv_ref[:, c] + dot(kv_ref[:length, c], suffix, 1, 0)
         gk_out[:, r] = gk.astype(BF16)
         gv_out[:, r] = gv.astype(BF16)
-        state_out[i] = total
-        gain_out[:, r] = gain
+        state_out[i] = message_ref[r, :].astype(F32) + parts[-1][r, :].astype(F32)
+        gain_out[:, r] = gains[i : i + 1, :]
 
 
 def swap(message, count, partner):

time: 47.9 us -> 47.9 us (level)
  no operation moved by 1% of the time
where the time goes in v6:
time: 47.9 us; the launch traced here: 47.7 us
  starting transfers between devices  33.1 us (69%)
  Pallas kernels  6.64 us (14%)
  waiting for transfers between devices  5.76 us (12%)
  local copies, waits for them, and re-layouts  1.06 us (2%)
  between operations  0.8 us (2%)
    ppermute x20, starting transfers between devices, swap(): lax.ppermute(message, 'seq', [(i, i ^ partner) for i in range(count)])  33.1 us
    ppermute x20, waiting for transfers between devices, swap(): lax.ppermute(message, 'seq', [(i, i ^ partner) for i in range(count)])  4.6 us
    pallas_call x2, Pallas kernels, on_device(): call(functools.partial(final_kernel, members, dim, partners, n == 0), (to...  1.99 us
    pallas_call x1, Pallas kernels, on_device(): call(functools.partial(attended_kernel, halves, dim, total_width), (token...  1.38 us
    ppermute x1, waiting for transfers between devices, on_device(): lax.ppermute(partner, 'head', [(i, (i + 1) % head_count) for i in range(h...  1.16 us
    unnamed x11, local copies, waits for them, and re-layouts  1.04 us
    pallas_call x1, Pallas kernels, scan(): work = beside[n, distance][0](*operands)  1 us
  transfers between devices with their start and end apart: 21, of which 11 were waited for; matrix products, arithmetic and copies ran while one was open for 1% of the time, Pallas kernels for 10%

profile of v6, /device:TPU:0, one launch (start us, length us, event | category | flops | bytes accessed | tf_op | source)
XLA Modules:
  0.0 47.7 jit_solution(10273384976473039890)
XLA Ops:
  0.6 1.0 %constant_dynamic-update-slice_fusion.1 = bf16[512,512]{1,0:T(8,128)(2,1)S(1)} fusion(bf16[256,512]{1,0:T(8,128)(2,1)} %param.7), kind=kLoop, calls=%fused_computation.11 | loop fusion | bytes 524288
  1.7 0.0 copy-done.4
  1.7 0.3 shard_map.109
  2.0 4.0 %collective-permute-start.2 = (bf16[256,128]{1,0:T(8,128)(2,1)S(1)}, bf16[256,128]{1,0:T(8,128)(2,1)S(1)}, u32[]{:S(2)}, u32[]{:S(2)}) collective-permute-start(bf16[256,128]{1,0:T(8,128)(2,1)S(1)} %get-tuple-element.44), channel_id=1, source_target_pairs={{0,6},{2,4},{4,2},{6,0},{8,14},{10,12},{12,10},{14,8},{16,22},{18,... | collective-permute-start | bytes 196616 | tf_op jit(solution)/shard_map/ppermute | solution.py:174
  5.9 0.5 %collective-permute-start.1 = (bf16[256,128]{1,0:T(8,128)(2,1)S(1)}, bf16[256,128]{1,0:T(8,128)(2,1)S(1)}, u32[]{:S(2)}, u32[]{:S(2)}) collective-permute-start(bf16[256,128]{1,0:T(8,128)(2,1)S(1)} %get-tuple-element.44), channel_id=1, source_target_pairs={{0,4},{2,6},{4,0},{6,2},{8,12},{10,14},{12,8},{14,10},{16,20},{18,... | collective-permute-start | bytes 196616 | tf_op jit(solution)/shard_map/ppermute | solution.py:174
  6.4 0.1 collective-permute-start
  6.6 2.8 %collective-permute-start.7 = (bf16[256,128]{1,0:T(8,128)(2,1)S(1)}, bf16[256,128]{1,0:T(8,128)(2,1)S(1)}, u32[]{:S(2)}, u32[]{:S(2)}) collective-permute-start(bf16[256,128]{1,0:T(8,128)(2,1)S(1)} %get-tuple-element.48), channel_id=1, source_target_pairs={{0,6},{2,4},{4,2},{6,0},{8,14},{10,12},{12,10},{14,8},{16,22},{18,... | collective-permute-start | bytes 196616 | tf_op jit(solution)/shard_map/ppermute | solution.py:174
  9.4 0.5 %collective-permute-start.6 = (bf16[256,128]{1,0:T(8,128)(2,1)S(1)}, bf16[256,128]{1,0:T(8,128)(2,1)S(1)}, u32[]{:S(2)}, u32[]{:S(2)}) collective-permute-start(bf16[256,128]{1,0:T(8,128)(2,1)S(1)} %get-tuple-element.48), channel_id=1, source_target_pairs={{0,4},{2,6},{4,0},{6,2},{8,12},{10,14},{12,8},{14,10},{16,20},{18,... | collective-permute-start | bytes 196616 | tf_op jit(solution)/shard_map/ppermute | solution.py:174
  9.9 0.6 %collective-permute-start.5 = (bf16[256,128]{1,0:T(8,128)(2,1)S(1)}, bf16[256,128]{1,0:T(8,128)(2,1)S(1)}, u32[]{:S(2)}, u32[]{:S(2)}) collective-permute-start(bf16[256,128]{1,0:T(8,128)(2,1)S(1)} %get-tuple-element.48), channel_id=1, source_target_pairs={{0,2},{2,0},{4,6},{6,4},{8,10},{10,8},{12,14},{14,12},{16,18},{18,... | collective-permute-start | bytes 196616 | tf_op jit(solution)/shard_map/ppermute | solution.py:174
  10.6 0.4 collective-permute-done.1.refs_1_
  11.0 1.6 %collective-permute-start.3 = (bf16[256,128]{1,0:T(8,128)(2,1)S(1)}, bf16[256,128]{1,0:T(8,128)(2,1)S(1)}, u32[]{:S(2)}, u32[]{:S(2)}) collective-permute-start(bf16[256,128]{1,0:T(8,128)(2,1)S(1)} %fusion), channel_id=1, source_target_pairs={{0,8},{2,10},{4,12},{6,14},{8,0},{10,2},{12,4},{14,6},{16,24},{18,... | collective-permute-start | bytes 196616 | tf_op jit(solution)/shard_map/ppermute | solution.py:174
  12.7 0.1 collective-permute-done.7.refs_2_
  12.8 0.9 %collective-permute-done.6.refs_1_ = bf16[256,128]{1,0:T(8,128)(2,1)S(1)} collective-permute-done((bf16[256,128]{1,0:T(8,128)(2,1)S(1)}, bf16[256,128]{1,0:T(8,128)(2,1)S(1)}, u32[]{:S(2)}, u32[]{:S(2)}) %collective-permute-start.6) | collective-permute-done | bytes 65568 | tf_op jit(solution)/shard_map/ppermute | solution.py:174
  13.7 0.5 %collective-permute-done.5.refs_0_ = bf16[256,128]{1,0:T(8,128)(2,1)S(1)} collective-permute-done((bf16[256,128]{1,0:T(8,128)(2,1)S(1)}, bf16[256,128]{1,0:T(8,128)(2,1)S(1)}, u32[]{:S(2)}, u32[]{:S(2)}) %collective-permute-start.5) | collective-permute-done | bytes 65568 | tf_op jit(solution)/shard_map/ppermute | solution.py:174
  14.2 1.6 %collective-permute-start.8 = (bf16[256,128]{1,0:T(8,128)(2,1)S(1)}, bf16[256,128]{1,0:T(8,128)(2,1)S(1)}, u32[]{:S(2)}, u32[]{:S(2)}) collective-permute-start(bf16[256,128]{1,0:T(8,128)(2,1)S(1)} %fusion.1), channel_id=1, source_target_pairs={{0,8},{2,10},{4,12},{6,14},{8,0},{10,2},{12,4},{14,6},{16,24},{18,... | collective-permute-start | bytes 196616 | tf_op jit(solution)/shard_map/ppermute | solution.py:174
  15.9 0.2 collective-permute-done.3.refs_3_
  16.1 0.0 copy-start.1
  16.1 2.6 %collective-permute-start.4 = (bf16[256,128]{1,0:T(8,128)(2,1)S(1)}, bf16[256,128]{1,0:T(8,128)(2,1)S(1)}, u32[]{:S(2)}, u32[]{:S(2)}) collective-permute-start(bf16[256,128]{1,0:T(8,128)(2,1)S(1)} %add_convert_fusion.5), channel_id=1, source_target_pairs={{0,16},{2,18},{4,20},{6,22},{8,24},{10,26},{12,28},{14,30},{16,0},... | collective-permute-start | bytes 196616 | tf_op jit(solution)/shard_map/ppermute | solution.py:174
  18.7 0.1 add_convert_fusion.4
  18.8 2.5 %collective-permute-start.9 = (bf16[256,128]{1,0:T(8,128)(2,1)S(1)}, bf16[256,128]{1,0:T(8,128)(2,1)S(1)}, u32[]{:S(2)}, u32[]{:S(2)}) collective-permute-start(bf16[256,128]{1,0:T(8,128)(2,1)S(1)} %add_convert_fusion.4), channel_id=1, source_target_pairs={{0,16},{2,18},{4,20},{6,22},{8,24},{10,26},{12,28},{14,30},{16,0},... | collective-permute-start | bytes 196616 | tf_op jit(solution)/shard_map/ppermute | solution.py:174
  21.3 0.7 %shard_map.110 = (f32[256,512]{1,0:T(8,128)S(1)}, bf16[512,256]{1,0:T(8,128)(2,1)S(1)}) custom-call(bf16[256,512]{1,0:T(8,128)(2,1)S(1)} %copy-done.1, bf16[512,512]{1,0:T(8,128)(2,1)S(1)} %constant_dynamic-update-slice_fusion.kv_ref.refs_9_.refs_3_.refs_6_), custom_call_target="tpu_custom_call" | custom-call | flops 134217728 | bytes 1310720 | tf_op jit(solution)/shard_map/pallas_call | solution.py:238
  22.0 0.8 %collective-permute-done.4.refs_4_ = bf16[256,128]{1,0:T(8,128)(2,1)S(1)} collective-permute-done((bf16[256,128]{1,0:T(8,128)(2,1)S(1)}, bf16[256,128]{1,0:T(8,128)(2,1)S(1)}, u32[]{:S(2)}, u32[]{:S(2)}) %collective-permute-start.4) | collective-permute-done | bytes 65568 | tf_op jit(solution)/shard_map/ppermute | solution.py:174
  22.7 0.4 shard_map.111
  23.1 0.9 %collective-permute-done.9.refs_4_ = bf16[256,128]{1,0:T(8,128)(2,1)S(1)} collective-permute-done((bf16[256,128]{1,0:T(8,128)(2,1)S(1)}, bf16[256,128]{1,0:T(8,128)(2,1)S(1)}, u32[]{:S(2)}, u32[]{:S(2)}) %collective-permute-start.9) | collective-permute-done | bytes 65568 | tf_op jit(solution)/shard_map/ppermute | solution.py:174
  24.0 0.4 shard_map.112
  24.4 0.1 collective-permute-start.10
  24.5 1.2 %collective-permute-done.10.other_ref.refs_7_ = f32[8,256]{1,0:T(8,128)S(1)} collective-permute-done((f32[8,256]{1,0:T(8,128)S(1)}, f32[8,256]{1,0:T(8,128)S(1)}, u32[]{:S(2)}, u32[]{:S(2)}) %collective-permute-start.10) | collective-permute-done | bytes 8224 | tf_op jit(solution)/shard_map/ppermute | solution.py:251
  25.7 0.3 shard_map.113
  26.0 1.7 %collective-permute-start.18 = (bf16[272,128]{1,0:T(8,128)(2,1)S(1)}, bf16[272,128]{1,0:T(8,128)(2,1)S(1)}, u32[]{:S(2)}, u32[]{:S(2)}) collective-permute-start(bf16[272,128]{1,0:T(8,128)(2,1)S(1)} %get-tuple-element.61), channel_id=1, source_target_pairs={{0,6},{2,4},{4,2},{6,0},{8,14},{10,12},{12,10},{14,8},{16,22},{18,... | collective-permute-start | bytes 208904 | tf_op jit(solution)/shard_map/ppermute | solution.py:174
  27.6 0.4 collective-permute-start.17
  28.0 1.5 %collective-permute-start.14 = (bf16[272,128]{1,0:T(8,128)(2,1)S(1)}, bf16[272,128]{1,0:T(8,128)(2,1)S(1)}, u32[]{:S(2)}, u32[]{:S(2)}) collective-permute-start(bf16[272,128]{1,0:T(8,128)(2,1)S(1)} %get-tuple-element.61), channel_id=1, source_target_pairs={{0,2},{2,0},{4,6},{6,4},{8,10},{10,8},{12,14},{14,12},{16,18},{18,... | collective-permute-start | bytes 208904 | tf_op jit(solution)/shard_map/ppermute | solution.py:174
  29.5 0.3 shard_map.114
  29.9 1.7 %collective-permute-start.13 = (bf16[272,128]{1,0:T(8,128)(2,1)S(1)}, bf16[272,128]{1,0:T(8,128)(2,1)S(1)}, u32[]{:S(2)}, u32[]{:S(2)}) collective-permute-start(bf16[272,128]{1,0:T(8,128)(2,1)S(1)} %get-tuple-element.60), channel_id=1, source_target_pairs={{0,6},{2,4},{4,2},{6,0},{8,14},{10,12},{12,10},{14,8},{16,22},{18,... | collective-permute-start | bytes 208904 | tf_op jit(solution)/shard_map/ppermute | solution.py:174
  31.5 0.4 collective-permute-start.12
  31.9 1.5 %collective-permute-start.11 = (bf16[272,128]{1,0:T(8,128)(2,1)S(1)}, bf16[272,128]{1,0:T(8,128)(2,1)S(1)}, u32[]{:S(2)}, u32[]{:S(2)}) collective-permute-start(bf16[272,128]{1,0:T(8,128)(2,1)S(1)} %get-tuple-element.60), channel_id=1, source_target_pairs={{0,2},{2,0},{4,6},{6,4},{8,10},{10,8},{12,14},{14,12},{16,18},{18,... | collective-permute-start | bytes 208904 | tf_op jit(solution)/shard_map/ppermute | solution.py:174
  33.5 1.6 %collective-permute-start.19 = (bf16[272,128]{1,0:T(8,128)(2,1)S(1)}, bf16[272,128]{1,0:T(8,128)(2,1)S(1)}, u32[]{:S(2)}, u32[]{:S(2)}) collective-permute-start(bf16[272,128]{1,0:T(8,128)(2,1)S(1)} %add_convert_fusion.1), channel_id=1, source_target_pairs={{0,8},{2,10},{4,12},{6,14},{8,0},{10,2},{12,4},{14,6},{16,24},{18,... | collective-permute-start | bytes 208904 | tf_op jit(solution)/shard_map/ppermute | solution.py:174
  35.1 1.0 %shard_map.116 = (f32[256,512]{1,0:T(8,128)S(1)}, f32[256,512]{1,0:T(8,128)S(1)}) custom-call(bf16[256,256]{1,0:T(8,128)(2,1)S(1)} %get-tuple-element.62.refs_2_.refs_0_, bf16[256,256]{1,0:T(8,128)(2,1)S(1)} %get-tuple-element.63.refs_3_.refs_1_, bf16[256,512]{1,0:T(8,128)(2,1)S(1)} %copy-done.1, ...), custom_call_target="tpu_custom_call" | custom-call | flops 268435456 | bytes 2097152 | tf_op jit(solution)/shard_map/pallas_call | solution.py:188
  36.1 0.1 collective-permute-done.12.refs_1_
  36.2 0.0 collective-permute-done.11.refs_0_
  36.3 1.6 %collective-permute-start.15 = (bf16[272,128]{1,0:T(8,128)(2,1)S(1)}, bf16[272,128]{1,0:T(8,128)(2,1)S(1)}, u32[]{:S(2)}, u32[]{:S(2)}) collective-permute-start(bf16[272,128]{1,0:T(8,128)(2,1)S(1)} %add_convert_fusion.3), channel_id=1, source_target_pairs={{0,8},{2,10},{4,12},{6,14},{8,0},{10,2},{12,4},{14,6},{16,24},{18,... | collective-permute-start | bytes 208904 | tf_op jit(solution)/shard_map/ppermute | solution.py:174
  38.0 3.4 %collective-permute-start.20 = (bf16[272,128]{1,0:T(8,128)(2,1)S(1)}, bf16[272,128]{1,0:T(8,128)(2,1)S(1)}, u32[]{:S(2)}, u32[]{:S(2)}) collective-permute-start(bf16[272,128]{1,0:T(8,128)(2,1)S(1)} %add_convert_fusion.refs_5_), channel_id=1, source_target_pairs={{0,16},{2,18},{4,20},{6,22},{8,24},{10,26},{12,28},{14,30},{16,0},... | collective-permute-start | bytes 208904 | tf_op jit(solution)/shard_map/ppermute | solution.py:174
  41.4 0.0 collective-permute-done.15.refs_3_
  41.4 2.3 %collective-permute-start.16 = (bf16[272,128]{1,0:T(8,128)(2,1)S(1)}, bf16[272,128]{1,0:T(8,128)(2,1)S(1)}, u32[]{:S(2)}, u32[]{:S(2)}) collective-permute-start(bf16[272,128]{1,0:T(8,128)(2,1)S(1)} %add_convert_fusion.2.refs_5_), channel_id=1, source_target_pairs={{0,16},{2,18},{4,20},{6,22},{8,24},{10,26},{12,28},{14,30},{16,0},... | collective-permute-start | bytes 208904 | tf_op jit(solution)/shard_map/ppermute | solution.py:174
  43.7 1.4 %shard_map.115 = (bf16[256,512]{1,0:T(8,128)(2,1)}, bf16[256,512]{1,0:T(8,128)(2,1)}) custom-call(f32[256,256]{1,0:T(8,128)S(1)} %get-tuple-element.47.un_ref.refs_0_, f32[256,256]{1,0:T(8,128)S(1)} %get-tuple-element.51.un_ref.refs_1_, bf16[256,256]{1,0:T(8,128)(2,1)S(1)} %get-tuple-element.62.refs_2_.refs_0_, ...), custom_call_target="tpu_custom_call" | custom-call | flops 167772160 | bytes 2097152 | tf_op jit(solution)/shard_map/pallas_call | solution.py:265
  45.1 0.3 collective-permute-done.20.refs_4_
  45.4 1.0 %shard_map.117 = (bf16[256,512]{1,0:T(8,128)(2,1)}, bf16[256,512]{1,0:T(8,128)(2,1)}, f32[4,128,128]{2,1,0:T(8,128)}, f32[1,512]{1,0:T(1,128)}) custom-call(bf16[272,128]{1,0:T(8,128)(2,1)S(1)} %collective-permute-done.14.refs_0_, bf16[272,128]{1,0:T(8,128)(2,1)S(1)} %collective-permute-done.17.refs_1_, ...), custom_call_target="tpu_custom_call" | custom-call | flops 33554432 | bytes 1835008 | tf_op jit(solution)/shard_map/pallas_call | solution.py:276
  46.4 0.3 collective-permute-done.16.refs_4_
  46.7 1.0 %shard_map.118 = (bf16[256,512]{1,0:T(8,128)(2,1)}, bf16[256,512]{1,0:T(8,128)(2,1)}, f32[4,128,128]{2,1,0:T(8,128)}, f32[1,512]{1,0:T(1,128)}) custom-call(bf16[272,128]{1,0:T(8,128)(2,1)S(1)} %collective-permute-done.11.refs_0_, ...), custom_call_target="tpu_custom_call", output_to_operand_aliasing={{0}: (9, {}), {1}: (10, {}), {2}: (11, {}), {3}: (12, {})} | custom-call | flops 33554432 | bytes 1835008 | tf_op jit(solution)/shard_map/pallas_call | solution.py:276
  (24 shorter events, 0.3 us)
Async XLA Ops:
  0.6 1.0 %copy-start.4 = (bf16[256,512]{1,0:T(8,128)(2,1)S(1)}, bf16[256,512]{1,0:T(8,128)(2,1)}, u32[]{:S(2)}) copy-start(bf16[256,512]{1,0:T(8,128)(2,1)} %param.8) | copy-start | bytes 786436
  2.0 8.0 %collective-permute-start.2 = (bf16[256,128]{1,0:T(8,128)(2,1)S(1)}, bf16[256,128]{1,0:T(8,128)(2,1)S(1)}, u32[]{:S(2)}, u32[]{:S(2)}) collective-permute-start(bf16[256,128]{1,0:T(8,128)(2,1)S(1)} %get-tuple-element.44), channel_id=1, source_target_pairs={{0,6},{2,4},{4,2},{6,0},{8,14},{10,12},{12,10},{14,8},{16,22},{18,... | collective-permute-start | bytes 196616 | tf_op jit(solution)/shard_map/ppermute | solution.py:174
  5.9 5.1 %collective-permute-start.1 = (bf16[256,128]{1,0:T(8,128)(2,1)S(1)}, bf16[256,128]{1,0:T(8,128)(2,1)S(1)}, u32[]{:S(2)}, u32[]{:S(2)}) collective-permute-start(bf16[256,128]{1,0:T(8,128)(2,1)S(1)} %get-tuple-element.44), channel_id=1, source_target_pairs={{0,4},{2,6},{4,0},{6,2},{8,12},{10,14},{12,8},{14,10},{16,20},{18,... | collective-permute-start | bytes 196616 | tf_op jit(solution)/shard_map/ppermute | solution.py:174
  6.4 4.6 %collective-permute-start = (bf16[256,128]{1,0:T(8,128)(2,1)S(1)}, bf16[256,128]{1,0:T(8,128)(2,1)S(1)}, u32[]{:S(2)}, u32[]{:S(2)}) collective-permute-start(bf16[256,128]{1,0:T(8,128)(2,1)S(1)} %get-tuple-element.44), channel_id=1, source_target_pairs={{0,2},{2,0},{4,6},{6,4},{8,10},{10,8},{12,14},{14,12},{16,18},{18,... | collective-permute-start | bytes 196616 | tf_op jit(solution)/shard_map/ppermute | solution.py:174
  6.6 6.2 %collective-permute-start.7 = (bf16[256,128]{1,0:T(8,128)(2,1)S(1)}, bf16[256,128]{1,0:T(8,128)(2,1)S(1)}, u32[]{:S(2)}, u32[]{:S(2)}) collective-permute-start(bf16[256,128]{1,0:T(8,128)(2,1)S(1)} %get-tuple-element.48), channel_id=1, source_target_pairs={{0,6},{2,4},{4,2},{6,0},{8,14},{10,12},{12,10},{14,8},{16,22},{18,... | collective-permute-start | bytes 196616 | tf_op jit(solution)/shard_map/ppermute | solution.py:174
  9.4 4.3 %collective-permute-start.6 = (bf16[256,128]{1,0:T(8,128)(2,1)S(1)}, bf16[256,128]{1,0:T(8,128)(2,1)S(1)}, u32[]{:S(2)}, u32[]{:S(2)}) collective-permute-start(bf16[256,128]{1,0:T(8,128)(2,1)S(1)} %get-tuple-element.48), channel_id=1, source_target_pairs={{0,4},{2,6},{4,0},{6,2},{8,12},{10,14},{12,8},{14,10},{16,20},{18,... | collective-permute-start | bytes 196616 | tf_op jit(solution)/shard_map/ppermute | solution.py:174
  9.9 4.3 %collective-permute-start.5 = (bf16[256,128]{1,0:T(8,128)(2,1)S(1)}, bf16[256,128]{1,0:T(8,128)(2,1)S(1)}, u32[]{:S(2)}, u32[]{:S(2)}) collective-permute-start(bf16[256,128]{1,0:T(8,128)(2,1)S(1)} %get-tuple-element.48), channel_id=1, source_target_pairs={{0,2},{2,0},{4,6},{6,4},{8,10},{10,8},{12,14},{14,12},{16,18},{18,... | collective-permute-start | bytes 196616 | tf_op jit(solution)/shard_map/ppermute | solution.py:174
  11.0 5.0 %collective-permute-start.3 = (bf16[256,128]{1,0:T(8,128)(2,1)S(1)}, bf16[256,128]{1,0:T(8,128)(2,1)S(1)}, u32[]{:S(2)}, u32[]{:S(2)}) collective-permute-start(bf16[256,128]{1,0:T(8,128)(2,1)S(1)} %fusion), channel_id=1, source_target_pairs={{0,8},{2,10},{4,12},{6,14},{8,0},{10,2},{12,4},{14,6},{16,24},{18,... | collective-permute-start | bytes 196616 | tf_op jit(solution)/shard_map/ppermute | solution.py:174
  14.2 4.5 %collective-permute-start.8 = (bf16[256,128]{1,0:T(8,128)(2,1)S(1)}, bf16[256,128]{1,0:T(8,128)(2,1)S(1)}, u32[]{:S(2)}, u32[]{:S(2)}) collective-permute-start(bf16[256,128]{1,0:T(8,128)(2,1)S(1)} %fusion.1), channel_id=1, source_target_pairs={{0,8},{2,10},{4,12},{6,14},{8,0},{10,2},{12,4},{14,6},{16,24},{18,... | collective-permute-start | bytes 196616 | tf_op jit(solution)/shard_map/ppermute | solution.py:174
  16.1 5.2 %copy-start.1 = (bf16[256,512]{1,0:T(8,128)(2,1)S(1)}, bf16[256,512]{1,0:T(8,128)(2,1)}, u32[]{:S(2)}) copy-start(bf16[256,512]{1,0:T(8,128)(2,1)} %refs_2_) | copy-start | bytes 786436
  16.1 6.6 %collective-permute-start.4 = (bf16[256,128]{1,0:T(8,128)(2,1)S(1)}, bf16[256,128]{1,0:T(8,128)(2,1)S(1)}, u32[]{:S(2)}, u32[]{:S(2)}) collective-permute-start(bf16[256,128]{1,0:T(8,128)(2,1)S(1)} %add_convert_fusion.5), channel_id=1, source_target_pairs={{0,16},{2,18},{4,20},{6,22},{8,24},{10,26},{12,28},{14,30},{16,0},... | collective-permute-start | bytes 196616 | tf_op jit(solution)/shard_map/ppermute | solution.py:174
  18.8 3.9 %copy-start = (bf16[256,512]{1,0:T(8,128)(2,1)S(1)}, bf16[256,512]{1,0:T(8,128)(2,1)}, u32[]{:S(2)}) copy-start(bf16[256,512]{1,0:T(8,128)(2,1)} %cot_ref.3) | copy-start | bytes 786436
  18.8 3.9 %copy-start.2 = (f32[4,128,128]{2,1,0:T(8,128)S(1)}, f32[4,128,128]{2,1,0:T(8,128)}, u32[]{:S(2)}) copy-start(f32[4,128,128]{2,1,0:T(8,128)} %refs_9_.1) | copy-start | bytes 786436
  18.8 5.2 %collective-permute-start.9 = (bf16[256,128]{1,0:T(8,128)(2,1)S(1)}, bf16[256,128]{1,0:T(8,128)(2,1)S(1)}, u32[]{:S(2)}, u32[]{:S(2)}) collective-permute-start(bf16[256,128]{1,0:T(8,128)(2,1)S(1)} %add_convert_fusion.4), channel_id=1, source_target_pairs={{0,16},{2,18},{4,20},{6,22},{8,24},{10,26},{12,28},{14,30},{16,0},... | collective-permute-start | bytes 196616 | tf_op jit(solution)/shard_map/ppermute | solution.py:174
  22.0 0.8 %copy-start.3 = (f32[512]{0:T(512)S(1)}, f32[512]{0:T(512)}, u32[]{:S(2)}) copy-start(f32[512]{0:T(512)} %param.11) | copy-start | bytes 6148
  24.4 1.2 %collective-permute-start.10 = (f32[8,256]{1,0:T(8,128)S(1)}, f32[8,256]{1,0:T(8,128)S(1)}, u32[]{:S(2)}, u32[]{:S(2)}) collective-permute-start(f32[8,256]{1,0:T(8,128)S(1)} %get-tuple-element.52.sums_ref.refs_6_), channel_id=1, source_target_pairs={{0,1},{1,0},{2,3},{3,2},{4,5},{5,4},{6,7},{7,6},{8,9},{9,8},{10,11... | collective-permute-start | bytes 24584 | tf_op jit(solution)/shard_map/ppermute | solution.py:251
  26.0 6.0 %collective-permute-start.18 = (bf16[272,128]{1,0:T(8,128)(2,1)S(1)}, bf16[272,128]{1,0:T(8,128)(2,1)S(1)}, u32[]{:S(2)}, u32[]{:S(2)}) collective-permute-start(bf16[272,128]{1,0:T(8,128)(2,1)S(1)} %get-tuple-element.61), channel_id=1, source_target_pairs={{0,6},{2,4},{4,2},{6,0},{8,14},{10,12},{12,10},{14,8},{16,22},{18,... | collective-permute-start | bytes 208904 | tf_op jit(solution)/shard_map/ppermute | solution.py:174
  27.6 5.8 %collective-permute-start.17 = (bf16[272,128]{1,0:T(8,128)(2,1)S(1)}, bf16[272,128]{1,0:T(8,128)(2,1)S(1)}, u32[]{:S(2)}, u32[]{:S(2)}) collective-permute-start(bf16[272,128]{1,0:T(8,128)(2,1)S(1)} %get-tuple-element.61), channel_id=1, source_target_pairs={{0,4},{2,6},{4,0},{6,2},{8,12},{10,14},{12,8},{14,10},{16,20},{18,... | collective-permute-start | bytes 208904 | tf_op jit(solution)/shard_map/ppermute | solution.py:174
  28.0 5.4 %collective-permute-start.14 = (bf16[272,128]{1,0:T(8,128)(2,1)S(1)}, bf16[272,128]{1,0:T(8,128)(2,1)S(1)}, u32[]{:S(2)}, u32[]{:S(2)}) collective-permute-start(bf16[272,128]{1,0:T(8,128)(2,1)S(1)} %get-tuple-element.61), channel_id=1, source_target_pairs={{0,2},{2,0},{4,6},{6,4},{8,10},{10,8},{12,14},{14,12},{16,18},{18,... | collective-permute-start | bytes 208904 | tf_op jit(solution)/shard_map/ppermute | solution.py:174
  29.9 6.3 %collective-permute-start.13 = (bf16[272,128]{1,0:T(8,128)(2,1)S(1)}, bf16[272,128]{1,0:T(8,128)(2,1)S(1)}, u32[]{:S(2)}, u32[]{:S(2)}) collective-permute-start(bf16[272,128]{1,0:T(8,128)(2,1)S(1)} %get-tuple-element.60), channel_id=1, source_target_pairs={{0,6},{2,4},{4,2},{6,0},{8,14},{10,12},{12,10},{14,8},{16,22},{18,... | collective-permute-start | bytes 208904 | tf_op jit(solution)/shard_map/ppermute | solution.py:174
  31.5 4.7 %collective-permute-start.12 = (bf16[272,128]{1,0:T(8,128)(2,1)S(1)}, bf16[272,128]{1,0:T(8,128)(2,1)S(1)}, u32[]{:S(2)}, u32[]{:S(2)}) collective-permute-start(bf16[272,128]{1,0:T(8,128)(2,1)S(1)} %get-tuple-element.60), channel_id=1, source_target_pairs={{0,4},{2,6},{4,0},{6,2},{8,12},{10,14},{12,8},{14,10},{16,20},{18,... | collective-permute-start | bytes 208904 | tf_op jit(solution)/shard_map/ppermute | solution.py:174
  31.9 4.3 %collective-permute-start.11 = (bf16[272,128]{1,0:T(8,128)(2,1)S(1)}, bf16[272,128]{1,0:T(8,128)(2,1)S(1)}, u32[]{:S(2)}, u32[]{:S(2)}) collective-permute-start(bf16[272,128]{1,0:T(8,128)(2,1)S(1)} %get-tuple-element.60), channel_id=1, source_target_pairs={{0,2},{2,0},{4,6},{6,4},{8,10},{10,8},{12,14},{14,12},{16,18},{18,... | collective-permute-start | bytes 208904 | tf_op jit(solution)/shard_map/ppermute | solution.py:174
  33.5 4.5 %collective-permute-start.19 = (bf16[272,128]{1,0:T(8,128)(2,1)S(1)}, bf16[272,128]{1,0:T(8,128)(2,1)S(1)}, u32[]{:S(2)}, u32[]{:S(2)}) collective-permute-start(bf16[272,128]{1,0:T(8,128)(2,1)S(1)} %add_convert_fusion.1), channel_id=1, source_target_pairs={{0,8},{2,10},{4,12},{6,14},{8,0},{10,2},{12,4},{14,6},{16,24},{18,... | collective-permute-start | bytes 208904 | tf_op jit(solution)/shard_map/ppermute | solution.py:174
  36.3 5.1 %collective-permute-start.15 = (bf16[272,128]{1,0:T(8,128)(2,1)S(1)}, bf16[272,128]{1,0:T(8,128)(2,1)S(1)}, u32[]{:S(2)}, u32[]{:S(2)}) collective-permute-start(bf16[272,128]{1,0:T(8,128)(2,1)S(1)} %add_convert_fusion.3), channel_id=1, source_target_pairs={{0,8},{2,10},{4,12},{6,14},{8,0},{10,2},{12,4},{14,6},{16,24},{18,... | collective-permute-start | bytes 208904 | tf_op jit(solution)/shard_map/ppermute | solution.py:174
  38.0 7.5 %collective-permute-start.20 = (bf16[272,128]{1,0:T(8,128)(2,1)S(1)}, bf16[272,128]{1,0:T(8,128)(2,1)S(1)}, u32[]{:S(2)}, u32[]{:S(2)}) collective-permute-start(bf16[272,128]{1,0:T(8,128)(2,1)S(1)} %add_convert_fusion.refs_5_), channel_id=1, source_target_pairs={{0,16},{2,18},{4,20},{6,22},{8,24},{10,26},{12,28},{14,30},{16,0},... | collective-permute-start | bytes 208904 | tf_op jit(solution)/shard_map/ppermute | solution.py:174
  41.4 5.3 %collective-permute-start.16 = (bf16[272,128]{1,0:T(8,128)(2,1)S(1)}, bf16[272,128]{1,0:T(8,128)(2,1)S(1)}, u32[]{:S(2)}, u32[]{:S(2)}) collective-permute-start(bf16[272,128]{1,0:T(8,128)(2,1)S(1)} %add_convert_fusion.2.refs_5_), channel_id=1, source_target_pairs={{0,16},{2,18},{4,20},{6,22},{8,24},{10,26},{12,28},{14,30},{16,0},... | collective-permute-start | bytes 208904 | tf_op jit(solution)/shard_map/ppermute | solution.py:174

commit v7 on v6

--- a/solution.py
+++ b/solution.py
@@ -103,8 +103,13 @@
     return [jnp.broadcast_to(row, (dim, length)).T for row in (inverse, factor)]
 
 
-def norm_kernel(heads, dim, width, sums_ref, other_ref, un_ref, cot_ref, gain_ref, q_ref, gun_ref, msg_ref):
-    inverse, factor = scales(sums_ref, other_ref, width, dim)
+def norm_kernel(heads, dim, width, first, a_ref, b_ref, un_ref, cot_ref, gain_ref, q_ref, gun_ref, msg_ref, *kept):
+    if first:
+        inverse, factor = scales(a_ref, b_ref, width, dim)
+        kept[0][...] = inverse
+        kept[1][...] = factor
+    else:
+        inverse, factor = a_ref[...], b_ref[...]
     row = lax.broadcasted_iota(jnp.int32, (EXTRA, dim), 0)
     gains = jnp.zeros((EXTRA, dim), F32)
     for i, h in enumerate(heads):
@@ -118,11 +123,11 @@
     msg_ref[len(heads) * dim :, :] = gains.astype(BF16)
 
 
-def attended_kernel(halves, dim, width, *refs):
+def attended_kernel(halves, dim, *refs):
     n = len(halves)
     uns, guns, prefixes = refs[:n], refs[n : 2 * n], refs[2 * n : 3 * n]
-    sums_ref, other_ref, gain_ref, kv_ref, att_ref, gq_ref = refs[3 * n :]
-    inverse, _ = scales(sums_ref, other_ref, width, dim)
+    inverse_ref, gain_ref, kv_ref, att_ref, gq_ref = refs[3 * n :]
+    inverse = inverse_ref[...]
     length = kv_ref.shape[0] // 2
     mask = causal(length)
     for heads, un_ref, gun_ref, prefix_ref in zip(halves, uns, guns, prefixes):
@@ -251,21 +256,24 @@
         partner = lax.ppermute(partner, "head", [(i, (i + 1) % head_count) for i in range(head_count)])
         other = other + partner if step > 1 else partner
 
-    guns, messages = [], []
+    guns, messages, scale = [], [], [sums, other]
+    column = shape((length, dim), F32)
     for n, members in enumerate(halves):
-        gun, message = call(
-            functools.partial(norm_kernel, members, dim, total_width),
-            (half_bf, shape((per * dim + EXTRA, dim), BF16)), block // 2, 3 * size,
-        )(sums, other, unnormed[n], cotangent, gain, turned)
+        gun, message, *kept = call(
+            functools.partial(norm_kernel, members, dim, total_width, n == 0),
+            (half_bf, shape((per * dim + EXTRA, dim), BF16)) + (column,) * (2 if n == 0 else 0),
+            block // 2, 3 * size,
+        )(*scale, unnormed[n], cotangent, gain, turned)
+        scale = kept or scale
         guns.append(gun)
         messages.append(message)
     inner = (call(
         functools.partial(local_kernel, halves, dim), (tokens_f32, tokens_f32), 4 * square, 8 * size,
     ), *guns, queries, kv)
     attended, grad_q = call(
-        functools.partial(attended_kernel, halves, dim, total_width),
+        functools.partial(attended_kernel, halves, dim),
         (tokens_bf, tokens_bf), 2 * square + block, 8 * size,
-    )(*unnormed, *guns, *prefixes, sums, other, gain, kv)
+    )(*unnormed, *guns, *prefixes, scale[0], gain, kv)
     partners, messages, received, done = scan(messages, None, count, {spot: inner})
     local_k, local_v = done[spot]
 

time: 47.9 us -> 47.8 us (level)
  no operation moved by 1% of the time
where the time goes in v7:
time: 47.8 us; the launch traced here: 47.6 us
  starting transfers between devices  33.2 us (69%)
  Pallas kernels  6.62 us (14%)
  waiting for transfers between devices  5.66 us (12%)
  local copies, waits for them, and re-layouts  1.06 us (2%)
  between operations  0.8 us (2%)
    ppermute x20, starting transfers between devices, swap(): lax.ppermute(message, 'seq', [(i, i ^ partner) for i in range(count)])  33.1 us
    ppermute x20, waiting for transfers between devices, swap(): lax.ppermute(message, 'seq', [(i, i ^ partner) for i in range(count)])  4.5 us
    pallas_call x2, Pallas kernels, on_device(): call(functools.partial(final_kernel, members, dim, partners, n == 0), (to...  1.98 us
    pallas_call x1, Pallas kernels, on_device(): call(functools.partial(attended_kernel, halves, dim), (tokens_bf, tokens_...  1.44 us
    ppermute x1, waiting for transfers between devices, on_device(): lax.ppermute(partner, 'head', [(i, (i + 1) % head_count) for i in range(h...  1.16 us
    unnamed x11, local copies, waits for them, and re-layouts  1.04 us
    pallas_call x1, Pallas kernels, scan(): work = beside[n, distance][0](*operands)  1 us
  transfers between devices with their start and end apart: 21, of which 11 were waited for; matrix products, arithmetic and copies ran while one was open for 1% of the time, Pallas kernels for 10%

profile of v7, /device:TPU:0, one launch (start us, length us, event | category | flops | bytes accessed | tf_op | source)
XLA Modules:
  0.0 47.6 jit_solution(13402980878217560348)
XLA Ops:
  0.6 1.0 %constant_dynamic-update-slice_fusion.1 = bf16[512,512]{1,0:T(8,128)(2,1)S(1)} fusion(bf16[256,512]{1,0:T(8,128)(2,1)} %param.7), kind=kLoop, calls=%fused_computation.11 | loop fusion | bytes 524288
  1.7 0.0 copy-done.4
  1.7 0.3 shard_map.109
  2.0 4.0 %collective-permute-start.2 = (bf16[256,128]{1,0:T(8,128)(2,1)S(1)}, bf16[256,128]{1,0:T(8,128)(2,1)S(1)}, u32[]{:S(2)}, u32[]{:S(2)}) collective-permute-start(bf16[256,128]{1,0:T(8,128)(2,1)S(1)} %get-tuple-element.46), channel_id=1, source_target_pairs={{0,6},{2,4},{4,2},{6,0},{8,14},{10,12},{12,10},{14,8},{16,22},{18,... | collective-permute-start | bytes 196616 | tf_op jit(solution)/shard_map/ppermute | solution.py:179
  5.9 0.5 %collective-permute-start.1 = (bf16[256,128]{1,0:T(8,128)(2,1)S(1)}, bf16[256,128]{1,0:T(8,128)(2,1)S(1)}, u32[]{:S(2)}, u32[]{:S(2)}) collective-permute-start(bf16[256,128]{1,0:T(8,128)(2,1)S(1)} %get-tuple-element.46), channel_id=1, source_target_pairs={{0,4},{2,6},{4,0},{6,2},{8,12},{10,14},{12,8},{14,10},{16,20},{18,... | collective-permute-start | bytes 196616 | tf_op jit(solution)/shard_map/ppermute | solution.py:179
  6.4 0.1 collective-permute-start
  6.6 2.8 %collective-permute-start.7 = (bf16[256,128]{1,0:T(8,128)(2,1)S(1)}, bf16[256,128]{1,0:T(8,128)(2,1)S(1)}, u32[]{:S(2)}, u32[]{:S(2)}) collective-permute-start(bf16[256,128]{1,0:T(8,128)(2,1)S(1)} %get-tuple-element.50), channel_id=1, source_target_pairs={{0,6},{2,4},{4,2},{6,0},{8,14},{10,12},{12,10},{14,8},{16,22},{18,... | collective-permute-start | bytes 196616 | tf_op jit(solution)/shard_map/ppermute | solution.py:179
  9.4 0.5 %collective-permute-start.6 = (bf16[256,128]{1,0:T(8,128)(2,1)S(1)}, bf16[256,128]{1,0:T(8,128)(2,1)S(1)}, u32[]{:S(2)}, u32[]{:S(2)}) collective-permute-start(bf16[256,128]{1,0:T(8,128)(2,1)S(1)} %get-tuple-element.50), channel_id=1, source_target_pairs={{0,4},{2,6},{4,0},{6,2},{8,12},{10,14},{12,8},{14,10},{16,20},{18,... | collective-permute-start | bytes 196616 | tf_op jit(solution)/shard_map/ppermute | solution.py:179
  9.9 0.6 %collective-permute-start.5 = (bf16[256,128]{1,0:T(8,128)(2,1)S(1)}, bf16[256,128]{1,0:T(8,128)(2,1)S(1)}, u32[]{:S(2)}, u32[]{:S(2)}) collective-permute-start(bf16[256,128]{1,0:T(8,128)(2,1)S(1)} %get-tuple-element.50), channel_id=1, source_target_pairs={{0,2},{2,0},{4,6},{6,4},{8,10},{10,8},{12,14},{14,12},{16,18},{18,... | collective-permute-start | bytes 196616 | tf_op jit(solution)/shard_map/ppermute | solution.py:179
  10.6 0.4 collective-permute-done.1.refs_1_
  11.0 1.6 %collective-permute-start.3 = (bf16[256,128]{1,0:T(8,128)(2,1)S(1)}, bf16[256,128]{1,0:T(8,128)(2,1)S(1)}, u32[]{:S(2)}, u32[]{:S(2)}) collective-permute-start(bf16[256,128]{1,0:T(8,128)(2,1)S(1)} %fusion), channel_id=1, source_target_pairs={{0,8},{2,10},{4,12},{6,14},{8,0},{10,2},{12,4},{14,6},{16,24},{18,... | collective-permute-start | bytes 196616 | tf_op jit(solution)/shard_map/ppermute | solution.py:179
  12.7 0.1 collective-permute-done.7.refs_2_
  12.8 0.9 %collective-permute-done.6.refs_1_ = bf16[256,128]{1,0:T(8,128)(2,1)S(1)} collective-permute-done((bf16[256,128]{1,0:T(8,128)(2,1)S(1)}, bf16[256,128]{1,0:T(8,128)(2,1)S(1)}, u32[]{:S(2)}, u32[]{:S(2)}) %collective-permute-start.6) | collective-permute-done | bytes 65568 | tf_op jit(solution)/shard_map/ppermute | solution.py:179
  13.7 0.5 %collective-permute-done.5.refs_0_ = bf16[256,128]{1,0:T(8,128)(2,1)S(1)} collective-permute-done((bf16[256,128]{1,0:T(8,128)(2,1)S(1)}, bf16[256,128]{1,0:T(8,128)(2,1)S(1)}, u32[]{:S(2)}, u32[]{:S(2)}) %collective-permute-start.5) | collective-permute-done | bytes 65568 | tf_op jit(solution)/shard_map/ppermute | solution.py:179
  14.2 1.6 %collective-permute-start.8 = (bf16[256,128]{1,0:T(8,128)(2,1)S(1)}, bf16[256,128]{1,0:T(8,128)(2,1)S(1)}, u32[]{:S(2)}, u32[]{:S(2)}) collective-permute-start(bf16[256,128]{1,0:T(8,128)(2,1)S(1)} %fusion.1), channel_id=1, source_target_pairs={{0,8},{2,10},{4,12},{6,14},{8,0},{10,2},{12,4},{14,6},{16,24},{18,... | collective-permute-start | bytes 196616 | tf_op jit(solution)/shard_map/ppermute | solution.py:179
  15.9 0.2 collective-permute-done.3.refs_3_
  16.1 2.6 %collective-permute-start.4 = (bf16[256,128]{1,0:T(8,128)(2,1)S(1)}, bf16[256,128]{1,0:T(8,128)(2,1)S(1)}, u32[]{:S(2)}, u32[]{:S(2)}) collective-permute-start(bf16[256,128]{1,0:T(8,128)(2,1)S(1)} %add_convert_fusion.5), channel_id=1, source_target_pairs={{0,16},{2,18},{4,20},{6,22},{8,24},{10,26},{12,28},{14,30},{16,0},... | collective-permute-start | bytes 196616 | tf_op jit(solution)/shard_map/ppermute | solution.py:179
  18.7 0.1 add_convert_fusion.4
  18.8 2.5 %collective-permute-start.9 = (bf16[256,128]{1,0:T(8,128)(2,1)S(1)}, bf16[256,128]{1,0:T(8,128)(2,1)S(1)}, u32[]{:S(2)}, u32[]{:S(2)}) collective-permute-start(bf16[256,128]{1,0:T(8,128)(2,1)S(1)} %add_convert_fusion.4), channel_id=1, source_target_pairs={{0,16},{2,18},{4,20},{6,22},{8,24},{10,26},{12,28},{14,30},{16,0},... | collective-permute-start | bytes 196616 | tf_op jit(solution)/shard_map/ppermute | solution.py:179
  21.3 0.7 %shard_map.110 = (f32[256,512]{1,0:T(8,128)S(1)}, bf16[512,256]{1,0:T(8,128)(2,1)S(1)}) custom-call(bf16[256,512]{1,0:T(8,128)(2,1)S(1)} %copy-done.1, bf16[512,512]{1,0:T(8,128)(2,1)S(1)} %constant_dynamic-update-slice_fusion.kv_ref.refs_8_.refs_3_.refs_6_), custom_call_target="tpu_custom_call" | custom-call | flops 134217728 | bytes 1310720 | tf_op jit(solution)/shard_map/pallas_call | solution.py:243
  22.0 0.0 copy-start.3
  22.0 0.8 %collective-permute-done.4.refs_4_ = bf16[256,128]{1,0:T(8,128)(2,1)S(1)} collective-permute-done((bf16[256,128]{1,0:T(8,128)(2,1)S(1)}, bf16[256,128]{1,0:T(8,128)(2,1)S(1)}, u32[]{:S(2)}, u32[]{:S(2)}) %collective-permute-start.4) | collective-permute-done | bytes 65568 | tf_op jit(solution)/shard_map/ppermute | solution.py:179
  22.7 0.4 shard_map.111
  23.1 0.9 %collective-permute-done.9.refs_4_ = bf16[256,128]{1,0:T(8,128)(2,1)S(1)} collective-permute-done((bf16[256,128]{1,0:T(8,128)(2,1)S(1)}, bf16[256,128]{1,0:T(8,128)(2,1)S(1)}, u32[]{:S(2)}, u32[]{:S(2)}) %collective-permute-start.9) | collective-permute-done | bytes 65568 | tf_op jit(solution)/shard_map/ppermute | solution.py:179
  24.0 0.4 shard_map.112
  24.4 0.1 collective-permute-start.10
  24.5 1.2 %collective-permute-done.10.b_ref = f32[8,256]{1,0:T(8,128)S(1)} collective-permute-done((f32[8,256]{1,0:T(8,128)S(1)}, f32[8,256]{1,0:T(8,128)S(1)}, u32[]{:S(2)}, u32[]{:S(2)}) %collective-permute-start.10) | collective-permute-done | bytes 8224 | tf_op jit(solution)/shard_map/ppermute | solution.py:256
  25.7 0.3 shard_map.113
  26.0 1.7 %collective-permute-start.18 = (bf16[272,128]{1,0:T(8,128)(2,1)S(1)}, bf16[272,128]{1,0:T(8,128)(2,1)S(1)}, u32[]{:S(2)}, u32[]{:S(2)}) collective-permute-start(bf16[272,128]{1,0:T(8,128)(2,1)S(1)} %get-tuple-element.65), channel_id=1, source_target_pairs={{0,6},{2,4},{4,2},{6,0},{8,14},{10,12},{12,10},{14,8},{16,22},{18,... | collective-permute-start | bytes 208904 | tf_op jit(solution)/shard_map/ppermute | solution.py:179
  27.6 0.4 collective-permute-start.17
  28.0 1.5 %collective-permute-start.14 = (bf16[272,128]{1,0:T(8,128)(2,1)S(1)}, bf16[272,128]{1,0:T(8,128)(2,1)S(1)}, u32[]{:S(2)}, u32[]{:S(2)}) collective-permute-start(bf16[272,128]{1,0:T(8,128)(2,1)S(1)} %get-tuple-element.65), channel_id=1, source_target_pairs={{0,2},{2,0},{4,6},{6,4},{8,10},{10,8},{12,14},{14,12},{16,18},{18,... | collective-permute-start | bytes 208904 | tf_op jit(solution)/shard_map/ppermute | solution.py:179
  29.5 0.2 shard_map.114
  29.8 1.7 %collective-permute-start.13 = (bf16[272,128]{1,0:T(8,128)(2,1)S(1)}, bf16[272,128]{1,0:T(8,128)(2,1)S(1)}, u32[]{:S(2)}, u32[]{:S(2)}) collective-permute-start(bf16[272,128]{1,0:T(8,128)(2,1)S(1)} %get-tuple-element.64), channel_id=1, source_target_pairs={{0,6},{2,4},{4,2},{6,0},{8,14},{10,12},{12,10},{14,8},{16,22},{18,... | collective-permute-start | bytes 208904 | tf_op jit(solution)/shard_map/ppermute | solution.py:179
  31.4 0.4 collective-permute-start.12
  31.9 1.5 %collective-permute-start.11 = (bf16[272,128]{1,0:T(8,128)(2,1)S(1)}, bf16[272,128]{1,0:T(8,128)(2,1)S(1)}, u32[]{:S(2)}, u32[]{:S(2)}) collective-permute-start(bf16[272,128]{1,0:T(8,128)(2,1)S(1)} %get-tuple-element.64), channel_id=1, source_target_pairs={{0,2},{2,0},{4,6},{6,4},{8,10},{10,8},{12,14},{14,12},{16,18},{18,... | collective-permute-start | bytes 208904 | tf_op jit(solution)/shard_map/ppermute | solution.py:179
  33.4 1.6 %collective-permute-start.19 = (bf16[272,128]{1,0:T(8,128)(2,1)S(1)}, bf16[272,128]{1,0:T(8,128)(2,1)S(1)}, u32[]{:S(2)}, u32[]{:S(2)}) collective-permute-start(bf16[272,128]{1,0:T(8,128)(2,1)S(1)} %add_convert_fusion.1), channel_id=1, source_target_pairs={{0,8},{2,10},{4,12},{6,14},{8,0},{10,2},{12,4},{14,6},{16,24},{18,... | collective-permute-start | bytes 208904 | tf_op jit(solution)/shard_map/ppermute | solution.py:179
  35.0 1.0 %shard_map.116 = (f32[256,512]{1,0:T(8,128)S(1)}, f32[256,512]{1,0:T(8,128)S(1)}) custom-call(bf16[256,256]{1,0:T(8,128)(2,1)S(1)} %get-tuple-element.66.refs_2_.refs_0_, bf16[256,256]{1,0:T(8,128)(2,1)S(1)} %get-tuple-element.67.refs_3_.refs_1_, bf16[256,512]{1,0:T(8,128)(2,1)S(1)} %copy-done.1, ...), custom_call_target="tpu_custom_call" | custom-call | flops 268435456 | bytes 2097152 | tf_op jit(solution)/shard_map/pallas_call | solution.py:193
  36.1 0.1 collective-permute-done.12.refs_1_
  36.2 0.0 collective-permute-done.11.refs_0_
  36.2 1.6 %collective-permute-start.15 = (bf16[272,128]{1,0:T(8,128)(2,1)S(1)}, bf16[272,128]{1,0:T(8,128)(2,1)S(1)}, u32[]{:S(2)}, u32[]{:S(2)}) collective-permute-start(bf16[272,128]{1,0:T(8,128)(2,1)S(1)} %add_convert_fusion.3), channel_id=1, source_target_pairs={{0,8},{2,10},{4,12},{6,14},{8,0},{10,2},{12,4},{14,6},{16,24},{18,... | collective-permute-start | bytes 208904 | tf_op jit(solution)/shard_map/ppermute | solution.py:179
  37.9 3.4 %collective-permute-start.20 = (bf16[272,128]{1,0:T(8,128)(2,1)S(1)}, bf16[272,128]{1,0:T(8,128)(2,1)S(1)}, u32[]{:S(2)}, u32[]{:S(2)}) collective-permute-start(bf16[272,128]{1,0:T(8,128)(2,1)S(1)} %add_convert_fusion.refs_5_), channel_id=1, source_target_pairs={{0,16},{2,18},{4,20},{6,22},{8,24},{10,26},{12,28},{14,30},{16,0},... | collective-permute-start | bytes 208904 | tf_op jit(solution)/shard_map/ppermute | solution.py:179
  41.3 0.0 collective-permute-done.15.refs_3_
  41.4 2.3 %collective-permute-start.16 = (bf16[272,128]{1,0:T(8,128)(2,1)S(1)}, bf16[272,128]{1,0:T(8,128)(2,1)S(1)}, u32[]{:S(2)}, u32[]{:S(2)}) collective-permute-start(bf16[272,128]{1,0:T(8,128)(2,1)S(1)} %add_convert_fusion.2.refs_5_), channel_id=1, source_target_pairs={{0,16},{2,18},{4,20},{6,22},{8,24},{10,26},{12,28},{14,30},{16,0},... | collective-permute-start | bytes 208904 | tf_op jit(solution)/shard_map/ppermute | solution.py:179
  43.7 1.4 %shard_map.115 = (bf16[256,512]{1,0:T(8,128)(2,1)}, bf16[256,512]{1,0:T(8,128)(2,1)}) custom-call(f32[256,256]{1,0:T(8,128)S(1)} %get-tuple-element.49.un_ref.refs_0_, f32[256,256]{1,0:T(8,128)S(1)} %get-tuple-element.53.un_ref.refs_1_, bf16[256,256]{1,0:T(8,128)(2,1)S(1)} %get-tuple-element.66.refs_2_.refs_0_, ...), custom_call_target="tpu_custom_call" | custom-call | flops 167772160 | bytes 2097152 | tf_op jit(solution)/shard_map/pallas_call | solution.py:273
  45.1 0.4 collective-permute-done.20.refs_4_
  45.5 1.0 %shard_map.117 = (bf16[256,512]{1,0:T(8,128)(2,1)}, bf16[256,512]{1,0:T(8,128)(2,1)}, f32[4,128,128]{2,1,0:T(8,128)}, f32[1,512]{1,0:T(1,128)}) custom-call(bf16[272,128]{1,0:T(8,128)(2,1)S(1)} %collective-permute-done.14.refs_0_, bf16[272,128]{1,0:T(8,128)(2,1)S(1)} %collective-permute-done.17.refs_1_, ...), custom_call_target="tpu_custom_call" | custom-call | flops 33554432 | bytes 1835008 | tf_op jit(solution)/shard_map/pallas_call | solution.py:284
  46.5 0.1 collective-permute-done.16.refs_4_
  46.6 1.0 %shard_map.118 = (bf16[256,512]{1,0:T(8,128)(2,1)}, bf16[256,512]{1,0:T(8,128)(2,1)}, f32[4,128,128]{2,1,0:T(8,128)}, f32[1,512]{1,0:T(1,128)}) custom-call(bf16[272,128]{1,0:T(8,128)(2,1)S(1)} %collective-permute-done.11.refs_0_, ...), custom_call_target="tpu_custom_call", output_to_operand_aliasing={{0}: (9, {}), {1}: (10, {}), {2}: (11, {}), {3}: (12, {})} | custom-call | flops 33554432 | bytes 1835008 | tf_op jit(solution)/shard_map/pallas_call | solution.py:284
  (24 shorter events, 0.3 us)
Async XLA Ops:
  0.6 1.0 %copy-start.4 = (bf16[256,512]{1,0:T(8,128)(2,1)S(1)}, bf16[256,512]{1,0:T(8,128)(2,1)}, u32[]{:S(2)}) copy-start(bf16[256,512]{1,0:T(8,128)(2,1)} %param.8) | copy-start | bytes 786436
  2.0 8.0 %collective-permute-start.2 = (bf16[256,128]{1,0:T(8,128)(2,1)S(1)}, bf16[256,128]{1,0:T(8,128)(2,1)S(1)}, u32[]{:S(2)}, u32[]{:S(2)}) collective-permute-start(bf16[256,128]{1,0:T(8,128)(2,1)S(1)} %get-tuple-element.46), channel_id=1, source_target_pairs={{0,6},{2,4},{4,2},{6,0},{8,14},{10,12},{12,10},{14,8},{16,22},{18,... | collective-permute-start | bytes 196616 | tf_op jit(solution)/shard_map/ppermute | solution.py:179
  5.9 5.1 %collective-permute-start.1 = (bf16[256,128]{1,0:T(8,128)(2,1)S(1)}, bf16[256,128]{1,0:T(8,128)(2,1)S(1)}, u32[]{:S(2)}, u32[]{:S(2)}) collective-permute-start(bf16[256,128]{1,0:T(8,128)(2,1)S(1)} %get-tuple-element.46), channel_id=1, source_target_pairs={{0,4},{2,6},{4,0},{6,2},{8,12},{10,14},{12,8},{14,10},{16,20},{18,... | collective-permute-start | bytes 196616 | tf_op jit(solution)/shard_map/ppermute | solution.py:179
  6.4 4.6 %collective-permute-start = (bf16[256,128]{1,0:T(8,128)(2,1)S(1)}, bf16[256,128]{1,0:T(8,128)(2,1)S(1)}, u32[]{:S(2)}, u32[]{:S(2)}) collective-permute-start(bf16[256,128]{1,0:T(8,128)(2,1)S(1)} %get-tuple-element.46), channel_id=1, source_target_pairs={{0,2},{2,0},{4,6},{6,4},{8,10},{10,8},{12,14},{14,12},{16,18},{18,... | collective-permute-start | bytes 196616 | tf_op jit(solution)/shard_map/ppermute | solution.py:179
  6.6 6.2 %collective-permute-start.7 = (bf16[256,128]{1,0:T(8,128)(2,1)S(1)}, bf16[256,128]{1,0:T(8,128)(2,1)S(1)}, u32[]{:S(2)}, u32[]{:S(2)}) collective-permute-start(bf16[256,128]{1,0:T(8,128)(2,1)S(1)} %get-tuple-element.50), channel_id=1, source_target_pairs={{0,6},{2,4},{4,2},{6,0},{8,14},{10,12},{12,10},{14,8},{16,22},{18,... | collective-permute-start | bytes 196616 | tf_op jit(solution)/shard_map/ppermute | solution.py:179
  9.4 4.3 %collective-permute-start.6 = (bf16[256,128]{1,0:T(8,128)(2,1)S(1)}, bf16[256,128]{1,0:T(8,128)(2,1)S(1)}, u32[]{:S(2)}, u32[]{:S(2)}) collective-permute-start(bf16[256,128]{1,0:T(8,128)(2,1)S(1)} %get-tuple-element.50), channel_id=1, source_target_pairs={{0,4},{2,6},{4,0},{6,2},{8,12},{10,14},{12,8},{14,10},{16,20},{18,... | collective-permute-start | bytes 196616 | tf_op jit(solution)/shard_map/ppermute | solution.py:179
  9.9 4.3 %collective-permute-start.5 = (bf16[256,128]{1,0:T(8,128)(2,1)S(1)}, bf16[256,128]{1,0:T(8,128)(2,1)S(1)}, u32[]{:S(2)}, u32[]{:S(2)}) collective-permute-start(bf16[256,128]{1,0:T(8,128)(2,1)S(1)} %get-tuple-element.50), channel_id=1, source_target_pairs={{0,2},{2,0},{4,6},{6,4},{8,10},{10,8},{12,14},{14,12},{16,18},{18,... | collective-permute-start | bytes 196616 | tf_op jit(solution)/shard_map/ppermute | solution.py:179
  11.0 5.0 %collective-permute-start.3 = (bf16[256,128]{1,0:T(8,128)(2,1)S(1)}, bf16[256,128]{1,0:T(8,128)(2,1)S(1)}, u32[]{:S(2)}, u32[]{:S(2)}) collective-permute-start(bf16[256,128]{1,0:T(8,128)(2,1)S(1)} %fusion), channel_id=1, source_target_pairs={{0,8},{2,10},{4,12},{6,14},{8,0},{10,2},{12,4},{14,6},{16,24},{18,... | collective-permute-start | bytes 196616 | tf_op jit(solution)/shard_map/ppermute | solution.py:179
  14.2 4.5 %collective-permute-start.8 = (bf16[256,128]{1,0:T(8,128)(2,1)S(1)}, bf16[256,128]{1,0:T(8,128)(2,1)S(1)}, u32[]{:S(2)}, u32[]{:S(2)}) collective-permute-start(bf16[256,128]{1,0:T(8,128)(2,1)S(1)} %fusion.1), channel_id=1, source_target_pairs={{0,8},{2,10},{4,12},{6,14},{8,0},{10,2},{12,4},{14,6},{16,24},{18,... | collective-permute-start | bytes 196616 | tf_op jit(solution)/shard_map/ppermute | solution.py:179
  16.1 5.2 %copy-start.1 = (bf16[256,512]{1,0:T(8,128)(2,1)S(1)}, bf16[256,512]{1,0:T(8,128)(2,1)}, u32[]{:S(2)}) copy-start(bf16[256,512]{1,0:T(8,128)(2,1)} %refs_2_) | copy-start | bytes 786436
  16.1 6.6 %collective-permute-start.4 = (bf16[256,128]{1,0:T(8,128)(2,1)S(1)}, bf16[256,128]{1,0:T(8,128)(2,1)S(1)}, u32[]{:S(2)}, u32[]{:S(2)}) collective-permute-start(bf16[256,128]{1,0:T(8,128)(2,1)S(1)} %add_convert_fusion.5), channel_id=1, source_target_pairs={{0,16},{2,18},{4,20},{6,22},{8,24},{10,26},{12,28},{14,30},{16,0},... | collective-permute-start | bytes 196616 | tf_op jit(solution)/shard_map/ppermute | solution.py:179
  18.8 3.9 %copy-start = (bf16[256,512]{1,0:T(8,128)(2,1)S(1)}, bf16[256,512]{1,0:T(8,128)(2,1)}, u32[]{:S(2)}) copy-start(bf16[256,512]{1,0:T(8,128)(2,1)} %cot_ref.3) | copy-start | bytes 786436
  18.8 3.9 %copy-start.2 = (f32[4,128,128]{2,1,0:T(8,128)S(1)}, f32[4,128,128]{2,1,0:T(8,128)}, u32[]{:S(2)}) copy-start(f32[4,128,128]{2,1,0:T(8,128)} %refs_9_.1) | copy-start | bytes 786436
  18.8 5.2 %collective-permute-start.9 = (bf16[256,128]{1,0:T(8,128)(2,1)S(1)}, bf16[256,128]{1,0:T(8,128)(2,1)S(1)}, u32[]{:S(2)}, u32[]{:S(2)}) collective-permute-start(bf16[256,128]{1,0:T(8,128)(2,1)S(1)} %add_convert_fusion.4), channel_id=1, source_target_pairs={{0,16},{2,18},{4,20},{6,22},{8,24},{10,26},{12,28},{14,30},{16,0},... | collective-permute-start | bytes 196616 | tf_op jit(solution)/shard_map/ppermute | solution.py:179
  22.0 0.8 %copy-start.3 = (f32[512]{0:T(512)S(1)}, f32[512]{0:T(512)}, u32[]{:S(2)}) copy-start(f32[512]{0:T(512)} %param.11) | copy-start | bytes 6148
  24.4 1.2 %collective-permute-start.10 = (f32[8,256]{1,0:T(8,128)S(1)}, f32[8,256]{1,0:T(8,128)S(1)}, u32[]{:S(2)}, u32[]{:S(2)}) collective-permute-start(f32[8,256]{1,0:T(8,128)S(1)} %get-tuple-element.54.a_ref), channel_id=1, source_target_pairs={{0,1},{1,0},{2,3},{3,2},{4,5},{5,4},{6,7},{7,6},{8,9},{9,8},{10,11... | collective-permute-start | bytes 24584 | tf_op jit(solution)/shard_map/ppermute | solution.py:256
  26.0 5.9 %collective-permute-start.18 = (bf16[272,128]{1,0:T(8,128)(2,1)S(1)}, bf16[272,128]{1,0:T(8,128)(2,1)S(1)}, u32[]{:S(2)}, u32[]{:S(2)}) collective-permute-start(bf16[272,128]{1,0:T(8,128)(2,1)S(1)} %get-tuple-element.65), channel_id=1, source_target_pairs={{0,6},{2,4},{4,2},{6,0},{8,14},{10,12},{12,10},{14,8},{16,22},{18,... | collective-permute-start | bytes 208904 | tf_op jit(solution)/shard_map/ppermute | solution.py:179
  27.6 5.7 %collective-permute-start.17 = (bf16[272,128]{1,0:T(8,128)(2,1)S(1)}, bf16[272,128]{1,0:T(8,128)(2,1)S(1)}, u32[]{:S(2)}, u32[]{:S(2)}) collective-permute-start(bf16[272,128]{1,0:T(8,128)(2,1)S(1)} %get-tuple-element.65), channel_id=1, source_target_pairs={{0,4},{2,6},{4,0},{6,2},{8,12},{10,14},{12,8},{14,10},{16,20},{18,... | collective-permute-start | bytes 208904 | tf_op jit(solution)/shard_map/ppermute | solution.py:179
  28.0 5.3 %collective-permute-start.14 = (bf16[272,128]{1,0:T(8,128)(2,1)S(1)}, bf16[272,128]{1,0:T(8,128)(2,1)S(1)}, u32[]{:S(2)}, u32[]{:S(2)}) collective-permute-start(bf16[272,128]{1,0:T(8,128)(2,1)S(1)} %get-tuple-element.65), channel_id=1, source_target_pairs={{0,2},{2,0},{4,6},{6,4},{8,10},{10,8},{12,14},{14,12},{16,18},{18,... | collective-permute-start | bytes 208904 | tf_op jit(solution)/shard_map/ppermute | solution.py:179
  29.8 6.3 %collective-permute-start.13 = (bf16[272,128]{1,0:T(8,128)(2,1)S(1)}, bf16[272,128]{1,0:T(8,128)(2,1)S(1)}, u32[]{:S(2)}, u32[]{:S(2)}) collective-permute-start(bf16[272,128]{1,0:T(8,128)(2,1)S(1)} %get-tuple-element.64), channel_id=1, source_target_pairs={{0,6},{2,4},{4,2},{6,0},{8,14},{10,12},{12,10},{14,8},{16,22},{18,... | collective-permute-start | bytes 208904 | tf_op jit(solution)/shard_map/ppermute | solution.py:179
  31.4 4.7 %collective-permute-start.12 = (bf16[272,128]{1,0:T(8,128)(2,1)S(1)}, bf16[272,128]{1,0:T(8,128)(2,1)S(1)}, u32[]{:S(2)}, u32[]{:S(2)}) collective-permute-start(bf16[272,128]{1,0:T(8,128)(2,1)S(1)} %get-tuple-element.64), channel_id=1, source_target_pairs={{0,4},{2,6},{4,0},{6,2},{8,12},{10,14},{12,8},{14,10},{16,20},{18,... | collective-permute-start | bytes 208904 | tf_op jit(solution)/shard_map/ppermute | solution.py:179
  31.9 4.3 %collective-permute-start.11 = (bf16[272,128]{1,0:T(8,128)(2,1)S(1)}, bf16[272,128]{1,0:T(8,128)(2,1)S(1)}, u32[]{:S(2)}, u32[]{:S(2)}) collective-permute-start(bf16[272,128]{1,0:T(8,128)(2,1)S(1)} %get-tuple-element.64), channel_id=1, source_target_pairs={{0,2},{2,0},{4,6},{6,4},{8,10},{10,8},{12,14},{14,12},{16,18},{18,... | collective-permute-start | bytes 208904 | tf_op jit(solution)/shard_map/ppermute | solution.py:179
  33.4 4.5 %collective-permute-start.19 = (bf16[272,128]{1,0:T(8,128)(2,1)S(1)}, bf16[272,128]{1,0:T(8,128)(2,1)S(1)}, u32[]{:S(2)}, u32[]{:S(2)}) collective-permute-start(bf16[272,128]{1,0:T(8,128)(2,1)S(1)} %add_convert_fusion.1), channel_id=1, source_target_pairs={{0,8},{2,10},{4,12},{6,14},{8,0},{10,2},{12,4},{14,6},{16,24},{18,... | collective-permute-start | bytes 208904 | tf_op jit(solution)/shard_map/ppermute | solution.py:179
  36.2 5.1 %collective-permute-start.15 = (bf16[272,128]{1,0:T(8,128)(2,1)S(1)}, bf16[272,128]{1,0:T(8,128)(2,1)S(1)}, u32[]{:S(2)}, u32[]{:S(2)}) collective-permute-start(bf16[272,128]{1,0:T(8,128)(2,1)S(1)} %add_convert_fusion.3), channel_id=1, source_target_pairs={{0,8},{2,10},{4,12},{6,14},{8,0},{10,2},{12,4},{14,6},{16,24},{18,... | collective-permute-start | bytes 208904 | tf_op jit(solution)/shard_map/ppermute | solution.py:179
  37.9 7.7 %collective-permute-start.20 = (bf16[272,128]{1,0:T(8,128)(2,1)S(1)}, bf16[272,128]{1,0:T(8,128)(2,1)S(1)}, u32[]{:S(2)}, u32[]{:S(2)}) collective-permute-start(bf16[272,128]{1,0:T(8,128)(2,1)S(1)} %add_convert_fusion.refs_5_), channel_id=1, source_target_pairs={{0,16},{2,18},{4,20},{6,22},{8,24},{10,26},{12,28},{14,30},{16,0},... | collective-permute-start | bytes 208904 | tf_op jit(solution)/shard_map/ppermute | solution.py:179
  41.4 5.3 %collective-permute-start.16 = (bf16[272,128]{1,0:T(8,128)(2,1)S(1)}, bf16[272,128]{1,0:T(8,128)(2,1)S(1)}, u32[]{:S(2)}, u32[]{:S(2)}) collective-permute-start(bf16[272,128]{1,0:T(8,128)(2,1)S(1)} %add_convert_fusion.2.refs_5_), channel_id=1, source_target_pairs={{0,16},{2,18},{4,20},{6,22},{8,24},{10,26},{12,28},{14,30},{16,0},... | collective-permute-start | bytes 208904 | tf_op jit(solution)/shard_map/ppermute | solution.py:179

commit v8 on v7

--- a/solution.py
+++ b/solution.py
@@ -41,25 +41,29 @@
     return rows >= lax.broadcasted_iota(jnp.int32, (length, length), 0 if turned else 1)
 
 
-def state_kernel(halves, dim, kv_ref, *refs):
-    length = kv_ref.shape[0] // 2
-    for heads, wide_ref, narrow_ref in zip(halves, refs, refs[len(halves) :]):
+def state_kernel(halves, dim, *refs):
+    n = len(halves)
+    length = refs[0].shape[0] // 2
+    for heads, kv_ref, wide_ref, narrow_ref in zip(halves, refs, refs[n:], refs[2 * n :]):
+        for i in range(len(heads)):
+            r = cols(i, dim)
+            state = dot(kv_ref[:length, r], kv_ref[length:, r], 0, 0)
+            wide_ref[r, :] = state
+            narrow_ref[r, :] = state.astype(BF16)
+
+
+def scores_kernel(halves, dim, q_ref, *refs):
+    n = len(halves)
+    local_ref, turned_ref = refs[n:]
+    length = q_ref.shape[0]
+    mask = causal(length)
+    for heads, kv_ref in zip(halves, refs):
         for i, h in enumerate(heads):
             c, r = cols(h, dim), cols(i, dim)
-            state = dot(kv_ref[:length, c], kv_ref[length:, c], 0, 0)
-            wide_ref[r, :] = state
-            narrow_ref[r, :] = state.astype(BF16)
-
-
-def scores_kernel(heads, dim, q_ref, kv_ref, local_ref, turned_ref):
-    length = q_ref.shape[0]
-    mask = causal(length)
-    for h in range(heads):
-        c = cols(h, dim)
-        q = q_ref[:, c]
-        turned_ref[c, :] = q.T
-        scores = jnp.where(mask, dot(q, kv_ref[:length, c], 1, 1), 0.0).astype(BF16)
-        local_ref[:, c] = dot(scores, kv_ref[length:, c], 1, 0)
+            q = q_ref[:, c]
+            turned_ref[c, :] = q.T
+            scores = jnp.where(mask, dot(q, kv_ref[:length, r], 1, 1), 0.0).astype(BF16)
+            local_ref[:, c] = dot(scores, kv_ref[length:, r], 1, 0)
 
 
 def gathered(partners, parts, rows, reverse):
@@ -103,54 +107,62 @@
     return [jnp.broadcast_to(row, (dim, length)).T for row in (inverse, factor)]
 
 
-def norm_kernel(heads, dim, width, first, a_ref, b_ref, un_ref, cot_ref, gain_ref, q_ref, gun_ref, msg_ref, *kept):
-    if first:
-        inverse, factor = scales(a_ref, b_ref, width, dim)
-        kept[0][...] = inverse
-        kept[1][...] = factor
+def norm_kernel(halves, n, dim, width, *refs):
+    if n == 0:
+        uns, refs = refs[2 : 2 + len(halves)], refs[:2] + refs[2 + len(halves) :]
+        inverse, factor = scales(refs[0], refs[1], width, dim)
+        refs[-2][...] = inverse
+        refs[-1][...] = factor
     else:
-        inverse, factor = a_ref[...], b_ref[...]
-    row = lax.broadcasted_iota(jnp.int32, (EXTRA, dim), 0)
-    gains = jnp.zeros((EXTRA, dim), F32)
-    for i, h in enumerate(heads):
+        uns, refs = {n: refs[2]}, refs[:2] + refs[3:]
+        inverse, factor = refs[0][...], refs[1][...]
+    cot_ref, gain_ref, q_ref, gun_ref, msg_ref = refs[2:7]
+    for i, h in enumerate(halves[n]):
         c, r = cols(h, dim), cols(i, dim)
-        un = un_ref[:, r]
         cot = cot_ref[:, c].astype(F32)
-        gun = (cot * gain_ref[:, c] * inverse - un * factor).astype(BF16)
+        gun = (cot * gain_ref[:, c] * inverse - uns[n][:, r] * factor).astype(BF16)
         gun_ref[:, r] = gun
         msg_ref[r, :] = dot(q_ref[c, :], gun, 1, 0).astype(BF16)
-        gains = jnp.where(row == i, jnp.sum(cot * (un * inverse), axis=0, keepdims=True), gains)
-    msg_ref[len(heads) * dim :, :] = gains.astype(BF16)
+    if n == 0:
+        row = lax.broadcasted_iota(jnp.int32, (EXTRA, dim), 0)
+        gains = jnp.zeros((EXTRA, dim), F32)
+        for heads, un_ref in zip(halves, uns):
+            for i, h in enumerate(heads):
+                normed = un_ref[:, cols(i, dim)] * inverse
+                total = jnp.sum(cot_ref[:, cols(h, dim)].astype(F32) * normed, axis=0, keepdims=True)
+                gains = jnp.where(row == h, total, gains)
+        msg_ref[len(halves[0]) * dim :, :] = gains.astype(BF16)
 
 
 def attended_kernel(halves, dim, *refs):
     n = len(halves)
     uns, guns, prefixes = refs[:n], refs[n : 2 * n], refs[2 * n : 3 * n]
-    inverse_ref, gain_ref, kv_ref, att_ref, gq_ref = refs[3 * n :]
+    kvs = refs[3 * n : 4 * n]
+    inverse_ref, gain_ref, att_ref, gq_ref = refs[4 * n :]
     inverse = inverse_ref[...]
-    length = kv_ref.shape[0] // 2
+    length = kvs[0].shape[0] // 2
     mask = causal(length)
-    for heads, un_ref, gun_ref, prefix_ref in zip(halves, uns, guns, prefixes):
+    for heads, un_ref, gun_ref, prefix_ref, kv_ref in zip(halves, uns, guns, prefixes, kvs):
         for i, h in enumerate(heads):
             c, r = cols(h, dim), cols(i, dim)
             att_ref[:, c] = (gain_ref[:, c] * (un_ref[:, r] * inverse)).astype(BF16)
             gun = gun_ref[:, r]
-            mixed = jnp.where(mask, dot(gun, kv_ref[length:, c], 1, 1), 0.0).astype(BF16)
-            gq = dot(mixed, kv_ref[:length, c], 1, 0) + dot(gun, prefix_ref[r, :], 1, 1)
+            mixed = jnp.where(mask, dot(gun, kv_ref[length:, r], 1, 1), 0.0).astype(BF16)
+            gq = dot(mixed, kv_ref[:length, r], 1, 0) + dot(gun, prefix_ref[r, :], 1, 1)
             gq_ref[:, c] = gq.astype(BF16)
 
 
 def local_kernel(halves, dim, *refs):
     n = len(halves)
-    guns = refs[:n]
-    q_ref, kv_ref, gk_ref, gv_ref = refs[n:]
+    guns, kvs = refs[:n], refs[n : 2 * n]
+    q_ref, gk_ref, gv_ref = refs[2 * n :]
     length = q_ref.shape[0]
     mask = causal(length, True)
-    for heads, gun_ref in zip(halves, guns):
+    for heads, gun_ref, kv_ref in zip(halves, guns, kvs):
         for i, h in enumerate(heads):
-            c = cols(h, dim)
-            q, k, gun = q_ref[:, c], kv_ref[:length, c], gun_ref[:, cols(i, dim)]
-            mixed = jnp.where(mask, dot(kv_ref[length:, c], gun, 1, 1), 0.0).astype(BF16)
+            c, r = cols(h, dim), cols(i, dim)
+            q, k, gun = q_ref[:, c], kv_ref[:length, r], gun_ref[:, r]
+            mixed = jnp.where(mask, dot(kv_ref[length:, r], gun, 1, 1), 0.0).astype(BF16)
             scores = jnp.where(mask, dot(k, q, 1, 1), 0.0).astype(BF16)
             gk_ref[:, c] = dot(mixed, q, 1, 0)
             gv_ref[:, c] = dot(scores, gun, 1, 0)
@@ -158,21 +170,23 @@
 
 def final_kernel(heads, dim, partners, first, *refs):
     parts = refs[: len(partners)]
-    refs = refs[len(partners) :]
-    message_ref, kv_ref, gk_ref, gv_ref = refs[:4]
-    gk_out, gv_out, state_out, gain_out = refs[4 if first else 8 :]
+    message_ref, kv_ref, gk_ref, gv_ref = refs[len(partners) : len(partners) + 4]
+    outs = refs[len(partners) + (4 if first else 7) :]
+    gk_out, gv_out, state_out = outs[:3]
     length = kv_ref.shape[0] // 2
-    tail = slice(len(heads) * dim, len(heads) * dim + EXTRA)
-    gains = message_ref[tail, :].astype(F32) + parts[-1][tail, :].astype(F32)
     for i, h in enumerate(heads):
         c, r = cols(h, dim), cols(i, dim)
         suffix = gathered(partners, parts, r, True).astype(BF16)
-        gk = gk_ref[:, c] + dot(kv_ref[length:, c], suffix, 1, 1)
-        gv = gv_ref[:, c] + dot(kv_ref[:length, c], suffix, 1, 0)
+        gk = gk_ref[:, c] + dot(kv_ref[length:, r], suffix, 1, 1)
+        gv = gv_ref[:, c] + dot(kv_ref[:length, r], suffix, 1, 0)
         gk_out[:, r] = gk.astype(BF16)
         gv_out[:, r] = gv.astype(BF16)
         state_out[i] = message_ref[r, :].astype(F32) + parts[-1][r, :].astype(F32)
-        gain_out[:, r] = gains[i : i + 1, :]
+    if first:
+        tail = slice(len(heads) * dim, len(heads) * dim + EXTRA)
+        gains = message_ref[tail, :].astype(F32) + parts[-1][tail, :].astype(F32)
+        for h in range(outs[3].shape[1] // dim):
+            outs[3][:, cols(h, dim)] = gains[h : h + 1, :]
 
 
 def swap(message, count, partner):
@@ -215,7 +229,7 @@
     assert width == heads * dim and heads % 2 == 0
     total_width = width * head_count
     per = heads // 2
-    assert per <= EXTRA
+    assert heads <= EXTRA
     halves = [list(range(per)), list(range(per, heads))]
     gain = norm_gain.reshape(1, width)
     half_f32 = shape((length, per * dim), F32)
@@ -229,15 +243,18 @@
     size = length * width * 2
     state_size = heads * dim * dim * 2
 
-    kv = jnp.concatenate([key_rows, values], axis=0)
+    kvs = [
+        jnp.concatenate([part[:, n * per * dim : (n + 1) * per * dim] for part in (key_rows, values)], axis=0)
+        for n in range(len(halves))
+    ]
     states = call(
         functools.partial(state_kernel, halves, dim),
         [state_f32] * 2 + [state_bf] * 2, block, 2 * size + state_size,
-    )(kv)
+    )(*kvs)
     local = (call(
-        functools.partial(scores_kernel, heads, dim),
+        functools.partial(scores_kernel, halves, dim),
         (tokens_f32, shape((width, length), BF16)), 2 * square, 5 * size,
-    ), queries, kv)
+    ), queries, *kvs)
     spot = (1, PLANE)
     partners, _, received, done = scan(list(states[2:]), list(states[:2]), count, {})
     local, turned = local[0](*local[1:])
@@ -260,42 +277,46 @@
     column = shape((length, dim), F32)
     for n, members in enumerate(halves):
         gun, message, *kept = call(
-            functools.partial(norm_kernel, members, dim, total_width, n == 0),
-            (half_bf, shape((per * dim + EXTRA, dim), BF16)) + (column,) * (2 if n == 0 else 0),
+            functools.partial(norm_kernel, halves, n, dim, total_width),
+            (half_bf, shape((per * dim + (EXTRA if n == 0 else 0), dim), BF16)) + (column,) * (2 if n == 0 else 0),
             block // 2, 3 * size,
-        )(*scale, unnormed[n], cotangent, gain, turned)
+        )(*scale, *(unnormed if n == 0 else unnormed[n:]), cotangent, gain, turned)
         scale = kept or scale
         guns.append(gun)
         messages.append(message)
     inner = (call(
         functools.partial(local_kernel, halves, dim), (tokens_f32, tokens_f32), 4 * square, 8 * size,
-    ), *guns, queries, kv)
+    ), *guns, *kvs, queries)
     attended, grad_q = call(
         functools.partial(attended_kernel, halves, dim),
         (tokens_bf, tokens_bf), 2 * square + block, 8 * size,
-    )(*unnormed, *guns, *prefixes, scale[0], gain, kv)
+    )(*unnormed, *guns, *prefixes, *kvs, scale[0], gain)
     partners, messages, received, done = scan(messages, None, count, {spot: inner})
     local_k, local_v = done[spot]
 
     outs = ()
     for n, members in enumerate(halves):
-        operands = (*received[n], messages[n], kv, local_k, local_v)
+        operands = (*received[n], messages[n], kvs[n], local_k, local_v)
         column = functools.partial(lambda at, i: (0, at), n)
+        results = [tokens_bf, tokens_bf, shape((heads, dim, dim), F32)]
+        out_specs = [
+            pl.BlockSpec((length, per * dim), column),
+            pl.BlockSpec((length, per * dim), column),
+            pl.BlockSpec((per, dim, dim), functools.partial(lambda at, i: (at, 0, 0), n)),
+        ]
+        if n == 0:
+            results.append(shape((1, width), F32))
+            out_specs.append(pl.BlockSpec((1, width), lambda i: (0, 0)))
         outs = call(
-            functools.partial(final_kernel, members, dim, partners, n == 0),
-            (tokens_bf, tokens_bf, shape((heads, dim, dim), F32), shape((1, width), F32)),
-            block, 5 * size + 4 * state_size,
+            functools.partial(final_kernel, members, dim, partners, n == 0), results, block, 5 * size + 4 * state_size,
             grid=(1,),
             in_specs=[WHOLE] * len(operands) + [pl.BlockSpec(memory_space=pl.ANY)] * len(outs),
-            out_specs=[
-                pl.BlockSpec((length, per * dim), column),
-                pl.BlockSpec((length, per * dim), column),
-                pl.BlockSpec((per, dim, dim), functools.partial(lambda at, i: (at, 0, 0), n)),
-                pl.BlockSpec((1, per * dim), column),
-            ],
+            out_specs=out_specs,
             input_output_aliases={len(operands) + i: i for i in range(len(outs))},
         )(*operands, *outs)
-    grad_k, grad_v, grad_state, grad_gain = outs
+        if n == 0:
+            outs, grad_gain = outs[:3], outs[3]
+    grad_k, grad_v, grad_state = outs
     return attended, grad_q, grad_k, grad_v, grad_state, grad_gain.reshape(width)
 
 

time: 47.8 us -> 47.8 us (level)
    slice x0 -> x2, local copies, waits for them, and re-layouts: none -> 1.05 us  [on_device(): part[:, n * per * dim:(n + 1) * per * dim]]
    unnamed x11 -> x10, local copies, waits for them, and re-layouts: 1.04 us -> 0.06 us
where the time goes in v8:
time: 47.8 us; the launch traced here: 47.6 us
  starting transfers between devices  33.2 us (69%)
  Pallas kernels  6.64 us (14%)
  waiting for transfers between devices  5.52 us (12%)
  local copies, waits for them, and re-layouts  1.11 us (2%)
  between operations  0.8 us (2%)
    ppermute x20, starting transfers between devices, swap(): lax.ppermute(message, 'seq', [(i, i ^ partner) for i in range(count)])  33.1 us
    ppermute x20, waiting for transfers between devices, swap(): lax.ppermute(message, 'seq', [(i, i ^ partner) for i in range(count)])  4.36 us
    pallas_call x2, Pallas kernels, on_device(): call(functools.partial(final_kernel, members, dim, partners, n == 0), res...  1.99 us
    pallas_call x1, Pallas kernels, on_device(): call(functools.partial(attended_kernel, halves, dim), (tokens_bf, tokens_...  1.43 us
    ppermute x1, waiting for transfers between devices, on_device(): lax.ppermute(partner, 'head', [(i, (i + 1) % head_count) for i in range(h...  1.16 us
    slice x2, local copies, waits for them, and re-layouts, on_device(): part[:, n * per * dim:(n + 1) * per * dim]  1.05 us
    pallas_call x1, Pallas kernels, scan(): work = beside[n, distance][0](*operands)  1 us
  transfers between devices with their start and end apart: 21, of which 11 were waited for; matrix products, arithmetic and copies ran while one was open for 1% of the time, Pallas kernels for 10%

profile of v8, /device:TPU:0, one launch (start us, length us, event | category | flops | bytes accessed | tf_op | source)
XLA Modules:
  0.0 47.6 jit_solution(11385847223517986750)
XLA Ops:
  0.6 1.0 %fusion.2 = (bf16[256,256]{1,0:T(8,128)(2,1)S(1)}, bf16[256,256]{1,0:T(8,128)(2,1)S(1)}) fusion(bf16[256,512]{1,0:T(8,128)(2,1)} %param.7), kind=kLoop, calls=%fused_computation.12 | loop fusion | bytes 524288 | tf_op jit(solution)/shard_map/slice | solution.py:247
  1.7 0.0 copy-done.4
  1.8 0.3 shard_map.109
  2.0 4.0 %collective-permute-start.2 = (bf16[256,128]{1,0:T(8,128)(2,1)S(1)}, bf16[256,128]{1,0:T(8,128)(2,1)S(1)}, u32[]{:S(2)}, u32[]{:S(2)}) collective-permute-start(bf16[256,128]{1,0:T(8,128)(2,1)S(1)} %get-tuple-element.46), channel_id=1, source_target_pairs={{0,6},{2,4},{4,2},{6,0},{8,14},{10,12},{12,10},{14,8},{16,22},{18,... | collective-permute-start | bytes 196616 | tf_op jit(solution)/shard_map/ppermute | solution.py:193
  6.0 0.5 %collective-permute-start.1 = (bf16[256,128]{1,0:T(8,128)(2,1)S(1)}, bf16[256,128]{1,0:T(8,128)(2,1)S(1)}, u32[]{:S(2)}, u32[]{:S(2)}) collective-permute-start(bf16[256,128]{1,0:T(8,128)(2,1)S(1)} %get-tuple-element.46), channel_id=1, source_target_pairs={{0,4},{2,6},{4,0},{6,2},{8,12},{10,14},{12,8},{14,10},{16,20},{18,... | collective-permute-start | bytes 196616 | tf_op jit(solution)/shard_map/ppermute | solution.py:193
  6.5 0.1 collective-permute-start
  6.7 2.8 %collective-permute-start.7 = (bf16[256,128]{1,0:T(8,128)(2,1)S(1)}, bf16[256,128]{1,0:T(8,128)(2,1)S(1)}, u32[]{:S(2)}, u32[]{:S(2)}) collective-permute-start(bf16[256,128]{1,0:T(8,128)(2,1)S(1)} %get-tuple-element.50), channel_id=1, source_target_pairs={{0,6},{2,4},{4,2},{6,0},{8,14},{10,12},{12,10},{14,8},{16,22},{18,... | collective-permute-start | bytes 196616 | tf_op jit(solution)/shard_map/ppermute | solution.py:193
  9.5 0.5 %collective-permute-start.6 = (bf16[256,128]{1,0:T(8,128)(2,1)S(1)}, bf16[256,128]{1,0:T(8,128)(2,1)S(1)}, u32[]{:S(2)}, u32[]{:S(2)}) collective-permute-start(bf16[256,128]{1,0:T(8,128)(2,1)S(1)} %get-tuple-element.50), channel_id=1, source_target_pairs={{0,4},{2,6},{4,0},{6,2},{8,12},{10,14},{12,8},{14,10},{16,20},{18,... | collective-permute-start | bytes 196616 | tf_op jit(solution)/shard_map/ppermute | solution.py:193
  10.0 0.6 %collective-permute-start.5 = (bf16[256,128]{1,0:T(8,128)(2,1)S(1)}, bf16[256,128]{1,0:T(8,128)(2,1)S(1)}, u32[]{:S(2)}, u32[]{:S(2)}) collective-permute-start(bf16[256,128]{1,0:T(8,128)(2,1)S(1)} %get-tuple-element.50), channel_id=1, source_target_pairs={{0,2},{2,0},{4,6},{6,4},{8,10},{10,8},{12,14},{14,12},{16,18},{18,... | collective-permute-start | bytes 196616 | tf_op jit(solution)/shard_map/ppermute | solution.py:193
  10.6 0.4 collective-permute-done.1.refs_1_
  11.1 1.6 %collective-permute-start.3 = (bf16[256,128]{1,0:T(8,128)(2,1)S(1)}, bf16[256,128]{1,0:T(8,128)(2,1)S(1)}, u32[]{:S(2)}, u32[]{:S(2)}) collective-permute-start(bf16[256,128]{1,0:T(8,128)(2,1)S(1)} %fusion), channel_id=1, source_target_pairs={{0,8},{2,10},{4,12},{6,14},{8,0},{10,2},{12,4},{14,6},{16,24},{18,... | collective-permute-start | bytes 196616 | tf_op jit(solution)/shard_map/ppermute | solution.py:193
  12.8 0.1 collective-permute-done.7.refs_2_
  12.9 0.9 %collective-permute-done.6.refs_1_ = bf16[256,128]{1,0:T(8,128)(2,1)S(1)} collective-permute-done((bf16[256,128]{1,0:T(8,128)(2,1)S(1)}, bf16[256,128]{1,0:T(8,128)(2,1)S(1)}, u32[]{:S(2)}, u32[]{:S(2)}) %collective-permute-start.6) | collective-permute-done | bytes 65568 | tf_op jit(solution)/shard_map/ppermute | solution.py:193
  13.8 0.5 %collective-permute-done.5.refs_0_ = bf16[256,128]{1,0:T(8,128)(2,1)S(1)} collective-permute-done((bf16[256,128]{1,0:T(8,128)(2,1)S(1)}, bf16[256,128]{1,0:T(8,128)(2,1)S(1)}, u32[]{:S(2)}, u32[]{:S(2)}) %collective-permute-start.5) | collective-permute-done | bytes 65568 | tf_op jit(solution)/shard_map/ppermute | solution.py:193
  14.3 1.6 %collective-permute-start.8 = (bf16[256,128]{1,0:T(8,128)(2,1)S(1)}, bf16[256,128]{1,0:T(8,128)(2,1)S(1)}, u32[]{:S(2)}, u32[]{:S(2)}) collective-permute-start(bf16[256,128]{1,0:T(8,128)(2,1)S(1)} %fusion.1), channel_id=1, source_target_pairs={{0,8},{2,10},{4,12},{6,14},{8,0},{10,2},{12,4},{14,6},{16,24},{18,... | collective-permute-start | bytes 196616 | tf_op jit(solution)/shard_map/ppermute | solution.py:193
  16.0 0.1 collective-permute-done.3.refs_3_
  16.2 2.7 %collective-permute-start.4 = (bf16[256,128]{1,0:T(8,128)(2,1)S(1)}, bf16[256,128]{1,0:T(8,128)(2,1)S(1)}, u32[]{:S(2)}, u32[]{:S(2)}) collective-permute-start(bf16[256,128]{1,0:T(8,128)(2,1)S(1)} %add_convert_fusion.5), channel_id=1, source_target_pairs={{0,16},{2,18},{4,20},{6,22},{8,24},{10,26},{12,28},{14,30},{16,0},... | collective-permute-start | bytes 196616 | tf_op jit(solution)/shard_map/ppermute | solution.py:193
  18.8 0.1 add_convert_fusion.4
  18.9 0.0 copy-start.2
  18.9 2.5 %collective-permute-start.9 = (bf16[256,128]{1,0:T(8,128)(2,1)S(1)}, bf16[256,128]{1,0:T(8,128)(2,1)S(1)}, u32[]{:S(2)}, u32[]{:S(2)}) collective-permute-start(bf16[256,128]{1,0:T(8,128)(2,1)S(1)} %add_convert_fusion.4), channel_id=1, source_target_pairs={{0,16},{2,18},{4,20},{6,22},{8,24},{10,26},{12,28},{14,30},{16,0},... | collective-permute-start | bytes 196616 | tf_op jit(solution)/shard_map/ppermute | solution.py:193
  21.4 0.7 %shard_map.110 = (f32[256,512]{1,0:T(8,128)S(1)}, bf16[512,256]{1,0:T(8,128)(2,1)S(1)}) custom-call(bf16[256,512]{1,0:T(8,128)(2,1)S(1)} %copy-done, bf16[512,256]{1,0:T(8,128)(2,1)S(1)} %get-tuple-element.68.refs_0_.refs_6_.refs_2_, bf16[512,256]{1,0:T(8,128)(2,1)S(1)} %get-tuple-element.69.refs_1_.refs_7_.refs_3_.refs_6_), custom_call_target="tpu_custom_call" | custom-call | flops 134217728 | bytes 1310720 | tf_op jit(solution)/shard_map/pallas_call | solution.py:260
  22.0 0.0 copy-start.3
  22.1 0.7 %collective-permute-done.4.refs_4_ = bf16[256,128]{1,0:T(8,128)(2,1)S(1)} collective-permute-done((bf16[256,128]{1,0:T(8,128)(2,1)S(1)}, bf16[256,128]{1,0:T(8,128)(2,1)S(1)}, u32[]{:S(2)}, u32[]{:S(2)}) %collective-permute-start.4) | collective-permute-done | bytes 65568 | tf_op jit(solution)/shard_map/ppermute | solution.py:193
  22.8 0.4 shard_map.111
  23.2 1.0 %collective-permute-done.9.refs_4_ = bf16[256,128]{1,0:T(8,128)(2,1)S(1)} collective-permute-done((bf16[256,128]{1,0:T(8,128)(2,1)S(1)}, bf16[256,128]{1,0:T(8,128)(2,1)S(1)}, u32[]{:S(2)}, u32[]{:S(2)}) %collective-permute-start.9) | collective-permute-done | bytes 65568 | tf_op jit(solution)/shard_map/ppermute | solution.py:193
  24.1 0.4 shard_map.112
  24.5 0.1 collective-permute-start.10
  24.6 1.2 %collective-permute-done.10.refs_1_ = f32[8,256]{1,0:T(8,128)S(1)} collective-permute-done((f32[8,256]{1,0:T(8,128)S(1)}, f32[8,256]{1,0:T(8,128)S(1)}, u32[]{:S(2)}, u32[]{:S(2)}) %collective-permute-start.10) | collective-permute-done | bytes 8224 | tf_op jit(solution)/shard_map/ppermute | solution.py:273
  25.7 0.4 shard_map.113
  26.1 1.7 %collective-permute-start.18 = (bf16[272,128]{1,0:T(8,128)(2,1)S(1)}, bf16[272,128]{1,0:T(8,128)(2,1)S(1)}, u32[]{:S(2)}, u32[]{:S(2)}) collective-permute-start(bf16[272,128]{1,0:T(8,128)(2,1)S(1)} %get-tuple-element.65), channel_id=1, source_target_pairs={{0,6},{2,4},{4,2},{6,0},{8,14},{10,12},{12,10},{14,8},{16,22},{18,... | collective-permute-start | bytes 208904 | tf_op jit(solution)/shard_map/ppermute | solution.py:193
  27.8 0.4 collective-permute-start.17
  28.2 1.5 %collective-permute-start.14 = (bf16[272,128]{1,0:T(8,128)(2,1)S(1)}, bf16[272,128]{1,0:T(8,128)(2,1)S(1)}, u32[]{:S(2)}, u32[]{:S(2)}) collective-permute-start(bf16[272,128]{1,0:T(8,128)(2,1)S(1)} %get-tuple-element.65), channel_id=1, source_target_pairs={{0,2},{2,0},{4,6},{6,4},{8,10},{10,8},{12,14},{14,12},{16,18},{18,... | collective-permute-start | bytes 208904 | tf_op jit(solution)/shard_map/ppermute | solution.py:193
  29.6 0.2 shard_map.114
  29.9 1.7 %collective-permute-start.13 = (bf16[256,128]{1,0:T(8,128)(2,1)S(1)}, bf16[256,128]{1,0:T(8,128)(2,1)S(1)}, u32[]{:S(2)}, u32[]{:S(2)}) collective-permute-start(bf16[256,128]{1,0:T(8,128)(2,1)S(1)} %get-tuple-element.64), channel_id=1, source_target_pairs={{0,6},{2,4},{4,2},{6,0},{8,14},{10,12},{12,10},{14,8},{16,22},{18,... | collective-permute-start | bytes 196616 | tf_op jit(solution)/shard_map/ppermute | solution.py:193
  31.5 0.4 collective-permute-start.12
  32.0 1.5 %collective-permute-start.11 = (bf16[256,128]{1,0:T(8,128)(2,1)S(1)}, bf16[256,128]{1,0:T(8,128)(2,1)S(1)}, u32[]{:S(2)}, u32[]{:S(2)}) collective-permute-start(bf16[256,128]{1,0:T(8,128)(2,1)S(1)} %get-tuple-element.64), channel_id=1, source_target_pairs={{0,2},{2,0},{4,6},{6,4},{8,10},{10,8},{12,14},{14,12},{16,18},{18,... | collective-permute-start | bytes 196616 | tf_op jit(solution)/shard_map/ppermute | solution.py:193
  33.5 1.6 %collective-permute-start.19 = (bf16[272,128]{1,0:T(8,128)(2,1)S(1)}, bf16[272,128]{1,0:T(8,128)(2,1)S(1)}, u32[]{:S(2)}, u32[]{:S(2)}) collective-permute-start(bf16[272,128]{1,0:T(8,128)(2,1)S(1)} %add_convert_fusion.1), channel_id=1, source_target_pairs={{0,8},{2,10},{4,12},{6,14},{8,0},{10,2},{12,4},{14,6},{16,24},{18,... | collective-permute-start | bytes 208904 | tf_op jit(solution)/shard_map/ppermute | solution.py:193
  35.1 1.0 %shard_map.116 = (f32[256,512]{1,0:T(8,128)S(1)}, f32[256,512]{1,0:T(8,128)S(1)}) custom-call(bf16[256,256]{1,0:T(8,128)(2,1)S(1)} %get-tuple-element.66.refs_2_.refs_0_, bf16[256,256]{1,0:T(8,128)(2,1)S(1)} %get-tuple-element.67.refs_3_.refs_1_, bf16[512,256]{1,0:T(8,128)(2,1)S(1)} %get-tuple-element.68.refs_0_.refs_6_.refs_2_, ...), custom_call_target="tpu_custom_call" | custom-call | flops 268435456 | bytes 2097152 | tf_op jit(solution)/shard_map/pallas_call | solution.py:207
  36.2 0.0 collective-permute-done.12.refs_1_
  36.2 0.1 collective-permute-done.11.refs_0_
  36.3 1.6 %collective-permute-start.15 = (bf16[256,128]{1,0:T(8,128)(2,1)S(1)}, bf16[256,128]{1,0:T(8,128)(2,1)S(1)}, u32[]{:S(2)}, u32[]{:S(2)}) collective-permute-start(bf16[256,128]{1,0:T(8,128)(2,1)S(1)} %add_convert_fusion.3), channel_id=1, source_target_pairs={{0,8},{2,10},{4,12},{6,14},{8,0},{10,2},{12,4},{14,6},{16,24},{18,... | collective-permute-start | bytes 196616 | tf_op jit(solution)/shard_map/ppermute | solution.py:193
  37.9 3.4 %collective-permute-start.20 = (bf16[272,128]{1,0:T(8,128)(2,1)S(1)}, bf16[272,128]{1,0:T(8,128)(2,1)S(1)}, u32[]{:S(2)}, u32[]{:S(2)}) collective-permute-start(bf16[272,128]{1,0:T(8,128)(2,1)S(1)} %add_convert_fusion.refs_5_), channel_id=1, source_target_pairs={{0,16},{2,18},{4,20},{6,22},{8,24},{10,26},{12,28},{14,30},{16,0},... | collective-permute-start | bytes 208904 | tf_op jit(solution)/shard_map/ppermute | solution.py:193
  41.4 2.3 %collective-permute-start.16 = (bf16[256,128]{1,0:T(8,128)(2,1)S(1)}, bf16[256,128]{1,0:T(8,128)(2,1)S(1)}, u32[]{:S(2)}, u32[]{:S(2)}) collective-permute-start(bf16[256,128]{1,0:T(8,128)(2,1)S(1)} %add_convert_fusion.2.refs_5_), channel_id=1, source_target_pairs={{0,16},{2,18},{4,20},{6,22},{8,24},{10,26},{12,28},{14,30},{16,0},... | collective-permute-start | bytes 196616 | tf_op jit(solution)/shard_map/ppermute | solution.py:193
  43.7 1.4 %shard_map.115 = (bf16[256,512]{1,0:T(8,128)(2,1)}, bf16[256,512]{1,0:T(8,128)(2,1)}) custom-call(f32[256,256]{1,0:T(8,128)S(1)} %get-tuple-element.49.refs_2_.refs_0_, f32[256,256]{1,0:T(8,128)S(1)} %get-tuple-element.53.refs_3_.refs_2_.refs_1_, bf16[256,256]{1,0:T(8,128)(2,1)S(1)} %get-tuple-element.66.refs_2_.refs_0_, ...), custom_call_target="tpu_custom_call" | custom-call | flops 167772160 | bytes 2097152 | tf_op jit(solution)/shard_map/pallas_call | solution.py:290
  45.1 0.2 collective-permute-done.20.refs_4_
  45.4 1.0 %shard_map.117 = (bf16[256,512]{1,0:T(8,128)(2,1)}, bf16[256,512]{1,0:T(8,128)(2,1)}, f32[4,128,128]{2,1,0:T(8,128)}, f32[1,512]{1,0:T(1,128)}) custom-call(bf16[272,128]{1,0:T(8,128)(2,1)S(1)} %collective-permute-done.14.refs_0_, bf16[272,128]{1,0:T(8,128)(2,1)S(1)} %collective-permute-done.17.refs_1_, ...), custom_call_target="tpu_custom_call" | custom-call | flops 33554432 | bytes 1835008 | tf_op jit(solution)/shard_map/pallas_call | solution.py:310
  46.4 0.2 collective-permute-done.16.refs_4_
  46.6 1.0 %shard_map.118 = (bf16[256,512]{1,0:T(8,128)(2,1)}, bf16[256,512]{1,0:T(8,128)(2,1)}, f32[4,128,128]{2,1,0:T(8,128)}) custom-call(bf16[256,128]{1,0:T(8,128)(2,1)S(1)} %collective-permute-done.11.refs_0_, bf16[256,128]{1,0:T(8,128)(2,1)S(1)} %collective-permute-done.12.refs_1_, ...), custom_call_target="tpu_custom_call", output_to_operand_aliasing={{0}: (9, {}), {1}: (10, {}), {2}: (11, {})} | custom-call | flops 33554432 | bytes 1835008 | tf_op jit(solution)/shard_map/pallas_call | solution.py:310
  (25 shorter events, 0.3 us)
Async XLA Ops:
  0.6 1.1 %copy-start.4 = (bf16[256,512]{1,0:T(8,128)(2,1)S(1)}, bf16[256,512]{1,0:T(8,128)(2,1)}, u32[]{:S(2)}) copy-start(bf16[256,512]{1,0:T(8,128)(2,1)} %param.8) | copy-start | bytes 786436
  2.0 8.0 %collective-permute-start.2 = (bf16[256,128]{1,0:T(8,128)(2,1)S(1)}, bf16[256,128]{1,0:T(8,128)(2,1)S(1)}, u32[]{:S(2)}, u32[]{:S(2)}) collective-permute-start(bf16[256,128]{1,0:T(8,128)(2,1)S(1)} %get-tuple-element.46), channel_id=1, source_target_pairs={{0,6},{2,4},{4,2},{6,0},{8,14},{10,12},{12,10},{14,8},{16,22},{18,... | collective-permute-start | bytes 196616 | tf_op jit(solution)/shard_map/ppermute | solution.py:193
  6.0 5.1 %collective-permute-start.1 = (bf16[256,128]{1,0:T(8,128)(2,1)S(1)}, bf16[256,128]{1,0:T(8,128)(2,1)S(1)}, u32[]{:S(2)}, u32[]{:S(2)}) collective-permute-start(bf16[256,128]{1,0:T(8,128)(2,1)S(1)} %get-tuple-element.46), channel_id=1, source_target_pairs={{0,4},{2,6},{4,0},{6,2},{8,12},{10,14},{12,8},{14,10},{16,20},{18,... | collective-permute-start | bytes 196616 | tf_op jit(solution)/shard_map/ppermute | solution.py:193
  6.5 4.6 %collective-permute-start = (bf16[256,128]{1,0:T(8,128)(2,1)S(1)}, bf16[256,128]{1,0:T(8,128)(2,1)S(1)}, u32[]{:S(2)}, u32[]{:S(2)}) collective-permute-start(bf16[256,128]{1,0:T(8,128)(2,1)S(1)} %get-tuple-element.46), channel_id=1, source_target_pairs={{0,2},{2,0},{4,6},{6,4},{8,10},{10,8},{12,14},{14,12},{16,18},{18,... | collective-permute-start | bytes 196616 | tf_op jit(solution)/shard_map/ppermute | solution.py:193
  6.7 6.2 %collective-permute-start.7 = (bf16[256,128]{1,0:T(8,128)(2,1)S(1)}, bf16[256,128]{1,0:T(8,128)(2,1)S(1)}, u32[]{:S(2)}, u32[]{:S(2)}) collective-permute-start(bf16[256,128]{1,0:T(8,128)(2,1)S(1)} %get-tuple-element.50), channel_id=1, source_target_pairs={{0,6},{2,4},{4,2},{6,0},{8,14},{10,12},{12,10},{14,8},{16,22},{18,... | collective-permute-start | bytes 196616 | tf_op jit(solution)/shard_map/ppermute | solution.py:193
  9.5 4.3 %collective-permute-start.6 = (bf16[256,128]{1,0:T(8,128)(2,1)S(1)}, bf16[256,128]{1,0:T(8,128)(2,1)S(1)}, u32[]{:S(2)}, u32[]{:S(2)}) collective-permute-start(bf16[256,128]{1,0:T(8,128)(2,1)S(1)} %get-tuple-element.50), channel_id=1, source_target_pairs={{0,4},{2,6},{4,0},{6,2},{8,12},{10,14},{12,8},{14,10},{16,20},{18,... | collective-permute-start | bytes 196616 | tf_op jit(solution)/shard_map/ppermute | solution.py:193
  10.0 4.3 %collective-permute-start.5 = (bf16[256,128]{1,0:T(8,128)(2,1)S(1)}, bf16[256,128]{1,0:T(8,128)(2,1)S(1)}, u32[]{:S(2)}, u32[]{:S(2)}) collective-permute-start(bf16[256,128]{1,0:T(8,128)(2,1)S(1)} %get-tuple-element.50), channel_id=1, source_target_pairs={{0,2},{2,0},{4,6},{6,4},{8,10},{10,8},{12,14},{14,12},{16,18},{18,... | collective-permute-start | bytes 196616 | tf_op jit(solution)/shard_map/ppermute | solution.py:193
  11.1 5.0 %collective-permute-start.3 = (bf16[256,128]{1,0:T(8,128)(2,1)S(1)}, bf16[256,128]{1,0:T(8,128)(2,1)S(1)}, u32[]{:S(2)}, u32[]{:S(2)}) collective-permute-start(bf16[256,128]{1,0:T(8,128)(2,1)S(1)} %fusion), channel_id=1, source_target_pairs={{0,8},{2,10},{4,12},{6,14},{8,0},{10,2},{12,4},{14,6},{16,24},{18,... | collective-permute-start | bytes 196616 | tf_op jit(solution)/shard_map/ppermute | solution.py:193
  14.3 4.5 %collective-permute-start.8 = (bf16[256,128]{1,0:T(8,128)(2,1)S(1)}, bf16[256,128]{1,0:T(8,128)(2,1)S(1)}, u32[]{:S(2)}, u32[]{:S(2)}) collective-permute-start(bf16[256,128]{1,0:T(8,128)(2,1)S(1)} %fusion.1), channel_id=1, source_target_pairs={{0,8},{2,10},{4,12},{6,14},{8,0},{10,2},{12,4},{14,6},{16,24},{18,... | collective-permute-start | bytes 196616 | tf_op jit(solution)/shard_map/ppermute | solution.py:193
  16.2 5.2 %copy-start = (bf16[256,512]{1,0:T(8,128)(2,1)S(1)}, bf16[256,512]{1,0:T(8,128)(2,1)}, u32[]{:S(2)}) copy-start(bf16[256,512]{1,0:T(8,128)(2,1)} %refs_4_.2) | copy-start | bytes 786436
  16.2 6.6 %collective-permute-start.4 = (bf16[256,128]{1,0:T(8,128)(2,1)S(1)}, bf16[256,128]{1,0:T(8,128)(2,1)S(1)}, u32[]{:S(2)}, u32[]{:S(2)}) collective-permute-start(bf16[256,128]{1,0:T(8,128)(2,1)S(1)} %add_convert_fusion.5), channel_id=1, source_target_pairs={{0,16},{2,18},{4,20},{6,22},{8,24},{10,26},{12,28},{14,30},{16,0},... | collective-permute-start | bytes 196616 | tf_op jit(solution)/shard_map/ppermute | solution.py:193
  18.9 3.9 %copy-start.1 = (bf16[256,512]{1,0:T(8,128)(2,1)S(1)}, bf16[256,512]{1,0:T(8,128)(2,1)}, u32[]{:S(2)}) copy-start(bf16[256,512]{1,0:T(8,128)(2,1)} %refs_3_.1) | copy-start | bytes 786436
  18.9 3.9 %copy-start.2 = (f32[4,128,128]{2,1,0:T(8,128)S(1)}, f32[4,128,128]{2,1,0:T(8,128)}, u32[]{:S(2)}) copy-start(f32[4,128,128]{2,1,0:T(8,128)} %refs_9_.1) | copy-start | bytes 786436
  18.9 5.2 %collective-permute-start.9 = (bf16[256,128]{1,0:T(8,128)(2,1)S(1)}, bf16[256,128]{1,0:T(8,128)(2,1)S(1)}, u32[]{:S(2)}, u32[]{:S(2)}) collective-permute-start(bf16[256,128]{1,0:T(8,128)(2,1)S(1)} %add_convert_fusion.4), channel_id=1, source_target_pairs={{0,16},{2,18},{4,20},{6,22},{8,24},{10,26},{12,28},{14,30},{16,0},... | collective-permute-start | bytes 196616 | tf_op jit(solution)/shard_map/ppermute | solution.py:193
  22.0 0.8 %copy-start.3 = (f32[512]{0:T(512)S(1)}, f32[512]{0:T(512)}, u32[]{:S(2)}) copy-start(f32[512]{0:T(512)} %param.11) | copy-start | bytes 6148
  24.5 1.2 %collective-permute-start.10 = (f32[8,256]{1,0:T(8,128)S(1)}, f32[8,256]{1,0:T(8,128)S(1)}, u32[]{:S(2)}, u32[]{:S(2)}) collective-permute-start(f32[8,256]{1,0:T(8,128)S(1)} %get-tuple-element.54.refs_0_), channel_id=1, source_target_pairs={{0,1},{1,0},{2,3},{3,2},{4,5},{5,4},{6,7},{7,6},{8,9},{9,8},{10,11... | collective-permute-start | bytes 24584 | tf_op jit(solution)/shard_map/ppermute | solution.py:273
  26.1 5.9 %collective-permute-start.18 = (bf16[272,128]{1,0:T(8,128)(2,1)S(1)}, bf16[272,128]{1,0:T(8,128)(2,1)S(1)}, u32[]{:S(2)}, u32[]{:S(2)}) collective-permute-start(bf16[272,128]{1,0:T(8,128)(2,1)S(1)} %get-tuple-element.65), channel_id=1, source_target_pairs={{0,6},{2,4},{4,2},{6,0},{8,14},{10,12},{12,10},{14,8},{16,22},{18,... | collective-permute-start | bytes 208904 | tf_op jit(solution)/shard_map/ppermute | solution.py:193
  27.8 5.7 %collective-permute-start.17 = (bf16[272,128]{1,0:T(8,128)(2,1)S(1)}, bf16[272,128]{1,0:T(8,128)(2,1)S(1)}, u32[]{:S(2)}, u32[]{:S(2)}) collective-permute-start(bf16[272,128]{1,0:T(8,128)(2,1)S(1)} %get-tuple-element.65), channel_id=1, source_target_pairs={{0,4},{2,6},{4,0},{6,2},{8,12},{10,14},{12,8},{14,10},{16,20},{18,... | collective-permute-start | bytes 208904 | tf_op jit(solution)/shard_map/ppermute | solution.py:193
  28.2 5.3 %collective-permute-start.14 = (bf16[272,128]{1,0:T(8,128)(2,1)S(1)}, bf16[272,128]{1,0:T(8,128)(2,1)S(1)}, u32[]{:S(2)}, u32[]{:S(2)}) collective-permute-start(bf16[272,128]{1,0:T(8,128)(2,1)S(1)} %get-tuple-element.65), channel_id=1, source_target_pairs={{0,2},{2,0},{4,6},{6,4},{8,10},{10,8},{12,14},{14,12},{16,18},{18,... | collective-permute-start | bytes 208904 | tf_op jit(solution)/shard_map/ppermute | solution.py:193
  29.9 6.3 %collective-permute-start.13 = (bf16[256,128]{1,0:T(8,128)(2,1)S(1)}, bf16[256,128]{1,0:T(8,128)(2,1)S(1)}, u32[]{:S(2)}, u32[]{:S(2)}) collective-permute-start(bf16[256,128]{1,0:T(8,128)(2,1)S(1)} %get-tuple-element.64), channel_id=1, source_target_pairs={{0,6},{2,4},{4,2},{6,0},{8,14},{10,12},{12,10},{14,8},{16,22},{18,... | collective-permute-start | bytes 196616 | tf_op jit(solution)/shard_map/ppermute | solution.py:193
  31.5 4.6 %collective-permute-start.12 = (bf16[256,128]{1,0:T(8,128)(2,1)S(1)}, bf16[256,128]{1,0:T(8,128)(2,1)S(1)}, u32[]{:S(2)}, u32[]{:S(2)}) collective-permute-start(bf16[256,128]{1,0:T(8,128)(2,1)S(1)} %get-tuple-element.64), channel_id=1, source_target_pairs={{0,4},{2,6},{4,0},{6,2},{8,12},{10,14},{12,8},{14,10},{16,20},{18,... | collective-permute-start | bytes 196616 | tf_op jit(solution)/shard_map/ppermute | solution.py:193
  32.0 4.3 %collective-permute-start.11 = (bf16[256,128]{1,0:T(8,128)(2,1)S(1)}, bf16[256,128]{1,0:T(8,128)(2,1)S(1)}, u32[]{:S(2)}, u32[]{:S(2)}) collective-permute-start(bf16[256,128]{1,0:T(8,128)(2,1)S(1)} %get-tuple-element.64), channel_id=1, source_target_pairs={{0,2},{2,0},{4,6},{6,4},{8,10},{10,8},{12,14},{14,12},{16,18},{18,... | collective-permute-start | bytes 196616 | tf_op jit(solution)/shard_map/ppermute | solution.py:193
  33.5 4.4 %collective-permute-start.19 = (bf16[272,128]{1,0:T(8,128)(2,1)S(1)}, bf16[272,128]{1,0:T(8,128)(2,1)S(1)}, u32[]{:S(2)}, u32[]{:S(2)}) collective-permute-start(bf16[272,128]{1,0:T(8,128)(2,1)S(1)} %add_convert_fusion.1), channel_id=1, source_target_pairs={{0,8},{2,10},{4,12},{6,14},{8,0},{10,2},{12,4},{14,6},{16,24},{18,... | collective-permute-start | bytes 208904 | tf_op jit(solution)/shard_map/ppermute | solution.py:193
  36.3 5.1 %collective-permute-start.15 = (bf16[256,128]{1,0:T(8,128)(2,1)S(1)}, bf16[256,128]{1,0:T(8,128)(2,1)S(1)}, u32[]{:S(2)}, u32[]{:S(2)}) collective-permute-start(bf16[256,128]{1,0:T(8,128)(2,1)S(1)} %add_convert_fusion.3), channel_id=1, source_target_pairs={{0,8},{2,10},{4,12},{6,14},{8,0},{10,2},{12,4},{14,6},{16,24},{18,... | collective-permute-start | bytes 196616 | tf_op jit(solution)/shard_map/ppermute | solution.py:193
  37.9 7.4 %collective-permute-start.20 = (bf16[272,128]{1,0:T(8,128)(2,1)S(1)}, bf16[272,128]{1,0:T(8,128)(2,1)S(1)}, u32[]{:S(2)}, u32[]{:S(2)}) collective-permute-start(bf16[272,128]{1,0:T(8,128)(2,1)S(1)} %add_convert_fusion.refs_5_), channel_id=1, source_target_pairs={{0,16},{2,18},{4,20},{6,22},{8,24},{10,26},{12,28},{14,30},{16,0},... | collective-permute-start | bytes 208904 | tf_op jit(solution)/shard_map/ppermute | solution.py:193
  41.4 5.2 %collective-permute-start.16 = (bf16[256,128]{1,0:T(8,128)(2,1)S(1)}, bf16[256,128]{1,0:T(8,128)(2,1)S(1)}, u32[]{:S(2)}, u32[]{:S(2)}) collective-permute-start(bf16[256,128]{1,0:T(8,128)(2,1)S(1)} %add_convert_fusion.2.refs_5_), channel_id=1, source_target_pairs={{0,16},{2,18},{4,20},{6,22},{8,24},{10,26},{12,28},{14,30},{16,0},... | collective-permute-start | bytes 196616 | tf_op jit(solution)/shard_map/ppermute | solution.py:193

commit v9 on v8

--- a/solution.py
+++ b/solution.py
@@ -77,6 +77,14 @@
     return total
 
 
+def partial_kernel(heads, dim, partners, reverse, *refs):
+    parts, out_ref = refs[: len(partners)], refs[-1]
+    for i, h in enumerate(heads):
+        r = cols(i, dim)
+        total = gathered(partners, parts, r, reverse)
+        out_ref[r, :] = total if reverse else refs[len(partners)][h] + total
+
+
 def unnormed_kernel(heads, dim, partners, first, *refs):
     parts = refs[: len(partners)]
     refs = refs[len(partners) :]
@@ -86,7 +94,8 @@
     square = product = 0.0
     for i, h in enumerate(heads):
         c, r = cols(h, dim), cols(i, dim)
-        prefix = (carried_ref[h] + gathered(partners, parts, r, False)).astype(BF16)
+        start = carried_ref[h] if first else carried_ref[r, :]
+        prefix = (start + gathered(partners, parts, r, False)).astype(BF16)
         prefix_ref[r, :] = prefix
         un = local_ref[:, c] + dot(q_ref[:, c], prefix, 1, 0)
         un_ref[:, r] = un
@@ -171,12 +180,15 @@
 def final_kernel(heads, dim, partners, first, *refs):
     parts = refs[: len(partners)]
     message_ref, kv_ref, gk_ref, gv_ref = refs[len(partners) : len(partners) + 4]
-    outs = refs[len(partners) + (4 if first else 7) :]
+    outs = refs[len(partners) + (4 if first else 8) :]
     gk_out, gv_out, state_out = outs[:3]
     length = kv_ref.shape[0] // 2
     for i, h in enumerate(heads):
         c, r = cols(h, dim), cols(i, dim)
-        suffix = gathered(partners, parts, r, True).astype(BF16)
+        suffix = gathered(partners, parts, r, True)
+        if not first:
+            suffix = suffix + refs[len(partners) + 4][r, :]
+        suffix = suffix.astype(BF16)
         gk = gk_ref[:, c] + dot(kv_ref[length:, r], suffix, 1, 1)
         gv = gv_ref[:, c] + dot(kv_ref[:length, r], suffix, 1, 0)
         gk_out[:, r] = gk.astype(BF16)
@@ -259,11 +271,14 @@
     partners, _, received, done = scan(list(states[2:]), list(states[:2]), count, {})
     local, turned = local[0](*local[1:])
     unnormed, prefixes, sums = [], [], ()
+    ahead = functools.partial(partial_kernel, halves[1], dim, partners[:-1])
+    start = call(functools.partial(ahead, False), state_f32, 0, 5 * state_size)(*received[1][:-1], carried_state)
     for n, members in enumerate(halves):
+        last = slice(0 if n == 0 else -1, None)
         un, prefix, both = call(
-            functools.partial(unnormed_kernel, members, dim, partners, n == 0),
+            functools.partial(unnormed_kernel, members, dim, partners[last], n == 0),
             (half_f32, state_bf, shape((ROWS, length), F32)), block // 2, 3 * size + 4 * state_size,
-        )(*received[n], *sums, queries, local, cotangent, carried_state, gain)
+        )(*received[n][last], *sums, queries, local, cotangent, carried_state if n == 0 else start, gain)
         unnormed.append(un)
         prefixes.append(prefix)
         sums = (both,)
@@ -295,8 +310,10 @@
     local_k, local_v = done[spot]
 
     outs = ()
+    start = call(functools.partial(ahead, True), state_f32, 0, 5 * state_size)(*received[1][:-1])
     for n, members in enumerate(halves):
-        operands = (*received[n], messages[n], kvs[n], local_k, local_v)
+        last = slice(0 if n == 0 else -1, None)
+        operands = (*received[n][last], messages[n], kvs[n], local_k, local_v) + ((start,) if n == 1 else ())
         column = functools.partial(lambda at, i: (0, at), n)
         results = [tokens_bf, tokens_bf, shape((heads, dim, dim), F32)]
         out_specs = [
@@ -308,7 +325,7 @@
             results.append(shape((1, width), F32))
             out_specs.append(pl.BlockSpec((1, width), lambda i: (0, 0)))
         outs = call(
-            functools.partial(final_kernel, members, dim, partners, n == 0), results, block, 5 * size + 4 * state_size,
+            functools.partial(final_kernel, members, dim, partners[last], n == 0), results, block, 5 * size + 4 * state_size,
             grid=(1,),
             in_specs=[WHOLE] * len(operands) + [pl.BlockSpec(memory_space=pl.ANY)] * len(outs),
             out_specs=out_specs,

time: 47.8 us -> 47.7 us (level)
    pallas_call x4 -> x6, Pallas kernels: 2.71 us -> 2.76 us  [the longest x2 1.96 us: on_device(): call(functools.partial(final_kernel, members, dim, partners[last], n == 0...]
  transfers between devices with their start and end apart: 21 -> 21, of which waited for: 11 -> 10; matrix products, arithmetic and copies ran while one was open for 1% -> 1% of each run, Pallas kernels for 10% -> 10%
where the time goes in v9:
time: 47.7 us; the launch traced here: 47.5 us
  starting transfers between devices  33.2 us (70%)
  Pallas kernels  6.68 us (14%)
  waiting for transfers between devices  5.2 us (11%)
  local copies, waits for them, and re-layouts  1.29 us (3%)
  between operations  0.82 us (2%)
    ppermute x20, starting transfers between devices, swap(): lax.ppermute(message, 'seq', [(i, i ^ partner) for i in range(count)])  33.1 us
    ppermute x20, waiting for transfers between devices, swap(): lax.ppermute(message, 'seq', [(i, i ^ partner) for i in range(count)])  4.04 us
    pallas_call x2, Pallas kernels, on_device(): call(functools.partial(final_kernel, members, dim, partners[last], n == 0...  1.96 us
    pallas_call x1, Pallas kernels, on_device(): call(functools.partial(attended_kernel, halves, dim), (tokens_bf, tokens_...  1.43 us
    ppermute x1, waiting for transfers between devices, on_device(): lax.ppermute(partner, 'head', [(i, (i + 1) % head_count) for i in range(h...  1.16 us
    slice x2, local copies, waits for them, and re-layouts, on_device(): part[:, n * per * dim:(n + 1) * per * dim]  1.05 us
    pallas_call x1, Pallas kernels, scan(): work = beside[n, distance][0](*operands)  1 us
  transfers between devices with their start and end apart: 21, of which 10 were waited for; matrix products, arithmetic and copies ran while one was open for 1% of the time, Pallas kernels for 10%

profile of v9, /device:TPU:0, one launch (start us, length us, event | category | flops | bytes accessed | tf_op | source)
XLA Modules:
  0.0 47.5 jit_solution(9575537223274473791)
XLA Ops:
  0.6 1.0 %fusion.2 = (bf16[256,256]{1,0:T(8,128)(2,1)S(1)}, bf16[256,256]{1,0:T(8,128)(2,1)S(1)}) fusion(bf16[256,512]{1,0:T(8,128)(2,1)} %param.7), kind=kLoop, calls=%fused_computation.12 | loop fusion | bytes 524288 | tf_op jit(solution)/shard_map/slice | solution.py:259
  1.7 0.0 copy-done.4
  1.8 0.3 shard_map.109
  2.0 4.0 %collective-permute-start.2 = (bf16[256,128]{1,0:T(8,128)(2,1)S(1)}, bf16[256,128]{1,0:T(8,128)(2,1)S(1)}, u32[]{:S(2)}, u32[]{:S(2)}) collective-permute-start(bf16[256,128]{1,0:T(8,128)(2,1)S(1)} %get-tuple-element.46), channel_id=1, source_target_pairs={{0,6},{2,4},{4,2},{6,0},{8,14},{10,12},{12,10},{14,8},{16,22},{18,... | collective-permute-start | bytes 196616 | tf_op jit(solution)/shard_map/ppermute | solution.py:205
  6.0 0.5 %collective-permute-start.1 = (bf16[256,128]{1,0:T(8,128)(2,1)S(1)}, bf16[256,128]{1,0:T(8,128)(2,1)S(1)}, u32[]{:S(2)}, u32[]{:S(2)}) collective-permute-start(bf16[256,128]{1,0:T(8,128)(2,1)S(1)} %get-tuple-element.46), channel_id=1, source_target_pairs={{0,4},{2,6},{4,0},{6,2},{8,12},{10,14},{12,8},{14,10},{16,20},{18,... | collective-permute-start | bytes 196616 | tf_op jit(solution)/shard_map/ppermute | solution.py:205
  6.5 0.1 collective-permute-start
  6.7 2.8 %collective-permute-start.7 = (bf16[256,128]{1,0:T(8,128)(2,1)S(1)}, bf16[256,128]{1,0:T(8,128)(2,1)S(1)}, u32[]{:S(2)}, u32[]{:S(2)}) collective-permute-start(bf16[256,128]{1,0:T(8,128)(2,1)S(1)} %get-tuple-element.51), channel_id=1, source_target_pairs={{0,6},{2,4},{4,2},{6,0},{8,14},{10,12},{12,10},{14,8},{16,22},{18,... | collective-permute-start | bytes 196616 | tf_op jit(solution)/shard_map/ppermute | solution.py:205
  9.5 0.5 %collective-permute-start.6 = (bf16[256,128]{1,0:T(8,128)(2,1)S(1)}, bf16[256,128]{1,0:T(8,128)(2,1)S(1)}, u32[]{:S(2)}, u32[]{:S(2)}) collective-permute-start(bf16[256,128]{1,0:T(8,128)(2,1)S(1)} %get-tuple-element.51), channel_id=1, source_target_pairs={{0,4},{2,6},{4,0},{6,2},{8,12},{10,14},{12,8},{14,10},{16,20},{18,... | collective-permute-start | bytes 196616 | tf_op jit(solution)/shard_map/ppermute | solution.py:205
  10.0 0.6 %collective-permute-start.5 = (bf16[256,128]{1,0:T(8,128)(2,1)S(1)}, bf16[256,128]{1,0:T(8,128)(2,1)S(1)}, u32[]{:S(2)}, u32[]{:S(2)}) collective-permute-start(bf16[256,128]{1,0:T(8,128)(2,1)S(1)} %get-tuple-element.51), channel_id=1, source_target_pairs={{0,2},{2,0},{4,6},{6,4},{8,10},{10,8},{12,14},{14,12},{16,18},{18,... | collective-permute-start | bytes 196616 | tf_op jit(solution)/shard_map/ppermute | solution.py:205
  10.6 0.4 collective-permute-done.1.refs_1_
  11.1 1.6 %collective-permute-start.3 = (bf16[256,128]{1,0:T(8,128)(2,1)S(1)}, bf16[256,128]{1,0:T(8,128)(2,1)S(1)}, u32[]{:S(2)}, u32[]{:S(2)}) collective-permute-start(bf16[256,128]{1,0:T(8,128)(2,1)S(1)} %fusion), channel_id=1, source_target_pairs={{0,8},{2,10},{4,12},{6,14},{8,0},{10,2},{12,4},{14,6},{16,24},{18,... | collective-permute-start | bytes 196616 | tf_op jit(solution)/shard_map/ppermute | solution.py:205
  12.8 0.1 collective-permute-done.7.refs_2_
  12.9 0.9 %collective-permute-done.6.refs_1_ = bf16[256,128]{1,0:T(8,128)(2,1)S(1)} collective-permute-done((bf16[256,128]{1,0:T(8,128)(2,1)S(1)}, bf16[256,128]{1,0:T(8,128)(2,1)S(1)}, u32[]{:S(2)}, u32[]{:S(2)}) %collective-permute-start.6) | collective-permute-done | bytes 65568 | tf_op jit(solution)/shard_map/ppermute | solution.py:205
  13.8 0.5 %collective-permute-done.5.refs_0_ = bf16[256,128]{1,0:T(8,128)(2,1)S(1)} collective-permute-done((bf16[256,128]{1,0:T(8,128)(2,1)S(1)}, bf16[256,128]{1,0:T(8,128)(2,1)S(1)}, u32[]{:S(2)}, u32[]{:S(2)}) %collective-permute-start.5) | collective-permute-done | bytes 65568 | tf_op jit(solution)/shard_map/ppermute | solution.py:205
  14.3 1.6 %collective-permute-start.8 = (bf16[256,128]{1,0:T(8,128)(2,1)S(1)}, bf16[256,128]{1,0:T(8,128)(2,1)S(1)}, u32[]{:S(2)}, u32[]{:S(2)}) collective-permute-start(bf16[256,128]{1,0:T(8,128)(2,1)S(1)} %fusion.1), channel_id=1, source_target_pairs={{0,8},{2,10},{4,12},{6,14},{8,0},{10,2},{12,4},{14,6},{16,24},{18,... | collective-permute-start | bytes 196616 | tf_op jit(solution)/shard_map/ppermute | solution.py:205
  16.0 0.2 collective-permute-done.3.refs_3_
  16.2 0.0 copy-start
  16.2 2.7 %collective-permute-start.4 = (bf16[256,128]{1,0:T(8,128)(2,1)S(1)}, bf16[256,128]{1,0:T(8,128)(2,1)S(1)}, u32[]{:S(2)}, u32[]{:S(2)}) collective-permute-start(bf16[256,128]{1,0:T(8,128)(2,1)S(1)} %add_convert_fusion.5), channel_id=1, source_target_pairs={{0,16},{2,18},{4,20},{6,22},{8,24},{10,26},{12,28},{14,30},{16,0},... | collective-permute-start | bytes 196616 | tf_op jit(solution)/shard_map/ppermute | solution.py:205
  18.9 2.5 %collective-permute-start.9 = (bf16[256,128]{1,0:T(8,128)(2,1)S(1)}, bf16[256,128]{1,0:T(8,128)(2,1)S(1)}, u32[]{:S(2)}, u32[]{:S(2)}) collective-permute-start(bf16[256,128]{1,0:T(8,128)(2,1)S(1)} %add_convert_fusion.4), channel_id=1, source_target_pairs={{0,16},{2,18},{4,20},{6,22},{8,24},{10,26},{12,28},{14,30},{16,0},... | collective-permute-start | bytes 196616 | tf_op jit(solution)/shard_map/ppermute | solution.py:205
  21.4 0.7 %shard_map.110 = (f32[256,512]{1,0:T(8,128)S(1)}, bf16[512,256]{1,0:T(8,128)(2,1)S(1)}) custom-call(bf16[256,512]{1,0:T(8,128)(2,1)S(1)} %copy-done, bf16[512,256]{1,0:T(8,128)(2,1)S(1)} %get-tuple-element.68.refs_0_.refs_6_.refs_2_, bf16[512,256]{1,0:T(8,128)(2,1)S(1)} %get-tuple-element.69.refs_1_.refs_7_.refs_3_.refs_2_), custom_call_target="tpu_custom_call" | custom-call | flops 134217728 | bytes 1310720 | tf_op jit(solution)/shard_map/pallas_call | solution.py:272
  22.0 0.1 shard_map.112.refs_5_
  22.1 0.7 %collective-permute-done.4.refs_4_ = bf16[256,128]{1,0:T(8,128)(2,1)S(1)} collective-permute-done((bf16[256,128]{1,0:T(8,128)(2,1)S(1)}, bf16[256,128]{1,0:T(8,128)(2,1)S(1)}, u32[]{:S(2)}, u32[]{:S(2)}) %collective-permute-start.4) | collective-permute-done | bytes 65568 | tf_op jit(solution)/shard_map/ppermute | solution.py:205
  22.8 0.2 copy-done.1
  23.0 0.4 shard_map.111
  23.4 0.8 %collective-permute-done.9.refs_0_ = bf16[256,128]{1,0:T(8,128)(2,1)S(1)} collective-permute-done((bf16[256,128]{1,0:T(8,128)(2,1)S(1)}, bf16[256,128]{1,0:T(8,128)(2,1)S(1)}, u32[]{:S(2)}, u32[]{:S(2)}) %collective-permute-start.9) | collective-permute-done | bytes 65568 | tf_op jit(solution)/shard_map/ppermute | solution.py:205
  24.1 0.3 shard_map.113
  24.4 0.1 collective-permute-start.10
  24.5 1.2 %collective-permute-done.10.refs_1_ = f32[8,256]{1,0:T(8,128)S(1)} collective-permute-done((f32[8,256]{1,0:T(8,128)S(1)}, f32[8,256]{1,0:T(8,128)S(1)}, u32[]{:S(2)}, u32[]{:S(2)}) %collective-permute-start.10) | collective-permute-done | bytes 8224 | tf_op jit(solution)/shard_map/ppermute | solution.py:288
  25.7 0.4 shard_map.114
  26.0 1.6 %collective-permute-start.18 = (bf16[272,128]{1,0:T(8,128)(2,1)S(1)}, bf16[272,128]{1,0:T(8,128)(2,1)S(1)}, u32[]{:S(2)}, u32[]{:S(2)}) collective-permute-start(bf16[272,128]{1,0:T(8,128)(2,1)S(1)} %get-tuple-element.65), channel_id=1, source_target_pairs={{0,6},{2,4},{4,2},{6,0},{8,14},{10,12},{12,10},{14,8},{16,22},{18,... | collective-permute-start | bytes 208904 | tf_op jit(solution)/shard_map/ppermute | solution.py:205
  27.7 0.4 collective-permute-start.17
  28.1 1.5 %collective-permute-start.14 = (bf16[272,128]{1,0:T(8,128)(2,1)S(1)}, bf16[272,128]{1,0:T(8,128)(2,1)S(1)}, u32[]{:S(2)}, u32[]{:S(2)}) collective-permute-start(bf16[272,128]{1,0:T(8,128)(2,1)S(1)} %get-tuple-element.65), channel_id=1, source_target_pairs={{0,2},{2,0},{4,6},{6,4},{8,10},{10,8},{12,14},{14,12},{16,18},{18,... | collective-permute-start | bytes 208904 | tf_op jit(solution)/shard_map/ppermute | solution.py:205
  29.6 0.2 shard_map.115
  29.8 1.6 %collective-permute-start.13 = (bf16[256,128]{1,0:T(8,128)(2,1)S(1)}, bf16[256,128]{1,0:T(8,128)(2,1)S(1)}, u32[]{:S(2)}, u32[]{:S(2)}) collective-permute-start(bf16[256,128]{1,0:T(8,128)(2,1)S(1)} %get-tuple-element.64), channel_id=1, source_target_pairs={{0,6},{2,4},{4,2},{6,0},{8,14},{10,12},{12,10},{14,8},{16,22},{18,... | collective-permute-start | bytes 196616 | tf_op jit(solution)/shard_map/ppermute | solution.py:205
  31.5 0.4 collective-permute-start.12
  31.9 1.5 %collective-permute-start.11 = (bf16[256,128]{1,0:T(8,128)(2,1)S(1)}, bf16[256,128]{1,0:T(8,128)(2,1)S(1)}, u32[]{:S(2)}, u32[]{:S(2)}) collective-permute-start(bf16[256,128]{1,0:T(8,128)(2,1)S(1)} %get-tuple-element.64), channel_id=1, source_target_pairs={{0,2},{2,0},{4,6},{6,4},{8,10},{10,8},{12,14},{14,12},{16,18},{18,... | collective-permute-start | bytes 196616 | tf_op jit(solution)/shard_map/ppermute | solution.py:205
  33.4 1.6 %collective-permute-start.19 = (bf16[272,128]{1,0:T(8,128)(2,1)S(1)}, bf16[272,128]{1,0:T(8,128)(2,1)S(1)}, u32[]{:S(2)}, u32[]{:S(2)}) collective-permute-start(bf16[272,128]{1,0:T(8,128)(2,1)S(1)} %add_convert_fusion.1), channel_id=1, source_target_pairs={{0,8},{2,10},{4,12},{6,14},{8,0},{10,2},{12,4},{14,6},{16,24},{18,... | collective-permute-start | bytes 208904 | tf_op jit(solution)/shard_map/ppermute | solution.py:205
  35.1 1.0 %shard_map.117 = (f32[256,512]{1,0:T(8,128)S(1)}, f32[256,512]{1,0:T(8,128)S(1)}) custom-call(bf16[256,256]{1,0:T(8,128)(2,1)S(1)} %get-tuple-element.66.refs_2_.refs_0_, bf16[256,256]{1,0:T(8,128)(2,1)S(1)} %get-tuple-element.67.refs_3_.refs_1_, bf16[512,256]{1,0:T(8,128)(2,1)S(1)} %get-tuple-element.68.refs_0_.refs_6_.refs_2_, ...), custom_call_target="tpu_custom_call" | custom-call | flops 268435456 | bytes 2097152 | tf_op jit(solution)/shard_map/pallas_call | solution.py:219
  36.1 0.0 collective-permute-done.11.refs_0_
  36.2 1.6 %collective-permute-start.15 = (bf16[256,128]{1,0:T(8,128)(2,1)S(1)}, bf16[256,128]{1,0:T(8,128)(2,1)S(1)}, u32[]{:S(2)}, u32[]{:S(2)}) collective-permute-start(bf16[256,128]{1,0:T(8,128)(2,1)S(1)} %add_convert_fusion.3), channel_id=1, source_target_pairs={{0,8},{2,10},{4,12},{6,14},{8,0},{10,2},{12,4},{14,6},{16,24},{18,... | collective-permute-start | bytes 196616 | tf_op jit(solution)/shard_map/ppermute | solution.py:205
  37.9 3.4 %collective-permute-start.20 = (bf16[272,128]{1,0:T(8,128)(2,1)S(1)}, bf16[272,128]{1,0:T(8,128)(2,1)S(1)}, u32[]{:S(2)}, u32[]{:S(2)}) collective-permute-start(bf16[272,128]{1,0:T(8,128)(2,1)S(1)} %add_convert_fusion.refs_5_), channel_id=1, source_target_pairs={{0,16},{2,18},{4,20},{6,22},{8,24},{10,26},{12,28},{14,30},{16,0},... | collective-permute-start | bytes 208904 | tf_op jit(solution)/shard_map/ppermute | solution.py:205
  41.3 2.3 %collective-permute-start.16 = (bf16[256,128]{1,0:T(8,128)(2,1)S(1)}, bf16[256,128]{1,0:T(8,128)(2,1)S(1)}, u32[]{:S(2)}, u32[]{:S(2)}) collective-permute-start(bf16[256,128]{1,0:T(8,128)(2,1)S(1)} %add_convert_fusion.2.refs_1_), channel_id=1, source_target_pairs={{0,16},{2,18},{4,20},{6,22},{8,24},{10,26},{12,28},{14,30},{16,0},... | collective-permute-start | bytes 196616 | tf_op jit(solution)/shard_map/ppermute | solution.py:205
  43.6 1.4 %shard_map.116 = (bf16[256,512]{1,0:T(8,128)(2,1)}, bf16[256,512]{1,0:T(8,128)(2,1)}) custom-call(f32[256,256]{1,0:T(8,128)S(1)} %get-tuple-element.49.refs_2_.refs_0_, f32[256,256]{1,0:T(8,128)S(1)} %get-tuple-element.53.refs_3_.refs_2_.refs_1_, bf16[256,256]{1,0:T(8,128)(2,1)S(1)} %get-tuple-element.66.refs_2_.refs_0_, ...), custom_call_target="tpu_custom_call" | custom-call | flops 167772160 | bytes 2097152 | tf_op jit(solution)/shard_map/pallas_call | solution.py:305
  45.1 0.1 shard_map.118.refs_5_
  45.1 0.2 collective-permute-done.20.refs_4_
  45.3 1.0 %shard_map.119 = (bf16[256,512]{1,0:T(8,128)(2,1)}, bf16[256,512]{1,0:T(8,128)(2,1)}, f32[4,128,128]{2,1,0:T(8,128)}, f32[1,512]{1,0:T(1,128)}) custom-call(bf16[272,128]{1,0:T(8,128)(2,1)S(1)} %collective-permute-done.14.refs_0_, bf16[272,128]{1,0:T(8,128)(2,1)S(1)} %collective-permute-done.17.refs_1_, ...), custom_call_target="tpu_custom_call" | custom-call | flops 33554432 | bytes 1835008 | tf_op jit(solution)/shard_map/pallas_call | solution.py:327
  46.3 0.3 collective-permute-done.16.refs_0_
  46.5 1.0 %shard_map.120 = (bf16[256,512]{1,0:T(8,128)(2,1)}, bf16[256,512]{1,0:T(8,128)(2,1)}, f32[4,128,128]{2,1,0:T(8,128)}) custom-call(bf16[256,128]{1,0:T(8,128)(2,1)S(1)} %collective-permute-done.16.refs_0_, bf16[256,128]{1,0:T(8,128)(2,1)S(1)} %add_convert_fusion.2.refs_1_, ...), custom_call_target="tpu_custom_call", output_to_operand_aliasing={{0}: (6, {}), {1}: (7, {}), {2}: (8, {})} | custom-call | flops 33554432 | bytes 1835008 | tf_op jit(solution)/shard_map/pallas_call | solution.py:327
  (27 shorter events, 0.4 us)
Async XLA Ops:
  0.6 1.1 %copy-start.4 = (bf16[256,512]{1,0:T(8,128)(2,1)S(1)}, bf16[256,512]{1,0:T(8,128)(2,1)}, u32[]{:S(2)}) copy-start(bf16[256,512]{1,0:T(8,128)(2,1)} %param.8) | copy-start | bytes 786436
  2.0 8.0 %collective-permute-start.2 = (bf16[256,128]{1,0:T(8,128)(2,1)S(1)}, bf16[256,128]{1,0:T(8,128)(2,1)S(1)}, u32[]{:S(2)}, u32[]{:S(2)}) collective-permute-start(bf16[256,128]{1,0:T(8,128)(2,1)S(1)} %get-tuple-element.46), channel_id=1, source_target_pairs={{0,6},{2,4},{4,2},{6,0},{8,14},{10,12},{12,10},{14,8},{16,22},{18,... | collective-permute-start | bytes 196616 | tf_op jit(solution)/shard_map/ppermute | solution.py:205
  6.0 5.1 %collective-permute-start.1 = (bf16[256,128]{1,0:T(8,128)(2,1)S(1)}, bf16[256,128]{1,0:T(8,128)(2,1)S(1)}, u32[]{:S(2)}, u32[]{:S(2)}) collective-permute-start(bf16[256,128]{1,0:T(8,128)(2,1)S(1)} %get-tuple-element.46), channel_id=1, source_target_pairs={{0,4},{2,6},{4,0},{6,2},{8,12},{10,14},{12,8},{14,10},{16,20},{18,... | collective-permute-start | bytes 196616 | tf_op jit(solution)/shard_map/ppermute | solution.py:205
  6.5 4.6 %collective-permute-start = (bf16[256,128]{1,0:T(8,128)(2,1)S(1)}, bf16[256,128]{1,0:T(8,128)(2,1)S(1)}, u32[]{:S(2)}, u32[]{:S(2)}) collective-permute-start(bf16[256,128]{1,0:T(8,128)(2,1)S(1)} %get-tuple-element.46), channel_id=1, source_target_pairs={{0,2},{2,0},{4,6},{6,4},{8,10},{10,8},{12,14},{14,12},{16,18},{18,... | collective-permute-start | bytes 196616 | tf_op jit(solution)/shard_map/ppermute | solution.py:205
  6.7 6.2 %collective-permute-start.7 = (bf16[256,128]{1,0:T(8,128)(2,1)S(1)}, bf16[256,128]{1,0:T(8,128)(2,1)S(1)}, u32[]{:S(2)}, u32[]{:S(2)}) collective-permute-start(bf16[256,128]{1,0:T(8,128)(2,1)S(1)} %get-tuple-element.51), channel_id=1, source_target_pairs={{0,6},{2,4},{4,2},{6,0},{8,14},{10,12},{12,10},{14,8},{16,22},{18,... | collective-permute-start | bytes 196616 | tf_op jit(solution)/shard_map/ppermute | solution.py:205
  9.5 4.3 %collective-permute-start.6 = (bf16[256,128]{1,0:T(8,128)(2,1)S(1)}, bf16[256,128]{1,0:T(8,128)(2,1)S(1)}, u32[]{:S(2)}, u32[]{:S(2)}) collective-permute-start(bf16[256,128]{1,0:T(8,128)(2,1)S(1)} %get-tuple-element.51), channel_id=1, source_target_pairs={{0,4},{2,6},{4,0},{6,2},{8,12},{10,14},{12,8},{14,10},{16,20},{18,... | collective-permute-start | bytes 196616 | tf_op jit(solution)/shard_map/ppermute | solution.py:205
  10.0 4.3 %collective-permute-start.5 = (bf16[256,128]{1,0:T(8,128)(2,1)S(1)}, bf16[256,128]{1,0:T(8,128)(2,1)S(1)}, u32[]{:S(2)}, u32[]{:S(2)}) collective-permute-start(bf16[256,128]{1,0:T(8,128)(2,1)S(1)} %get-tuple-element.51), channel_id=1, source_target_pairs={{0,2},{2,0},{4,6},{6,4},{8,10},{10,8},{12,14},{14,12},{16,18},{18,... | collective-permute-start | bytes 196616 | tf_op jit(solution)/shard_map/ppermute | solution.py:205
  11.1 5.0 %collective-permute-start.3 = (bf16[256,128]{1,0:T(8,128)(2,1)S(1)}, bf16[256,128]{1,0:T(8,128)(2,1)S(1)}, u32[]{:S(2)}, u32[]{:S(2)}) collective-permute-start(bf16[256,128]{1,0:T(8,128)(2,1)S(1)} %fusion), channel_id=1, source_target_pairs={{0,8},{2,10},{4,12},{6,14},{8,0},{10,2},{12,4},{14,6},{16,24},{18,... | collective-permute-start | bytes 196616 | tf_op jit(solution)/shard_map/ppermute | solution.py:205
  14.3 4.5 %collective-permute-start.8 = (bf16[256,128]{1,0:T(8,128)(2,1)S(1)}, bf16[256,128]{1,0:T(8,128)(2,1)S(1)}, u32[]{:S(2)}, u32[]{:S(2)}) collective-permute-start(bf16[256,128]{1,0:T(8,128)(2,1)S(1)} %fusion.1), channel_id=1, source_target_pairs={{0,8},{2,10},{4,12},{6,14},{8,0},{10,2},{12,4},{14,6},{16,24},{18,... | collective-permute-start | bytes 196616 | tf_op jit(solution)/shard_map/ppermute | solution.py:205
  16.2 5.2 %copy-start = (bf16[256,512]{1,0:T(8,128)(2,1)S(1)}, bf16[256,512]{1,0:T(8,128)(2,1)}, u32[]{:S(2)}) copy-start(bf16[256,512]{1,0:T(8,128)(2,1)} %refs_4_.6) | copy-start | bytes 786436
  16.2 6.6 %collective-permute-start.4 = (bf16[256,128]{1,0:T(8,128)(2,1)S(1)}, bf16[256,128]{1,0:T(8,128)(2,1)S(1)}, u32[]{:S(2)}, u32[]{:S(2)}) collective-permute-start(bf16[256,128]{1,0:T(8,128)(2,1)S(1)} %add_convert_fusion.5), channel_id=1, source_target_pairs={{0,16},{2,18},{4,20},{6,22},{8,24},{10,26},{12,28},{14,30},{16,0},... | collective-permute-start | bytes 196616 | tf_op jit(solution)/shard_map/ppermute | solution.py:205
  18.9 3.1 %copy-start.2 = (f32[4,128,128]{2,1,0:T(8,128)S(1)}, f32[4,128,128]{2,1,0:T(8,128)}, u32[]{:S(2)}) copy-start(f32[4,128,128]{2,1,0:T(8,128)} %refs_4_.3) | copy-start | bytes 786436
  18.9 5.2 %collective-permute-start.9 = (bf16[256,128]{1,0:T(8,128)(2,1)S(1)}, bf16[256,128]{1,0:T(8,128)(2,1)S(1)}, u32[]{:S(2)}, u32[]{:S(2)}) collective-permute-start(bf16[256,128]{1,0:T(8,128)(2,1)S(1)} %add_convert_fusion.4), channel_id=1, source_target_pairs={{0,16},{2,18},{4,20},{6,22},{8,24},{10,26},{12,28},{14,30},{16,0},... | collective-permute-start | bytes 196616 | tf_op jit(solution)/shard_map/ppermute | solution.py:205
  22.0 1.0 %copy-start.1 = (bf16[256,512]{1,0:T(8,128)(2,1)S(1)}, bf16[256,512]{1,0:T(8,128)(2,1)}, u32[]{:S(2)}) copy-start(bf16[256,512]{1,0:T(8,128)(2,1)} %refs_3_.1) | copy-start | bytes 786436
  22.1 0.9 %copy-start.3 = (f32[512]{0:T(512)S(1)}, f32[512]{0:T(512)}, u32[]{:S(2)}) copy-start(f32[512]{0:T(512)} %param.11) | copy-start | bytes 6148
  24.4 1.2 %collective-permute-start.10 = (f32[8,256]{1,0:T(8,128)S(1)}, f32[8,256]{1,0:T(8,128)S(1)}, u32[]{:S(2)}, u32[]{:S(2)}) collective-permute-start(f32[8,256]{1,0:T(8,128)S(1)} %get-tuple-element.54.refs_0_), channel_id=1, source_target_pairs={{0,1},{1,0},{2,3},{3,2},{4,5},{5,4},{6,7},{7,6},{8,9},{9,8},{10,11... | collective-permute-start | bytes 24584 | tf_op jit(solution)/shard_map/ppermute | solution.py:288
  26.0 5.8 %collective-permute-start.18 = (bf16[272,128]{1,0:T(8,128)(2,1)S(1)}, bf16[272,128]{1,0:T(8,128)(2,1)S(1)}, u32[]{:S(2)}, u32[]{:S(2)}) collective-permute-start(bf16[272,128]{1,0:T(8,128)(2,1)S(1)} %get-tuple-element.65), channel_id=1, source_target_pairs={{0,6},{2,4},{4,2},{6,0},{8,14},{10,12},{12,10},{14,8},{16,22},{18,... | collective-permute-start | bytes 208904 | tf_op jit(solution)/shard_map/ppermute | solution.py:205
  27.7 5.7 %collective-permute-start.17 = (bf16[272,128]{1,0:T(8,128)(2,1)S(1)}, bf16[272,128]{1,0:T(8,128)(2,1)S(1)}, u32[]{:S(2)}, u32[]{:S(2)}) collective-permute-start(bf16[272,128]{1,0:T(8,128)(2,1)S(1)} %get-tuple-element.65), channel_id=1, source_target_pairs={{0,4},{2,6},{4,0},{6,2},{8,12},{10,14},{12,8},{14,10},{16,20},{18,... | collective-permute-start | bytes 208904 | tf_op jit(solution)/shard_map/ppermute | solution.py:205
  28.1 5.3 %collective-permute-start.14 = (bf16[272,128]{1,0:T(8,128)(2,1)S(1)}, bf16[272,128]{1,0:T(8,128)(2,1)S(1)}, u32[]{:S(2)}, u32[]{:S(2)}) collective-permute-start(bf16[272,128]{1,0:T(8,128)(2,1)S(1)} %get-tuple-element.65), channel_id=1, source_target_pairs={{0,2},{2,0},{4,6},{6,4},{8,10},{10,8},{12,14},{14,12},{16,18},{18,... | collective-permute-start | bytes 208904 | tf_op jit(solution)/shard_map/ppermute | solution.py:205
  29.8 6.3 %collective-permute-start.13 = (bf16[256,128]{1,0:T(8,128)(2,1)S(1)}, bf16[256,128]{1,0:T(8,128)(2,1)S(1)}, u32[]{:S(2)}, u32[]{:S(2)}) collective-permute-start(bf16[256,128]{1,0:T(8,128)(2,1)S(1)} %get-tuple-element.64), channel_id=1, source_target_pairs={{0,6},{2,4},{4,2},{6,0},{8,14},{10,12},{12,10},{14,8},{16,22},{18,... | collective-permute-start | bytes 196616 | tf_op jit(solution)/shard_map/ppermute | solution.py:205
  31.5 4.6 %collective-permute-start.12 = (bf16[256,128]{1,0:T(8,128)(2,1)S(1)}, bf16[256,128]{1,0:T(8,128)(2,1)S(1)}, u32[]{:S(2)}, u32[]{:S(2)}) collective-permute-start(bf16[256,128]{1,0:T(8,128)(2,1)S(1)} %get-tuple-element.64), channel_id=1, source_target_pairs={{0,4},{2,6},{4,0},{6,2},{8,12},{10,14},{12,8},{14,10},{16,20},{18,... | collective-permute-start | bytes 196616 | tf_op jit(solution)/shard_map/ppermute | solution.py:205
  31.9 4.3 %collective-permute-start.11 = (bf16[256,128]{1,0:T(8,128)(2,1)S(1)}, bf16[256,128]{1,0:T(8,128)(2,1)S(1)}, u32[]{:S(2)}, u32[]{:S(2)}) collective-permute-start(bf16[256,128]{1,0:T(8,128)(2,1)S(1)} %get-tuple-element.64), channel_id=1, source_target_pairs={{0,2},{2,0},{4,6},{6,4},{8,10},{10,8},{12,14},{14,12},{16,18},{18,... | collective-permute-start | bytes 196616 | tf_op jit(solution)/shard_map/ppermute | solution.py:205
  33.4 4.4 %collective-permute-start.19 = (bf16[272,128]{1,0:T(8,128)(2,1)S(1)}, bf16[272,128]{1,0:T(8,128)(2,1)S(1)}, u32[]{:S(2)}, u32[]{:S(2)}) collective-permute-start(bf16[272,128]{1,0:T(8,128)(2,1)S(1)} %add_convert_fusion.1), channel_id=1, source_target_pairs={{0,8},{2,10},{4,12},{6,14},{8,0},{10,2},{12,4},{14,6},{16,24},{18,... | collective-permute-start | bytes 208904 | tf_op jit(solution)/shard_map/ppermute | solution.py:205
  36.2 5.1 %collective-permute-start.15 = (bf16[256,128]{1,0:T(8,128)(2,1)S(1)}, bf16[256,128]{1,0:T(8,128)(2,1)S(1)}, u32[]{:S(2)}, u32[]{:S(2)}) collective-permute-start(bf16[256,128]{1,0:T(8,128)(2,1)S(1)} %add_convert_fusion.3), channel_id=1, source_target_pairs={{0,8},{2,10},{4,12},{6,14},{8,0},{10,2},{12,4},{14,6},{16,24},{18,... | collective-permute-start | bytes 196616 | tf_op jit(solution)/shard_map/ppermute | solution.py:205
  37.9 7.4 %collective-permute-start.20 = (bf16[272,128]{1,0:T(8,128)(2,1)S(1)}, bf16[272,128]{1,0:T(8,128)(2,1)S(1)}, u32[]{:S(2)}, u32[]{:S(2)}) collective-permute-start(bf16[272,128]{1,0:T(8,128)(2,1)S(1)} %add_convert_fusion.refs_5_), channel_id=1, source_target_pairs={{0,16},{2,18},{4,20},{6,22},{8,24},{10,26},{12,28},{14,30},{16,0},... | collective-permute-start | bytes 208904 | tf_op jit(solution)/shard_map/ppermute | solution.py:205
  41.3 5.2 %collective-permute-start.16 = (bf16[256,128]{1,0:T(8,128)(2,1)S(1)}, bf16[256,128]{1,0:T(8,128)(2,1)S(1)}, u32[]{:S(2)}, u32[]{:S(2)}) collective-permute-start(bf16[256,128]{1,0:T(8,128)(2,1)S(1)} %add_convert_fusion.2.refs_1_), channel_id=1, source_target_pairs={{0,16},{2,18},{4,20},{6,22},{8,24},{10,26},{12,28},{14,30},{16,0},... | collective-permute-start | bytes 196616 | tf_op jit(solution)/shard_map/ppermute | solution.py:205

commit v10 on v8

--- a/solution.py
+++ b/solution.py
@@ -107,31 +107,26 @@
     return [jnp.broadcast_to(row, (dim, length)).T for row in (inverse, factor)]
 
 
-def norm_kernel(halves, n, dim, width, *refs):
-    if n == 0:
-        uns, refs = refs[2 : 2 + len(halves)], refs[:2] + refs[2 + len(halves) :]
-        inverse, factor = scales(refs[0], refs[1], width, dim)
-        refs[-2][...] = inverse
-        refs[-1][...] = factor
-    else:
-        uns, refs = {n: refs[2]}, refs[:2] + refs[3:]
-        inverse, factor = refs[0][...], refs[1][...]
-    cot_ref, gain_ref, q_ref, gun_ref, msg_ref = refs[2:7]
-    for i, h in enumerate(halves[n]):
-        c, r = cols(h, dim), cols(i, dim)
-        cot = cot_ref[:, c].astype(F32)
-        gun = (cot * gain_ref[:, c] * inverse - uns[n][:, r] * factor).astype(BF16)
-        gun_ref[:, r] = gun
-        msg_ref[r, :] = dot(q_ref[c, :], gun, 1, 0).astype(BF16)
-    if n == 0:
-        row = lax.broadcasted_iota(jnp.int32, (EXTRA, dim), 0)
-        gains = jnp.zeros((EXTRA, dim), F32)
-        for heads, un_ref in zip(halves, uns):
-            for i, h in enumerate(heads):
-                normed = un_ref[:, cols(i, dim)] * inverse
-                total = jnp.sum(cot_ref[:, cols(h, dim)].astype(F32) * normed, axis=0, keepdims=True)
-                gains = jnp.where(row == h, total, gains)
-        msg_ref[len(halves[0]) * dim :, :] = gains.astype(BF16)
+def norm_kernel(halves, dim, width, *refs):
+    n = len(halves)
+    sums_ref, other_ref = refs[:2]
+    uns = refs[2 : 2 + n]
+    cot_ref, gain_ref, q_ref = refs[2 + n : 5 + n]
+    guns, messages, inverse_ref = refs[5 + n : 5 + 2 * n], refs[5 + 2 * n : 5 + 3 * n], refs[5 + 3 * n]
+    inverse, factor = scales(sums_ref, other_ref, width, dim)
+    inverse_ref[...] = inverse
+    row = lax.broadcasted_iota(jnp.int32, (EXTRA, dim), 0)
+    gains = jnp.zeros((EXTRA, dim), F32)
+    for heads, un_ref, gun_ref, msg_ref in zip(halves, uns, guns, messages):
+        for i, h in enumerate(heads):
+            c, r = cols(h, dim), cols(i, dim)
+            un = un_ref[:, r]
+            cot = cot_ref[:, c].astype(F32)
+            gun = (cot * gain_ref[:, c] * inverse - un * factor).astype(BF16)
+            gun_ref[:, r] = gun
+            msg_ref[r, :] = dot(q_ref[c, :], gun, 1, 0).astype(BF16)
+            gains = jnp.where(row == h, jnp.sum(cot * (un * inverse), axis=0, keepdims=True), gains)
+    messages[0][len(halves[0]) * dim :, :] = gains.astype(BF16)
 
 
 def attended_kernel(halves, dim, *refs):
@@ -273,24 +268,19 @@
         partner = lax.ppermute(partner, "head", [(i, (i + 1) % head_count) for i in range(head_count)])
         other = other + partner if step > 1 else partner
 
-    guns, messages, scale = [], [], [sums, other]
-    column = shape((length, dim), F32)
-    for n, members in enumerate(halves):
-        gun, message, *kept = call(
-            functools.partial(norm_kernel, halves, n, dim, total_width),
-            (half_bf, shape((per * dim + (EXTRA if n == 0 else 0), dim), BF16)) + (column,) * (2 if n == 0 else 0),
-            block // 2, 3 * size,
-        )(*scale, *(unnormed if n == 0 else unnormed[n:]), cotangent, gain, turned)
-        scale = kept or scale
-        guns.append(gun)
-        messages.append(message)
+    *made, inverse = call(
+        functools.partial(norm_kernel, halves, dim, total_width),
+        (half_bf, half_bf, shape((per * dim + EXTRA, dim), BF16), state_bf, shape((length, dim), F32)),
+        block, 6 * size,
+    )(sums, other, *unnormed, cotangent, gain, turned)
+    guns, messages = made[:2], made[2:]
     inner = (call(
         functools.partial(local_kernel, halves, dim), (tokens_f32, tokens_f32), 4 * square, 8 * size,
     ), *guns, *kvs, queries)
     attended, grad_q = call(
         functools.partial(attended_kernel, halves, dim),
         (tokens_bf, tokens_bf), 2 * square + block, 8 * size,
-    )(*unnormed, *guns, *prefixes, *kvs, scale[0], gain)
+    )(*unnormed, *guns, *prefixes, *kvs, inverse, gain)
     partners, messages, received, done = scan(messages, None, count, {spot: inner})
     local_k, local_v = done[spot]
 

time: 47.8 us -> 47.9 us (level)
  waiting for transfers between devices: 5.52 us -> 6.58 us
  starting transfers between devices: 33.2 us -> 32.4 us
    ppermute x20, waiting for transfers between devices: 4.36 us -> 5.42 us  [swap(): lax.ppermute(message, 'seq', [(i, i ^ partner) for i in range(count)])]
    ppermute x20, starting transfers between devices: 33.1 us -> 32.3 us  [swap(): lax.ppermute(message, 'seq', [(i, i ^ partner) for i in range(count)])]
  transfers between devices with their start and end apart: 21 -> 21, of which waited for: 11 -> 13; matrix products, arithmetic and copies ran while one was open for 1% -> 1% of each run, Pallas kernels for 10% -> 9%
where the time goes in v10:
time: 47.9 us; the launch traced here: 47.7 us
  starting transfers between devices  32.4 us (68%)
  waiting for transfers between devices  6.58 us (14%)
  Pallas kernels  6.5 us (14%)
  local copies, waits for them, and re-layouts  1.11 us (2%)
  between operations  0.81 us (2%)
    ppermute x20, starting transfers between devices, swap(): lax.ppermute(message, 'seq', [(i, i ^ partner) for i in range(count)])  32.3 us
    ppermute x20, waiting for transfers between devices, swap(): lax.ppermute(message, 'seq', [(i, i ^ partner) for i in range(count)])  5.42 us
    pallas_call x2, Pallas kernels, on_device(): call(functools.partial(final_kernel, members, dim, partners, n == 0), res...  1.98 us
    pallas_call x1, Pallas kernels, on_device(): call(functools.partial(attended_kernel, halves, dim), (tokens_bf, tokens_...  1.43 us
    ppermute x1, waiting for transfers between devices, on_device(): lax.ppermute(partner, 'head', [(i, (i + 1) % head_count) for i in range(h...  1.16 us
    slice x2, local copies, waits for them, and re-layouts, on_device(): part[:, n * per * dim:(n + 1) * per * dim]  1.05 us
    pallas_call x1, Pallas kernels, scan(): work = beside[n, distance][0](*operands)  1 us
  transfers between devices with their start and end apart: 21, of which 13 were waited for; matrix products, arithmetic and copies ran while one was open for 1% of the time, Pallas kernels for 9%

profile of v10, /device:TPU:0, one launch (start us, length us, event | category | flops | bytes accessed | tf_op | source)
XLA Modules:
  0.0 47.7 jit_solution(1199763030533092062)
XLA Ops:
  0.6 1.0 %fusion.2 = (bf16[256,256]{1,0:T(8,128)(2,1)S(1)}, bf16[256,256]{1,0:T(8,128)(2,1)S(1)}) fusion(bf16[256,512]{1,0:T(8,128)(2,1)} %param.7), kind=kLoop, calls=%fused_computation.12 | loop fusion | bytes 524288 | tf_op jit(solution)/shard_map/slice | solution.py:242
  1.7 0.0 copy-done.4
  1.8 0.3 shard_map.109
  2.0 4.0 %collective-permute-start.2 = (bf16[256,128]{1,0:T(8,128)(2,1)S(1)}, bf16[256,128]{1,0:T(8,128)(2,1)S(1)}, u32[]{:S(2)}, u32[]{:S(2)}) collective-permute-start(bf16[256,128]{1,0:T(8,128)(2,1)S(1)} %get-tuple-element.45), channel_id=1, source_target_pairs={{0,6},{2,4},{4,2},{6,0},{8,14},{10,12},{12,10},{14,8},{16,22},{18,... | collective-permute-start | bytes 196616 | tf_op jit(solution)/shard_map/ppermute | solution.py:188
  6.0 0.5 %collective-permute-start.1 = (bf16[256,128]{1,0:T(8,128)(2,1)S(1)}, bf16[256,128]{1,0:T(8,128)(2,1)S(1)}, u32[]{:S(2)}, u32[]{:S(2)}) collective-permute-start(bf16[256,128]{1,0:T(8,128)(2,1)S(1)} %get-tuple-element.45), channel_id=1, source_target_pairs={{0,4},{2,6},{4,0},{6,2},{8,12},{10,14},{12,8},{14,10},{16,20},{18,... | collective-permute-start | bytes 196616 | tf_op jit(solution)/shard_map/ppermute | solution.py:188
  6.5 0.1 collective-permute-start
  6.7 2.8 %collective-permute-start.7 = (bf16[256,128]{1,0:T(8,128)(2,1)S(1)}, bf16[256,128]{1,0:T(8,128)(2,1)S(1)}, u32[]{:S(2)}, u32[]{:S(2)}) collective-permute-start(bf16[256,128]{1,0:T(8,128)(2,1)S(1)} %get-tuple-element.49), channel_id=1, source_target_pairs={{0,6},{2,4},{4,2},{6,0},{8,14},{10,12},{12,10},{14,8},{16,22},{18,... | collective-permute-start | bytes 196616 | tf_op jit(solution)/shard_map/ppermute | solution.py:188
  9.5 0.5 %collective-permute-start.6 = (bf16[256,128]{1,0:T(8,128)(2,1)S(1)}, bf16[256,128]{1,0:T(8,128)(2,1)S(1)}, u32[]{:S(2)}, u32[]{:S(2)}) collective-permute-start(bf16[256,128]{1,0:T(8,128)(2,1)S(1)} %get-tuple-element.49), channel_id=1, source_target_pairs={{0,4},{2,6},{4,0},{6,2},{8,12},{10,14},{12,8},{14,10},{16,20},{18,... | collective-permute-start | bytes 196616 | tf_op jit(solution)/shard_map/ppermute | solution.py:188
  10.0 0.6 %collective-permute-start.5 = (bf16[256,128]{1,0:T(8,128)(2,1)S(1)}, bf16[256,128]{1,0:T(8,128)(2,1)S(1)}, u32[]{:S(2)}, u32[]{:S(2)}) collective-permute-start(bf16[256,128]{1,0:T(8,128)(2,1)S(1)} %get-tuple-element.49), channel_id=1, source_target_pairs={{0,2},{2,0},{4,6},{6,4},{8,10},{10,8},{12,14},{14,12},{16,18},{18,... | collective-permute-start | bytes 196616 | tf_op jit(solution)/shard_map/ppermute | solution.py:188
  10.6 0.4 collective-permute-done.1.refs_1_
  11.1 1.6 %collective-permute-start.3 = (bf16[256,128]{1,0:T(8,128)(2,1)S(1)}, bf16[256,128]{1,0:T(8,128)(2,1)S(1)}, u32[]{:S(2)}, u32[]{:S(2)}) collective-permute-start(bf16[256,128]{1,0:T(8,128)(2,1)S(1)} %fusion), channel_id=1, source_target_pairs={{0,8},{2,10},{4,12},{6,14},{8,0},{10,2},{12,4},{14,6},{16,24},{18,... | collective-permute-start | bytes 196616 | tf_op jit(solution)/shard_map/ppermute | solution.py:188
  12.8 0.1 collective-permute-done.7.refs_2_
  12.9 0.9 %collective-permute-done.6.refs_1_ = bf16[256,128]{1,0:T(8,128)(2,1)S(1)} collective-permute-done((bf16[256,128]{1,0:T(8,128)(2,1)S(1)}, bf16[256,128]{1,0:T(8,128)(2,1)S(1)}, u32[]{:S(2)}, u32[]{:S(2)}) %collective-permute-start.6) | collective-permute-done | bytes 65568 | tf_op jit(solution)/shard_map/ppermute | solution.py:188
  13.8 0.5 %collective-permute-done.5.refs_0_ = bf16[256,128]{1,0:T(8,128)(2,1)S(1)} collective-permute-done((bf16[256,128]{1,0:T(8,128)(2,1)S(1)}, bf16[256,128]{1,0:T(8,128)(2,1)S(1)}, u32[]{:S(2)}, u32[]{:S(2)}) %collective-permute-start.5) | collective-permute-done | bytes 65568 | tf_op jit(solution)/shard_map/ppermute | solution.py:188
  14.3 1.6 %collective-permute-start.8 = (bf16[256,128]{1,0:T(8,128)(2,1)S(1)}, bf16[256,128]{1,0:T(8,128)(2,1)S(1)}, u32[]{:S(2)}, u32[]{:S(2)}) collective-permute-start(bf16[256,128]{1,0:T(8,128)(2,1)S(1)} %fusion.1), channel_id=1, source_target_pairs={{0,8},{2,10},{4,12},{6,14},{8,0},{10,2},{12,4},{14,6},{16,24},{18,... | collective-permute-start | bytes 196616 | tf_op jit(solution)/shard_map/ppermute | solution.py:188
  16.0 0.2 collective-permute-done.3.refs_3_
  16.2 0.0 copy-start
  16.2 2.7 %collective-permute-start.4 = (bf16[256,128]{1,0:T(8,128)(2,1)S(1)}, bf16[256,128]{1,0:T(8,128)(2,1)S(1)}, u32[]{:S(2)}, u32[]{:S(2)}) collective-permute-start(bf16[256,128]{1,0:T(8,128)(2,1)S(1)} %add_convert_fusion.5), channel_id=1, source_target_pairs={{0,16},{2,18},{4,20},{6,22},{8,24},{10,26},{12,28},{14,30},{16,0},... | collective-permute-start | bytes 196616 | tf_op jit(solution)/shard_map/ppermute | solution.py:188
  18.9 0.0 copy-start.1
  18.9 2.5 %collective-permute-start.9 = (bf16[256,128]{1,0:T(8,128)(2,1)S(1)}, bf16[256,128]{1,0:T(8,128)(2,1)S(1)}, u32[]{:S(2)}, u32[]{:S(2)}) collective-permute-start(bf16[256,128]{1,0:T(8,128)(2,1)S(1)} %add_convert_fusion.4), channel_id=1, source_target_pairs={{0,16},{2,18},{4,20},{6,22},{8,24},{10,26},{12,28},{14,30},{16,0},... | collective-permute-start | bytes 196616 | tf_op jit(solution)/shard_map/ppermute | solution.py:188
  21.4 0.7 %shard_map.110 = (f32[256,512]{1,0:T(8,128)S(1)}, bf16[512,256]{1,0:T(8,128)(2,1)S(1)}) custom-call(bf16[256,512]{1,0:T(8,128)(2,1)S(1)} %copy-done, bf16[512,256]{1,0:T(8,128)(2,1)S(1)} %get-tuple-element.66.refs_0_.refs_6_.refs_2_, bf16[512,256]{1,0:T(8,128)(2,1)S(1)} %get-tuple-element.67.refs_1_.refs_7_.refs_3_.refs_6_), custom_call_target="tpu_custom_call" | custom-call | flops 134217728 | bytes 1310720 | tf_op jit(solution)/shard_map/pallas_call | solution.py:255
  22.0 0.0 copy-start.3
  22.0 0.8 %collective-permute-done.4.refs_4_ = bf16[256,128]{1,0:T(8,128)(2,1)S(1)} collective-permute-done((bf16[256,128]{1,0:T(8,128)(2,1)S(1)}, bf16[256,128]{1,0:T(8,128)(2,1)S(1)}, u32[]{:S(2)}, u32[]{:S(2)}) %collective-permute-start.4) | collective-permute-done | bytes 65568 | tf_op jit(solution)/shard_map/ppermute | solution.py:188
  22.8 0.4 shard_map.111
  23.2 0.9 %collective-permute-done.9.refs_4_ = bf16[256,128]{1,0:T(8,128)(2,1)S(1)} collective-permute-done((bf16[256,128]{1,0:T(8,128)(2,1)S(1)}, bf16[256,128]{1,0:T(8,128)(2,1)S(1)}, u32[]{:S(2)}, u32[]{:S(2)}) %collective-permute-start.9) | collective-permute-done | bytes 65568 | tf_op jit(solution)/shard_map/ppermute | solution.py:188
  24.1 0.4 shard_map.112
  24.5 0.1 collective-permute-start.10
  24.6 1.2 %collective-permute-done.10.refs_1_ = f32[8,256]{1,0:T(8,128)S(1)} collective-permute-done((f32[8,256]{1,0:T(8,128)S(1)}, f32[8,256]{1,0:T(8,128)S(1)}, u32[]{:S(2)}, u32[]{:S(2)}) %collective-permute-start.10) | collective-permute-done | bytes 8224 | tf_op jit(solution)/shard_map/ppermute | solution.py:268
  25.7 0.4 shard_map.113
  26.2 1.7 %collective-permute-start.18 = (bf16[272,128]{1,0:T(8,128)(2,1)S(1)}, bf16[272,128]{1,0:T(8,128)(2,1)S(1)}, u32[]{:S(2)}, u32[]{:S(2)}) collective-permute-start(bf16[272,128]{1,0:T(8,128)(2,1)S(1)} %get-tuple-element.63), channel_id=1, source_target_pairs={{0,6},{2,4},{4,2},{6,0},{8,14},{10,12},{12,10},{14,8},{16,22},{18,... | collective-permute-start | bytes 208904 | tf_op jit(solution)/shard_map/ppermute | solution.py:188
  27.8 0.4 collective-permute-start.17
  28.2 1.5 %collective-permute-start.14 = (bf16[272,128]{1,0:T(8,128)(2,1)S(1)}, bf16[272,128]{1,0:T(8,128)(2,1)S(1)}, u32[]{:S(2)}, u32[]{:S(2)}) collective-permute-start(bf16[272,128]{1,0:T(8,128)(2,1)S(1)} %get-tuple-element.63), channel_id=1, source_target_pairs={{0,2},{2,0},{4,6},{6,4},{8,10},{10,8},{12,14},{14,12},{16,18},{18,... | collective-permute-start | bytes 208904 | tf_op jit(solution)/shard_map/ppermute | solution.py:188
  29.7 1.6 %collective-permute-start.13 = (bf16[256,128]{1,0:T(8,128)(2,1)S(1)}, bf16[256,128]{1,0:T(8,128)(2,1)S(1)}, u32[]{:S(2)}, u32[]{:S(2)}) collective-permute-start(bf16[256,128]{1,0:T(8,128)(2,1)S(1)} %get-tuple-element.62), channel_id=1, source_target_pairs={{0,6},{2,4},{4,2},{6,0},{8,14},{10,12},{12,10},{14,8},{16,22},{18,... | collective-permute-start | bytes 196616 | tf_op jit(solution)/shard_map/ppermute | solution.py:188
  31.3 0.4 collective-permute-start.12
  31.7 1.5 %collective-permute-start.11 = (bf16[256,128]{1,0:T(8,128)(2,1)S(1)}, bf16[256,128]{1,0:T(8,128)(2,1)S(1)}, u32[]{:S(2)}, u32[]{:S(2)}) collective-permute-start(bf16[256,128]{1,0:T(8,128)(2,1)S(1)} %get-tuple-element.62), channel_id=1, source_target_pairs={{0,2},{2,0},{4,6},{6,4},{8,10},{10,8},{12,14},{14,12},{16,18},{18,... | collective-permute-start | bytes 196616 | tf_op jit(solution)/shard_map/ppermute | solution.py:188
  33.2 0.5 collective-permute-done.17.refs_1_
  33.7 1.6 %collective-permute-start.19 = (bf16[272,128]{1,0:T(8,128)(2,1)S(1)}, bf16[272,128]{1,0:T(8,128)(2,1)S(1)}, u32[]{:S(2)}, u32[]{:S(2)}) collective-permute-start(bf16[272,128]{1,0:T(8,128)(2,1)S(1)} %add_convert_fusion.1), channel_id=1, source_target_pairs={{0,8},{2,10},{4,12},{6,14},{8,0},{10,2},{12,4},{14,6},{16,24},{18,... | collective-permute-start | bytes 208904 | tf_op jit(solution)/shard_map/ppermute | solution.py:188
  35.3 1.0 %shard_map.115 = (f32[256,512]{1,0:T(8,128)S(1)}, f32[256,512]{1,0:T(8,128)S(1)}) custom-call(bf16[256,256]{1,0:T(8,128)(2,1)S(1)} %get-tuple-element.64.refs_2_.refs_0_, bf16[256,256]{1,0:T(8,128)(2,1)S(1)} %get-tuple-element.65.refs_3_.refs_1_, bf16[512,256]{1,0:T(8,128)(2,1)S(1)} %get-tuple-element.66.refs_0_.refs_6_.refs_2_, ...), custom_call_target="tpu_custom_call" | custom-call | flops 268435456 | bytes 2097152 | tf_op jit(solution)/shard_map/pallas_call | solution.py:202
  36.4 1.3 %collective-permute-start.15 = (bf16[256,128]{1,0:T(8,128)(2,1)S(1)}, bf16[256,128]{1,0:T(8,128)(2,1)S(1)}, u32[]{:S(2)}, u32[]{:S(2)}) collective-permute-start(bf16[256,128]{1,0:T(8,128)(2,1)S(1)} %add_convert_fusion.3), channel_id=1, source_target_pairs={{0,8},{2,10},{4,12},{6,14},{8,0},{10,2},{12,4},{14,6},{16,24},{18,... | collective-permute-start | bytes 196616 | tf_op jit(solution)/shard_map/ppermute | solution.py:188
  37.7 0.4 collective-permute-done.19.refs_3_
  38.1 3.0 %collective-permute-start.20 = (bf16[272,128]{1,0:T(8,128)(2,1)S(1)}, bf16[272,128]{1,0:T(8,128)(2,1)S(1)}, u32[]{:S(2)}, u32[]{:S(2)}) collective-permute-start(bf16[272,128]{1,0:T(8,128)(2,1)S(1)} %add_convert_fusion.refs_5_), channel_id=1, source_target_pairs={{0,16},{2,18},{4,20},{6,22},{8,24},{10,26},{12,28},{14,30},{16,0},... | collective-permute-start | bytes 208904 | tf_op jit(solution)/shard_map/ppermute | solution.py:188
  41.1 0.3 collective-permute-done.15.refs_3_
  41.5 2.4 %collective-permute-start.16 = (bf16[256,128]{1,0:T(8,128)(2,1)S(1)}, bf16[256,128]{1,0:T(8,128)(2,1)S(1)}, u32[]{:S(2)}, u32[]{:S(2)}) collective-permute-start(bf16[256,128]{1,0:T(8,128)(2,1)S(1)} %add_convert_fusion.2.refs_5_), channel_id=1, source_target_pairs={{0,16},{2,18},{4,20},{6,22},{8,24},{10,26},{12,28},{14,30},{16,0},... | collective-permute-start | bytes 196616 | tf_op jit(solution)/shard_map/ppermute | solution.py:188
  43.9 1.4 %shard_map.114 = (bf16[256,512]{1,0:T(8,128)(2,1)}, bf16[256,512]{1,0:T(8,128)(2,1)}) custom-call(f32[256,256]{1,0:T(8,128)S(1)} %get-tuple-element.48.refs_2_.refs_0_, f32[256,256]{1,0:T(8,128)S(1)} %get-tuple-element.52.refs_3_.refs_1_, bf16[256,256]{1,0:T(8,128)(2,1)S(1)} %get-tuple-element.64.refs_2_.refs_0_, ...), custom_call_target="tpu_custom_call" | custom-call | flops 167772160 | bytes 2097152 | tf_op jit(solution)/shard_map/pallas_call | solution.py:280
  45.4 0.1 collective-permute-done.20.refs_4_
  45.5 1.0 %shard_map.116 = (bf16[256,512]{1,0:T(8,128)(2,1)}, bf16[256,512]{1,0:T(8,128)(2,1)}, f32[4,128,128]{2,1,0:T(8,128)}, f32[1,512]{1,0:T(1,128)}) custom-call(bf16[272,128]{1,0:T(8,128)(2,1)S(1)} %collective-permute-done.14.refs_0_, bf16[272,128]{1,0:T(8,128)(2,1)S(1)} %collective-permute-done.17.refs_1_, ...), custom_call_target="tpu_custom_call" | custom-call | flops 33554432 | bytes 1835008 | tf_op jit(solution)/shard_map/pallas_call | solution.py:300
  46.5 0.3 collective-permute-done.16.refs_4_
  46.7 1.0 %shard_map.117 = (bf16[256,512]{1,0:T(8,128)(2,1)}, bf16[256,512]{1,0:T(8,128)(2,1)}, f32[4,128,128]{2,1,0:T(8,128)}) custom-call(bf16[256,128]{1,0:T(8,128)(2,1)S(1)} %collective-permute-done.11.refs_0_, bf16[256,128]{1,0:T(8,128)(2,1)S(1)} %collective-permute-done.12.refs_1_, ...), custom_call_target="tpu_custom_call", output_to_operand_aliasing={{0}: (9, {}), {1}: (10, {}), {2}: (11, {})} | custom-call | flops 33554432 | bytes 1835008 | tf_op jit(solution)/shard_map/pallas_call | solution.py:300
  (24 shorter events, 0.4 us)
Async XLA Ops:
  0.6 1.1 %copy-start.4 = (bf16[256,512]{1,0:T(8,128)(2,1)S(1)}, bf16[256,512]{1,0:T(8,128)(2,1)}, u32[]{:S(2)}) copy-start(bf16[256,512]{1,0:T(8,128)(2,1)} %param.8) | copy-start | bytes 786436
  2.0 8.0 %collective-permute-start.2 = (bf16[256,128]{1,0:T(8,128)(2,1)S(1)}, bf16[256,128]{1,0:T(8,128)(2,1)S(1)}, u32[]{:S(2)}, u32[]{:S(2)}) collective-permute-start(bf16[256,128]{1,0:T(8,128)(2,1)S(1)} %get-tuple-element.45), channel_id=1, source_target_pairs={{0,6},{2,4},{4,2},{6,0},{8,14},{10,12},{12,10},{14,8},{16,22},{18,... | collective-permute-start | bytes 196616 | tf_op jit(solution)/shard_map/ppermute | solution.py:188
  6.0 5.1 %collective-permute-start.1 = (bf16[256,128]{1,0:T(8,128)(2,1)S(1)}, bf16[256,128]{1,0:T(8,128)(2,1)S(1)}, u32[]{:S(2)}, u32[]{:S(2)}) collective-permute-start(bf16[256,128]{1,0:T(8,128)(2,1)S(1)} %get-tuple-element.45), channel_id=1, source_target_pairs={{0,4},{2,6},{4,0},{6,2},{8,12},{10,14},{12,8},{14,10},{16,20},{18,... | collective-permute-start | bytes 196616 | tf_op jit(solution)/shard_map/ppermute | solution.py:188
  6.5 4.6 %collective-permute-start = (bf16[256,128]{1,0:T(8,128)(2,1)S(1)}, bf16[256,128]{1,0:T(8,128)(2,1)S(1)}, u32[]{:S(2)}, u32[]{:S(2)}) collective-permute-start(bf16[256,128]{1,0:T(8,128)(2,1)S(1)} %get-tuple-element.45), channel_id=1, source_target_pairs={{0,2},{2,0},{4,6},{6,4},{8,10},{10,8},{12,14},{14,12},{16,18},{18,... | collective-permute-start | bytes 196616 | tf_op jit(solution)/shard_map/ppermute | solution.py:188
  6.7 6.2 %collective-permute-start.7 = (bf16[256,128]{1,0:T(8,128)(2,1)S(1)}, bf16[256,128]{1,0:T(8,128)(2,1)S(1)}, u32[]{:S(2)}, u32[]{:S(2)}) collective-permute-start(bf16[256,128]{1,0:T(8,128)(2,1)S(1)} %get-tuple-element.49), channel_id=1, source_target_pairs={{0,6},{2,4},{4,2},{6,0},{8,14},{10,12},{12,10},{14,8},{16,22},{18,... | collective-permute-start | bytes 196616 | tf_op jit(solution)/shard_map/ppermute | solution.py:188
  9.5 4.3 %collective-permute-start.6 = (bf16[256,128]{1,0:T(8,128)(2,1)S(1)}, bf16[256,128]{1,0:T(8,128)(2,1)S(1)}, u32[]{:S(2)}, u32[]{:S(2)}) collective-permute-start(bf16[256,128]{1,0:T(8,128)(2,1)S(1)} %get-tuple-element.49), channel_id=1, source_target_pairs={{0,4},{2,6},{4,0},{6,2},{8,12},{10,14},{12,8},{14,10},{16,20},{18,... | collective-permute-start | bytes 196616 | tf_op jit(solution)/shard_map/ppermute | solution.py:188
  10.0 4.3 %collective-permute-start.5 = (bf16[256,128]{1,0:T(8,128)(2,1)S(1)}, bf16[256,128]{1,0:T(8,128)(2,1)S(1)}, u32[]{:S(2)}, u32[]{:S(2)}) collective-permute-start(bf16[256,128]{1,0:T(8,128)(2,1)S(1)} %get-tuple-element.49), channel_id=1, source_target_pairs={{0,2},{2,0},{4,6},{6,4},{8,10},{10,8},{12,14},{14,12},{16,18},{18,... | collective-permute-start | bytes 196616 | tf_op jit(solution)/shard_map/ppermute | solution.py:188
  11.1 5.0 %collective-permute-start.3 = (bf16[256,128]{1,0:T(8,128)(2,1)S(1)}, bf16[256,128]{1,0:T(8,128)(2,1)S(1)}, u32[]{:S(2)}, u32[]{:S(2)}) collective-permute-start(bf16[256,128]{1,0:T(8,128)(2,1)S(1)} %fusion), channel_id=1, source_target_pairs={{0,8},{2,10},{4,12},{6,14},{8,0},{10,2},{12,4},{14,6},{16,24},{18,... | collective-permute-start | bytes 196616 | tf_op jit(solution)/shard_map/ppermute | solution.py:188
  14.3 4.5 %collective-permute-start.8 = (bf16[256,128]{1,0:T(8,128)(2,1)S(1)}, bf16[256,128]{1,0:T(8,128)(2,1)S(1)}, u32[]{:S(2)}, u32[]{:S(2)}) collective-permute-start(bf16[256,128]{1,0:T(8,128)(2,1)S(1)} %fusion.1), channel_id=1, source_target_pairs={{0,8},{2,10},{4,12},{6,14},{8,0},{10,2},{12,4},{14,6},{16,24},{18,... | collective-permute-start | bytes 196616 | tf_op jit(solution)/shard_map/ppermute | solution.py:188
  16.2 5.2 %copy-start = (bf16[256,512]{1,0:T(8,128)(2,1)S(1)}, bf16[256,512]{1,0:T(8,128)(2,1)}, u32[]{:S(2)}) copy-start(bf16[256,512]{1,0:T(8,128)(2,1)} %refs_4_.2) | copy-start | bytes 786436
  16.2 6.6 %collective-permute-start.4 = (bf16[256,128]{1,0:T(8,128)(2,1)S(1)}, bf16[256,128]{1,0:T(8,128)(2,1)S(1)}, u32[]{:S(2)}, u32[]{:S(2)}) collective-permute-start(bf16[256,128]{1,0:T(8,128)(2,1)S(1)} %add_convert_fusion.5), channel_id=1, source_target_pairs={{0,16},{2,18},{4,20},{6,22},{8,24},{10,26},{12,28},{14,30},{16,0},... | collective-permute-start | bytes 196616 | tf_op jit(solution)/shard_map/ppermute | solution.py:188
  18.9 3.9 %copy-start.1 = (bf16[256,512]{1,0:T(8,128)(2,1)S(1)}, bf16[256,512]{1,0:T(8,128)(2,1)}, u32[]{:S(2)}) copy-start(bf16[256,512]{1,0:T(8,128)(2,1)} %refs_4_.1) | copy-start | bytes 786436
  18.9 3.9 %copy-start.2 = (f32[4,128,128]{2,1,0:T(8,128)S(1)}, f32[4,128,128]{2,1,0:T(8,128)}, u32[]{:S(2)}) copy-start(f32[4,128,128]{2,1,0:T(8,128)} %refs_9_.1) | copy-start | bytes 786436
  18.9 5.2 %collective-permute-start.9 = (bf16[256,128]{1,0:T(8,128)(2,1)S(1)}, bf16[256,128]{1,0:T(8,128)(2,1)S(1)}, u32[]{:S(2)}, u32[]{:S(2)}) collective-permute-start(bf16[256,128]{1,0:T(8,128)(2,1)S(1)} %add_convert_fusion.4), channel_id=1, source_target_pairs={{0,16},{2,18},{4,20},{6,22},{8,24},{10,26},{12,28},{14,30},{16,0},... | collective-permute-start | bytes 196616 | tf_op jit(solution)/shard_map/ppermute | solution.py:188
  22.0 0.8 %copy-start.3 = (f32[512]{0:T(512)S(1)}, f32[512]{0:T(512)}, u32[]{:S(2)}) copy-start(f32[512]{0:T(512)} %param.11) | copy-start | bytes 6148
  24.5 1.2 %collective-permute-start.10 = (f32[8,256]{1,0:T(8,128)S(1)}, f32[8,256]{1,0:T(8,128)S(1)}, u32[]{:S(2)}, u32[]{:S(2)}) collective-permute-start(f32[8,256]{1,0:T(8,128)S(1)} %get-tuple-element.53.refs_0_), channel_id=1, source_target_pairs={{0,1},{1,0},{2,3},{3,2},{4,5},{5,4},{6,7},{7,6},{8,9},{9,8},{10,11... | collective-permute-start | bytes 24584 | tf_op jit(solution)/shard_map/ppermute | solution.py:268
  26.2 5.6 %collective-permute-start.18 = (bf16[272,128]{1,0:T(8,128)(2,1)S(1)}, bf16[272,128]{1,0:T(8,128)(2,1)S(1)}, u32[]{:S(2)}, u32[]{:S(2)}) collective-permute-start(bf16[272,128]{1,0:T(8,128)(2,1)S(1)} %get-tuple-element.63), channel_id=1, source_target_pairs={{0,6},{2,4},{4,2},{6,0},{8,14},{10,12},{12,10},{14,8},{16,22},{18,... | collective-permute-start | bytes 208904 | tf_op jit(solution)/shard_map/ppermute | solution.py:188
  27.8 5.9 %collective-permute-start.17 = (bf16[272,128]{1,0:T(8,128)(2,1)S(1)}, bf16[272,128]{1,0:T(8,128)(2,1)S(1)}, u32[]{:S(2)}, u32[]{:S(2)}) collective-permute-start(bf16[272,128]{1,0:T(8,128)(2,1)S(1)} %get-tuple-element.63), channel_id=1, source_target_pairs={{0,4},{2,6},{4,0},{6,2},{8,12},{10,14},{12,8},{14,10},{16,20},{18,... | collective-permute-start | bytes 208904 | tf_op jit(solution)/shard_map/ppermute | solution.py:188
  28.2 5.5 %collective-permute-start.14 = (bf16[272,128]{1,0:T(8,128)(2,1)S(1)}, bf16[272,128]{1,0:T(8,128)(2,1)S(1)}, u32[]{:S(2)}, u32[]{:S(2)}) collective-permute-start(bf16[272,128]{1,0:T(8,128)(2,1)S(1)} %get-tuple-element.63), channel_id=1, source_target_pairs={{0,2},{2,0},{4,6},{6,4},{8,10},{10,8},{12,14},{14,12},{16,18},{18,... | collective-permute-start | bytes 208904 | tf_op jit(solution)/shard_map/ppermute | solution.py:188
  29.7 6.6 %collective-permute-start.13 = (bf16[256,128]{1,0:T(8,128)(2,1)S(1)}, bf16[256,128]{1,0:T(8,128)(2,1)S(1)}, u32[]{:S(2)}, u32[]{:S(2)}) collective-permute-start(bf16[256,128]{1,0:T(8,128)(2,1)S(1)} %get-tuple-element.62), channel_id=1, source_target_pairs={{0,6},{2,4},{4,2},{6,0},{8,14},{10,12},{12,10},{14,8},{16,22},{18,... | collective-permute-start | bytes 196616 | tf_op jit(solution)/shard_map/ppermute | solution.py:188
  31.3 5.0 %collective-permute-start.12 = (bf16[256,128]{1,0:T(8,128)(2,1)S(1)}, bf16[256,128]{1,0:T(8,128)(2,1)S(1)}, u32[]{:S(2)}, u32[]{:S(2)}) collective-permute-start(bf16[256,128]{1,0:T(8,128)(2,1)S(1)} %get-tuple-element.62), channel_id=1, source_target_pairs={{0,4},{2,6},{4,0},{6,2},{8,12},{10,14},{12,8},{14,10},{16,20},{18,... | collective-permute-start | bytes 196616 | tf_op jit(solution)/shard_map/ppermute | solution.py:188
  31.7 4.6 %collective-permute-start.11 = (bf16[256,128]{1,0:T(8,128)(2,1)S(1)}, bf16[256,128]{1,0:T(8,128)(2,1)S(1)}, u32[]{:S(2)}, u32[]{:S(2)}) collective-permute-start(bf16[256,128]{1,0:T(8,128)(2,1)S(1)} %get-tuple-element.62), channel_id=1, source_target_pairs={{0,2},{2,0},{4,6},{6,4},{8,10},{10,8},{12,14},{14,12},{16,18},{18,... | collective-permute-start | bytes 196616 | tf_op jit(solution)/shard_map/ppermute | solution.py:188
  33.7 4.4 %collective-permute-start.19 = (bf16[272,128]{1,0:T(8,128)(2,1)S(1)}, bf16[272,128]{1,0:T(8,128)(2,1)S(1)}, u32[]{:S(2)}, u32[]{:S(2)}) collective-permute-start(bf16[272,128]{1,0:T(8,128)(2,1)S(1)} %add_convert_fusion.1), channel_id=1, source_target_pairs={{0,8},{2,10},{4,12},{6,14},{8,0},{10,2},{12,4},{14,6},{16,24},{18,... | collective-permute-start | bytes 208904 | tf_op jit(solution)/shard_map/ppermute | solution.py:188
  36.4 5.1 %collective-permute-start.15 = (bf16[256,128]{1,0:T(8,128)(2,1)S(1)}, bf16[256,128]{1,0:T(8,128)(2,1)S(1)}, u32[]{:S(2)}, u32[]{:S(2)}) collective-permute-start(bf16[256,128]{1,0:T(8,128)(2,1)S(1)} %add_convert_fusion.3), channel_id=1, source_target_pairs={{0,8},{2,10},{4,12},{6,14},{8,0},{10,2},{12,4},{14,6},{16,24},{18,... | collective-permute-start | bytes 196616 | tf_op jit(solution)/shard_map/ppermute | solution.py:188
  38.1 7.3 %collective-permute-start.20 = (bf16[272,128]{1,0:T(8,128)(2,1)S(1)}, bf16[272,128]{1,0:T(8,128)(2,1)S(1)}, u32[]{:S(2)}, u32[]{:S(2)}) collective-permute-start(bf16[272,128]{1,0:T(8,128)(2,1)S(1)} %add_convert_fusion.refs_5_), channel_id=1, source_target_pairs={{0,16},{2,18},{4,20},{6,22},{8,24},{10,26},{12,28},{14,30},{16,0},... | collective-permute-start | bytes 208904 | tf_op jit(solution)/shard_map/ppermute | solution.py:188
  41.5 5.2 %collective-permute-start.16 = (bf16[256,128]{1,0:T(8,128)(2,1)S(1)}, bf16[256,128]{1,0:T(8,128)(2,1)S(1)}, u32[]{:S(2)}, u32[]{:S(2)}) collective-permute-start(bf16[256,128]{1,0:T(8,128)(2,1)S(1)} %add_convert_fusion.2.refs_5_), channel_id=1, source_target_pairs={{0,16},{2,18},{4,20},{6,22},{8,24},{10,26},{12,28},{14,30},{16,0},... | collective-permute-start | bytes 196616 | tf_op jit(solution)/shard_map/ppermute | solution.py:188
